TPU v7x, 32 devices: a whole 2x2x4 slice. The times are simulated.
32 devices in a mesh: seq: 4 (over z), head: 8 (over y, x, core).
Axes of the slice: x: 2, y: 2, z: 4, core: 2. Of those that a mesh axis runs over, the one named last changes fastest.
Arguments:
- tokens: bfloat16 [128, 3, 2048], P('seq', None, 'head'), may hold values from -6 to 6
- states: float32 [128, 32, 128, 128], P('seq', 'head'), may hold values from -4 to 4
- router_ids: int32 [128, 3, 10], P('seq'), may hold values from 0 to 31, all different within a row; in each aligned block of 96 rows (0 to 95, 96 to 191, ..., all dimensions but the last counted through in order) at most 92 rows name the same one
- router_weights: float32 [128, 3, 10], P('seq'), may hold values from 0.02 to 0.3
- input_gain: float32 [2048], replicated, may hold values from 0.25 to 1.75
- w_query: bfloat16 [2048, 2048], P(None, 'head'), may hold values from -0.125 to 0.125
- w_key: bfloat16 [2048, 2048], P(None, 'head'), may hold values from -0.125 to 0.125
- w_value: bfloat16 [2048, 4096], P(None, 'head'), may hold values from -0.125 to 0.125
- w_zgate: bfloat16 [2048, 4096], P(None, 'head'), may hold values from -0.125 to 0.125
- w_beta: bfloat16 [2048, 32], P(None, 'head'), may hold values from -0.125 to 0.125
- w_alpha: bfloat16 [2048, 32], P(None, 'head'), may hold values from -0.125 to 0.125
- decay_scale: float32 [32], P('head'), may hold values from 0.05 to 2
- dt_bias: float32 [32], P('head'), may hold values from -2 to 1
- gated_gain: float32 [128], replicated, may hold values from 0.25 to 1.75
- w_out: bfloat16 [4096, 2048], P('head'), may hold values from -0.09375 to 0.09375
- post_gain: float32 [2048], replicated, may hold values from 0.25 to 1.75
- w_shared_in: bfloat16 [2048, 1024], P('head'), may hold values from -0.125 to 0.125
- w_shared_out: bfloat16 [512, 2048], P(None, 'head'), may hold values from -0.25 to 0.25
- w_expert_in: bfloat16 [32, 2048, 1024], P(('seq', 'head')), may hold values from -0.125 to 0.125
- w_expert_out: bfloat16 [32, 512, 2048], P(('seq', 'head')), may hold values from -0.25 to 0.25
Outputs:
- layer_out: bfloat16 [128, 3, 2048], P('seq', None, 'head')
- states_out: float32 [128, 32, 128, 128], P('seq', 'head')
Inputs may be any that keep to these rules, and one draw needn't show every extreme that they name: `router_ids`: each row names 10 different experts; among the 96 rows of one device (sequence-major order), no expert is named by more than 92 rows, and some expert reaches 92 in some blocks.
All inputs are finite; a program needn't handle non-finite values.
Results may differ from a plain program's by a relative error of at most 0.0061.
Values may be sent and summed in bfloat16 or wider, within the bound.
No kernel may reach another device: no remote copies, remote signals or barrier semaphores. Data moves between devices by JAX's collectives and lax.ppermute only.
A program may use at most 128 MiB of HBM per device.

v0:
```python
import functools

import jax
import jax.numpy as jnp
from jax import lax
from jax.experimental import pallas as pl
from jax.experimental.pallas import tpu as pltpu
from jax.sharding import PartitionSpec as P

DK = 128
DV = 128
EPS = 1e-06
SLOTS = 16
F32 = jnp.float32
BF16 = jnp.bfloat16
VMEM_LIMIT = 56 * 1024 * 1024


def dot(a, b):
    return jnp.dot(a, b, preferred_element_type=F32)


def silu(v):
    return v / (1.0 + jnp.exp(-v))


def split(v):
    high = v.astype(BF16)
    low = (v - high.astype(F32)).astype(BF16)
    return high, low


def exchange(x, axis, bit):
    size = lax.axis_size(axis)
    return lax.ppermute(x, axis, [(i, i ^ bit) for i in range(size)])


def front_kernel(
    steps,
    head_count,
    me_ref,
    x_ref,
    gain_ref,
    small_ref,
    scale_ref,
    bias_ref,
    ggain_ref,
    wq_hbm,
    wk_hbm,
    wv_hbm,
    wz_hbm,
    wo_hbm,
    states_hbm,
    own_ref,
    sib_ref,
    keys_ref,
    delta_ref,
    total_ref,
    wq,
    wk,
    wv,
    wz,
    wo,
    states,
    left,
    recalls,
    sems,
    state_sems,
):
    me = me_ref[0]
    rows = x_ref.shape[1]
    width = x_ref.shape[2]
    seqs = rows // steps
    key_heads = wq.shape[1] // DK
    value_heads = wv.shape[1] // DV
    group = value_heads // key_heads
    pair = group * DV
    copies = []
    for n, (src, dst) in enumerate(((wq_hbm, wq), (wk_hbm, wk), (wv_hbm, wv), (wz_hbm, wz))):
        copies.append(pltpu.make_async_copy(src, dst, sems.at[n]))
        copies[-1].start()
    parts = state_sems.shape[0]
    part = seqs // parts
    state_copies = []
    for n in range(parts):
        span = pl.ds(n * part, part)
        state_copies.append(
            pltpu.make_async_copy(states_hbm.at[span], states.at[span], state_sems.at[n])
        )
        state_copies[-1].start()
    out_copy = pltpu.make_async_copy(wo_hbm, wo, sems.at[4])
    out_copy.start()

    squares = jnp.zeros((rows, 1), F32)
    for j in range(head_count):
        xj = x_ref[j].astype(F32)
        squares = squares + jnp.sum(xj * xj, axis=1, keepdims=True)
    inverse = lax.rsqrt(squares / (head_count * width) + EPS)
    normed = []
    spans = []
    for j in range(head_count):
        block = me ^ j
        normed.append((x_ref[j].astype(F32) * inverse * gain_ref[block]).astype(BF16))
        spans.append(pl.ds(pl.multiple_of(block * width, width), width))

    def project(w_ref):
        total = None
        for j in range(head_count):
            term = dot(normed[j], w_ref[spans[j], :])
            total = term if total is None else total + term
        return total

    small = None
    for j in range(head_count):
        term = lax.dot_general(
            normed[j],
            small_ref[me ^ j],
            (((1,), (1,)), ((), ())),
            preferred_element_type=F32,
        )
        small = term if small is None else small + term
    betas = 1.0 / (1.0 + jnp.exp(-small[:, :value_heads]))
    alphas = small[:, value_heads : 2 * value_heads] + bias_ref[...]
    softplus = jnp.maximum(alphas, 0.0) + jnp.log1p(jnp.exp(-jnp.abs(alphas)))
    decays = jnp.exp(-scale_ref[...] * softplus)

    def units(v):
        return v * lax.rsqrt(jnp.sum(v * v, axis=1, keepdims=True) + EPS)

    copies[0].wait()
    queries_all = silu(project(wq))
    copies[1].wait()
    keys_all = silu(project(wk))
    keys, queries = [], []
    for i in range(key_heads):
        k = units(keys_all[:, i * DK : (i + 1) * DK])
        q = units(queries_all[:, i * DK : (i + 1) * DK]) * DK ** (-0.5)
        keys_ref[i] = k
        keys.append([k[t * seqs : (t + 1) * seqs] for t in range(steps)])
        queries.append([q[t * seqs : (t + 1) * seqs] for t in range(steps)])
        for t in range(steps):
            for at, v in ((t, keys[i][t]), (steps + t, queries[i][t])):
                high = v.astype(BF16).astype(F32)
                left[i, pl.ds(at, seqs, stride=SLOTS), :] = high
                left[i, pl.ds(2 * steps + at, seqs, stride=SLOTS), :] = v - high
        for at in range(4 * steps, SLOTS):
            left[i, pl.ds(at, seqs, stride=SLOTS), :] = jnp.zeros((seqs, DK), F32)
    copies[2].wait()
    values_all = silu(project(wv))
    copies[3].wait()
    gates = silu(project(wz))

    for n in range(parts):
        state_copies[n].wait()

        def one(s, carry):
            base = pl.multiple_of(s * SLOTS, SLOTS)
            for i in range(key_heads):
                lhs = left[i, pl.ds(base, SLOTS), :].astype(BF16)
                rhs = jnp.concatenate([states[s, i * group + u] for u in range(group)], axis=1)
                high, low = split(rhs)
                answer = dot(
                    jnp.concatenate([lhs, lhs], axis=1), jnp.concatenate([high, low], axis=0)
                )
                for u in range(group):
                    recalls[i * group + u, pl.ds(base, SLOTS), :] = answer[:, u * DV : (u + 1) * DV]
            return carry

        lax.fori_loop(n * part, (n + 1) * part, one, 0, unroll=2)

    def wide(columns, t, i):
        return jnp.concatenate(
            [
                jnp.broadcast_to(
                    columns[t * seqs : (t + 1) * seqs, i * group + u : i * group + u + 1],
                    (seqs, DV),
                )
                for u in range(group)
            ],
            axis=1,
        )

    mixed_rows = [[] for _ in range(steps)]
    for i in range(key_heads):
        decay = [wide(decays, t, i) for t in range(steps)]
        beta = [wide(betas, t, i) for t in range(steps)]

        def read(at):
            return jnp.concatenate(
                [
                    recalls[i * group + u, pl.ds(at, seqs, stride=SLOTS), :]
                    + recalls[i * group + u, pl.ds(2 * steps + at, seqs, stride=SLOTS), :]
                    for u in range(group)
                ],
                axis=1,
            )

        deltas = []
        running = None
        for t in range(steps):
            running = decay[t] if running is None else running * decay[t]
            recall = running * read(t)
            answer = running * read(steps + t)
            deltas = [d * decay[t] for d in deltas]
            for u, d in enumerate(deltas):
                recall = recall + d * jnp.sum(keys[i][t] * keys[i][u], axis=1, keepdims=True)
                answer = answer + d * jnp.sum(queries[i][t] * keys[i][u], axis=1, keepdims=True)
            value = values_all[t * seqs : (t + 1) * seqs, i * pair : (i + 1) * pair]
            delta = beta[t] * (value - recall)
            answer = answer + delta * jnp.sum(queries[i][t] * keys[i][t], axis=1, keepdims=True)
            deltas.append(delta)
            mixed_rows[t].append(answer)
        for t in range(steps):
            delta_ref[i, t] = deltas[t]
        total_ref[i] = running
    mixed = jnp.concatenate([jnp.concatenate(m, axis=1) for m in mixed_rows], axis=0)
    gated = []
    for h in range(value_heads):
        m = mixed[:, h * DV : (h + 1) * DV]
        m = m * lax.rsqrt(jnp.mean(m * m, axis=1, keepdims=True) + EPS)
        gated.append((m * ggain_ref[...] * gates[:, h * DV : (h + 1) * DV]).astype(BF16))
    gated = jnp.concatenate(gated, axis=1)
    out_copy.wait()
    for c in range(head_count):
        piece = dot(gated, wo[:, c * width : (c + 1) * width]).astype(BF16)
        away = me ^ c

        @pl.when(away % 2 == 0)
        def _():
            own_ref[away // 2] = piece

        @pl.when(away % 2 == 1)
        def _():
            sib_ref[away // 2] = piece


def front(me, x, gain, small, scale, bias, ggain, wq, wk, wv, wz, wo, states, steps):
    head_count, rows, width = x.shape
    seqs = rows // steps
    key_heads = wq.shape[1] // DK
    value_heads = wv.shape[1] // DV
    pair = value_heads // key_heads * DV
    vmem = pl.BlockSpec(memory_space=pltpu.VMEM)
    any_ = pl.BlockSpec(memory_space=pl.ANY)
    parts = 4
    return pl.pallas_call(
        functools.partial(front_kernel, steps, head_count),
        out_shape=(
            jax.ShapeDtypeStruct((head_count // 2, rows, width), BF16),
            jax.ShapeDtypeStruct((head_count // 2, rows, width), BF16),
            jax.ShapeDtypeStruct((key_heads, rows, DK), F32),
            jax.ShapeDtypeStruct((key_heads, steps, seqs, pair), F32),
            jax.ShapeDtypeStruct((key_heads, seqs, pair), F32),
        ),
        in_specs=[pl.BlockSpec(memory_space=pltpu.SMEM)] + [vmem] * 6 + [any_] * 6,
        out_specs=(vmem,) * 5,
        scratch_shapes=[
            pltpu.VMEM(wq.shape, BF16),
            pltpu.VMEM(wk.shape, BF16),
            pltpu.VMEM(wv.shape, BF16),
            pltpu.VMEM(wz.shape, BF16),
            pltpu.VMEM(wo.shape, BF16),
            pltpu.VMEM(states.shape, F32),
            pltpu.VMEM((key_heads, seqs * SLOTS, DK), F32),
            pltpu.VMEM((value_heads, seqs * SLOTS, DV), F32),
            pltpu.SemaphoreType.DMA((5,)),
            pltpu.SemaphoreType.DMA((parts,)),
        ],
        compiler_params=pltpu.CompilerParams(vmem_limit_bytes=VMEM_LIMIT),
        name="front",
    )(me, x, gain, small, scale, bias, ggain, wq, wk, wv, wz, wo, states)


def update_kernel(steps, keys_ref, delta_ref, total_ref, states_ref, out_ref, left, right):
    key_heads, rows, _ = keys_ref.shape
    seqs = rows // steps
    block = states_ref.shape[0]
    group = states_ref.shape[1] // key_heads
    at_block = pl.program_id(0)

    @pl.when(at_block == 0)
    def _():
        for i in range(key_heads):
            for at in range(SLOTS):
                rows_at = pl.ds(at, seqs, stride=SLOTS)
                t = at % steps
                k = keys_ref[i, t * seqs : (t + 1) * seqs, :]
                k_high = k.astype(BF16).astype(F32)
                k = k - k_high if at >= 2 * steps else k_high
                left[i, rows_at, :] = k if at < 3 * steps else jnp.zeros_like(k)
                for u in range(group):
                    d = delta_ref[i, t, :, u * DV : (u + 1) * DV]
                    d_high = d.astype(BF16).astype(F32)
                    d = d - d_high if steps <= at < 2 * steps else d_high
                    right[i * group + u, rows_at, :] = d if at < 3 * steps else jnp.zeros_like(d)

    def one(s, carry):
        here = at_block * block + s
        base = pl.multiple_of(here * SLOTS, SLOTS)
        for i in range(key_heads):
            lhs = left[i, pl.ds(base, SLOTS), :].astype(BF16)
            rhs = jnp.concatenate(
                [right[i * group + u, pl.ds(base, SLOTS), :] for u in range(group)], axis=1
            ).astype(BF16)
            change = lax.dot_general(
                lhs, rhs, (((0,), (0,)), ((), ())), preferred_element_type=F32
            )
            total = total_ref[i, pl.ds(here, 1), :]
            for u in range(group):
                columns = slice(u * DV, (u + 1) * DV)
                h = i * group + u
                out_ref[s, h] = states_ref[s, h] * total[:, columns] + change[:, columns]
        return carry

    lax.fori_loop(0, block, one, 0, unroll=2)


def update(keys, deltas, totals, states):
    key_heads, steps, seqs, pair = deltas.shape
    blocks = 8
    block = seqs // blocks
    vmem = pl.BlockSpec(memory_space=pltpu.VMEM)
    spec = pl.BlockSpec((block, *states.shape[1:]), lambda n: (n, 0, 0, 0))
    return pl.pallas_call(
        functools.partial(update_kernel, steps),
        out_shape=jax.ShapeDtypeStruct(states.shape, F32),
        grid=(blocks,),
        in_specs=[vmem, vmem, vmem, spec],
        out_specs=spec,
        scratch_shapes=[
            pltpu.VMEM((key_heads, seqs * SLOTS, DK), F32),
            pltpu.VMEM((states.shape[1], seqs * SLOTS, DV), F32),
        ],
        compiler_params=pltpu.CompilerParams(vmem_limit_bytes=VMEM_LIMIT),
        name="update",
    )(keys, deltas, totals, states)


def expert_in_kernel(orders, odd, first, me_ref, *refs):
    a_ref, b_ref, gain_inv_ref, w_ref = refs[:4]
    if first:
        pre_ref, sq_ref = refs[4:]
    else:
        pre_in, sq_in, pre_ref, sq_ref = refs[4:]
    me = me_ref[0]
    start = 0
    for ref, order in zip((a_ref, b_ref), orders):
        count, zs, rows, width = ref.shape
        total, squares = None, None
        for n in range(count):
            block = me ^ (2 * order[n] + odd)
            x = ref[n].reshape(zs * rows, width)
            term = dot(x, w_ref[0, pl.ds(pl.multiple_of(block * width, width), width), :])
            plain = x.astype(F32) * gain_inv_ref[block]
            sq = jnp.sum(plain * plain, axis=1, keepdims=True)
            total = term if total is None else total + term
            squares = sq if squares is None else squares + sq
        span = slice(start, start + zs * rows)
        start += zs * rows
        if not first:
            total = total + pre_in[span, :]
            squares = squares + sq_in[span, :]
        pre_ref[span, :] = total
        sq_ref[span, :] = squares


def expert_in(me, a, b, gain_inv, w, orders, odd, before=None):
    count, zs, rows, width = a.shape
    total = (zs + b.shape[1]) * rows
    vmem = pl.BlockSpec(memory_space=pltpu.VMEM)
    args = (me, a, b, gain_inv, w) + (() if before is None else tuple(before))
    return pl.pallas_call(
        functools.partial(expert_in_kernel, orders, odd, before is None),
        out_shape=(
            jax.ShapeDtypeStruct((total, w.shape[2]), F32),
            jax.ShapeDtypeStruct((total, 1), F32),
        ),
        in_specs=[pl.BlockSpec(memory_space=pltpu.SMEM)] + [vmem] * (len(args) - 1),
        out_specs=(vmem, vmem),
        compiler_params=pltpu.CompilerParams(vmem_limit_bytes=VMEM_LIMIT),
        name="expert_in",
    )(*args)


def expert_out_kernel(orders, me_ref, pre_ref, sq_ref, weight_ref, w_ref, *outs):
    a_own, a_sib, b_own, b_sib = outs
    me = me_ref[0]
    count, zs, rows, width = a_own.shape
    features = w_ref.shape[2]
    hidden_width = w_ref.shape[1]
    start = 0
    for own, sib, order in ((a_own, a_sib, orders[0]), (b_own, b_sib, orders[1])):
        zs = own.shape[1]
        span = slice(start, start + zs * rows)
        start += zs * rows
        inverse = lax.rsqrt(sq_ref[span, :] / features + EPS)
        gate = pre_ref[span, :hidden_width] * inverse
        up = pre_ref[span, hidden_width:] * inverse
        hidden = (silu(gate) * up).astype(BF16)
        weight = weight_ref[span, :]
        for odd, ref in ((1, sib), (0, own)):
            for n in range(count):
                block = me ^ (2 * order[n] + odd)
                columns = pl.ds(pl.multiple_of(block * width, width), width)
                result = dot(hidden, w_ref[0, :, columns]) * weight
                ref[n] = result.astype(BF16).reshape(zs, rows, width)


def expert_out(me, pre, sq, weight, w, orders, shapes):
    vmem = pl.BlockSpec(memory_space=pltpu.VMEM)
    return pl.pallas_call(
        functools.partial(expert_out_kernel, orders),
        out_shape=tuple(jax.ShapeDtypeStruct(s, BF16) for s in shapes),
        in_specs=[pl.BlockSpec(memory_space=pltpu.SMEM)] + [vmem] * 4,
        out_specs=(vmem,) * len(shapes),
        compiler_params=pltpu.CompilerParams(vmem_limit_bytes=VMEM_LIMIT),
        name="expert_out",
    )(me, pre, sq, weight, w)


def bit_reversed(count):
    bits = count.bit_length() - 1
    return [int(format(n, "b").zfill(bits)[::-1], 2) if bits else 0 for n in range(count)]


def add(a, b):
    return (a.astype(F32) + b.astype(F32)).astype(BF16)


def on_device(
    tokens,
    states,
    router_ids,
    router_weights,
    input_gain,
    w_query,
    w_key,
    w_value,
    w_zgate,
    w_beta,
    w_alpha,
    decay_scale,
    dt_bias,
    gated_gain,
    w_out,
    post_gain,
    w_shared_in,
    w_shared_out,
    w_expert_in,
    w_expert_out,
):
    seq_count = lax.axis_size("seq")
    head_count = lax.axis_size("head")
    head_index = lax.axis_index("head")
    seq_index = lax.axis_index("seq")
    me = head_index.astype(jnp.int32).reshape(1)
    seqs, steps, width = tokens.shape
    rows = seqs * steps
    features = head_count * width
    pairs = head_count // 2
    axes = [1 << n for n in range(1, head_count.bit_length() - 1)]

    mine = jnp.transpose(tokens, (1, 0, 2)).reshape(rows, width)

    both = jnp.stack([mine, exchange(mine, "head", 1)])
    gathered = jnp.concatenate(
        [both] + [exchange(both, "head", 2 * p) for p in range(1, pairs)], axis=0
    )

    ids = jnp.transpose(router_ids, (1, 0, 2)).reshape(rows, -1)
    chosen = jnp.transpose(router_weights, (1, 0, 2)).reshape(rows, -1)
    row_weights = []
    for z in range(seq_count):
        target = (seq_index ^ z) * head_count + head_index
        weight = jnp.sum(jnp.where(ids == target, chosen, 0.0), axis=1).reshape(1, rows)
        row_weights.append(exchange(weight, "seq", z) if z else weight)
    row_weight = jnp.concatenate(row_weights, axis=1).reshape(seq_count * rows, 1)

    value_heads = w_beta.shape[1]
    small = jnp.concatenate([w_beta, w_alpha], axis=1)
    small = jnp.transpose(small.reshape(head_count, width, 2 * value_heads), (0, 2, 1))
    small = jnp.pad(small, ((0, 0), (0, -2 * value_heads % 16), (0, 0)))

    own, sib, keys, deltas, totals = front(
        me,
        gathered,
        input_gain.reshape(head_count, 1, width),
        small,
        decay_scale.reshape(1, value_heads),
        dt_bias.reshape(1, value_heads),
        gated_gain.reshape(1, DV),
        w_query,
        w_key,
        w_value,
        w_zgate,
        w_out,
        states,
        steps,
    )

    merged = add(own, exchange(sib, "head", 1))
    resid = mine.astype(F32) + merged[0].astype(F32)
    for p in range(1, pairs):
        resid = resid + exchange(merged[p], "head", 2 * p).astype(F32)
    gain_mine = lax.dynamic_slice_in_dim(post_gain, head_index * width, width, 0)
    x = (resid * gain_mine).astype(BF16)

    half = seq_count // 2
    slabs = [x] + [exchange(x, "seq", z) for z in range(1, seq_count)]
    sides = []
    for slab, bits in ((slabs[:half], axes), (slabs[half:], axes[::-1])):
        side = jnp.stack(slab)[None]
        for bit in bits:
            side = jnp.concatenate([side, exchange(side, "head", bit)], axis=0)
        sides.append(side)
    natural, reverse = list(range(pairs)), bit_reversed(pairs)
    siblings = [exchange(side, "head", 1) for side in sides]

    states_out = update(keys, deltas, totals, states)

    gain_inv = (1.0 / post_gain).reshape(head_count, 1, width)
    orders = (natural, reverse)
    pre = expert_in(me, *sides, gain_inv, w_expert_in, orders, 0)
    pre, squares = expert_in(me, *siblings, gain_inv, w_expert_in, orders, 1, pre)
    shape = (pairs, half, rows, width)
    a_own, a_sib, b_own, b_sib = expert_out(
        me, pre, squares, row_weight, w_expert_out, (reverse, natural), (shape,) * 4
    )
    sums = []
    for own, sib, bits in ((a_own, a_sib, axes), (b_own, b_sib, axes[::-1])):
        total = add(own, exchange(sib, "head", 1))
        for bit in bits:
            middle = total.shape[0] // 2
            total = add(total[:middle], exchange(total[middle:], "head", bit))
        sums.append(total[0])

    shared_pre = dot(x, w_shared_in)
    for bit in [1] + axes:
        sent = shared_pre.astype(BF16)
        shared_pre = sent.astype(F32) + exchange(sent, "head", bit).astype(F32)
    shared_pre = shared_pre * lax.rsqrt(squares[:rows] / features + EPS)
    half_shared = shared_pre.shape[1] // 2
    hidden = (silu(shared_pre[:, :half_shared]) * shared_pre[:, half_shared:]).astype(BF16)
    result = resid + dot(hidden, w_shared_out)

    for z in range(seq_count):
        part = sums[z // half][z % half]
        result = result + (exchange(part, "seq", z) if z else part).astype(F32)
    layer_out = jnp.transpose(result.astype(BF16).reshape(steps, seqs, width), (1, 0, 2))
    return (layer_out, states_out)


def solution(mesh):
    in_specs = (
        P("seq", None, "head"),
        P("seq", "head", None, None),
        P("seq", None, None),
        P("seq", None, None),
        P(),
        P(None, "head"),
        P(None, "head"),
        P(None, "head"),
        P(None, "head"),
        P(None, "head"),
        P(None, "head"),
        P("head"),
        P("head"),
        P(),
        P("head", None),
        P(),
        P("head", None),
        P(None, "head"),
        P(("seq", "head"), None, None),
        P(("seq", "head"), None, None),
    )
    out_specs = (P("seq", None, "head"), P("seq", "head", None, None))
    return jax.shard_map(
        on_device, mesh=mesh, in_specs=in_specs, out_specs=out_specs, check_vma=False
    )
```

profile of v0, /device:TPU:0, one launch (start us, length us, event | category | flops | bytes accessed | tf_op | source)
XLA Modules:
  0.0 116.8 jit_solution(17665356502864029006)
XLA Ops:
  1.2 0.8 pad_maximum_fusion.5
  1.9 0.8 constant_dynamic-update-slice_fusion.4
  2.7 0.6 pad.4.small_ref
  3.4 0.8 pad_maximum_fusion.4
  4.2 3.6 %collective-permute-start.3 = (bf16[2,96,256]{2,1,0:T(8,128)(2,1)S(1)}, bf16[2,96,256]{2,1,0:T(8,128)(2,1)S(1)}, u32[]{:S(2)}, u32[]{:S(2)}) collective-permute-start(bf16[2,96,256]{2,1,0:T(8,128)(2,1)S(1)} %pad_maximum_fusion.4), channel_id=1, source_target_pairs={{0,6},{1,7},{2,4},{3,5},{4,2},{5,3},{6,0},{7,1},{8,14},{9,15},{10,... | collective-permute-start | bytes 294920 | tf_op jit(solution)/shard_map/ppermute | solution.py:35
  8.4 5.1 %collective-permute-done.1 = bf16[2,96,256]{2,1,0:T(8,128)(2,1)S(1)} collective-permute-done((bf16[2,96,256]{2,1,0:T(8,128)(2,1)S(1)}, bf16[2,96,256]{2,1,0:T(8,128)(2,1)S(1)}, u32[]{:S(2)}, u32[]{:S(2)}) %collective-permute-start.1) | collective-permute-done | bytes 98336 | tf_op jit(solution)/shard_map/ppermute | solution.py:35
  13.6 0.7 copy-done.3
  14.3 11.0 %front.1 = (bf16[4,96,256]{2,1,0:T(8,128)(2,1)}, bf16[4,96,256]{2,1,0:T(8,128)(2,1)}, f32[2,96,128]{2,1,0:T(8,128)}, f32[2,3,32,256]{3,2,1,0:T(8,128)}, f32[2,32,256]{2,1,0:T(8,128)}) custom-call(s32[1]{0:T(128)} %bitcast.2.me_ref, bf16[8,96,256]{2,1,0:T(8,128)(2,1)} %copy-done.3, f32[8,1,256]{2,1,0:T(1,128)} %bitcast.72, bf16[8,16,256]{2,1,0:T(8,128)(2,1)} %pad.4.small_ref, ...), custom_call_target="tpu_custom_call" | custom-call | tf_op jit(solution)/shard_map/front/pallas_call | solution.py:246
  25.4 1.6 %collective-permute-done.4 = bf16[4,96,256]{2,1,0:T(8,128)(2,1)S(1)} collective-permute-done((bf16[4,96,256]{2,1,0:T(8,128)(2,1)}, bf16[4,96,256]{2,1,0:T(8,128)(2,1)S(1)}, u32[]{:S(2)}, u32[]{:S(2)}) %collective-permute-start.4) | collective-permute-done | bytes 196640 | tf_op jit(solution)/shard_map/ppermute | solution.py:35
  27.1 1.0 add_convert_fusion.6
  28.1 1.6 %collective-permute-start.5 = (bf16[96,256]{1,0:T(8,128)(2,1)S(1)}, bf16[96,256]{1,0:T(8,128)(2,1)S(1)}, u32[]{:S(2)}, u32[]{:S(2)}) collective-permute-start(bf16[96,256]{1,0:T(8,128)(2,1)S(1)} %get-tuple-element.34), channel_id=1, source_target_pairs={{0,2},{1,3},{2,0},{3,1},{4,6},{5,7},{6,4},{7,5},{8,10},{9,11},{10,... | collective-permute-start | bytes 147464 | tf_op jit(solution)/shard_map/ppermute | solution.py:35
  29.7 1.4 %collective-permute-start.7 = (bf16[96,256]{1,0:T(8,128)(2,1)S(1)}, bf16[96,256]{1,0:T(8,128)(2,1)S(1)}, u32[]{:S(2)}, u32[]{:S(2)}) collective-permute-start(bf16[96,256]{1,0:T(8,128)(2,1)S(1)} %get-tuple-element.35), channel_id=1, source_target_pairs={{0,6},{1,7},{2,4},{3,5},{4,2},{5,3},{6,0},{7,1},{8,14},{9,15},{10,... | collective-permute-start | bytes 147464 | tf_op jit(solution)/shard_map/ppermute | solution.py:35
  31.7 0.7 collective-permute-done.5
  32.4 2.3 %collective-permute-done.7 = bf16[96,256]{1,0:T(8,128)(2,1)S(1)} collective-permute-done((bf16[96,256]{1,0:T(8,128)(2,1)S(1)}, bf16[96,256]{1,0:T(8,128)(2,1)S(1)}, u32[]{:S(2)}, u32[]{:S(2)}) %collective-permute-start.7) | collective-permute-done | bytes 49184 | tf_op jit(solution)/shard_map/ppermute | solution.py:35
  35.2 1.6 %collective-permute-start.11 = (bf16[96,256]{1,0:T(8,128)(2,1)S(1)}, bf16[96,256]{1,0:T(8,128)(2,1)S(1)}, u32[]{:S(2)}, u32[]{:S(2)}) collective-permute-start(bf16[96,256]{1,0:T(8,128)(2,1)S(1)} %get-tuple-element.32), channel_id=1, source_target_pairs={{0,8},{8,0},{16,24},{24,16},{1,9},{9,1},{17,25},{25,17},{2,10},{10... | collective-permute-start | bytes 147464 | tf_op jit(solution)/shard_map/ppermute | solution.py:35
  37.0 2.6 %collective-permute-start.21 = (f32[1,96]{1,0:T(1,128)S(1)}, f32[1,96]{1,0:T(1,128)S(1)}, u32[]{:S(2)}, u32[]{:S(2)}) collective-permute-start(f32[1,96]{1,0:T(1,128)S(1)} %reshape.79), channel_id=1, source_target_pairs={{0,16},{8,24},{16,0},{24,8},{1,17},{9,25},{17,1},{25,9},{2,18},{10... | collective-permute-start | bytes 1160 | tf_op jit(solution)/shard_map/ppermute | solution.py:35
  40.0 0.7 collective-permute-start.20
  40.6 2.9 %collective-permute-start.16 = (bf16[96,256]{1,0:T(8,128)(2,1)S(1)}, bf16[96,256]{1,0:T(8,128)(2,1)S(1)}, u32[]{:S(2)}, u32[]{:S(2)}) collective-permute-start(bf16[96,256]{1,0:T(8,128)(2,1)S(1)} %get-tuple-element.32), channel_id=1, source_target_pairs={{0,24},{8,16},{16,8},{24,0},{1,25},{9,17},{17,9},{25,1},{2,26},{10... | collective-permute-start | bytes 147464 | tf_op jit(solution)/shard_map/ppermute | solution.py:35
  44.2 2.4 %collective-permute-done.16 = bf16[96,256]{1,0:T(8,128)(2,1)S(1)} collective-permute-done((bf16[96,256]{1,0:T(8,128)(2,1)S(1)}, bf16[96,256]{1,0:T(8,128)(2,1)S(1)}, u32[]{:S(2)}, u32[]{:S(2)}) %collective-permute-start.16) | collective-permute-done | bytes 49184 | tf_op jit(solution)/shard_map/ppermute | solution.py:35
  46.6 0.9 collective-permute-start.12
  47.5 1.1 collective-permute-done.15
  48.6 0.8 collective-permute-start.17
  49.3 1.9 %collective-permute-done.12 = bf16[1,2,96,256]{3,2,1,0:T(8,128)(2,1)S(1)} collective-permute-done((bf16[1,2,96,256]{3,2,1,0:T(8,128)(2,1)S(1)}, bf16[1,2,96,256]{3,2,1,0:T(8,128)(2,1)S(1)}, u32[]{:S(2)}, u32[]{:S(2)}) %collective-permute-start.12) | collective-permute-done | bytes 98336 | tf_op jit(solution)/shard_map/ppermute | solution.py:35
  51.2 0.8 collective-permute-start.13
  52.0 1.3 %collective-permute-done.17 = bf16[1,2,96,256]{3,2,1,0:T(8,128)(2,1)S(1)} collective-permute-done((bf16[1,2,96,256]{3,2,1,0:T(8,128)(2,1)S(1)}, bf16[1,2,96,256]{3,2,1,0:T(8,128)(2,1)S(1)}, u32[]{:S(2)}, u32[]{:S(2)}) %collective-permute-start.17) | collective-permute-done | bytes 98336 | tf_op jit(solution)/shard_map/ppermute | solution.py:35
  53.3 1.6 %collective-permute-start.18 = (bf16[2,2,96,256]{3,2,1,0:T(8,128)(2,1)S(1)}, bf16[2,2,96,256]{3,2,1,0:T(8,128)(2,1)S(1)}, u32[]{:S(2)}, u32[]{:S(2)}) collective-permute-start(bf16[2,2,96,256]{3,2,1,0:T(8,128)(2,1)S(1)} %pad_maximum_fusion.3), channel_id=1, source_target_pairs={{0,2},{1,3},{2,0},{3,1},{4,6},{5,7},{6,4},{7,5},{8,10},{9,11},{10,... | collective-permute-start | bytes 589832 | tf_op jit(solution)/shard_map/ppermute | solution.py:35
  55.1 4.0 %collective-permute-done.18 = bf16[2,2,96,256]{3,2,1,0:T(8,128)(2,1)S(1)} collective-permute-done((bf16[2,2,96,256]{3,2,1,0:T(8,128)(2,1)S(1)}, bf16[2,2,96,256]{3,2,1,0:T(8,128)(2,1)S(1)}, u32[]{:S(2)}, u32[]{:S(2)}) %collective-permute-start.18) | collective-permute-done | bytes 196640 | tf_op jit(solution)/shard_map/ppermute | solution.py:35
  59.7 0.7 collective-permute-done.8
  60.7 1.6 %collective-permute-start.9 = (bf16[96,1024]{1,0:T(8,128)(2,1)S(1)}, bf16[96,1024]{1,0:T(8,128)(2,1)S(1)}, u32[]{:S(2)}, u32[]{:S(2)}) collective-permute-start(bf16[96,1024]{1,0:T(8,128)(2,1)S(1)} %add_convert_fusion.5), channel_id=1, source_target_pairs={{0,2},{1,3},{2,0},{3,1},{4,6},{5,7},{6,4},{7,5},{8,10},{9,11},{10,... | collective-permute-start | bytes 589832 | tf_op jit(solution)/shard_map/ppermute | solution.py:35
  62.2 0.6 broadcast_divide_fusion
  63.0 0.8 copy.22.weight_ref
  63.9 4.6 %expert_in.2 = (f32[384,1024]{1,0:T(8,128)}, f32[384,1]{1,0:T(8,128)}) custom-call(s32[1]{0:T(128)} %bitcast.2.me_ref, bf16[4,2,96,256]{3,2,1,0:T(8,128)(2,1)} %copy-done.2, bf16[4,2,96,256]{3,2,1,0:T(8,128)(2,1)} %copy-done.1, f32[8,1,256]{2,1,0:T(1,128)} %bitcast.67, bf16[1,2048,1024]{2,1,0:T(8,128)(2,1)} %refs_3_.3), custom_call_target="tpu_custom_call" | custom-call | tf_op jit(solution)/shard_map/expert_in/pallas_call | solution.py:372
  68.5 0.7 copy-done.7
  69.4 5.2 %expert_in.3 = (f32[384,1024]{1,0:T(8,128)}, f32[384,1]{1,0:T(8,128)}) custom-call(s32[1]{0:T(128)} %bitcast.2.me_ref, bf16[4,2,96,256]{3,2,1,0:T(8,128)(2,1)} %copy-done.8, bf16[4,2,96,256]{3,2,1,0:T(8,128)(2,1)} %copy-done.7, f32[8,1,256]{2,1,0:T(1,128)} %bitcast.68, bf16[1,2048,1024]{2,1,0:T(8,128)(2,1)} %refs_3_.3, ...), custom_call_target="tpu_custom_call" | custom-call | tf_op jit(solution)/shard_map/expert_in/pallas_call | solution.py:372
  74.6 4.2 %expert_out.1 = (bf16[4,2,96,256]{3,2,1,0:T(8,128)(2,1)}, bf16[4,2,96,256]{3,2,1,0:T(8,128)(2,1)}, bf16[4,2,96,256]{3,2,1,0:T(8,128)(2,1)}, bf16[4,2,96,256]{3,2,1,0:T(8,128)(2,1)}) custom-call(s32[1]{0:T(128)} %bitcast.2.me_ref, f32[384,1024]{1,0:T(8,128)} %get-tuple-element.20.pre_ref, f32[384,1]{1,0:T(8,128)} %get-tuple-element.19.sq_ref, ...), custom_call_target="tpu_custom_call" | custom-call | tf_op jit(solution)/shard_map/expert_out/pallas_call | solution.py:411
  78.9 11.6 %update.1 = f32[32,4,128,128]{3,2,1,0:T(8,128)} custom-call(f32[2,96,128]{2,1,0:T(8,128)} %get-tuple-element.25.keys_ref, f32[2,3,32,256]{3,2,1,0:T(8,128)} %get-tuple-element.26.delta_ref, f32[2,32,256]{2,1,0:T(8,128)} %get-tuple-element.27.total_ref, f32[32,4,128,128]{3,2,1,0:T(8,128)} %states_ref.1), custom_call_target="tpu_custom_call" | custom-call | tf_op jit(solution)/shard_map/update/pallas_call | solution.py:324
  91.0 1.3 %collective-permute-start.10 = (bf16[96,1024]{1,0:T(8,128)(2,1)S(1)}, bf16[96,1024]{1,0:T(8,128)(2,1)S(1)}, u32[]{:S(2)}, u32[]{:S(2)}) collective-permute-start(bf16[96,1024]{1,0:T(8,128)(2,1)S(1)} %add_convert_fusion.4), channel_id=1, source_target_pairs={{0,4},{1,5},{2,6},{3,7},{4,0},{5,1},{6,2},{7,3},{8,12},{9,13},{10,... | collective-permute-start | bytes 589832 | tf_op jit(solution)/shard_map/ppermute | solution.py:35
  92.3 0.9 rsqrt_reduce_fusion
  93.6 1.4 %collective-permute-start.28 = (bf16[2,2,96,256]{3,2,1,0:T(8,128)(2,1)S(1)}, bf16[2,2,96,256]{3,2,1,0:T(8,128)(2,1)S(1)}, u32[]{:S(2)}, u32[]{:S(2)}) collective-permute-start(bf16[2,2,96,256]{3,2,1,0:T(8,128)(2,1)S(1)} %slice.93), channel_id=1, source_target_pairs={{0,4},{1,5},{2,6},{3,7},{4,0},{5,1},{6,2},{7,3},{8,12},{9,13},{10,... | collective-permute-start | bytes 589832 | tf_op jit(solution)/shard_map/ppermute | solution.py:35
  95.0 5.0 %collective-permute-done.24 = bf16[2,2,96,256]{3,2,1,0:T(8,128)(2,1)S(1)} collective-permute-done((bf16[2,2,96,256]{3,2,1,0:T(8,128)(2,1)S(1)}, bf16[2,2,96,256]{3,2,1,0:T(8,128)(2,1)S(1)}, u32[]{:S(2)}, u32[]{:S(2)}) %collective-permute-start.24) | collective-permute-done | bytes 196640 | tf_op jit(solution)/shard_map/ppermute | solution.py:35
  100.1 0.9 collective-permute-start.25
  100.9 1.6 %collective-permute-done.28 = bf16[2,2,96,256]{3,2,1,0:T(8,128)(2,1)S(1)} collective-permute-done((bf16[2,2,96,256]{3,2,1,0:T(8,128)(2,1)S(1)}, bf16[2,2,96,256]{3,2,1,0:T(8,128)(2,1)S(1)}, u32[]{:S(2)}, u32[]{:S(2)}) %collective-permute-start.28) | collective-permute-done | bytes 196640 | tf_op jit(solution)/shard_map/ppermute | solution.py:35
  103.1 1.6 %collective-permute-done.25 = bf16[1,2,96,256]{3,2,1,0:T(8,128)(2,1)S(1)} collective-permute-done((bf16[1,2,96,256]{3,2,1,0:T(8,128)(2,1)S(1)}, bf16[1,2,96,256]{3,2,1,0:T(8,128)(2,1)S(1)}, u32[]{:S(2)}, u32[]{:S(2)}) %collective-permute-start.25) | collective-permute-done | bytes 98336 | tf_op jit(solution)/shard_map/ppermute | solution.py:35
  105.3 2.0 %collective-permute-done.29 = bf16[1,2,96,256]{3,2,1,0:T(8,128)(2,1)S(1)} collective-permute-done((bf16[1,2,96,256]{3,2,1,0:T(8,128)(2,1)S(1)}, bf16[1,2,96,256]{3,2,1,0:T(8,128)(2,1)S(1)}, u32[]{:S(2)}, u32[]{:S(2)}) %collective-permute-start.29) | collective-permute-done | bytes 98336 | tf_op jit(solution)/shard_map/ppermute | solution.py:35
  107.4 2.7 %collective-permute-start.30 = (bf16[96,256]{1,0:T(8,128)(2,1)S(1)}, bf16[96,256]{1,0:T(8,128)(2,1)S(1)}, u32[]{:S(2)}, u32[]{:S(2)}) collective-permute-start(bf16[96,256]{1,0:T(8,128)(2,1)S(1)} %get-tuple-element.37), channel_id=1, source_target_pairs={{0,16},{8,24},{16,0},{24,8},{1,17},{9,25},{17,1},{25,9},{2,18},{10... | collective-permute-start | bytes 147464 | tf_op jit(solution)/shard_map/ppermute | solution.py:35
  110.2 2.7 %collective-permute-done.30 = bf16[96,256]{1,0:T(8,128)(2,1)S(1)} collective-permute-done((bf16[96,256]{1,0:T(8,128)(2,1)S(1)}, bf16[96,256]{1,0:T(8,128)(2,1)S(1)}, u32[]{:S(2)}, u32[]{:S(2)}) %collective-permute-start.30) | collective-permute-done | bytes 49184 | tf_op jit(solution)/shard_map/ppermute | solution.py:35
  113.0 3.0 %collective-permute-done.31 = bf16[96,256]{1,0:T(8,128)(2,1)S(1)} collective-permute-done((bf16[96,256]{1,0:T(8,128)(2,1)S(1)}, bf16[96,256]{1,0:T(8,128)(2,1)S(1)}, u32[]{:S(2)}, u32[]{:S(2)}) %collective-permute-start.31) | collective-permute-done | bytes 49184 | tf_op jit(solution)/shard_map/ppermute | solution.py:35
  116.0 0.8 fusion.4
  (93 shorter events, 7.3 us)
Async XLA Ops:
  0.6 54.2 %copy-start = (bf16[256,1024]{1,0:T(8,128)(2,1)S(1)}, bf16[256,1024]{1,0:T(8,128)(2,1)}, u32[]{:S(2)}) copy-start(bf16[256,1024]{1,0:T(8,128)(2,1)} %param.36) | copy-start | bytes 1572868
  0.6 2.7 %collective-permute-start = (bf16[96,256]{1,0:T(8,128)(2,1)}, bf16[96,256]{1,0:T(8,128)(2,1)S(1)}, u32[]{:S(2)}, u32[]{:S(2)}) collective-permute-start(bf16[96,256]{1,0:T(8,128)(2,1)} %bitcast.61), channel_id=1, source_target_pairs={{0,1},{1,0},{2,3},{3,2},{4,5},{5,4},{6,7},{7,6},{8,9},{9,8},{10,11... | collective-permute-start | bytes 147464 | tf_op jit(solution)/shard_map/ppermute | solution.py:35
  4.2 9.4 %collective-permute-start.3 = (bf16[2,96,256]{2,1,0:T(8,128)(2,1)S(1)}, bf16[2,96,256]{2,1,0:T(8,128)(2,1)S(1)}, u32[]{:S(2)}, u32[]{:S(2)}) collective-permute-start(bf16[2,96,256]{2,1,0:T(8,128)(2,1)S(1)} %pad_maximum_fusion.4), channel_id=1, source_target_pairs={{0,6},{1,7},{2,4},{3,5},{4,2},{5,3},{6,0},{7,1},{8,14},{9,15},{10,... | collective-permute-start | bytes 294920 | tf_op jit(solution)/shard_map/ppermute | solution.py:35
  7.7 5.8 %collective-permute-start.2 = (bf16[2,96,256]{2,1,0:T(8,128)(2,1)S(1)}, bf16[2,96,256]{2,1,0:T(8,128)(2,1)S(1)}, u32[]{:S(2)}, u32[]{:S(2)}) collective-permute-start(bf16[2,96,256]{2,1,0:T(8,128)(2,1)S(1)} %pad_maximum_fusion.4), channel_id=1, source_target_pairs={{0,4},{1,5},{2,6},{3,7},{4,0},{5,1},{6,2},{7,3},{8,12},{9,13},{10,... | collective-permute-start | bytes 294920 | tf_op jit(solution)/shard_map/ppermute | solution.py:35
  8.2 5.3 %collective-permute-start.1 = (bf16[2,96,256]{2,1,0:T(8,128)(2,1)S(1)}, bf16[2,96,256]{2,1,0:T(8,128)(2,1)S(1)}, u32[]{:S(2)}, u32[]{:S(2)}) collective-permute-start(bf16[2,96,256]{2,1,0:T(8,128)(2,1)S(1)} %pad_maximum_fusion.4), channel_id=1, source_target_pairs={{0,2},{1,3},{2,0},{3,1},{4,6},{5,7},{6,4},{7,5},{8,10},{9,11},{10,... | collective-permute-start | bytes 294920 | tf_op jit(solution)/shard_map/ppermute | solution.py:35
  13.6 0.7 copy-start.3
  14.3 17.3 %copy-start.11 = (f32[2048]{0:T(1024)S(1)}, f32[2048]{0:T(1024)}, u32[]{:S(2)}) copy-start(f32[2048]{0:T(1024)} %param.35) | copy-start | bytes 24580
  14.3 20.9 %copy-start.4 = (bf16[32,3,256]{2,0,1:T(8,128)(2,1)S(1)}, bf16[32,3,256]{2,0,1:T(8,128)(2,1)}, u32[]{:S(2)}) copy-start(bf16[32,3,256]{2,0,1:T(8,128)(2,1)} %param.20) | copy-start | bytes 147460
  14.3 22.5 %copy-start.9 = (f32[32,3,10]{0,1,2:T(4,128)S(1)}, f32[32,3,10]{0,1,2:T(4,128)}, u32[]{:S(2)}) copy-start(f32[32,3,10]{0,1,2:T(4,128)} %param.23) | copy-start | bytes 11524
  14.3 22.5 %copy-start.10 = (s32[32,3,10]{0,1,2:T(4,128)S(1)}, s32[32,3,10]{0,1,2:T(4,128)}, u32[]{:S(2)}) copy-start(s32[32,3,10]{0,1,2:T(4,128)} %param.22) | copy-start | bytes 11524
  25.3 1.7 %collective-permute-start.4 = (bf16[4,96,256]{2,1,0:T(8,128)(2,1)}, bf16[4,96,256]{2,1,0:T(8,128)(2,1)S(1)}, u32[]{:S(2)}, u32[]{:S(2)}) collective-permute-start(bf16[4,96,256]{2,1,0:T(8,128)(2,1)} %get-tuple-element.16), channel_id=1, source_target_pairs={{0,1},{1,0},{2,3},{3,2},{4,5},{5,4},{6,7},{7,6},{8,9},{9,8},{10,11... | collective-permute-start | bytes 589832 | tf_op jit(solution)/shard_map/ppermute | solution.py:35
  28.1 4.3 %collective-permute-start.5 = (bf16[96,256]{1,0:T(8,128)(2,1)S(1)}, bf16[96,256]{1,0:T(8,128)(2,1)S(1)}, u32[]{:S(2)}, u32[]{:S(2)}) collective-permute-start(bf16[96,256]{1,0:T(8,128)(2,1)S(1)} %get-tuple-element.34), channel_id=1, source_target_pairs={{0,2},{1,3},{2,0},{3,1},{4,6},{5,7},{6,4},{7,5},{8,10},{9,11},{10,... | collective-permute-start | bytes 147464 | tf_op jit(solution)/shard_map/ppermute | solution.py:35
  29.7 5.0 %collective-permute-start.7 = (bf16[96,256]{1,0:T(8,128)(2,1)S(1)}, bf16[96,256]{1,0:T(8,128)(2,1)S(1)}, u32[]{:S(2)}, u32[]{:S(2)}) collective-permute-start(bf16[96,256]{1,0:T(8,128)(2,1)S(1)} %get-tuple-element.35), channel_id=1, source_target_pairs={{0,6},{1,7},{2,4},{3,5},{4,2},{5,3},{6,0},{7,1},{8,14},{9,15},{10,... | collective-permute-start | bytes 147464 | tf_op jit(solution)/shard_map/ppermute | solution.py:35
  31.0 4.2 %collective-permute-start.6 = (bf16[96,256]{1,0:T(8,128)(2,1)S(1)}, bf16[96,256]{1,0:T(8,128)(2,1)S(1)}, u32[]{:S(2)}, u32[]{:S(2)}) collective-permute-start(bf16[96,256]{1,0:T(8,128)(2,1)S(1)} %get-tuple-element.36), channel_id=1, source_target_pairs={{0,4},{1,5},{2,6},{3,7},{4,0},{5,1},{6,2},{7,3},{8,12},{9,13},{10,... | collective-permute-start | bytes 147464 | tf_op jit(solution)/shard_map/ppermute | solution.py:35
  35.2 8.4 %collective-permute-start.11 = (bf16[96,256]{1,0:T(8,128)(2,1)S(1)}, bf16[96,256]{1,0:T(8,128)(2,1)S(1)}, u32[]{:S(2)}, u32[]{:S(2)}) collective-permute-start(bf16[96,256]{1,0:T(8,128)(2,1)S(1)} %get-tuple-element.32), channel_id=1, source_target_pairs={{0,8},{8,0},{16,24},{24,16},{1,9},{9,1},{17,25},{25,17},{2,10},{10... | collective-permute-start | bytes 147464 | tf_op jit(solution)/shard_map/ppermute | solution.py:35
  37.0 23.7 %collective-permute-start.21 = (f32[1,96]{1,0:T(1,128)S(1)}, f32[1,96]{1,0:T(1,128)S(1)}, u32[]{:S(2)}, u32[]{:S(2)}) collective-permute-start(f32[1,96]{1,0:T(1,128)S(1)} %reshape.79), channel_id=1, source_target_pairs={{0,16},{8,24},{16,0},{24,8},{1,17},{9,25},{17,1},{25,9},{2,18},{10... | collective-permute-start | bytes 1160 | tf_op jit(solution)/shard_map/ppermute | solution.py:35
  39.7 23.3 %collective-permute-start.22 = (f32[1,96]{1,0:T(1,128)S(1)}, f32[1,96]{1,0:T(1,128)S(1)}, u32[]{:S(2)}, u32[]{:S(2)}) collective-permute-start(f32[1,96]{1,0:T(1,128)S(1)} %reshape.80), channel_id=1, source_target_pairs={{0,24},{8,16},{16,8},{24,0},{1,25},{9,17},{17,9},{25,1},{2,26},{10... | collective-permute-start | bytes 1160 | tf_op jit(solution)/shard_map/ppermute | solution.py:35
  40.0 23.0 %collective-permute-start.20 = (f32[1,96]{1,0:T(1,128)S(1)}, f32[1,96]{1,0:T(1,128)S(1)}, u32[]{:S(2)}, u32[]{:S(2)}) collective-permute-start(f32[1,96]{1,0:T(1,128)S(1)} %reshape.78), channel_id=1, source_target_pairs={{0,8},{8,0},{16,24},{24,16},{1,9},{9,1},{17,25},{25,17},{2,10},{10... | collective-permute-start | bytes 1160 | tf_op jit(solution)/shard_map/ppermute | solution.py:35
  40.6 5.9 %collective-permute-start.16 = (bf16[96,256]{1,0:T(8,128)(2,1)S(1)}, bf16[96,256]{1,0:T(8,128)(2,1)S(1)}, u32[]{:S(2)}, u32[]{:S(2)}) collective-permute-start(bf16[96,256]{1,0:T(8,128)(2,1)S(1)} %get-tuple-element.32), channel_id=1, source_target_pairs={{0,24},{8,16},{16,8},{24,0},{1,25},{9,17},{17,9},{25,1},{2,26},{10... | collective-permute-start | bytes 147464 | tf_op jit(solution)/shard_map/ppermute | solution.py:35
  43.6 5.0 %collective-permute-start.15 = (bf16[96,256]{1,0:T(8,128)(2,1)S(1)}, bf16[96,256]{1,0:T(8,128)(2,1)S(1)}, u32[]{:S(2)}, u32[]{:S(2)}) collective-permute-start(bf16[96,256]{1,0:T(8,128)(2,1)S(1)} %get-tuple-element.32), channel_id=1, source_target_pairs={{0,16},{8,24},{16,0},{24,8},{1,17},{9,25},{17,1},{25,9},{2,18},{10... | collective-permute-start | bytes 147464 | tf_op jit(solution)/shard_map/ppermute | solution.py:35
  46.6 4.6 %collective-permute-start.12 = (bf16[1,2,96,256]{3,2,1,0:T(8,128)(2,1)S(1)}, bf16[1,2,96,256]{3,2,1,0:T(8,128)(2,1)S(1)}, u32[]{:S(2)}, u32[]{:S(2)}) collective-permute-start(bf16[1,2,96,256]{3,2,1,0:T(8,128)(2,1)S(1)} %maximum_bitcast_fusion), channel_id=1, source_target_pairs={{0,2},{1,3},{2,0},{3,1},{4,6},{5,7},{6,4},{7,5},{8,10},{9,11},{10,... | collective-permute-start | bytes 294920 | tf_op jit(solution)/shard_map/ppermute | solution.py:35
  48.6 4.7 %collective-permute-start.17 = (bf16[1,2,96,256]{3,2,1,0:T(8,128)(2,1)S(1)}, bf16[1,2,96,256]{3,2,1,0:T(8,128)(2,1)S(1)}, u32[]{:S(2)}, u32[]{:S(2)}) collective-permute-start(bf16[1,2,96,256]{3,2,1,0:T(8,128)(2,1)S(1)} %maximum_bitcast_fusion.1), channel_id=1, source_target_pairs={{0,4},{1,5},{2,6},{3,7},{4,0},{5,1},{6,2},{7,3},{8,12},{9,13},{10,... | collective-permute-start | bytes 294920 | tf_op jit(solution)/shard_map/ppermute | solution.py:35
  51.2 7.9 %collective-permute-start.13 = (bf16[2,2,96,256]{3,2,1,0:T(8,128)(2,1)S(1)}, bf16[2,2,96,256]{3,2,1,0:T(8,128)(2,1)S(1)}, u32[]{:S(2)}, u32[]{:S(2)}) collective-permute-start(bf16[2,2,96,256]{3,2,1,0:T(8,128)(2,1)S(1)} %pad_maximum_fusion.2), channel_id=1, source_target_pairs={{0,4},{1,5},{2,6},{3,7},{4,0},{5,1},{6,2},{7,3},{8,12},{9,13},{10,... | collective-permute-start | bytes 589832 | tf_op jit(solution)/shard_map/ppermute | solution.py:35
  53.3 5.7 %collective-permute-start.18 = (bf16[2,2,96,256]{3,2,1,0:T(8,128)(2,1)S(1)}, bf16[2,2,96,256]{3,2,1,0:T(8,128)(2,1)S(1)}, u32[]{:S(2)}, u32[]{:S(2)}) collective-permute-start(bf16[2,2,96,256]{3,2,1,0:T(8,128)(2,1)S(1)} %pad_maximum_fusion.3), channel_id=1, source_target_pairs={{0,2},{1,3},{2,0},{3,1},{4,6},{5,7},{6,4},{7,5},{8,10},{9,11},{10,... | collective-permute-start | bytes 589832 | tf_op jit(solution)/shard_map/ppermute | solution.py:35
  59.0 1.4 %collective-permute-start.8 = (bf16[96,1024]{1,0:T(8,128)(2,1)S(1)}, bf16[96,1024]{1,0:T(8,128)(2,1)S(1)}, u32[]{:S(2)}, u32[]{:S(2)}) collective-permute-start(bf16[96,1024]{1,0:T(8,128)(2,1)S(1)} %convolution_convert_fusion), channel_id=1, source_target_pairs={{0,1},{1,0},{2,3},{3,2},{4,5},{5,4},{6,7},{7,6},{8,9},{9,8},{10,11... | collective-permute-start | bytes 589832 | tf_op jit(solution)/shard_map/ppermute | solution.py:35
  59.1 4.8 %copy-start.1 = (bf16[4,2,96,256]{3,2,1,0:T(8,128)(2,1)}, bf16[4,2,96,256]{3,2,1,0:T(8,128)(2,1)S(1)}, u32[]{:S(2)}) copy-start(bf16[4,2,96,256]{3,2,1,0:T(8,128)(2,1)S(1)} %pad_maximum_fusion.1.refs_1_) | copy-start | bytes 1179652
  59.1 9.4 %collective-permute-start.19 = (bf16[4,2,96,256]{3,2,1,0:T(8,128)(2,1)S(1)}, bf16[4,2,96,256]{3,2,1,0:T(8,128)(2,1)S(1)}, u32[]{:S(2)}, u32[]{:S(2)}) collective-permute-start(bf16[4,2,96,256]{3,2,1,0:T(8,128)(2,1)S(1)} %pad_maximum_fusion.1.refs_1_), channel_id=1, source_target_pairs={{0,1},{1,0},{2,3},{3,2},{4,5},{5,4},{6,7},{7,6},{8,9},{9,8},{10,11... | collective-permute-start | bytes 1179656 | tf_op jit(solution)/shard_map/ppermute | solution.py:35
  59.7 4.2 %copy-start.2 = (bf16[4,2,96,256]{3,2,1,0:T(8,128)(2,1)}, bf16[4,2,96,256]{3,2,1,0:T(8,128)(2,1)S(1)}, u32[]{:S(2)}) copy-start(bf16[4,2,96,256]{3,2,1,0:T(8,128)(2,1)S(1)} %pad_maximum_fusion.refs_0_) | copy-start | bytes 1179652
  60.5 8.1 %collective-permute-start.14 = (bf16[4,2,96,256]{3,2,1,0:T(8,128)(2,1)S(1)}, bf16[4,2,96,256]{3,2,1,0:T(8,128)(2,1)S(1)}, u32[]{:S(2)}, u32[]{:S(2)}) collective-permute-start(bf16[4,2,96,256]{3,2,1,0:T(8,128)(2,1)S(1)} %pad_maximum_fusion.refs_0_), channel_id=1, source_target_pairs={{0,1},{1,0},{2,3},{3,2},{4,5},{5,4},{6,7},{7,6},{8,9},{9,8},{10,11... | collective-permute-start | bytes 1179656 | tf_op jit(solution)/shard_map/ppermute | solution.py:35
  60.7 30.3 %collective-permute-start.9 = (bf16[96,1024]{1,0:T(8,128)(2,1)S(1)}, bf16[96,1024]{1,0:T(8,128)(2,1)S(1)}, u32[]{:S(2)}, u32[]{:S(2)}) collective-permute-start(bf16[96,1024]{1,0:T(8,128)(2,1)S(1)} %add_convert_fusion.5), channel_id=1, source_target_pairs={{0,2},{1,3},{2,0},{3,1},{4,6},{5,7},{6,4},{7,5},{8,10},{9,11},{10,... | collective-permute-start | bytes 589832 | tf_op jit(solution)/shard_map/ppermute | solution.py:35
  68.5 0.7 copy-start.7
  68.5 0.9 copy-start.8
  78.8 14.4 %collective-permute-start.23 = (bf16[4,2,96,256]{3,2,1,0:T(8,128)(2,1)}, bf16[4,2,96,256]{3,2,1,0:T(8,128)(2,1)S(1)}, u32[]{:S(2)}, u32[]{:S(2)}) collective-permute-start(bf16[4,2,96,256]{3,2,1,0:T(8,128)(2,1)} %get-tuple-element.22), channel_id=1, source_target_pairs={{0,1},{1,0},{2,3},{3,2},{4,5},{5,4},{6,7},{7,6},{8,9},{9,8},{10,11... | collective-permute-start | bytes 1179656 | tf_op jit(solution)/shard_map/ppermute | solution.py:35
  78.9 11.6 %copy-start.12 = (bf16[4,2,96,256]{3,2,1,0:T(8,128)(2,1)S(1)}, bf16[4,2,96,256]{3,2,1,0:T(8,128)(2,1)}, u32[]{:S(2)}) copy-start(bf16[4,2,96,256]{3,2,1,0:T(8,128)(2,1)} %get-tuple-element.24) | copy-start | bytes 1179652
  78.9 14.3 %copy-start.6 = (bf16[4,2,96,256]{3,2,1,0:T(8,128)(2,1)S(1)}, bf16[4,2,96,256]{3,2,1,0:T(8,128)(2,1)}, u32[]{:S(2)}) copy-start(bf16[4,2,96,256]{3,2,1,0:T(8,128)(2,1)} %get-tuple-element.21) | copy-start | bytes 1179652
  90.5 3.0 %copy-start.5 = (bf16[4,2,96,256]{3,2,1,0:T(8,128)(2,1)S(1)}, bf16[4,2,96,256]{3,2,1,0:T(8,128)(2,1)}, u32[]{:S(2)}) copy-start(bf16[4,2,96,256]{3,2,1,0:T(8,128)(2,1)} %get-tuple-element.23) | copy-start | bytes 1179652
  90.5 3.0 %collective-permute-start.27 = (bf16[4,2,96,256]{3,2,1,0:T(8,128)(2,1)S(1)}, bf16[4,2,96,256]{3,2,1,0:T(8,128)(2,1)S(1)}, u32[]{:S(2)}, u32[]{:S(2)}) collective-permute-start(bf16[4,2,96,256]{3,2,1,0:T(8,128)(2,1)S(1)} %copy-done.12), channel_id=1, source_target_pairs={{0,1},{1,0},{2,3},{3,2},{4,5},{5,4},{6,7},{7,6},{8,9},{9,8},{10,11... | collective-permute-start | bytes 1179656 | tf_op jit(solution)/shard_map/ppermute | solution.py:35
  91.0 19.1 %collective-permute-start.10 = (bf16[96,1024]{1,0:T(8,128)(2,1)S(1)}, bf16[96,1024]{1,0:T(8,128)(2,1)S(1)}, u32[]{:S(2)}, u32[]{:S(2)}) collective-permute-start(bf16[96,1024]{1,0:T(8,128)(2,1)S(1)} %add_convert_fusion.4), channel_id=1, source_target_pairs={{0,4},{1,5},{2,6},{3,7},{4,0},{5,1},{6,2},{7,3},{8,12},{9,13},{10,... | collective-permute-start | bytes 589832 | tf_op jit(solution)/shard_map/ppermute | solution.py:35
  93.3 6.6 %collective-permute-start.24 = (bf16[2,2,96,256]{3,2,1,0:T(8,128)(2,1)S(1)}, bf16[2,2,96,256]{3,2,1,0:T(8,128)(2,1)S(1)}, u32[]{:S(2)}, u32[]{:S(2)}) collective-permute-start(bf16[2,2,96,256]{3,2,1,0:T(8,128)(2,1)S(1)} %slice.87), channel_id=1, source_target_pairs={{0,2},{1,3},{2,0},{3,1},{4,6},{5,7},{6,4},{7,5},{8,10},{9,11},{10,... | collective-permute-start | bytes 589832 | tf_op jit(solution)/shard_map/ppermute | solution.py:35
  93.6 22.4 %copy-start.13 = (bf16[512,256]{1,0:T(8,128)(2,1)S(1)}, bf16[512,256]{1,0:T(8,128)(2,1)}, u32[]{:S(2)}) copy-start(bf16[512,256]{1,0:T(8,128)(2,1)} %param.37) | copy-start | bytes 786436
  93.6 9.0 %collective-permute-start.28 = (bf16[2,2,96,256]{3,2,1,0:T(8,128)(2,1)S(1)}, bf16[2,2,96,256]{3,2,1,0:T(8,128)(2,1)S(1)}, u32[]{:S(2)}, u32[]{:S(2)}) collective-permute-start(bf16[2,2,96,256]{3,2,1,0:T(8,128)(2,1)S(1)} %slice.93), channel_id=1, source_target_pairs={{0,4},{1,5},{2,6},{3,7},{4,0},{5,1},{6,2},{7,3},{8,12},{9,13},{10,... | collective-permute-start | bytes 589832 | tf_op jit(solution)/shard_map/ppermute | solution.py:35
  100.1 4.7 %collective-permute-start.25 = (bf16[1,2,96,256]{3,2,1,0:T(8,128)(2,1)S(1)}, bf16[1,2,96,256]{3,2,1,0:T(8,128)(2,1)S(1)}, u32[]{:S(2)}, u32[]{:S(2)}) collective-permute-start(bf16[1,2,96,256]{3,2,1,0:T(8,128)(2,1)S(1)} %slice.89), channel_id=1, source_target_pairs={{0,4},{1,5},{2,6},{3,7},{4,0},{5,1},{6,2},{7,3},{8,12},{9,13},{10,... | collective-permute-start | bytes 294920 | tf_op jit(solution)/shard_map/ppermute | solution.py:35
  102.6 4.7 %collective-permute-start.29 = (bf16[1,2,96,256]{3,2,1,0:T(8,128)(2,1)S(1)}, bf16[1,2,96,256]{3,2,1,0:T(8,128)(2,1)S(1)}, u32[]{:S(2)}, u32[]{:S(2)}) collective-permute-start(bf16[1,2,96,256]{3,2,1,0:T(8,128)(2,1)S(1)} %slice.95), channel_id=1, source_target_pairs={{0,2},{1,3},{2,0},{3,1},{4,6},{5,7},{6,4},{7,5},{8,10},{9,11},{10,... | collective-permute-start | bytes 294920 | tf_op jit(solution)/shard_map/ppermute | solution.py:35
  104.8 5.4 %collective-permute-start.26 = (bf16[96,256]{1,0:T(8,128)(2,1)S(1)}, bf16[96,256]{1,0:T(8,128)(2,1)S(1)}, u32[]{:S(2)}, u32[]{:S(2)}) collective-permute-start(bf16[96,256]{1,0:T(8,128)(2,1)S(1)} %slice_bitcast_fusion.2), channel_id=1, source_target_pairs={{0,8},{8,0},{16,24},{24,16},{1,9},{9,1},{17,25},{25,17},{2,10},{10... | collective-permute-start | bytes 147464 | tf_op jit(solution)/shard_map/ppermute | solution.py:35
  107.4 5.6 %collective-permute-start.30 = (bf16[96,256]{1,0:T(8,128)(2,1)S(1)}, bf16[96,256]{1,0:T(8,128)(2,1)S(1)}, u32[]{:S(2)}, u32[]{:S(2)}) collective-permute-start(bf16[96,256]{1,0:T(8,128)(2,1)S(1)} %get-tuple-element.37), channel_id=1, source_target_pairs={{0,16},{8,24},{16,0},{24,8},{1,17},{9,25},{17,1},{25,9},{2,18},{10... | collective-permute-start | bytes 147464 | tf_op jit(solution)/shard_map/ppermute | solution.py:35
  110.1 5.9 %collective-permute-start.31 = (bf16[96,256]{1,0:T(8,128)(2,1)S(1)}, bf16[96,256]{1,0:T(8,128)(2,1)S(1)}, u32[]{:S(2)}, u32[]{:S(2)}) collective-permute-start(bf16[96,256]{1,0:T(8,128)(2,1)S(1)} %get-tuple-element.38), channel_id=1, source_target_pairs={{0,24},{8,16},{16,8},{24,0},{1,25},{9,17},{17,9},{25,1},{2,26},{10... | collective-permute-start | bytes 147464 | tf_op jit(solution)/shard_map/ppermute | solution.py:35
where the time goes:
time: 117 us
  waiting for transfers between devices  37.7 us (32%)
  Pallas kernels  36.6 us (31%)
  starting transfers between devices  31.1 us (27%)
  other arithmetic  4.9 us (4%)
  local copies, waits for them, and re-layouts  4.43 us (4%)
    ppermute x32, waiting for transfers between devices, exchange(): return lax.ppermute(x, axis, [(i, i ^ bit) for i in range(size)])  37.7 us
    ppermute x32, starting transfers between devices, exchange(): return lax.ppermute(x, axis, [(i, i ^ bit) for i in range(size)])  31.1 us
    pallas_call x1, Pallas kernels, update(): pl.pallas_call(functools.partial(update_kernel, steps), out_shape=jax.Sha...  11.6 us
    pallas_call x1, Pallas kernels, front(): pl.pallas_call(functools.partial(front_kernel, steps, head_count), out_sh...  11 us
    pallas_call x2, Pallas kernels, expert_in(): pl.pallas_call(functools.partial(expert_in_kernel, orders, odd, before is...  9.86 us
    pallas_call x1, Pallas kernels, expert_out(): pl.pallas_call(functools.partial(expert_out_kernel, orders), out_shape=tu...  4.22 us
    unnamed x32, local copies, waits for them, and re-layouts  2.48 us
  transfers between devices with their start and end apart: 32, of which 17 were waited for; matrix products, arithmetic and copies ran while one was open for 5% of the time, Pallas kernels for 22%

commit v1 on v0

v1 whole, which is shorter than its diff:
```python
import functools

import jax
import jax.numpy as jnp
from jax import lax
from jax.experimental import pallas as pl
from jax.experimental.pallas import tpu as pltpu
from jax.sharding import PartitionSpec as P

DK = 128
DV = 128
EPS = 1e-06
SLOTS = 16
F32 = jnp.float32
BF16 = jnp.bfloat16
VMEM_LIMIT = 16 * 1024 * 1024


def dot(a, b):
    return jnp.dot(a, b, preferred_element_type=F32)


def silu(v):
    return v / (1.0 + jnp.exp(-v))


def split(v):
    high = v.astype(BF16)
    low = (v - high.astype(F32)).astype(BF16)
    return high, low


def pin(x):
    return pltpu.with_memory_space_constraint(x, pltpu.VMEM)


VMEM_SPEC = pl.BlockSpec(memory_space=pltpu.VMEM)
SMEM_SPEC = pl.BlockSpec(memory_space=pltpu.SMEM)
ANY_SPEC = pl.BlockSpec(memory_space=pl.ANY)


def call(body, name, out_shapes, smem, pinned, loose=(), scratch=(), aliases=None, outs=None):
    return pl.pallas_call(
        body,
        out_shape=tuple(out_shapes),
        in_specs=[SMEM_SPEC] * len(smem) + [VMEM_SPEC] * len(pinned) + [ANY_SPEC] * len(loose),
        out_specs=tuple(outs or [VMEM_SPEC] * len(out_shapes)),
        scratch_shapes=list(scratch),
        input_output_aliases=aliases or {},
        compiler_params=pltpu.CompilerParams(vmem_limit_bytes=VMEM_LIMIT),
        name=name,
    )(*smem, *(pin(x) for x in pinned), *loose)


def exchange(x, axis, bit):
    size = lax.axis_size(axis)
    return lax.ppermute(x, axis, [(i, i ^ bit) for i in range(size)])


def stack_kernel(a_ref, b_ref, out_ref):
    out_ref[0] = a_ref[...]
    out_ref[1] = b_ref[...]


def stack(a, b):
    [out] = call(stack_kernel, "stack", [pltpu.VMEM((2, *a.shape), a.dtype)], (), (a, b))
    return out


def front_kernel(
    steps,
    head_count,
    me_ref,
    *refs,
):
    x_refs = refs[: head_count // 2]
    (
        gain_ref,
        small_ref,
        scale_ref,
        bias_ref,
        ggain_ref,
        wq,
        wk,
        wv,
        wz,
        wo,
        states,
        _,
        own_ref,
        sib_ref,
        keys_ref,
        delta_ref,
        total_ref,
        left,
        recalls,
    ) = refs[head_count // 2 :]
    me = me_ref[0]
    _, rows, width = x_refs[0].shape
    seqs = rows // steps
    key_heads = wq.shape[1] // DK
    value_heads = wv.shape[1] // DV
    group = value_heads // key_heads
    pair = group * DV

    squares = jnp.zeros((rows, 1), F32)
    for j in range(head_count):
        xj = x_refs[j // 2][j % 2].astype(F32)
        squares = squares + jnp.sum(xj * xj, axis=1, keepdims=True)
    inverse = lax.rsqrt(squares / (head_count * width) + EPS)
    normed = []
    spans = []
    for j in range(head_count):
        block = me ^ j
        normed.append((x_refs[j // 2][j % 2].astype(F32) * inverse * gain_ref[block]).astype(BF16))
        spans.append(pl.ds(pl.multiple_of(block * width, width), width))

    def project(w_ref):
        total = None
        for j in range(head_count):
            term = dot(normed[j], w_ref[spans[j], :])
            total = term if total is None else total + term
        return total

    small = None
    for j in range(head_count):
        term = lax.dot_general(
            normed[j],
            small_ref[me ^ j],
            (((1,), (1,)), ((), ())),
            preferred_element_type=F32,
        )
        small = term if small is None else small + term
    betas = 1.0 / (1.0 + jnp.exp(-small[:, :value_heads]))
    alphas = small[:, value_heads : 2 * value_heads] + bias_ref[...]
    softplus = jnp.maximum(alphas, 0.0) + jnp.log1p(jnp.exp(-jnp.abs(alphas)))
    decays = jnp.exp(-scale_ref[...] * softplus)

    def units(v):
        return v * lax.rsqrt(jnp.sum(v * v, axis=1, keepdims=True) + EPS)

    queries_all = silu(project(wq))
    keys_all = silu(project(wk))
    keys, queries = [], []
    for i in range(key_heads):
        k = units(keys_all[:, i * DK : (i + 1) * DK])
        q = units(queries_all[:, i * DK : (i + 1) * DK]) * DK ** (-0.5)
        keys_ref[i] = k
        keys.append([k[t * seqs : (t + 1) * seqs] for t in range(steps)])
        queries.append([q[t * seqs : (t + 1) * seqs] for t in range(steps)])
        for t in range(steps):
            for at, v in ((t, keys[i][t]), (steps + t, queries[i][t])):
                high = v.astype(BF16).astype(F32)
                left[i, pl.ds(at, seqs, stride=SLOTS), :] = high
                left[i, pl.ds(2 * steps + at, seqs, stride=SLOTS), :] = v - high
        for at in range(4 * steps, SLOTS):
            left[i, pl.ds(at, seqs, stride=SLOTS), :] = jnp.zeros((seqs, DK), F32)
    values_all = silu(project(wv))
    gates = silu(project(wz))

    def one(s, carry):
        base = pl.multiple_of(s * SLOTS, SLOTS)
        for i in range(key_heads):
            lhs = left[i, pl.ds(base, SLOTS), :].astype(BF16)
            rhs = jnp.concatenate([states[s, i * group + u] for u in range(group)], axis=1)
            high, low = split(rhs)
            answer = dot(jnp.concatenate([lhs, lhs], axis=1), jnp.concatenate([high, low], axis=0))
            for u in range(group):
                recalls[i * group + u, pl.ds(base, SLOTS), :] = answer[:, u * DV : (u + 1) * DV]
        return carry

    lax.fori_loop(0, seqs, one, 0, unroll=4)

    def wide(columns, t, i):
        return jnp.concatenate(
            [
                jnp.broadcast_to(
                    columns[t * seqs : (t + 1) * seqs, i * group + u : i * group + u + 1],
                    (seqs, DV),
                )
                for u in range(group)
            ],
            axis=1,
        )

    mixed_rows = [[] for _ in range(steps)]
    for i in range(key_heads):
        decay = [wide(decays, t, i) for t in range(steps)]
        beta = [wide(betas, t, i) for t in range(steps)]

        def read(at):
            return jnp.concatenate(
                [
                    recalls[i * group + u, pl.ds(at, seqs, stride=SLOTS), :]
                    + recalls[i * group + u, pl.ds(2 * steps + at, seqs, stride=SLOTS), :]
                    for u in range(group)
                ],
                axis=1,
            )

        deltas = []
        running = None
        for t in range(steps):
            running = decay[t] if running is None else running * decay[t]
            recall = running * read(t)
            answer = running * read(steps + t)
            deltas = [d * decay[t] for d in deltas]
            for u, d in enumerate(deltas):
                recall = recall + d * jnp.sum(keys[i][t] * keys[i][u], axis=1, keepdims=True)
                answer = answer + d * jnp.sum(queries[i][t] * keys[i][u], axis=1, keepdims=True)
            value = values_all[t * seqs : (t + 1) * seqs, i * pair : (i + 1) * pair]
            delta = beta[t] * (value - recall)
            answer = answer + delta * jnp.sum(queries[i][t] * keys[i][t], axis=1, keepdims=True)
            deltas.append(delta)
            mixed_rows[t].append(answer)
        for t in range(steps):
            delta_ref[i, t] = deltas[t]
        total_ref[i] = running
    mixed = jnp.concatenate([jnp.concatenate(m, axis=1) for m in mixed_rows], axis=0)
    gated = []
    for h in range(value_heads):
        m = mixed[:, h * DV : (h + 1) * DV]
        m = m * lax.rsqrt(jnp.mean(m * m, axis=1, keepdims=True) + EPS)
        gated.append((m * ggain_ref[...] * gates[:, h * DV : (h + 1) * DV]).astype(BF16))
    gated = jnp.concatenate(gated, axis=1)
    for c in range(head_count):
        piece = dot(gated, wo[:, c * width : (c + 1) * width]).astype(BF16)
        away = me ^ c

        @pl.when(away % 2 == 0)
        def _():
            own_ref[away // 2] = piece

        @pl.when(away % 2 == 1)
        def _():
            sib_ref[away // 2] = piece


def front(me, xs, gain, small, scale, bias, ggain, wq, wk, wv, wz, wo, states, after, steps):
    _, rows, width = xs[0].shape
    head_count = 2 * len(xs)
    seqs = rows // steps
    key_heads = wq.shape[1] // DK
    value_heads = wv.shape[1] // DV
    pair = value_heads // key_heads * DV
    return call(
        functools.partial(front_kernel, steps, head_count),
        "front",
        [
            pltpu.VMEM((head_count // 2, rows, width), BF16),
            pltpu.VMEM((head_count // 2, rows, width), BF16),
            pltpu.VMEM((key_heads, rows, DK), F32),
            pltpu.VMEM((key_heads, steps, seqs, pair), F32),
            pltpu.VMEM((key_heads, seqs, pair), F32),
        ],
        (me,),
        (*xs, gain, small, scale, bias, ggain, wq, wk, wv, wz, wo, states),
        (after,),
        [
            pltpu.VMEM((key_heads, seqs * SLOTS, DK), F32),
            pltpu.VMEM((value_heads, seqs * SLOTS, DV), F32),
        ],
    )


PER_BLOCK = DK // SLOTS


def update_kernel(steps, blocks, aliased, keys_ref, delta_ref, total_ref, states_ref, *refs):
    if aliased:
        refs = refs[1:]
    _, out_ref, done_ref, left, right, buffers, sems = refs
    key_heads, rows, _ = keys_ref.shape
    seqs = rows // steps
    group = states_ref.shape[1] // key_heads
    first, count = blocks[0] * PER_BLOCK, len(blocks) * PER_BLOCK
    for i in range(key_heads):
        for at in range(SLOTS):
            rows_at = pl.ds(at, count, stride=SLOTS)
            t = at % steps
            k = keys_ref[i, t * seqs + first : t * seqs + first + count, :]
            k_high = k.astype(BF16).astype(F32)
            k = k - k_high if at >= 2 * steps else k_high
            left[i, rows_at, :] = k if at < 3 * steps else jnp.zeros_like(k)
            for u in range(group):
                d = delta_ref[i, t, first : first + count, u * DV : (u + 1) * DV]
                d_high = d.astype(BF16).astype(F32)
                d = d - d_high if steps <= at < 2 * steps else d_high
                right[i * group + u, rows_at, :] = d if at < 3 * steps else jnp.zeros_like(d)
    slot_of = lax.broadcasted_iota(jnp.int32, (DK, DK), 1) // SLOTS
    copies = []
    for n, block in enumerate(blocks):
        if n >= 2:
            copies[n - 2].wait()
        buffer = buffers.at[n % 2]
        span = slice(n * DK, (n + 1) * DK)
        for i in range(key_heads):
            lhs = jnp.transpose(left[i, span, :])
            rhs = jnp.concatenate([right[i * group + u, span, :] for u in range(group)], axis=1)
            rhs = rhs.astype(BF16)
            for m in range(PER_BLOCK):
                s = block * PER_BLOCK + m
                masked = jnp.where(slot_of == m, lhs, 0.0).astype(BF16)
                change = dot(masked, rhs)
                for u in range(group):
                    columns = slice(u * DV, (u + 1) * DV)
                    h = i * group + u
                    total = total_ref[i, s : s + 1, columns]
                    buffer[m, h] = states_ref[s, h] * total + change[:, columns]
        span = pl.ds(block * PER_BLOCK, PER_BLOCK)
        copies.append(pltpu.make_async_copy(buffer, out_ref.at[span], sems.at[n % 2]))
        copies[-1].start()
    for copy in copies[-2:]:
        copy.wait()
    done_ref[...] = jnp.zeros_like(done_ref)


def update(keys, deltas, totals, states, blocks, after, before=None):
    key_heads, steps, seqs, pair = deltas.shape
    rows = len(blocks) * DK
    value_heads = states.shape[1]
    loose = (after,) if before is None else (before, after)
    return call(
        functools.partial(update_kernel, steps, blocks, before is not None),
        "update",
        [jax.ShapeDtypeStruct(states.shape, F32), jax.ShapeDtypeStruct((8, 128), F32)],
        (),
        (keys, deltas, totals, states),
        loose,
        [
            pltpu.VMEM((key_heads, rows, DK), F32),
            pltpu.VMEM((value_heads, rows, DV), F32),
            pltpu.VMEM((2, PER_BLOCK, *states.shape[1:]), F32),
            pltpu.SemaphoreType.DMA((2,)),
        ],
        None if before is None else {4: 0},
        [ANY_SPEC, VMEM_SPEC],
    )


def expert_in_kernel(orders, odd, first, me_ref, *refs):
    pieces = refs[: sum(map(len, orders))]
    refs = refs[len(pieces) :]
    gain_inv_ref, w_ref = refs[:2]
    if first:
        pre_ref, sq_ref = refs[-2:]
    else:
        pre_in, sq_in = refs[2:4]
        pre_ref, sq_ref = refs[-2:]
    me = me_ref[0]
    start, at = 0, 0
    for order in orders:
        blocks, xs = [], []
        for part in order:
            ref = pieces[at]
            at += 1
            _, zs, rows, width = ref.shape
            for n, place in enumerate(part):
                xs.append(ref[n].reshape(zs * rows, width))
                blocks.append(me ^ (2 * place + odd))
        spans = [pl.ds(pl.multiple_of(b * width, width), width) for b in blocks]
        span = slice(start, start + zs * rows)
        start += zs * rows
        for c in range(0, w_ref.shape[2], 256):
            columns = slice(c, c + 256)
            total = None if first else pre_in[span, columns]
            for x, where in zip(xs, spans):
                term = dot(x, w_ref[0, where, columns])
                total = term if total is None else total + term
            pre_ref[span, columns] = total
        squares = None
        for x, block in zip(xs, blocks):
            plain = x.astype(F32) * gain_inv_ref[block]
            plain = plain * plain
            for c in range(0, width, 128):
                part = plain[:, c : c + 128]
                squares = part if squares is None else squares + part
        squares = jnp.sum(squares, axis=1, keepdims=True)
        sq_ref[span, :] = squares if first else squares + sq_in[span, :]


def expert_in(me, sides, gain_inv, w, orders, odd, before=(), after=()):
    pieces = [piece for side in sides for piece in side]
    rows = pieces[0].shape[2]
    total = sum(side[0].shape[1] for side in sides) * rows
    return call(
        functools.partial(expert_in_kernel, orders, odd, not before),
        "expert_in",
        [pltpu.VMEM((total, w.shape[2]), F32), pltpu.VMEM((total, 1), F32)],
        (me,),
        (*pieces, gain_inv, w, *before),
        after,
    )


def expert_out_kernel(orders, me_ref, pre_ref, sq_ref, weight_ref, w_ref, *outs):
    me = me_ref[0]
    features = w_ref.shape[2]
    hidden_width = w_ref.shape[1]
    start = 0
    for side, order in enumerate(orders):
        own, sib = outs[2 * side : 2 * side + 2]
        count, zs, rows, width = own.shape
        span = slice(start, start + zs * rows)
        start += zs * rows
        inverse = lax.rsqrt(sq_ref[span, :] / features + EPS)
        gate = pre_ref[span, :hidden_width] * inverse
        up = pre_ref[span, hidden_width:] * inverse
        hidden = (silu(gate) * up).astype(BF16)
        weight = weight_ref[span, :]
        for odd, ref in ((1, sib), (0, own)):
            for n in range(count):
                block = me ^ (2 * order[n] + odd)
                columns = pl.ds(pl.multiple_of(block * width, width), width)
                result = dot(hidden, w_ref[0, :, columns]) * weight
                ref[n] = result.astype(BF16).reshape(zs, rows, width)


def expert_out(me, pre, sq, weight, w, orders, shapes):
    return call(
        functools.partial(expert_out_kernel, orders),
        "expert_out",
        [pltpu.VMEM(shape, BF16) for shape in shapes],
        (me,),
        (pre, sq, weight, w),
    )


def bit_reversed(count):
    bits = count.bit_length() - 1
    return [int(format(n, "b").zfill(bits)[::-1], 2) if bits else 0 for n in range(count)]


def add(a, b):
    return (a.astype(F32) + b.astype(F32)).astype(BF16)


def half_sum_kernel(a_ref, b_ref, keep_ref, send_ref):
    half = a_ref.shape[0] // 2
    keep_ref[...] = add(a_ref[:half], b_ref[:half])
    send_ref[...] = add(a_ref[half:], b_ref[half:])


def half_sum(a, b):
    shape = (a.shape[0] // 2, *a.shape[1:])
    return call(
        half_sum_kernel, "half_sum", [pltpu.VMEM(shape, BF16), pltpu.VMEM(shape, BF16)], (), (a, b)
    )


def on_device(
    tokens,
    states,
    router_ids,
    router_weights,
    input_gain,
    w_query,
    w_key,
    w_value,
    w_zgate,
    w_beta,
    w_alpha,
    decay_scale,
    dt_bias,
    gated_gain,
    w_out,
    post_gain,
    w_shared_in,
    w_shared_out,
    w_expert_in,
    w_expert_out,
):
    seq_count = lax.axis_size("seq")
    head_count = lax.axis_size("head")
    head_index = lax.axis_index("head")
    seq_index = lax.axis_index("seq")
    me = head_index.astype(jnp.int32).reshape(1)
    seqs, steps, width = tokens.shape
    rows = seqs * steps
    features = head_count * width
    pairs = head_count // 2
    axes = [1 << n for n in range(1, head_count.bit_length() - 1)]

    mine = jnp.transpose(tokens, (1, 0, 2)).reshape(rows, width)

    both = stack(mine, exchange(mine, "head", 1))
    gathered = [both] + [exchange(both, "head", 2 * p) for p in range(1, pairs)]

    ids = jnp.transpose(router_ids, (1, 0, 2)).reshape(rows, -1)
    chosen = jnp.transpose(router_weights, (1, 0, 2)).reshape(rows, -1)
    row_weights = []
    for z in range(seq_count):
        target = (seq_index ^ z) * head_count + head_index
        weight = jnp.sum(jnp.where(ids == target, chosen, 0.0), axis=1).reshape(1, rows)
        row_weights.append(exchange(weight, "seq", z) if z else weight)
    row_weight = jnp.concatenate(row_weights, axis=1).reshape(seq_count * rows, 1)

    value_heads = w_beta.shape[1]
    small = jnp.concatenate([w_beta, w_alpha], axis=1)
    small = jnp.transpose(small.reshape(head_count, width, 2 * value_heads), (0, 2, 1))
    small = jnp.pad(small, ((0, 0), (0, -2 * value_heads % 16), (0, 0)))

    own, sib, keys, deltas, totals = front(
        me,
        gathered,
        input_gain.reshape(head_count, 1, width),
        small,
        decay_scale.reshape(1, value_heads),
        dt_bias.reshape(1, value_heads),
        gated_gain.reshape(1, DV),
        w_query,
        w_key,
        w_value,
        w_zgate,
        w_out,
        states,
        row_weight,
        steps,
    )

    merged = add(own, exchange(sib, "head", 1))
    resid = mine.astype(F32) + merged[0].astype(F32)
    for p in range(1, pairs):
        resid = resid + exchange(merged[p], "head", 2 * p).astype(F32)
    gain_mine = lax.dynamic_slice_in_dim(post_gain, head_index * width, width, 0)
    x = (resid * gain_mine).astype(BF16)

    half = seq_count // 2
    slabs = [x] + [exchange(x, "seq", z) for z in range(1, seq_count)]
    natural, reverse = list(range(pairs)), bit_reversed(pairs)
    sides, siblings, firsts = [], [], []
    for slab, bits in ((slabs[:half], axes), (slabs[half:], axes[::-1])):
        side = slab[0][None]
        side = stack(*slab)[None] if half == 2 else jnp.stack(slab)[None]
        for bit in bits[:-1]:
            received = exchange(side, "head", bit)
            firsts.append(received)
            side = stack(side[0], received[0]) if side.shape[0] == 1 else jnp.concatenate([side, received])
        sides.append([side, exchange(side, "head", bits[-1])])
        siblings.append([exchange(piece, "head", 1) for piece in sides[-1]])
    gain_inv = (1.0 / post_gain).reshape(head_count, 1, width)
    middle = pairs // 2
    orders = tuple((tuple(o[:middle]), tuple(o[middle:])) for o in (natural, reverse))

    blocks = tuple(range(seqs // PER_BLOCK))
    cut = len(blocks) // 2
    states_out, done_1 = update(keys, deltas, totals, states, blocks[:cut], slabs[1])
    states_out, done_2 = update(
        keys, deltas, totals, states, blocks[cut:], firsts[0], states_out
    )
    pre = expert_in(me, sides, gain_inv, w_expert_in, orders, 0, after=(done_1, done_2))
    pre, squares = expert_in(me, siblings, gain_inv, w_expert_in, orders, 1, pre)
    shape = (pairs, half, rows, width)
    a_own, a_sib, b_own, b_sib = expert_out(
        me, pre, squares, row_weight, w_expert_out, (reverse, natural), (shape,) * 4
    )
    sums = []
    for own, sib, bits in ((a_own, a_sib, axes), (b_own, b_sib, axes[::-1])):
        received = exchange(sib, "head", 1)
        for bit in bits:
            own, sent = half_sum(own, received)
            received = exchange(sent, "head", bit)
        sums.append(add(own[0], received[0]))

    shared_pre = dot(x, w_shared_in)
    for bit in [1] + axes:
        sent = shared_pre.astype(BF16)
        shared_pre = sent.astype(F32) + exchange(sent, "head", bit).astype(F32)
    shared_pre = shared_pre * lax.rsqrt(squares[:rows] / features + EPS)
    half_shared = shared_pre.shape[1] // 2
    hidden = (silu(shared_pre[:, :half_shared]) * shared_pre[:, half_shared:]).astype(BF16)
    result = resid + dot(hidden, w_shared_out)

    for z in range(seq_count):
        part = sums[z // half][z % half]
        result = result + (exchange(part, "seq", z) if z else part).astype(F32)
    layer_out = jnp.transpose(result.astype(BF16).reshape(steps, seqs, width), (1, 0, 2))
    return (layer_out, states_out)


def solution(mesh):
    in_specs = (
        P("seq", None, "head"),
        P("seq", "head", None, None),
        P("seq", None, None),
        P("seq", None, None),
        P(),
        P(None, "head"),
        P(None, "head"),
        P(None, "head"),
        P(None, "head"),
        P(None, "head"),
        P(None, "head"),
        P("head"),
        P("head"),
        P(),
        P("head", None),
        P(),
        P("head", None),
        P(None, "head"),
        P(("seq", "head"), None, None),
        P(("seq", "head"), None, None),
    )
    out_specs = (P("seq", None, "head"), P("seq", "head", None, None))
    return jax.shard_map(
        on_device, mesh=mesh, in_specs=in_specs, out_specs=out_specs, check_vma=False
    )
```

time: 117 us -> 107 us (0.915)
  Pallas kernels: 36.6 us -> 15 us
  local copies, waits for them, and re-layouts: 4.43 us -> 19.3 us
  waiting for transfers between devices: 37.7 us -> 34.9 us
  other arithmetic: 4.9 us -> 2.12 us
  starting transfers between devices: 31.1 us -> 32.9 us
    pallas_call x5 -> x15, Pallas kernels: 36.6 us -> 15 us  [call(): pl.pallas_call(body, out_shape=tuple(out_shapes), in_specs=[SMEM_SPEC] *...]
    unnamed x32 -> x36, local copies, waits for them, and re-layouts: 2.48 us -> 18.7 us
    ppermute x32 -> x34, waiting for transfers between devices: 37.7 us -> 34.9 us  [exchange(): return lax.ppermute(x, axis, [(i, i ^ bit) for i in range(size)])]
    ppermute x32 -> x34, starting transfers between devices: 31.1 us -> 32.9 us  [exchange(): return lax.ppermute(x, axis, [(i, i ^ bit) for i in range(size)])]
    convert_element_type x7 -> x3, other arithmetic: 1.33 us -> 0.11 us  [add(): return (a.astype(F32) + b.astype(F32)).astype(BF16)]
  transfers between devices with their start and end apart: 32 -> 34, of which waited for: 17 -> 21; matrix products, arithmetic and copies ran while one was open for 5% -> 2% of each run, Pallas kernels for 22% -> 9%
where the time goes in v1:
time: 107 us; the launch traced here: 106 us
  waiting for transfers between devices  34.9 us (33%)
  starting transfers between devices  32.9 us (31%)
  local copies, waits for them, and re-layouts  19.3 us (18%)
  Pallas kernels  15 us (14%)
  other arithmetic  2.12 us (2%)
    ppermute x34, waiting for transfers between devices, exchange(): return lax.ppermute(x, axis, [(i, i ^ bit) for i in range(size)])  34.9 us
    ppermute x34, starting transfers between devices, exchange(): return lax.ppermute(x, axis, [(i, i ^ bit) for i in range(size)])  32.9 us
    unnamed x36, local copies, waits for them, and re-layouts  18.7 us
    pallas_call x15, Pallas kernels, call(): pl.pallas_call(body, out_shape=tuple(out_shapes), in_specs=[SMEM_SPEC] *...  15 us
  transfers between devices with their start and end apart: 34, of which 21 were waited for; matrix products, arithmetic and copies ran while one was open for 2% of the time, Pallas kernels for 9%

profile of v1, /device:TPU:0, one launch (start us, length us, event | category | flops | bytes accessed | tf_op | source)
XLA Modules:
  0.0 106.1 jit_solution(5794950786704292089)
XLA Ops:
  1.6 3.0 %collective-permute-start.4 = (f32[1,96]{1,0:T(1,128)S(1)}, f32[1,96]{1,0:T(1,128)S(1)}, u32[]{:S(2)}, u32[]{:S(2)}) collective-permute-start(f32[1,96]{1,0:T(1,128)S(1)} %reshape.86), channel_id=1, source_target_pairs={{0,8},{8,0},{16,24},{24,16},{1,9},{9,1},{17,25},{25,17},{2,10},{10... | collective-permute-start | bytes 1160 | tf_op jit(solution)/shard_map/ppermute | solution.py:57
  4.7 2.6 %collective-permute-start.5 = (f32[1,96]{1,0:T(1,128)S(1)}, f32[1,96]{1,0:T(1,128)S(1)}, u32[]{:S(2)}, u32[]{:S(2)}) collective-permute-start(f32[1,96]{1,0:T(1,128)S(1)} %reshape.87), channel_id=1, source_target_pairs={{0,16},{8,24},{16,0},{24,8},{1,17},{9,25},{17,1},{25,9},{2,18},{10... | collective-permute-start | bytes 1160 | tf_op jit(solution)/shard_map/ppermute | solution.py:57
  9.6 1.8 %collective-permute-start.1 = (bf16[2,96,256]{2,1,0:T(8,128)(2,1)S(1)}, bf16[2,96,256]{2,1,0:T(8,128)(2,1)S(1)}, u32[]{:S(2)}, u32[]{:S(2)}) collective-permute-start(bf16[2,96,256]{2,1,0:T(8,128)(2,1)S(1)} %stack.5.refs_0_), channel_id=1, source_target_pairs={{0,2},{1,3},{2,0},{3,1},{4,6},{5,7},{6,4},{7,5},{8,10},{9,11},{10,... | collective-permute-start | bytes 294920 | tf_op jit(solution)/shard_map/ppermute | solution.py:57
  11.4 1.5 %collective-permute-start.2 = (bf16[2,96,256]{2,1,0:T(8,128)(2,1)S(1)}, bf16[2,96,256]{2,1,0:T(8,128)(2,1)S(1)}, u32[]{:S(2)}, u32[]{:S(2)}) collective-permute-start(bf16[2,96,256]{2,1,0:T(8,128)(2,1)S(1)} %stack.5.refs_0_), channel_id=1, source_target_pairs={{0,4},{1,5},{2,6},{3,7},{4,0},{5,1},{6,2},{7,3},{8,12},{9,13},{10,... | collective-permute-start | bytes 294920 | tf_op jit(solution)/shard_map/ppermute | solution.py:57
  13.4 1.1 %collective-permute-done.1.refs_1_ = bf16[2,96,256]{2,1,0:T(8,128)(2,1)S(1)} collective-permute-done((bf16[2,96,256]{2,1,0:T(8,128)(2,1)S(1)}, bf16[2,96,256]{2,1,0:T(8,128)(2,1)S(1)}, u32[]{:S(2)}, u32[]{:S(2)}) %collective-permute-start.1) | collective-permute-done | bytes 98336 | tf_op jit(solution)/shard_map/ppermute | solution.py:57
  14.5 2.6 %collective-permute-done.2.refs_2_ = bf16[2,96,256]{2,1,0:T(8,128)(2,1)S(1)} collective-permute-done((bf16[2,96,256]{2,1,0:T(8,128)(2,1)S(1)}, bf16[2,96,256]{2,1,0:T(8,128)(2,1)S(1)}, u32[]{:S(2)}, u32[]{:S(2)}) %collective-permute-start.2) | collective-permute-done | bytes 98336 | tf_op jit(solution)/shard_map/ppermute | solution.py:57
  17.1 1.3 %collective-permute-done.3.refs_3_ = bf16[2,96,256]{2,1,0:T(8,128)(2,1)S(1)} collective-permute-done((bf16[2,96,256]{2,1,0:T(8,128)(2,1)S(1)}, bf16[2,96,256]{2,1,0:T(8,128)(2,1)S(1)}, u32[]{:S(2)}, u32[]{:S(2)}) %collective-permute-start.3) | collective-permute-done | bytes 98336 | tf_op jit(solution)/shard_map/ppermute | solution.py:57
  18.4 3.4 %copy-done.1 = f32[32,4,128,128]{3,2,1,0:T(8,128)S(1)} copy-done((f32[32,4,128,128]{3,2,1,0:T(8,128)S(1)}, f32[32,4,128,128]{3,2,1,0:T(8,128)}, u32[]{:S(2)}) %copy-start.1) | copy-done | bytes 8388632
  21.8 1.6 %copy-done.5 = bf16[2048,512]{1,0:T(8,128)(2,1)S(1)} copy-done((bf16[2048,512]{1,0:T(8,128)(2,1)S(1)}, bf16[2048,512]{1,0:T(8,128)(2,1)}, u32[]{:S(2)}) %copy-start.5) | copy-done | bytes 2097176
  23.4 1.6 %copy-done.6 = bf16[2048,512]{1,0:T(8,128)(2,1)S(1)} copy-done((bf16[2048,512]{1,0:T(8,128)(2,1)S(1)}, bf16[2048,512]{1,0:T(8,128)(2,1)}, u32[]{:S(2)}) %copy-start.6) | copy-done | bytes 2097176
  25.0 1.6 %copy-done.7 = bf16[512,2048]{1,0:T(8,128)(2,1)S(1)} copy-done((bf16[512,2048]{1,0:T(8,128)(2,1)S(1)}, bf16[512,2048]{1,0:T(8,128)(2,1)}, u32[]{:S(2)}) %copy-start.7) | copy-done | bytes 2097176
  26.6 1.2 %copy-done.8 = bf16[2048,256]{1,0:T(8,128)(2,1)S(1)} copy-done((bf16[2048,256]{1,0:T(8,128)(2,1)S(1)}, bf16[2048,256]{1,0:T(8,128)(2,1)}, u32[]{:S(2)}) %copy-start.8) | copy-done | bytes 1048600
  27.8 1.2 %copy-done.9 = bf16[2048,256]{1,0:T(8,128)(2,1)S(1)} copy-done((bf16[2048,256]{1,0:T(8,128)(2,1)S(1)}, bf16[2048,256]{1,0:T(8,128)(2,1)}, u32[]{:S(2)}) %copy-start.9) | copy-done | bytes 1048600
  31.7 5.8 %front.1 = (bf16[4,96,256]{2,1,0:T(8,128)(2,1)S(1)}, bf16[4,96,256]{2,1,0:T(8,128)(2,1)S(1)}, f32[2,96,128]{2,1,0:T(8,128)S(1)}, f32[2,3,32,256]{3,2,1,0:T(8,128)S(1)}, f32[2,32,256]{2,1,0:T(8,128)S(1)}) custom-call(s32[1]{0:T(128)} %bitcast.2.me_ref, bf16[2,96,256]{2,1,0:T(8,128)(2,1)S(1)} %stack.5.refs_0_, ...), custom_call_target="tpu_custom_call" | custom-call | tf_op jit(solution)/shard_map/front/pallas_call | solution.py:43
  37.5 1.4 %collective-permute-done.7 = bf16[4,96,256]{2,1,0:T(8,128)(2,1)S(1)} collective-permute-done((bf16[4,96,256]{2,1,0:T(8,128)(2,1)S(1)}, bf16[4,96,256]{2,1,0:T(8,128)(2,1)S(1)}, u32[]{:S(2)}, u32[]{:S(2)}) %collective-permute-start.7) | collective-permute-done | bytes 196640 | tf_op jit(solution)/shard_map/ppermute | solution.py:57
  39.1 1.2 %collective-permute-start.10 = (bf16[96,256]{1,0:T(8,128)(2,1)S(1)}, bf16[96,256]{1,0:T(8,128)(2,1)S(1)}, u32[]{:S(2)}, u32[]{:S(2)}) collective-permute-start(bf16[96,256]{1,0:T(8,128)(2,1)S(1)} %get-tuple-element.59), channel_id=1, source_target_pairs={{0,6},{1,7},{2,4},{3,5},{4,2},{5,3},{6,0},{7,1},{8,14},{9,15},{10,... | collective-permute-start | bytes 147464 | tf_op jit(solution)/shard_map/ppermute | solution.py:57
  40.3 1.5 %collective-permute-start.8 = (bf16[96,256]{1,0:T(8,128)(2,1)S(1)}, bf16[96,256]{1,0:T(8,128)(2,1)S(1)}, u32[]{:S(2)}, u32[]{:S(2)}) collective-permute-start(bf16[96,256]{1,0:T(8,128)(2,1)S(1)} %get-tuple-element.58), channel_id=1, source_target_pairs={{0,2},{1,3},{2,0},{3,1},{4,6},{5,7},{6,4},{7,5},{8,10},{9,11},{10,... | collective-permute-start | bytes 147464 | tf_op jit(solution)/shard_map/ppermute | solution.py:57
  42.7 1.8 %collective-permute-done.10 = bf16[96,256]{1,0:T(8,128)(2,1)S(1)} collective-permute-done((bf16[96,256]{1,0:T(8,128)(2,1)S(1)}, bf16[96,256]{1,0:T(8,128)(2,1)S(1)}, u32[]{:S(2)}, u32[]{:S(2)}) %collective-permute-start.10) | collective-permute-done | bytes 49184 | tf_op jit(solution)/shard_map/ppermute | solution.py:57
  44.6 1.3 %collective-permute-done.9 = bf16[96,256]{1,0:T(8,128)(2,1)S(1)} collective-permute-done((bf16[96,256]{1,0:T(8,128)(2,1)S(1)}, bf16[96,256]{1,0:T(8,128)(2,1)S(1)}, u32[]{:S(2)}, u32[]{:S(2)}) %collective-permute-start.9) | collective-permute-done | bytes 49184 | tf_op jit(solution)/shard_map/ppermute | solution.py:57
  45.9 1.8 %collective-permute-start.19 = (bf16[96,256]{1,0:T(8,128)(2,1)S(1)}, bf16[96,256]{1,0:T(8,128)(2,1)S(1)}, u32[]{:S(2)}, u32[]{:S(2)}) collective-permute-start(bf16[96,256]{1,0:T(8,128)(2,1)S(1)} %get-tuple-element.56.a_ref), channel_id=1, source_target_pairs={{0,16},{8,24},{16,0},{24,8},{1,17},{9,25},{17,1},{25,9},{2,18},{10... | collective-permute-start | bytes 147464 | tf_op jit(solution)/shard_map/ppermute | solution.py:57
  47.7 2.0 %collective-permute-start.20 = (bf16[96,256]{1,0:T(8,128)(2,1)S(1)}, bf16[96,256]{1,0:T(8,128)(2,1)S(1)}, u32[]{:S(2)}, u32[]{:S(2)}) collective-permute-start(bf16[96,256]{1,0:T(8,128)(2,1)S(1)} %get-tuple-element.56.a_ref), channel_id=1, source_target_pairs={{0,24},{8,16},{16,8},{24,0},{1,25},{9,17},{17,9},{25,1},{2,26},{10... | collective-permute-start | bytes 147464 | tf_op jit(solution)/shard_map/ppermute | solution.py:57
  50.2 2.1 %collective-permute-done.19.a_ref = bf16[96,256]{1,0:T(8,128)(2,1)S(1)} collective-permute-done((bf16[96,256]{1,0:T(8,128)(2,1)S(1)}, bf16[96,256]{1,0:T(8,128)(2,1)S(1)}, u32[]{:S(2)}, u32[]{:S(2)}) %collective-permute-start.19) | collective-permute-done | bytes 49184 | tf_op jit(solution)/shard_map/ppermute | solution.py:57
  52.3 1.3 %collective-permute-done.20.b_ref = bf16[96,256]{1,0:T(8,128)(2,1)S(1)} collective-permute-done((bf16[96,256]{1,0:T(8,128)(2,1)S(1)}, bf16[96,256]{1,0:T(8,128)(2,1)S(1)}, u32[]{:S(2)}, u32[]{:S(2)}) %collective-permute-start.20) | collective-permute-done | bytes 49184 | tf_op jit(solution)/shard_map/ppermute | solution.py:57
  54.5 0.9 collective-permute-start.15
  55.5 2.8 %collective-permute-done.21 = bf16[1,2,96,256]{3,2,1,0:T(8,128)(2,1)S(1)} collective-permute-done((bf16[1,2,96,256]{3,2,1,0:T(8,128)(2,1)S(1)}, bf16[1,2,96,256]{3,2,1,0:T(8,128)(2,1)S(1)}, u32[]{:S(2)}, u32[]{:S(2)}) %collective-permute-start.21) | collective-permute-done | bytes 98336 | tf_op jit(solution)/shard_map/ppermute | solution.py:57
  58.9 1.3 %collective-permute-done.15.refs_1_ = bf16[1,2,96,256]{3,2,1,0:T(8,128)(2,1)S(1)} collective-permute-done((bf16[1,2,96,256]{3,2,1,0:T(8,128)(2,1)S(1)}, bf16[1,2,96,256]{3,2,1,0:T(8,128)(2,1)S(1)}, u32[]{:S(2)}, u32[]{:S(2)}) %collective-permute-start.15) | collective-permute-done | bytes 98336 | tf_op jit(solution)/shard_map/ppermute | solution.py:57
  60.2 1.3 %collective-permute-start.17 = (bf16[2,2,96,256]{3,2,1,0:T(8,128)(2,1)S(1)}, bf16[2,2,96,256]{3,2,1,0:T(8,128)(2,1)S(1)}, u32[]{:S(2)}, u32[]{:S(2)}) collective-permute-start(bf16[2,2,96,256]{3,2,1,0:T(8,128)(2,1)S(1)} %stack.7.refs_0_), channel_id=1, source_target_pairs={{0,4},{1,5},{2,6},{3,7},{4,0},{5,1},{6,2},{7,3},{8,12},{9,13},{10,... | collective-permute-start | bytes 589832 | tf_op jit(solution)/shard_map/ppermute | solution.py:57
  62.4 1.6 %collective-permute-done.23.refs_3_ = bf16[2,2,96,256]{3,2,1,0:T(8,128)(2,1)S(1)} collective-permute-done((bf16[2,2,96,256]{3,2,1,0:T(8,128)(2,1)S(1)}, bf16[2,2,96,256]{3,2,1,0:T(8,128)(2,1)S(1)}, u32[]{:S(2)}, u32[]{:S(2)}) %collective-permute-start.23) | collective-permute-done | bytes 196640 | tf_op jit(solution)/shard_map/ppermute | solution.py:57
  64.1 1.9 %collective-permute-done.17.refs_1_ = bf16[2,2,96,256]{3,2,1,0:T(8,128)(2,1)S(1)} collective-permute-done((bf16[2,2,96,256]{3,2,1,0:T(8,128)(2,1)S(1)}, bf16[2,2,96,256]{3,2,1,0:T(8,128)(2,1)S(1)}, u32[]{:S(2)}, u32[]{:S(2)}) %collective-permute-start.17) | collective-permute-done | bytes 196640 | tf_op jit(solution)/shard_map/ppermute | solution.py:57
  66.0 3.4 %copy-done.2 = f32[32,4,128,128]{3,2,1,0:T(8,128)S(1)} copy-done((f32[32,4,128,128]{3,2,1,0:T(8,128)S(1)}, f32[32,4,128,128]{3,2,1,0:T(8,128)}, u32[]{:S(2)}) %copy-start.2) | copy-done | bytes 8388632
  69.4 2.7 %update.2 = (f32[32,4,128,128]{3,2,1,0:T(8,128)}, f32[8,128]{1,0:T(8,128)S(1)}) custom-call(f32[2,96,128]{2,1,0:T(8,128)S(1)} %get-tuple-element.29.keys_ref, f32[2,3,32,256]{3,2,1,0:T(8,128)S(1)} %get-tuple-element.30.delta_ref, f32[2,32,256]{2,1,0:T(8,128)S(1)} %get-tuple-element.31.total_ref, f32[32,4,128,128]{3,2,1,0:T(8,128)S(1)} %copy-done.2, ...), custom_call_target="tpu_custom_call" | custom-call | tf_op jit(solution)/shard_map/update/pallas_call | solution.py:43
  72.1 2.8 %update.3 = (f32[32,4,128,128]{3,2,1,0:T(8,128)}, f32[8,128]{1,0:T(8,128)S(1)}) custom-call(f32[2,96,128]{2,1,0:T(8,128)S(1)} %get-tuple-element.29.keys_ref, f32[2,3,32,256]{3,2,1,0:T(8,128)S(1)} %get-tuple-element.30.delta_ref, f32[2,32,256]{2,1,0:T(8,128)S(1)} %get-tuple-element.31.total_ref, ...), custom_call_target="tpu_custom_call", output_to_operand_aliasing={{0}: (4, {})} | custom-call | tf_op jit(solution)/shard_map/update/pallas_call | solution.py:43
  75.7 1.1 %expert_in.2 = (f32[384,1024]{1,0:T(8,128)S(1)}, f32[384,1]{1,0:T(8,128)S(1)}) custom-call(s32[1]{0:T(128)} %bitcast.2.me_ref, bf16[2,2,96,256]{3,2,1,0:T(8,128)(2,1)S(1)} %stack.7.refs_0_, bf16[2,2,96,256]{3,2,1,0:T(8,128)(2,1)S(1)} %collective-permute-done.17.refs_1_, bf16[2,2,96,256]{3,2,1,0:T(8,128)(2,1)S(1)} %stack.9.refs_2_, ...), custom_call_target="tpu_custom_call" | custom-call | tf_op jit(solution)/shard_map/expert_in/pallas_call | solution.py:43
  76.8 1.1 %expert_in.3 = (f32[384,1024]{1,0:T(8,128)S(1)}, f32[384,1]{1,0:T(8,128)S(1)}) custom-call(s32[1]{0:T(128)} %bitcast.2.me_ref, bf16[2,2,96,256]{3,2,1,0:T(8,128)(2,1)S(1)} %collective-permute-done.16.refs_0_, bf16[2,2,96,256]{3,2,1,0:T(8,128)(2,1)S(1)} %collective-permute-done.18.refs_1_, bf16[2,2,96,256]{3,2,1,0:T(8,128)(2,1)S(1)} %collective-permute-done.22.refs_2_, ...), custom_call_target="tpu_custom_call" | custom-call | tf_op jit(solution)/shard_map/expert_in/pallas_call | solution.py:43
  78.4 1.2 %expert_out.1 = (bf16[4,2,96,256]{3,2,1,0:T(8,128)(2,1)S(1)}, bf16[4,2,96,256]{3,2,1,0:T(8,128)(2,1)S(1)}, bf16[4,2,96,256]{3,2,1,0:T(8,128)(2,1)S(1)}, bf16[4,2,96,256]{3,2,1,0:T(8,128)(2,1)S(1)}) custom-call(s32[1]{0:T(128)} %bitcast.2.me_ref, f32[384,1024]{1,0:T(8,128)S(1)} %get-tuple-element.38.pre_ref, f32[384,1]{1,0:T(8,128)S(1)} %get-tuple-element.37.sq_ref, ...), custom_call_target="tpu_custom_call" | custom-call | tf_op jit(solution)/shard_map/expert_out/pallas_call | solution.py:43
  80.3 0.9 collective-permute-start.12
  81.6 0.9 collective-permute-start.26
  82.7 1.3 %collective-permute-start.30 = (bf16[2,2,96,256]{3,2,1,0:T(8,128)(2,1)S(1)}, bf16[2,2,96,256]{3,2,1,0:T(8,128)(2,1)S(1)}, u32[]{:S(2)}, u32[]{:S(2)}) collective-permute-start(bf16[2,2,96,256]{3,2,1,0:T(8,128)(2,1)S(1)} %get-tuple-element.48), channel_id=1, source_target_pairs={{0,4},{1,5},{2,6},{3,7},{4,0},{5,1},{6,2},{7,3},{8,12},{9,13},{10,... | collective-permute-start | bytes 589832 | tf_op jit(solution)/shard_map/ppermute | solution.py:57
  84.0 4.1 %collective-permute-done.12 = bf16[96,1024]{1,0:T(8,128)(2,1)S(1)} collective-permute-done((bf16[96,1024]{1,0:T(8,128)(2,1)S(1)}, bf16[96,1024]{1,0:T(8,128)(2,1)S(1)}, u32[]{:S(2)}, u32[]{:S(2)}) %collective-permute-start.12) | collective-permute-done | bytes 196640 | tf_op jit(solution)/shard_map/ppermute | solution.py:57
  88.1 1.3 %collective-permute-start.13 = (bf16[96,1024]{1,0:T(8,128)(2,1)S(1)}, bf16[96,1024]{1,0:T(8,128)(2,1)S(1)}, u32[]{:S(2)}, u32[]{:S(2)}) collective-permute-start(bf16[96,1024]{1,0:T(8,128)(2,1)S(1)} %add_convert_fusion), channel_id=1, source_target_pairs={{0,4},{1,5},{2,6},{3,7},{4,0},{5,1},{6,2},{7,3},{8,12},{9,13},{10,... | collective-permute-start | bytes 589832 | tf_op jit(solution)/shard_map/ppermute | solution.py:57
  89.4 2.4 %collective-permute-done.26.b_ref = bf16[2,2,96,256]{3,2,1,0:T(8,128)(2,1)S(1)} collective-permute-done((bf16[2,2,96,256]{3,2,1,0:T(8,128)(2,1)S(1)}, bf16[2,2,96,256]{3,2,1,0:T(8,128)(2,1)S(1)}, u32[]{:S(2)}, u32[]{:S(2)}) %collective-permute-start.26) | collective-permute-done | bytes 196640 | tf_op jit(solution)/shard_map/ppermute | solution.py:57
  91.9 1.3 %collective-permute-start.27 = (bf16[1,2,96,256]{3,2,1,0:T(8,128)(2,1)S(1)}, bf16[1,2,96,256]{3,2,1,0:T(8,128)(2,1)S(1)}, u32[]{:S(2)}, u32[]{:S(2)}) collective-permute-start(bf16[1,2,96,256]{3,2,1,0:T(8,128)(2,1)S(1)} %get-tuple-element.44), channel_id=1, source_target_pairs={{0,4},{1,5},{2,6},{3,7},{4,0},{5,1},{6,2},{7,3},{8,12},{9,13},{10,... | collective-permute-start | bytes 294920 | tf_op jit(solution)/shard_map/ppermute | solution.py:57
  94.0 2.6 %collective-permute-done.27 = bf16[1,2,96,256]{3,2,1,0:T(8,128)(2,1)S(1)} collective-permute-done((bf16[1,2,96,256]{3,2,1,0:T(8,128)(2,1)S(1)}, bf16[1,2,96,256]{3,2,1,0:T(8,128)(2,1)S(1)}, u32[]{:S(2)}, u32[]{:S(2)}) %collective-permute-start.27) | collective-permute-done | bytes 98336 | tf_op jit(solution)/shard_map/ppermute | solution.py:57
  96.6 1.1 %collective-permute-start.28 = (bf16[96,256]{1,0:T(8,128)(2,1)S(1)}, bf16[96,256]{1,0:T(8,128)(2,1)S(1)}, u32[]{:S(2)}, u32[]{:S(2)}) collective-permute-start(bf16[96,256]{1,0:T(8,128)(2,1)S(1)} %slice_bitcast_fusion.2), channel_id=1, source_target_pairs={{0,8},{8,0},{16,24},{24,16},{1,9},{9,1},{17,25},{25,17},{2,10},{10... | collective-permute-start | bytes 147464 | tf_op jit(solution)/shard_map/ppermute | solution.py:57
  98.1 1.3 %collective-permute-start.32 = (bf16[96,256]{1,0:T(8,128)(2,1)S(1)}, bf16[96,256]{1,0:T(8,128)(2,1)S(1)}, u32[]{:S(2)}, u32[]{:S(2)}) collective-permute-start(bf16[96,256]{1,0:T(8,128)(2,1)S(1)} %get-tuple-element.61), channel_id=1, source_target_pairs={{0,16},{8,24},{16,0},{24,8},{1,17},{9,25},{17,1},{25,9},{2,18},{10... | collective-permute-start | bytes 147464 | tf_op jit(solution)/shard_map/ppermute | solution.py:57
  99.4 2.1 %collective-permute-start.33 = (bf16[96,256]{1,0:T(8,128)(2,1)S(1)}, bf16[96,256]{1,0:T(8,128)(2,1)S(1)}, u32[]{:S(2)}, u32[]{:S(2)}) collective-permute-start(bf16[96,256]{1,0:T(8,128)(2,1)S(1)} %get-tuple-element.62), channel_id=1, source_target_pairs={{0,24},{8,16},{16,8},{24,0},{1,25},{9,17},{17,9},{25,1},{2,26},{10... | collective-permute-start | bytes 147464 | tf_op jit(solution)/shard_map/ppermute | solution.py:57
  101.6 1.5 %collective-permute-done.32 = bf16[96,256]{1,0:T(8,128)(2,1)S(1)} collective-permute-done((bf16[96,256]{1,0:T(8,128)(2,1)S(1)}, bf16[96,256]{1,0:T(8,128)(2,1)S(1)}, u32[]{:S(2)}, u32[]{:S(2)}) %collective-permute-start.32) | collective-permute-done | bytes 49184 | tf_op jit(solution)/shard_map/ppermute | solution.py:57
  103.2 2.1 %collective-permute-done.33 = bf16[96,256]{1,0:T(8,128)(2,1)S(1)} collective-permute-done((bf16[96,256]{1,0:T(8,128)(2,1)S(1)}, bf16[96,256]{1,0:T(8,128)(2,1)S(1)}, u32[]{:S(2)}, u32[]{:S(2)}) %collective-permute-start.33) | collective-permute-done | bytes 49184 | tf_op jit(solution)/shard_map/ppermute | solution.py:57
  (95 shorter events, 15.1 us)
Async XLA Ops:
  0.6 60.9 %copy-start = (bf16[256,1024]{1,0:T(8,128)(2,1)S(1)}, bf16[256,1024]{1,0:T(8,128)(2,1)}, u32[]{:S(2)}) copy-start(bf16[256,1024]{1,0:T(8,128)(2,1)} %param.36) | copy-start | bytes 1572868
  1.6 11.3 %collective-permute-start.4 = (f32[1,96]{1,0:T(1,128)S(1)}, f32[1,96]{1,0:T(1,128)S(1)}, u32[]{:S(2)}, u32[]{:S(2)}) collective-permute-start(f32[1,96]{1,0:T(1,128)S(1)} %reshape.86), channel_id=1, source_target_pairs={{0,8},{8,0},{16,24},{24,16},{1,9},{9,1},{17,25},{25,17},{2,10},{10... | collective-permute-start | bytes 1160 | tf_op jit(solution)/shard_map/ppermute | solution.py:57
  4.7 8.5 %collective-permute-start.5 = (f32[1,96]{1,0:T(1,128)S(1)}, f32[1,96]{1,0:T(1,128)S(1)}, u32[]{:S(2)}, u32[]{:S(2)}) collective-permute-start(f32[1,96]{1,0:T(1,128)S(1)} %reshape.87), channel_id=1, source_target_pairs={{0,16},{8,24},{16,0},{24,8},{1,17},{9,25},{17,1},{25,9},{2,18},{10... | collective-permute-start | bytes 1160 | tf_op jit(solution)/shard_map/ppermute | solution.py:57
  7.4 5.8 %collective-permute-start.6 = (f32[1,96]{1,0:T(1,128)S(1)}, f32[1,96]{1,0:T(1,128)S(1)}, u32[]{:S(2)}, u32[]{:S(2)}) collective-permute-start(f32[1,96]{1,0:T(1,128)S(1)} %reshape.88), channel_id=1, source_target_pairs={{0,24},{8,16},{16,8},{24,0},{1,25},{9,17},{17,9},{25,1},{2,26},{10... | collective-permute-start | bytes 1160 | tf_op jit(solution)/shard_map/ppermute | solution.py:57
  7.4 1.4 %collective-permute-start = (bf16[96,256]{1,0:T(8,128)(2,1)}, bf16[96,256]{1,0:T(8,128)(2,1)S(1)}, u32[]{:S(2)}, u32[]{:S(2)}) collective-permute-start(bf16[96,256]{1,0:T(8,128)(2,1)} %bitcast.56), channel_id=1, source_target_pairs={{0,1},{1,0},{2,3},{3,2},{4,5},{5,4},{6,7},{7,6},{8,9},{9,8},{10,11... | collective-permute-start | bytes 147464 | tf_op jit(solution)/shard_map/ppermute | solution.py:57
  8.8 0.8 copy-start.10
  9.6 4.9 %collective-permute-start.1 = (bf16[2,96,256]{2,1,0:T(8,128)(2,1)S(1)}, bf16[2,96,256]{2,1,0:T(8,128)(2,1)S(1)}, u32[]{:S(2)}, u32[]{:S(2)}) collective-permute-start(bf16[2,96,256]{2,1,0:T(8,128)(2,1)S(1)} %stack.5.refs_0_), channel_id=1, source_target_pairs={{0,2},{1,3},{2,0},{3,1},{4,6},{5,7},{6,4},{7,5},{8,10},{9,11},{10,... | collective-permute-start | bytes 294920 | tf_op jit(solution)/shard_map/ppermute | solution.py:57
  11.4 5.8 %collective-permute-start.2 = (bf16[2,96,256]{2,1,0:T(8,128)(2,1)S(1)}, bf16[2,96,256]{2,1,0:T(8,128)(2,1)S(1)}, u32[]{:S(2)}, u32[]{:S(2)}) collective-permute-start(bf16[2,96,256]{2,1,0:T(8,128)(2,1)S(1)} %stack.5.refs_0_), channel_id=1, source_target_pairs={{0,4},{1,5},{2,6},{3,7},{4,0},{5,1},{6,2},{7,3},{8,12},{9,13},{10,... | collective-permute-start | bytes 294920 | tf_op jit(solution)/shard_map/ppermute | solution.py:57
  12.9 5.5 %collective-permute-start.3 = (bf16[2,96,256]{2,1,0:T(8,128)(2,1)S(1)}, bf16[2,96,256]{2,1,0:T(8,128)(2,1)S(1)}, u32[]{:S(2)}, u32[]{:S(2)}) collective-permute-start(bf16[2,96,256]{2,1,0:T(8,128)(2,1)S(1)} %stack.5.refs_0_), channel_id=1, source_target_pairs={{0,6},{1,7},{2,4},{3,5},{4,2},{5,3},{6,0},{7,1},{8,14},{9,15},{10,... | collective-permute-start | bytes 294920 | tf_op jit(solution)/shard_map/ppermute | solution.py:57
  18.4 3.4 %copy-start.1 = (f32[32,4,128,128]{3,2,1,0:T(8,128)S(1)}, f32[32,4,128,128]{3,2,1,0:T(8,128)}, u32[]{:S(2)}) copy-start(f32[32,4,128,128]{3,2,1,0:T(8,128)} %states_ref.3) | copy-start | bytes 25165828
  21.8 1.6 %copy-start.5 = (bf16[2048,512]{1,0:T(8,128)(2,1)S(1)}, bf16[2048,512]{1,0:T(8,128)(2,1)}, u32[]{:S(2)}) copy-start(bf16[2048,512]{1,0:T(8,128)(2,1)} %refs_11_.1) | copy-start | bytes 6291460
  23.4 1.6 %copy-start.6 = (bf16[2048,512]{1,0:T(8,128)(2,1)S(1)}, bf16[2048,512]{1,0:T(8,128)(2,1)}, u32[]{:S(2)}) copy-start(bf16[2048,512]{1,0:T(8,128)(2,1)} %refs_12_.1) | copy-start | bytes 6291460
  25.0 1.6 %copy-start.7 = (bf16[512,2048]{1,0:T(8,128)(2,1)S(1)}, bf16[512,2048]{1,0:T(8,128)(2,1)}, u32[]{:S(2)}) copy-start(bf16[512,2048]{1,0:T(8,128)(2,1)} %refs_13_.1) | copy-start | bytes 6291460
  26.6 1.2 %copy-start.8 = (bf16[2048,256]{1,0:T(8,128)(2,1)S(1)}, bf16[2048,256]{1,0:T(8,128)(2,1)}, u32[]{:S(2)}) copy-start(bf16[2048,256]{1,0:T(8,128)(2,1)} %refs_9_.1) | copy-start | bytes 3145732
  27.8 1.2 %copy-start.9 = (bf16[2048,256]{1,0:T(8,128)(2,1)S(1)}, bf16[2048,256]{1,0:T(8,128)(2,1)}, u32[]{:S(2)}) copy-start(bf16[2048,256]{1,0:T(8,128)(2,1)} %refs_10_.1) | copy-start | bytes 3145732
  31.7 10.9 %copy-start.16 = (f32[2048]{0:T(1024)S(1)}, f32[2048]{0:T(1024)}, u32[]{:S(2)}) copy-start(f32[2048]{0:T(1024)} %param.35) | copy-start | bytes 24580
  31.7 14.2 %copy-start.11 = (bf16[32,3,256]{2,0,1:T(8,128)(2,1)S(1)}, bf16[32,3,256]{2,0,1:T(8,128)(2,1)}, u32[]{:S(2)}) copy-start(bf16[32,3,256]{2,0,1:T(8,128)(2,1)} %param.20) | copy-start | bytes 147460
  37.5 1.5 %collective-permute-start.7 = (bf16[4,96,256]{2,1,0:T(8,128)(2,1)S(1)}, bf16[4,96,256]{2,1,0:T(8,128)(2,1)S(1)}, u32[]{:S(2)}, u32[]{:S(2)}) collective-permute-start(bf16[4,96,256]{2,1,0:T(8,128)(2,1)S(1)} %get-tuple-element.28), channel_id=1, source_target_pairs={{0,1},{1,0},{2,3},{3,2},{4,5},{5,4},{6,7},{7,6},{8,9},{9,8},{10,11... | collective-permute-start | bytes 589832 | tf_op jit(solution)/shard_map/ppermute | solution.py:57
  39.1 5.5 %collective-permute-start.10 = (bf16[96,256]{1,0:T(8,128)(2,1)S(1)}, bf16[96,256]{1,0:T(8,128)(2,1)S(1)}, u32[]{:S(2)}, u32[]{:S(2)}) collective-permute-start(bf16[96,256]{1,0:T(8,128)(2,1)S(1)} %get-tuple-element.59), channel_id=1, source_target_pairs={{0,6},{1,7},{2,4},{3,5},{4,2},{5,3},{6,0},{7,1},{8,14},{9,15},{10,... | collective-permute-start | bytes 147464 | tf_op jit(solution)/shard_map/ppermute | solution.py:57
  40.3 4.3 %collective-permute-start.8 = (bf16[96,256]{1,0:T(8,128)(2,1)S(1)}, bf16[96,256]{1,0:T(8,128)(2,1)S(1)}, u32[]{:S(2)}, u32[]{:S(2)}) collective-permute-start(bf16[96,256]{1,0:T(8,128)(2,1)S(1)} %get-tuple-element.58), channel_id=1, source_target_pairs={{0,2},{1,3},{2,0},{3,1},{4,6},{5,7},{6,4},{7,5},{8,10},{9,11},{10,... | collective-permute-start | bytes 147464 | tf_op jit(solution)/shard_map/ppermute | solution.py:57
  41.8 4.1 %collective-permute-start.9 = (bf16[96,256]{1,0:T(8,128)(2,1)S(1)}, bf16[96,256]{1,0:T(8,128)(2,1)S(1)}, u32[]{:S(2)}, u32[]{:S(2)}) collective-permute-start(bf16[96,256]{1,0:T(8,128)(2,1)S(1)} %get-tuple-element.60), channel_id=1, source_target_pairs={{0,4},{1,5},{2,6},{3,7},{4,0},{5,1},{6,2},{7,3},{8,12},{9,13},{10,... | collective-permute-start | bytes 147464 | tf_op jit(solution)/shard_map/ppermute | solution.py:57
  45.9 6.4 %collective-permute-start.19 = (bf16[96,256]{1,0:T(8,128)(2,1)S(1)}, bf16[96,256]{1,0:T(8,128)(2,1)S(1)}, u32[]{:S(2)}, u32[]{:S(2)}) collective-permute-start(bf16[96,256]{1,0:T(8,128)(2,1)S(1)} %get-tuple-element.56.a_ref), channel_id=1, source_target_pairs={{0,16},{8,24},{16,0},{24,8},{1,17},{9,25},{17,1},{25,9},{2,18},{10... | collective-permute-start | bytes 147464 | tf_op jit(solution)/shard_map/ppermute | solution.py:57
  47.7 5.9 %collective-permute-start.20 = (bf16[96,256]{1,0:T(8,128)(2,1)S(1)}, bf16[96,256]{1,0:T(8,128)(2,1)S(1)}, u32[]{:S(2)}, u32[]{:S(2)}) collective-permute-start(bf16[96,256]{1,0:T(8,128)(2,1)S(1)} %get-tuple-element.56.a_ref), channel_id=1, source_target_pairs={{0,24},{8,16},{16,8},{24,0},{1,25},{9,17},{17,9},{25,1},{2,26},{10... | collective-permute-start | bytes 147464 | tf_op jit(solution)/shard_map/ppermute | solution.py:57
  49.7 4.8 %collective-permute-start.14 = (bf16[96,256]{1,0:T(8,128)(2,1)S(1)}, bf16[96,256]{1,0:T(8,128)(2,1)S(1)}, u32[]{:S(2)}, u32[]{:S(2)}) collective-permute-start(bf16[96,256]{1,0:T(8,128)(2,1)S(1)} %get-tuple-element.56.a_ref), channel_id=1, source_target_pairs={{0,8},{8,0},{16,24},{24,16},{1,9},{9,1},{17,25},{25,17},{2,10},{10... | collective-permute-start | bytes 147464 | tf_op jit(solution)/shard_map/ppermute | solution.py:57
  53.6 4.7 %collective-permute-start.21 = (bf16[1,2,96,256]{3,2,1,0:T(8,128)(2,1)S(1)}, bf16[1,2,96,256]{3,2,1,0:T(8,128)(2,1)S(1)}, u32[]{:S(2)}, u32[]{:S(2)}) collective-permute-start(bf16[1,2,96,256]{3,2,1,0:T(8,128)(2,1)S(1)} %bitcast.54), channel_id=1, source_target_pairs={{0,4},{1,5},{2,6},{3,7},{4,0},{5,1},{6,2},{7,3},{8,12},{9,13},{10,... | collective-permute-start | bytes 294920 | tf_op jit(solution)/shard_map/ppermute | solution.py:57
  54.5 5.7 %collective-permute-start.15 = (bf16[1,2,96,256]{3,2,1,0:T(8,128)(2,1)S(1)}, bf16[1,2,96,256]{3,2,1,0:T(8,128)(2,1)S(1)}, u32[]{:S(2)}, u32[]{:S(2)}) collective-permute-start(bf16[1,2,96,256]{3,2,1,0:T(8,128)(2,1)S(1)} %bitcast.55), channel_id=1, source_target_pairs={{0,2},{1,3},{2,0},{3,1},{4,6},{5,7},{6,4},{7,5},{8,10},{9,11},{10,... | collective-permute-start | bytes 294920 | tf_op jit(solution)/shard_map/ppermute | solution.py:57
  58.3 5.7 %collective-permute-start.23 = (bf16[2,2,96,256]{3,2,1,0:T(8,128)(2,1)S(1)}, bf16[2,2,96,256]{3,2,1,0:T(8,128)(2,1)S(1)}, u32[]{:S(2)}, u32[]{:S(2)}) collective-permute-start(bf16[2,2,96,256]{3,2,1,0:T(8,128)(2,1)S(1)} %stack.9.refs_2_), channel_id=1, source_target_pairs={{0,2},{1,3},{2,0},{3,1},{4,6},{5,7},{6,4},{7,5},{8,10},{9,11},{10,... | collective-permute-start | bytes 589832 | tf_op jit(solution)/shard_map/ppermute | solution.py:57
  60.2 5.7 %collective-permute-start.17 = (bf16[2,2,96,256]{3,2,1,0:T(8,128)(2,1)S(1)}, bf16[2,2,96,256]{3,2,1,0:T(8,128)(2,1)S(1)}, u32[]{:S(2)}, u32[]{:S(2)}) collective-permute-start(bf16[2,2,96,256]{3,2,1,0:T(8,128)(2,1)S(1)} %stack.7.refs_0_), channel_id=1, source_target_pairs={{0,4},{1,5},{2,6},{3,7},{4,0},{5,1},{6,2},{7,3},{8,12},{9,13},{10,... | collective-permute-start | bytes 589832 | tf_op jit(solution)/shard_map/ppermute | solution.py:57
  61.8 18.5 %collective-permute-start.11 = (bf16[96,1024]{1,0:T(8,128)(2,1)S(1)}, bf16[96,1024]{1,0:T(8,128)(2,1)S(1)}, u32[]{:S(2)}, u32[]{:S(2)}) collective-permute-start(bf16[96,1024]{1,0:T(8,128)(2,1)S(1)} %convolution_convert_fusion), channel_id=1, source_target_pairs={{0,1},{1,0},{2,3},{3,2},{4,5},{5,4},{6,7},{7,6},{8,9},{9,8},{10,11... | collective-permute-start | bytes 589832 | tf_op jit(solution)/shard_map/ppermute | solution.py:57
  61.8 14.9 %collective-permute-start.22 = (bf16[2,2,96,256]{3,2,1,0:T(8,128)(2,1)S(1)}, bf16[2,2,96,256]{3,2,1,0:T(8,128)(2,1)S(1)}, u32[]{:S(2)}, u32[]{:S(2)}) collective-permute-start(bf16[2,2,96,256]{3,2,1,0:T(8,128)(2,1)S(1)} %stack.9.refs_2_), channel_id=1, source_target_pairs={{0,1},{1,0},{2,3},{3,2},{4,5},{5,4},{6,7},{7,6},{8,9},{9,8},{10,11... | collective-permute-start | bytes 589832 | tf_op jit(solution)/shard_map/ppermute | solution.py:57
  62.3 14.4 %collective-permute-start.16 = (bf16[2,2,96,256]{3,2,1,0:T(8,128)(2,1)S(1)}, bf16[2,2,96,256]{3,2,1,0:T(8,128)(2,1)S(1)}, u32[]{:S(2)}, u32[]{:S(2)}) collective-permute-start(bf16[2,2,96,256]{3,2,1,0:T(8,128)(2,1)S(1)} %stack.7.refs_0_), channel_id=1, source_target_pairs={{0,1},{1,0},{2,3},{3,2},{4,5},{5,4},{6,7},{7,6},{8,9},{9,8},{10,11... | collective-permute-start | bytes 589832 | tf_op jit(solution)/shard_map/ppermute | solution.py:57
  64.1 12.7 %collective-permute-start.24 = (bf16[2,2,96,256]{3,2,1,0:T(8,128)(2,1)S(1)}, bf16[2,2,96,256]{3,2,1,0:T(8,128)(2,1)S(1)}, u32[]{:S(2)}, u32[]{:S(2)}) collective-permute-start(bf16[2,2,96,256]{3,2,1,0:T(8,128)(2,1)S(1)} %collective-permute-done.23.refs_3_), channel_id=1, source_target_pairs={{0,1},{1,0},{2,3},{3,2},{4,5},{5,4},{6,7},{7,6},{8,9},{9,8},{10,11... | collective-permute-start | bytes 589832 | tf_op jit(solution)/shard_map/ppermute | solution.py:57
  66.0 10.8 %collective-permute-start.18 = (bf16[2,2,96,256]{3,2,1,0:T(8,128)(2,1)S(1)}, bf16[2,2,96,256]{3,2,1,0:T(8,128)(2,1)S(1)}, u32[]{:S(2)}, u32[]{:S(2)}) collective-permute-start(bf16[2,2,96,256]{3,2,1,0:T(8,128)(2,1)S(1)} %collective-permute-done.17.refs_1_), channel_id=1, source_target_pairs={{0,1},{1,0},{2,3},{3,2},{4,5},{5,4},{6,7},{7,6},{8,9},{9,8},{10,11... | collective-permute-start | bytes 589832 | tf_op jit(solution)/shard_map/ppermute | solution.py:57
  66.0 3.4 %copy-start.2 = (f32[32,4,128,128]{3,2,1,0:T(8,128)S(1)}, f32[32,4,128,128]{3,2,1,0:T(8,128)}, u32[]{:S(2)}) copy-start(f32[32,4,128,128]{3,2,1,0:T(8,128)} %states_ref.3) | copy-start | bytes 25165828
  72.1 3.6 %copy-start.3 = (bf16[1,2048,1024]{2,1,0:T(8,128)(2,1)S(1)}, bf16[1,2048,1024]{2,1,0:T(8,128)(2,1)}, u32[]{:S(2)}) copy-start(bf16[1,2048,1024]{2,1,0:T(8,128)(2,1)} %refs_5_.3) | copy-start | bytes 12582916
  76.8 1.6 %copy-start.4 = (bf16[1,512,2048]{2,1,0:T(8,128)(2,1)S(1)}, bf16[1,512,2048]{2,1,0:T(8,128)(2,1)}, u32[]{:S(2)}) copy-start(bf16[1,512,2048]{2,1,0:T(8,128)(2,1)} %w_ref.1) | copy-start | bytes 6291460
  79.6 1.9 %collective-permute-start.25 = (bf16[4,2,96,256]{3,2,1,0:T(8,128)(2,1)S(1)}, bf16[4,2,96,256]{3,2,1,0:T(8,128)(2,1)S(1)}, u32[]{:S(2)}, u32[]{:S(2)}) collective-permute-start(bf16[4,2,96,256]{3,2,1,0:T(8,128)(2,1)S(1)} %get-tuple-element.40), channel_id=1, source_target_pairs={{0,1},{1,0},{2,3},{3,2},{4,5},{5,4},{6,7},{7,6},{8,9},{9,8},{10,11... | collective-permute-start | bytes 1179656 | tf_op jit(solution)/shard_map/ppermute | solution.py:57
  80.2 2.4 %collective-permute-start.29 = (bf16[4,2,96,256]{3,2,1,0:T(8,128)(2,1)S(1)}, bf16[4,2,96,256]{3,2,1,0:T(8,128)(2,1)S(1)}, u32[]{:S(2)}, u32[]{:S(2)}) collective-permute-start(bf16[4,2,96,256]{3,2,1,0:T(8,128)(2,1)S(1)} %get-tuple-element.46), channel_id=1, source_target_pairs={{0,1},{1,0},{2,3},{3,2},{4,5},{5,4},{6,7},{7,6},{8,9},{9,8},{10,11... | collective-permute-start | bytes 1179656 | tf_op jit(solution)/shard_map/ppermute | solution.py:57
  80.3 7.8 %collective-permute-start.12 = (bf16[96,1024]{1,0:T(8,128)(2,1)S(1)}, bf16[96,1024]{1,0:T(8,128)(2,1)S(1)}, u32[]{:S(2)}, u32[]{:S(2)}) collective-permute-start(bf16[96,1024]{1,0:T(8,128)(2,1)S(1)} %add_convert_fusion.1), channel_id=1, source_target_pairs={{0,2},{1,3},{2,0},{3,1},{4,6},{5,7},{6,4},{7,5},{8,10},{9,11},{10,... | collective-permute-start | bytes 589832 | tf_op jit(solution)/shard_map/ppermute | solution.py:57
  81.6 23.7 %copy-start.17 = (bf16[512,256]{1,0:T(8,128)(2,1)S(1)}, bf16[512,256]{1,0:T(8,128)(2,1)}, u32[]{:S(2)}) copy-start(bf16[512,256]{1,0:T(8,128)(2,1)} %param.37) | copy-start | bytes 786436
  81.6 10.2 %collective-permute-start.26 = (bf16[2,2,96,256]{3,2,1,0:T(8,128)(2,1)S(1)}, bf16[2,2,96,256]{3,2,1,0:T(8,128)(2,1)S(1)}, u32[]{:S(2)}, u32[]{:S(2)}) collective-permute-start(bf16[2,2,96,256]{3,2,1,0:T(8,128)(2,1)S(1)} %get-tuple-element.42), channel_id=1, source_target_pairs={{0,2},{1,3},{2,0},{3,1},{4,6},{5,7},{6,4},{7,5},{8,10},{9,11},{10,... | collective-permute-start | bytes 589832 | tf_op jit(solution)/shard_map/ppermute | solution.py:57
  82.7 10.6 %collective-permute-start.30 = (bf16[2,2,96,256]{3,2,1,0:T(8,128)(2,1)S(1)}, bf16[2,2,96,256]{3,2,1,0:T(8,128)(2,1)S(1)}, u32[]{:S(2)}, u32[]{:S(2)}) collective-permute-start(bf16[2,2,96,256]{3,2,1,0:T(8,128)(2,1)S(1)} %get-tuple-element.48), channel_id=1, source_target_pairs={{0,4},{1,5},{2,6},{3,7},{4,0},{5,1},{6,2},{7,3},{8,12},{9,13},{10,... | collective-permute-start | bytes 589832 | tf_op jit(solution)/shard_map/ppermute | solution.py:57
  88.1 13.4 %collective-permute-start.13 = (bf16[96,1024]{1,0:T(8,128)(2,1)S(1)}, bf16[96,1024]{1,0:T(8,128)(2,1)S(1)}, u32[]{:S(2)}, u32[]{:S(2)}) collective-permute-start(bf16[96,1024]{1,0:T(8,128)(2,1)S(1)} %add_convert_fusion), channel_id=1, source_target_pairs={{0,4},{1,5},{2,6},{3,7},{4,0},{5,1},{6,2},{7,3},{8,12},{9,13},{10,... | collective-permute-start | bytes 589832 | tf_op jit(solution)/shard_map/ppermute | solution.py:57
  91.9 4.7 %collective-permute-start.27 = (bf16[1,2,96,256]{3,2,1,0:T(8,128)(2,1)S(1)}, bf16[1,2,96,256]{3,2,1,0:T(8,128)(2,1)S(1)}, u32[]{:S(2)}, u32[]{:S(2)}) collective-permute-start(bf16[1,2,96,256]{3,2,1,0:T(8,128)(2,1)S(1)} %get-tuple-element.44), channel_id=1, source_target_pairs={{0,4},{1,5},{2,6},{3,7},{4,0},{5,1},{6,2},{7,3},{8,12},{9,13},{10,... | collective-permute-start | bytes 294920 | tf_op jit(solution)/shard_map/ppermute | solution.py:57
  93.4 4.7 %collective-permute-start.31 = (bf16[1,2,96,256]{3,2,1,0:T(8,128)(2,1)S(1)}, bf16[1,2,96,256]{3,2,1,0:T(8,128)(2,1)S(1)}, u32[]{:S(2)}, u32[]{:S(2)}) collective-permute-start(bf16[1,2,96,256]{3,2,1,0:T(8,128)(2,1)S(1)} %get-tuple-element.50), channel_id=1, source_target_pairs={{0,2},{1,3},{2,0},{3,1},{4,6},{5,7},{6,4},{7,5},{8,10},{9,11},{10,... | collective-permute-start | bytes 294920 | tf_op jit(solution)/shard_map/ppermute | solution.py:57
  96.6 5.0 %collective-permute-start.28 = (bf16[96,256]{1,0:T(8,128)(2,1)S(1)}, bf16[96,256]{1,0:T(8,128)(2,1)S(1)}, u32[]{:S(2)}, u32[]{:S(2)}) collective-permute-start(bf16[96,256]{1,0:T(8,128)(2,1)S(1)} %slice_bitcast_fusion.2), channel_id=1, source_target_pairs={{0,8},{8,0},{16,24},{24,16},{1,9},{9,1},{17,25},{25,17},{2,10},{10... | collective-permute-start | bytes 147464 | tf_op jit(solution)/shard_map/ppermute | solution.py:57
  98.1 5.1 %collective-permute-start.32 = (bf16[96,256]{1,0:T(8,128)(2,1)S(1)}, bf16[96,256]{1,0:T(8,128)(2,1)S(1)}, u32[]{:S(2)}, u32[]{:S(2)}) collective-permute-start(bf16[96,256]{1,0:T(8,128)(2,1)S(1)} %get-tuple-element.61), channel_id=1, source_target_pairs={{0,16},{8,24},{16,0},{24,8},{1,17},{9,25},{17,1},{25,9},{2,18},{10... | collective-permute-start | bytes 147464 | tf_op jit(solution)/shard_map/ppermute | solution.py:57
  99.4 5.9 %collective-permute-start.33 = (bf16[96,256]{1,0:T(8,128)(2,1)S(1)}, bf16[96,256]{1,0:T(8,128)(2,1)S(1)}, u32[]{:S(2)}, u32[]{:S(2)}) collective-permute-start(bf16[96,256]{1,0:T(8,128)(2,1)S(1)} %get-tuple-element.62), channel_id=1, source_target_pairs={{0,24},{8,16},{16,8},{24,0},{1,25},{9,17},{17,9},{25,1},{2,26},{10... | collective-permute-start | bytes 147464 | tf_op jit(solution)/shard_map/ppermute | solution.py:57
  (4 other events, 2.7 us)

commit v2 on v1

--- a/solution.py
+++ b/solution.py
@@ -57,14 +57,36 @@
     return lax.ppermute(x, axis, [(i, i ^ bit) for i in range(size)])
 
 
-def stack_kernel(a_ref, b_ref, out_ref):
+def stack_kernel(a_ref, b_ref, *refs):
+    out_ref = refs[-1]
     out_ref[0] = a_ref[...]
     out_ref[1] = b_ref[...]
 
 
-def stack(a, b):
-    [out] = call(stack_kernel, "stack", [pltpu.VMEM((2, *a.shape), a.dtype)], (), (a, b))
+def stack(a, b, after=()):
+    [out] = call(stack_kernel, "stack", [pltpu.VMEM((2, *a.shape), a.dtype)], (), (a, b), after)
     return out
+
+
+def load_kernel(count, *refs):
+    sources, targets, sems = refs[:count], refs[-1 - count : -1], refs[-1]
+    copies = [pltpu.make_async_copy(a, b, sems.at[n]) for n, (a, b) in enumerate(zip(sources, targets))]
+    for copy in copies:
+        copy.start()
+    for copy in copies:
+        copy.wait()
+
+
+def load(arrays, after=()):
+    return call(
+        functools.partial(load_kernel, len(arrays)),
+        "load",
+        [pltpu.VMEM(x.shape, x.dtype) for x in arrays],
+        (),
+        (),
+        (*(pltpu.with_memory_space_constraint(x, pltpu.HBM) for x in arrays), *after),
+        [pltpu.SemaphoreType.DMA((len(arrays),))],
+    )
 
 
 def front_kernel(
@@ -77,9 +99,7 @@
     (
         gain_ref,
         small_ref,
-        scale_ref,
-        bias_ref,
-        ggain_ref,
+        pack_ref,
         wq,
         wk,
         wv,
@@ -132,9 +152,9 @@
         )
         small = term if small is None else small + term
     betas = 1.0 / (1.0 + jnp.exp(-small[:, :value_heads]))
-    alphas = small[:, value_heads : 2 * value_heads] + bias_ref[...]
+    alphas = small[:, value_heads : 2 * value_heads] + pack_ref[1:2, :value_heads]
     softplus = jnp.maximum(alphas, 0.0) + jnp.log1p(jnp.exp(-jnp.abs(alphas)))
-    decays = jnp.exp(-scale_ref[...] * softplus)
+    decays = jnp.exp(-pack_ref[0:1, :value_heads] * softplus)
 
     def units(v):
         return v * lax.rsqrt(jnp.sum(v * v, axis=1, keepdims=True) + EPS)
@@ -221,7 +241,7 @@
     for h in range(value_heads):
         m = mixed[:, h * DV : (h + 1) * DV]
         m = m * lax.rsqrt(jnp.mean(m * m, axis=1, keepdims=True) + EPS)
-        gated.append((m * ggain_ref[...] * gates[:, h * DV : (h + 1) * DV]).astype(BF16))
+        gated.append((m * pack_ref[2:3, :DV] * gates[:, h * DV : (h + 1) * DV]).astype(BF16))
     gated = jnp.concatenate(gated, axis=1)
     for c in range(head_count):
         piece = dot(gated, wo[:, c * width : (c + 1) * width]).astype(BF16)
@@ -236,7 +256,7 @@
             sib_ref[away // 2] = piece
 
 
-def front(me, xs, gain, small, scale, bias, ggain, wq, wk, wv, wz, wo, states, after, steps):
+def front(me, xs, gain, small, pack, wq, wk, wv, wz, wo, states, after, steps):
     _, rows, width = xs[0].shape
     head_count = 2 * len(xs)
     seqs = rows // steps
@@ -254,7 +274,7 @@
             pltpu.VMEM((key_heads, seqs, pair), F32),
         ],
         (me,),
-        (*xs, gain, small, scale, bias, ggain, wq, wk, wv, wz, wo, states),
+        (*xs, gain, small, pack, wq, wk, wv, wz, wo, states),
         (after,),
         [
             pltpu.VMEM((key_heads, seqs * SLOTS, DK), F32),
@@ -263,13 +283,63 @@
     )
 
 
+def rows_kernel(pairs, *refs):
+    merged_ref, received = refs[0], refs[1:pairs]
+    mine_ref, gain_ref, extra_ref, w_ref, _ = refs[pairs : pairs + 5]
+    resid_ref, x_ref, shared_ref = refs[pairs + 5 : pairs + 8]
+    messages = refs[pairs + 8 :]
+    rows = mine_ref.shape[0]
+    resid = mine_ref[...].astype(F32) + merged_ref[0].astype(F32)
+    for ref in received:
+        resid = resid + ref[...].astype(F32)
+    resid_ref[...] = resid
+    x = (resid * gain_ref[...]).astype(BF16)
+    x_ref[...] = x
+    for z, ref in enumerate(messages):
+        ref[:rows, :] = x
+        ref[rows:, :] = extra_ref[z + 1]
+    shared_ref[...] = dot(x, w_ref[...]).astype(BF16)
+
+
+def make_rows(merged, received, mine, gain, extra, w, after):
+    rows, width = mine.shape
+    message = pltpu.VMEM((rows + extra.shape[1], width), BF16)
+    return call(
+        functools.partial(rows_kernel, merged.shape[0]),
+        "rows",
+        [
+            pltpu.VMEM((rows, width), F32),
+            pltpu.VMEM((rows, width), BF16),
+            pltpu.VMEM((rows, w.shape[1]), BF16),
+            *([message] * (extra.shape[0] - 1)),
+        ],
+        (),
+        (merged, *received, mine, gain, extra, w),
+        after,
+    )
+
+
+def slab_kernel(a_ref, b_ref, out_ref):
+    rows = out_ref.shape[1]
+    out_ref[0] = a_ref[:rows, :]
+    out_ref[1] = b_ref[:rows, :]
+
+
+def slab_pair(a, b, rows):
+    [out] = call(slab_kernel, "slab", [pltpu.VMEM((2, rows, a.shape[1]), BF16)], (), (a, b))
+    return out
+
+
 PER_BLOCK = DK // SLOTS
 
 
-def update_kernel(steps, blocks, aliased, keys_ref, delta_ref, total_ref, states_ref, *refs):
-    if aliased:
-        refs = refs[1:]
-    _, out_ref, done_ref, left, right, buffers, sems = refs
+def update_kernel(steps, blocks, keys_ref, delta_ref, total_ref, states_ref, *refs):
+    out_ref, done_ref, left, right, olds, buffers, old_sems, sems = refs[-8:]
+    loads = []
+    for n, block in enumerate(blocks):
+        span = pl.ds(block * PER_BLOCK, PER_BLOCK)
+        loads.append(pltpu.make_async_copy(states_ref.at[span], olds.at[n], old_sems.at[n]))
+        loads[-1].start()
     key_heads, rows, _ = keys_ref.shape
     seqs = rows // steps
     group = states_ref.shape[1] // key_heads
@@ -292,6 +362,7 @@
     for n, block in enumerate(blocks):
         if n >= 2:
             copies[n - 2].wait()
+        loads[n].wait()
         buffer = buffers.at[n % 2]
         span = slice(n * DK, (n + 1) * DK)
         for i in range(key_heads):
@@ -306,7 +377,7 @@
                     columns = slice(u * DV, (u + 1) * DV)
                     h = i * group + u
                     total = total_ref[i, s : s + 1, columns]
-                    buffer[m, h] = states_ref[s, h] * total + change[:, columns]
+                    buffer[m, h] = olds[n, m, h] * total + change[:, columns]
         span = pl.ds(block * PER_BLOCK, PER_BLOCK)
         copies.append(pltpu.make_async_copy(buffer, out_ref.at[span], sems.at[n % 2]))
         copies[-1].start()
@@ -319,18 +390,20 @@
     key_heads, steps, seqs, pair = deltas.shape
     rows = len(blocks) * DK
     value_heads = states.shape[1]
-    loose = (after,) if before is None else (before, after)
+    loose = after if before is None else (before, *after)
     return call(
-        functools.partial(update_kernel, steps, blocks, before is not None),
+        functools.partial(update_kernel, steps, blocks),
         "update",
         [jax.ShapeDtypeStruct(states.shape, F32), jax.ShapeDtypeStruct((8, 128), F32)],
         (),
-        (keys, deltas, totals, states),
-        loose,
+        (keys, deltas, totals),
+        (pltpu.with_memory_space_constraint(states, pltpu.HBM), *loose),
         [
             pltpu.VMEM((key_heads, rows, DK), F32),
             pltpu.VMEM((value_heads, rows, DV), F32),
+            pltpu.VMEM((len(blocks), PER_BLOCK, *states.shape[1:]), F32),
             pltpu.VMEM((2, PER_BLOCK, *states.shape[1:]), F32),
+            pltpu.SemaphoreType.DMA((len(blocks),)),
             pltpu.SemaphoreType.DMA((2,)),
         ],
         None if before is None else {4: 0},
@@ -393,8 +466,9 @@
     )
 
 
-def expert_out_kernel(orders, me_ref, pre_ref, sq_ref, weight_ref, w_ref, *outs):
+def expert_out_kernel(orders, me_ref, pre_ref, sq_ref, extra_ref, w_ref, *refs):
     me = me_ref[0]
+    messages, outs = refs[:-4], refs[-4:]
     features = w_ref.shape[2]
     hidden_width = w_ref.shape[1]
     start = 0
@@ -407,7 +481,12 @@
         gate = pre_ref[span, :hidden_width] * inverse
         up = pre_ref[span, hidden_width:] * inverse
         hidden = (silu(gate) * up).astype(BF16)
-        weight = weight_ref[span, :]
+        weight = []
+        for z in range(side * zs, (side + 1) * zs):
+            extra = messages[z - 1][rows:, :] if z else extra_ref[0]
+            columns = jnp.transpose(extra.astype(F32))
+            weight.append(columns[:rows, 0:1] + columns[:rows, 1:2])
+        weight = jnp.concatenate(weight, axis=0)
         for odd, ref in ((1, sib), (0, own)):
             for n in range(count):
                 block = me ^ (2 * order[n] + odd)
@@ -416,13 +495,14 @@
                 ref[n] = result.astype(BF16).reshape(zs, rows, width)
 
 
-def expert_out(me, pre, sq, weight, w, orders, shapes):
+def expert_out(me, pre, sq, extra, w, messages, orders, shapes, after):
     return call(
         functools.partial(expert_out_kernel, orders),
         "expert_out",
         [pltpu.VMEM(shape, BF16) for shape in shapes],
         (me,),
-        (pre, sq, weight, w),
+        (pre, sq, extra, w, *messages),
+        after,
     )
 
 
@@ -446,6 +526,45 @@
     return call(
         half_sum_kernel, "half_sum", [pltpu.VMEM(shape, BF16), pltpu.VMEM(shape, BF16)], (), (a, b)
     )
+
+
+def last_sum_kernel(a_ref, b_ref, *outs):
+    for z, ref in enumerate(outs):
+        ref[...] = add(a_ref[0, z], b_ref[0, z])
+
+
+def last_sum(a, b):
+    _, zs, rows, width = a.shape
+    return call(last_sum_kernel, "last_sum", [pltpu.VMEM((rows, width), BF16)] * zs, (), (a, b))
+
+
+def one_sum_kernel(a_ref, b_ref, *refs):
+    refs[-1][...] = add(a_ref[...], b_ref[...])
+
+
+def one_sum(a, b, after=()):
+    [out] = call(one_sum_kernel, "one_sum", [pltpu.VMEM(a.shape, BF16)], (), (a, b), after)
+    return out
+
+
+def shared_kernel(features, a_ref, b_ref, sq_ref, resid_ref, w_ref, out_ref):
+    rows = a_ref.shape[0]
+    half = a_ref.shape[1] // 2
+    inverse = lax.rsqrt(sq_ref[:rows, :] / features + EPS)
+    pre = (a_ref[...].astype(F32) + b_ref[...].astype(F32)) * inverse
+    hidden = (silu(pre[:, :half]) * pre[:, half:]).astype(BF16)
+    out_ref[...] = resid_ref[...] + dot(hidden, w_ref[...])
+
+
+def shared_tail(features, a, b, sq, resid, w):
+    [out] = call(
+        functools.partial(shared_kernel, features),
+        "shared",
+        [pltpu.VMEM(resid.shape, F32)],
+        (),
+        (a, b, sq, resid, w),
+    )
+    return out
 
 
 def on_device(
@@ -482,98 +601,106 @@
     axes = [1 << n for n in range(1, head_count.bit_length() - 1)]
 
     mine = jnp.transpose(tokens, (1, 0, 2)).reshape(rows, width)
-
-    both = stack(mine, exchange(mine, "head", 1))
+    value_heads = w_beta.shape[1]
+    gain = input_gain.reshape(head_count, 1, width)
+    gain_after = post_gain.reshape(head_count, 1, width)
+
+    neighbour = exchange(mine, "head", 1)
+    mine, gain, gain_after, w_query, w_key, w_value, w_zgate = load(
+        (mine, gain, gain_after, w_query, w_key, w_value, w_zgate)
+    )
+    both = stack(mine, neighbour)
     gathered = [both] + [exchange(both, "head", 2 * p) for p in range(1, pairs)]
+    states_here, w_out, w_shared_in, w_shared_out = load(
+        (states, w_out, w_shared_in, w_shared_out), (both,)
+    )
 
     ids = jnp.transpose(router_ids, (1, 0, 2)).reshape(rows, -1)
     chosen = jnp.transpose(router_weights, (1, 0, 2)).reshape(rows, -1)
-    row_weights = []
-    for z in range(seq_count):
-        target = (seq_index ^ z) * head_count + head_index
-        weight = jnp.sum(jnp.where(ids == target, chosen, 0.0), axis=1).reshape(1, rows)
-        row_weights.append(exchange(weight, "seq", z) if z else weight)
-    row_weight = jnp.concatenate(row_weights, axis=1).reshape(seq_count * rows, 1)
-
-    value_heads = w_beta.shape[1]
+    targets = (seq_index ^ jnp.arange(seq_count, dtype=jnp.int32)) * head_count + head_index
+    named = ids[None] == targets[:, None, None]
+    weights = jnp.sum(jnp.where(named, chosen[None], 0.0), axis=2)
+    high, low = split(weights)
+    extra = jnp.stack([high, low], axis=1)
+    extra = jnp.pad(extra, ((0, 0), (0, 14), (0, width - rows)))
+
     small = jnp.concatenate([w_beta, w_alpha], axis=1)
     small = jnp.transpose(small.reshape(head_count, width, 2 * value_heads), (0, 2, 1))
     small = jnp.pad(small, ((0, 0), (0, -2 * value_heads % 16), (0, 0)))
+    pack = jnp.stack(
+        [
+            jnp.pad(decay_scale, (0, DV - value_heads)),
+            jnp.pad(dt_bias, (0, DV - value_heads)),
+            gated_gain,
+        ]
+    )
 
     own, sib, keys, deltas, totals = front(
-        me,
-        gathered,
-        input_gain.reshape(head_count, 1, width),
-        small,
-        decay_scale.reshape(1, value_heads),
-        dt_bias.reshape(1, value_heads),
-        gated_gain.reshape(1, DV),
-        w_query,
-        w_key,
-        w_value,
-        w_zgate,
-        w_out,
-        states,
-        row_weight,
-        steps,
-    )
-
-    merged = add(own, exchange(sib, "head", 1))
-    resid = mine.astype(F32) + merged[0].astype(F32)
-    for p in range(1, pairs):
-        resid = resid + exchange(merged[p], "head", 2 * p).astype(F32)
-    gain_mine = lax.dynamic_slice_in_dim(post_gain, head_index * width, width, 0)
-    x = (resid * gain_mine).astype(BF16)
+        me, gathered, gain, small, pack, w_query, w_key, w_value, w_zgate, w_out, states_here, extra, steps
+    )
+
+    merged = one_sum(own, exchange(sib, "head", 1))
+    received = [exchange(merged[p], "head", 2 * p) for p in range(1, pairs)]
+    w_in, w_down = load((w_expert_in, w_expert_out), (merged,))
+    gain_mine = lax.dynamic_index_in_dim(gain_after, head_index, 0, keepdims=False)
+    resid, x, shared_pre, *messages = make_rows(
+        merged, received, mine, gain_mine, extra, w_shared_in, (w_in,)
+    )
 
     half = seq_count // 2
-    slabs = [x] + [exchange(x, "seq", z) for z in range(1, seq_count)]
+    messages = [exchange(m, "seq", z + 1) for z, m in enumerate(messages)]
+    shared_pre = one_sum(shared_pre, exchange(shared_pre, "head", axes[0]))
+    shared_next = one_sum(shared_pre, exchange(shared_pre, "head", 1))
+    slabs = [x] + messages
     natural, reverse = list(range(pairs)), bit_reversed(pairs)
-    sides, siblings, firsts = [], [], []
+    blocks = tuple(range(seqs // PER_BLOCK))
+    cut = len(blocks) // 2
+    sides, siblings, tie = [], [], ()
     for slab, bits in ((slabs[:half], axes), (slabs[half:], axes[::-1])):
-        side = slab[0][None]
-        side = stack(*slab)[None] if half == 2 else jnp.stack(slab)[None]
+        if half == 2:
+            side = slab_pair(*slab, rows)[None]
+        else:
+            side = jnp.stack([m[:rows] for m in slab])[None]
         for bit in bits[:-1]:
             received = exchange(side, "head", bit)
-            firsts.append(received)
-            side = stack(side[0], received[0]) if side.shape[0] == 1 else jnp.concatenate([side, received])
+            if not tie:
+                states_out, done_1 = update(keys, deltas, totals, states, blocks[:cut], (side, shared_pre))
+                tie = (done_1,)
+            if side.shape[0] == 1:
+                side = stack(side[0], received[0], tie)
+            else:
+                side = jnp.concatenate([side, received])
         sides.append([side, exchange(side, "head", bits[-1])])
         siblings.append([exchange(piece, "head", 1) for piece in sides[-1]])
-    gain_inv = (1.0 / post_gain).reshape(head_count, 1, width)
+    gain_inv = 1.0 / gain_after
     middle = pairs // 2
     orders = tuple((tuple(o[:middle]), tuple(o[middle:])) for o in (natural, reverse))
 
-    blocks = tuple(range(seqs // PER_BLOCK))
-    cut = len(blocks) // 2
-    states_out, done_1 = update(keys, deltas, totals, states, blocks[:cut], slabs[1])
     states_out, done_2 = update(
-        keys, deltas, totals, states, blocks[cut:], firsts[0], states_out
-    )
-    pre = expert_in(me, sides, gain_inv, w_expert_in, orders, 0, after=(done_1, done_2))
-    pre, squares = expert_in(me, siblings, gain_inv, w_expert_in, orders, 1, pre)
+        keys, deltas, totals, states, blocks[cut:], (sides[1][0], shared_next), states_out
+    )
+    pre = expert_in(me, sides, gain_inv, w_in, orders, 0, after=(done_2,))
+    pre, squares = expert_in(me, siblings, gain_inv, w_in, orders, 1, pre)
+    shared_pre, shared_received = shared_next, None
+    for bit in axes[1:]:
+        if shared_received is not None:
+            shared_pre = one_sum(shared_pre, shared_received)
+        shared_received = exchange(shared_pre, "head", bit)
     shape = (pairs, half, rows, width)
     a_own, a_sib, b_own, b_sib = expert_out(
-        me, pre, squares, row_weight, w_expert_out, (reverse, natural), (shape,) * 4
-    )
-    sums = []
+        me, pre, squares, extra, w_down, messages, (reverse, natural), (shape,) * 4, (shared_received,)
+    )
+    base = shared_tail(features, shared_pre, shared_received, squares, resid, w_shared_out)
+    slabs = []
     for own, sib, bits in ((a_own, a_sib, axes), (b_own, b_sib, axes[::-1])):
         received = exchange(sib, "head", 1)
         for bit in bits:
             own, sent = half_sum(own, received)
             received = exchange(sent, "head", bit)
-        sums.append(add(own[0], received[0]))
-
-    shared_pre = dot(x, w_shared_in)
-    for bit in [1] + axes:
-        sent = shared_pre.astype(BF16)
-        shared_pre = sent.astype(F32) + exchange(sent, "head", bit).astype(F32)
-    shared_pre = shared_pre * lax.rsqrt(squares[:rows] / features + EPS)
-    half_shared = shared_pre.shape[1] // 2
-    hidden = (silu(shared_pre[:, :half_shared]) * shared_pre[:, half_shared:]).astype(BF16)
-    result = resid + dot(hidden, w_shared_out)
-
-    for z in range(seq_count):
-        part = sums[z // half][z % half]
-        result = result + (exchange(part, "seq", z) if z else part).astype(F32)
+        slabs += last_sum(own, received)
+    result = base + slabs[0].astype(F32)
+    for z in range(1, seq_count):
+        result = result + exchange(slabs[z], "seq", z).astype(F32)
     layer_out = jnp.transpose(result.astype(BF16).reshape(steps, seqs, width), (1, 0, 2))
     return (layer_out, states_out)
 

time: 107 us -> 88.1 us (0.82)
  local copies, waits for them, and re-layouts: 19.3 us -> 2.31 us
  Pallas kernels: 15 us -> 28.7 us
  waiting for transfers between devices: 34.9 us -> 26.6 us
  starting transfers between devices: 32.9 us -> 27.6 us
    unnamed x36 -> x2, local copies, waits for them, and re-layouts: 18.7 us -> 0.01 us
    pallas_call x15 -> x25, Pallas kernels: 15 us -> 28.7 us  [call(): pl.pallas_call(body, out_shape=tuple(out_shapes), in_specs=[SMEM_SPEC] *...]
    ppermute x34 -> x31, waiting for transfers between devices: 34.9 us -> 26.6 us  [exchange(): return lax.ppermute(x, axis, [(i, i ^ bit) for i in range(size)])]
    ppermute x34 -> x31, starting transfers between devices: 32.9 us -> 27.6 us  [exchange(): return lax.ppermute(x, axis, [(i, i ^ bit) for i in range(size)])]
  transfers between devices with their start and end apart: 34 -> 31, of which waited for: 21 -> 14; matrix products, arithmetic and copies ran while one was open for 2% -> 4% of each run, Pallas kernels for 9% -> 25%
where the time goes in v2:
time: 88.1 us; the launch traced here: 87.7 us
  Pallas kernels  28.7 us (33%)
  starting transfers between devices  27.6 us (31%)
  waiting for transfers between devices  26.6 us (30%)
  local copies, waits for them, and re-layouts  2.31 us (3%)
  other arithmetic  1.56 us (2%)
  between operations  0.9 us (1%)
    pallas_call x25, Pallas kernels, call(): pl.pallas_call(body, out_shape=tuple(out_shapes), in_specs=[SMEM_SPEC] *...  28.7 us
    ppermute x31, starting transfers between devices, exchange(): return lax.ppermute(x, axis, [(i, i ^ bit) for i in range(size)])  27.6 us
    ppermute x31, waiting for transfers between devices, exchange(): return lax.ppermute(x, axis, [(i, i ^ bit) for i in range(size)])  26.6 us
  transfers between devices with their start and end apart: 31, of which 14 were waited for; matrix products, arithmetic and copies ran while one was open for 4% of the time, Pallas kernels for 25%

profile of v2, /device:TPU:0, one launch (start us, length us, event | category | flops | bytes accessed | tf_op | source)
XLA Modules:
  0.0 87.7 jit_solution(3829654265820364987)
XLA Ops:
  0.6 0.5 collective-permute-start
  1.1 0.8 broadcast_in_dim.21
  2.0 0.8 eq.15
  2.9 0.8 pad_maximum_fusion
  3.7 0.7 pad_bitcast_fusion
  4.4 3.0 %load.3 = (bf16[96,256]{1,0:T(8,128)(2,1)S(1)}, f32[8,1,256]{2,1,0:T(1,128)S(1)}, f32[8,1,256]{2,1,0:T(1,128)S(1)}, bf16[2048,256]{1,0:T(8,128)(2,1)S(1)}, bf16[...) custom-call(bf16[96,256]{1,0:T(8,128)(2,1)} %bitcast.43, ...), custom_call_target="tpu_custom_call" | custom-call | tf_op jit(solution)/shard_map/load/pallas_call | solution.py:43
  7.4 2.6 %collective-permute-start.1 = (bf16[2,96,256]{2,1,0:T(8,128)(2,1)S(1)}, bf16[2,96,256]{2,1,0:T(8,128)(2,1)S(1)}, u32[]{:S(2)}, u32[]{:S(2)}) collective-permute-start(bf16[2,96,256]{2,1,0:T(8,128)(2,1)S(1)} %stack.25.refs_4_.refs_0_), channel_id=1, source_target_pairs={{0,2},{1,3},{2,0},{3,1},{4,6},{5,7},{6,4},{7,5},{8,10},{9,11},{10,... | collective-permute-start | bytes 294920 | tf_op jit(solution)/shard_map/ppermute | solution.py:57
  9.9 1.5 %collective-permute-start.2 = (bf16[2,96,256]{2,1,0:T(8,128)(2,1)S(1)}, bf16[2,96,256]{2,1,0:T(8,128)(2,1)S(1)}, u32[]{:S(2)}, u32[]{:S(2)}) collective-permute-start(bf16[2,96,256]{2,1,0:T(8,128)(2,1)S(1)} %stack.25.refs_4_.refs_0_), channel_id=1, source_target_pairs={{0,4},{1,5},{2,6},{3,7},{4,0},{5,1},{6,2},{7,3},{8,12},{9,13},{10,... | collective-permute-start | bytes 294920 | tf_op jit(solution)/shard_map/ppermute | solution.py:57
  11.5 4.1 %load.4 = (f32[32,4,128,128]{3,2,1,0:T(8,128)S(1)}, bf16[512,2048]{1,0:T(8,128)(2,1)S(1)}, bf16[256,1024]{1,0:T(8,128)(2,1)S(1)}, bf16[512,256]{1,0:T(8,128)(2,1)S(1)}) custom-call(f32[32,4,128,128]{3,2,1,0:T(8,128)} %states_ref.3, bf16[512,2048]{1,0:T(8,128)(2,1)} %refs_1_.2, bf16[256,1024]{1,0:T(8,128)(2,1)} %refs_2_.1, bf16[512,256]{1,0:T(8,128)(2,1)} %refs_3_.3, ...), custom_call_target="tpu_custom_call" | custom-call | tf_op jit(solution)/shard_map/load/pallas_call | solution.py:43
  16.0 1.0 %collective-permute-done.3.refs_3_ = bf16[2,96,256]{2,1,0:T(8,128)(2,1)S(1)} collective-permute-done((bf16[2,96,256]{2,1,0:T(8,128)(2,1)S(1)}, bf16[2,96,256]{2,1,0:T(8,128)(2,1)S(1)}, u32[]{:S(2)}, u32[]{:S(2)}) %collective-permute-start.3) | collective-permute-done | bytes 98336 | tf_op jit(solution)/shard_map/ppermute | solution.py:57
  17.0 5.7 %front.1 = (bf16[4,96,256]{2,1,0:T(8,128)(2,1)S(1)}, bf16[4,96,256]{2,1,0:T(8,128)(2,1)S(1)}, f32[2,96,128]{2,1,0:T(8,128)S(1)}, f32[2,3,32,256]{3,2,1,0:T(8,128)S(1)}, f32[2,32,256]{2,1,0:T(8,128)S(1)}) custom-call(s32[1]{0:T(128)} %bitcast.me_ref, bf16[2,96,256]{2,1,0:T(8,128)(2,1)S(1)} %stack.25.refs_4_.refs_0_, ...), custom_call_target="tpu_custom_call" | custom-call | tf_op jit(solution)/shard_map/front/pallas_call | solution.py:43
  22.8 1.4 %collective-permute-done.4.b_ref = bf16[4,96,256]{2,1,0:T(8,128)(2,1)S(1)} collective-permute-done((bf16[4,96,256]{2,1,0:T(8,128)(2,1)S(1)}, bf16[4,96,256]{2,1,0:T(8,128)(2,1)S(1)}, u32[]{:S(2)}, u32[]{:S(2)}) %collective-permute-start.4) | collective-permute-done | bytes 196640 | tf_op jit(solution)/shard_map/ppermute | solution.py:57
  24.3 1.3 %collective-permute-start.5 = (bf16[96,256]{1,0:T(8,128)(2,1)S(1)}, bf16[96,256]{1,0:T(8,128)(2,1)S(1)}, u32[]{:S(2)}, u32[]{:S(2)}) collective-permute-start(bf16[96,256]{1,0:T(8,128)(2,1)S(1)} %get-tuple-element.100), channel_id=1, source_target_pairs={{0,2},{1,3},{2,0},{3,1},{4,6},{5,7},{6,4},{7,5},{8,10},{9,11},{10,... | collective-permute-start | bytes 147464 | tf_op jit(solution)/shard_map/ppermute | solution.py:57
  25.5 0.9 %collective-permute-start.6 = (bf16[96,256]{1,0:T(8,128)(2,1)S(1)}, bf16[96,256]{1,0:T(8,128)(2,1)S(1)}, u32[]{:S(2)}, u32[]{:S(2)}) collective-permute-start(bf16[96,256]{1,0:T(8,128)(2,1)S(1)} %get-tuple-element.99), channel_id=1, source_target_pairs={{0,4},{1,5},{2,6},{3,7},{4,0},{5,1},{6,2},{7,3},{8,12},{9,13},{10,... | collective-permute-start | bytes 147464 | tf_op jit(solution)/shard_map/ppermute | solution.py:57
  26.5 1.4 %collective-permute-start.7 = (bf16[96,256]{1,0:T(8,128)(2,1)S(1)}, bf16[96,256]{1,0:T(8,128)(2,1)S(1)}, u32[]{:S(2)}, u32[]{:S(2)}) collective-permute-start(bf16[96,256]{1,0:T(8,128)(2,1)S(1)} %get-tuple-element.98), channel_id=1, source_target_pairs={{0,6},{1,7},{2,4},{3,5},{4,2},{5,3},{6,0},{7,1},{8,14},{9,15},{10,... | collective-permute-start | bytes 147464 | tf_op jit(solution)/shard_map/ppermute | solution.py:57
  27.8 2.9 %load.5 = (bf16[1,2048,1024]{2,1,0:T(8,128)(2,1)S(1)}, bf16[1,512,2048]{2,1,0:T(8,128)(2,1)S(1)}) custom-call(bf16[1,2048,1024]{2,1,0:T(8,128)(2,1)} %refs_0_.3, bf16[1,512,2048]{2,1,0:T(8,128)(2,1)} %refs_1_.3, bf16[4,96,256]{2,1,0:T(8,128)(2,1)S(1)} %one_sum.3.refs_2_.refs_0_), custom_call_target="tpu_custom_call" | custom-call | tf_op jit(solution)/shard_map/load/pallas_call | solution.py:43
  30.7 0.7 collective-permute-done.7.refs_3_
  31.7 1.4 %collective-permute-start.8 = (bf16[96,1024]{1,0:T(8,128)(2,1)S(1)}, bf16[96,1024]{1,0:T(8,128)(2,1)S(1)}, u32[]{:S(2)}, u32[]{:S(2)}) collective-permute-start(bf16[96,1024]{1,0:T(8,128)(2,1)S(1)} %get-tuple-element.63.a_ref), channel_id=1, source_target_pairs={{0,2},{1,3},{2,0},{3,1},{4,6},{5,7},{6,4},{7,5},{8,10},{9,11},{10,... | collective-permute-start | bytes 589832 | tf_op jit(solution)/shard_map/ppermute | solution.py:57
  33.1 2.6 %collective-permute-start.16 = (bf16[112,256]{1,0:T(8,128)(2,1)S(1)}, bf16[112,256]{1,0:T(8,128)(2,1)S(1)}, u32[]{:S(2)}, u32[]{:S(2)}) collective-permute-start(bf16[112,256]{1,0:T(8,128)(2,1)S(1)} %get-tuple-element.70), channel_id=1, source_target_pairs={{0,16},{8,24},{16,0},{24,8},{1,17},{9,25},{17,1},{25,9},{2,18},{10... | collective-permute-start | bytes 172040 | tf_op jit(solution)/shard_map/ppermute | solution.py:57
  35.7 1.3 %collective-permute-start.17 = (bf16[112,256]{1,0:T(8,128)(2,1)S(1)}, bf16[112,256]{1,0:T(8,128)(2,1)S(1)}, u32[]{:S(2)}, u32[]{:S(2)}) collective-permute-start(bf16[112,256]{1,0:T(8,128)(2,1)S(1)} %get-tuple-element.71), channel_id=1, source_target_pairs={{0,24},{8,16},{16,8},{24,0},{1,25},{9,17},{17,9},{25,1},{2,26},{10... | collective-permute-start | bytes 172040 | tf_op jit(solution)/shard_map/ppermute | solution.py:57
  37.3 2.2 %collective-permute-done.16.a_ref.refs_1_ = bf16[112,256]{1,0:T(8,128)(2,1)S(1)} collective-permute-done((bf16[112,256]{1,0:T(8,128)(2,1)S(1)}, bf16[112,256]{1,0:T(8,128)(2,1)S(1)}, u32[]{:S(2)}, u32[]{:S(2)}) %collective-permute-start.16) | collective-permute-done | bytes 57376 | tf_op jit(solution)/shard_map/ppermute | solution.py:57
  39.5 2.3 %collective-permute-done.17.b_ref.refs_2_ = bf16[112,256]{1,0:T(8,128)(2,1)S(1)} collective-permute-done((bf16[112,256]{1,0:T(8,128)(2,1)S(1)}, bf16[112,256]{1,0:T(8,128)(2,1)S(1)}, u32[]{:S(2)}, u32[]{:S(2)}) %collective-permute-start.17) | collective-permute-done | bytes 57376 | tf_op jit(solution)/shard_map/ppermute | solution.py:57
  41.8 0.6 collective-permute-start.18
  42.4 1.3 %collective-permute-start.12 = (bf16[1,2,96,256]{3,2,1,0:T(8,128)(2,1)S(1)}, bf16[1,2,96,256]{3,2,1,0:T(8,128)(2,1)S(1)}, u32[]{:S(2)}, u32[]{:S(2)}) collective-permute-start(bf16[1,2,96,256]{3,2,1,0:T(8,128)(2,1)S(1)} %bitcast.36), channel_id=1, source_target_pairs={{0,2},{1,3},{2,0},{3,1},{4,6},{5,7},{6,4},{7,5},{8,10},{9,11},{10,... | collective-permute-start | bytes 294920 | tf_op jit(solution)/shard_map/ppermute | solution.py:57
  43.8 4.3 %update.2 = (f32[32,4,128,128]{3,2,1,0:T(8,128)}, f32[8,128]{1,0:T(8,128)S(1)}) custom-call(f32[2,96,128]{2,1,0:T(8,128)S(1)} %get-tuple-element.66.keys_ref, f32[2,3,32,256]{3,2,1,0:T(8,128)S(1)} %get-tuple-element.67.delta_ref, f32[2,32,256]{2,1,0:T(8,128)S(1)} %get-tuple-element.68.total_ref, f32[32,4,128,128]{3,2,1,0:T(8,128)} %states_ref.3, ...), custom_call_target="tpu_custom_call" | custom-call | tf_op jit(solution)/shard_map/update/pallas_call | solution.py:43
  48.2 0.9 %collective-permute-start.20 = (bf16[2,2,96,256]{3,2,1,0:T(8,128)(2,1)S(1)}, bf16[2,2,96,256]{3,2,1,0:T(8,128)(2,1)S(1)}, u32[]{:S(2)}, u32[]{:S(2)}) collective-permute-start(bf16[2,2,96,256]{3,2,1,0:T(8,128)(2,1)S(1)} %stack.27.refs_1_.refs_2_), channel_id=1, source_target_pairs={{0,2},{1,3},{2,0},{3,1},{4,6},{5,7},{6,4},{7,5},{8,10},{9,11},{10,... | collective-permute-start | bytes 589832 | tf_op jit(solution)/shard_map/ppermute | solution.py:57
  49.1 1.6 %collective-permute-start.14 = (bf16[2,2,96,256]{3,2,1,0:T(8,128)(2,1)S(1)}, bf16[2,2,96,256]{3,2,1,0:T(8,128)(2,1)S(1)}, u32[]{:S(2)}, u32[]{:S(2)}) collective-permute-start(bf16[2,2,96,256]{3,2,1,0:T(8,128)(2,1)S(1)} %stack.26.refs_0_), channel_id=1, source_target_pairs={{0,4},{1,5},{2,6},{3,7},{4,0},{5,1},{6,2},{7,3},{8,12},{9,13},{10,... | collective-permute-start | bytes 589832 | tf_op jit(solution)/shard_map/ppermute | solution.py:57
  51.2 0.6 collective-permute-start.10
  51.8 3.7 %collective-permute-done.20.refs_3_ = bf16[2,2,96,256]{3,2,1,0:T(8,128)(2,1)S(1)} collective-permute-done((bf16[2,2,96,256]{3,2,1,0:T(8,128)(2,1)S(1)}, bf16[2,2,96,256]{3,2,1,0:T(8,128)(2,1)S(1)}, u32[]{:S(2)}, u32[]{:S(2)}) %collective-permute-start.20) | collective-permute-done | bytes 196640 | tf_op jit(solution)/shard_map/ppermute | solution.py:57
  55.5 1.3 %collective-permute-done.14.refs_1_ = bf16[2,2,96,256]{3,2,1,0:T(8,128)(2,1)S(1)} collective-permute-done((bf16[2,2,96,256]{3,2,1,0:T(8,128)(2,1)S(1)}, bf16[2,2,96,256]{3,2,1,0:T(8,128)(2,1)S(1)}, u32[]{:S(2)}, u32[]{:S(2)}) %collective-permute-start.14) | collective-permute-done | bytes 196640 | tf_op jit(solution)/shard_map/ppermute | solution.py:57
  56.9 4.3 %update.3 = (f32[32,4,128,128]{3,2,1,0:T(8,128)}, f32[8,128]{1,0:T(8,128)S(1)}) custom-call(f32[2,96,128]{2,1,0:T(8,128)S(1)} %get-tuple-element.66.keys_ref, f32[2,3,32,256]{3,2,1,0:T(8,128)S(1)} %get-tuple-element.67.delta_ref, f32[2,32,256]{2,1,0:T(8,128)S(1)} %get-tuple-element.68.total_ref, ...), custom_call_target="tpu_custom_call", output_to_operand_aliasing={{0}: (4, {})} | custom-call | tf_op jit(solution)/shard_map/update/pallas_call | solution.py:43
  61.2 1.1 %expert_in.2 = (f32[384,1024]{1,0:T(8,128)S(1)}, f32[384,1]{1,0:T(8,128)S(1)}) custom-call(s32[1]{0:T(128)} %bitcast.me_ref, bf16[2,2,96,256]{3,2,1,0:T(8,128)(2,1)S(1)} %stack.26.refs_0_, bf16[2,2,96,256]{3,2,1,0:T(8,128)(2,1)S(1)} %collective-permute-done.14.refs_1_, bf16[2,2,96,256]{3,2,1,0:T(8,128)(2,1)S(1)} %stack.27.refs_1_.refs_2_, ...), custom_call_target="tpu_custom_call" | custom-call | tf_op jit(solution)/shard_map/expert_in/pallas_call | solution.py:43
  62.3 1.1 %expert_in.3 = (f32[384,1024]{1,0:T(8,128)S(1)}, f32[384,1]{1,0:T(8,128)S(1)}) custom-call(s32[1]{0:T(128)} %bitcast.me_ref, bf16[2,2,96,256]{3,2,1,0:T(8,128)(2,1)S(1)} %collective-permute-done.13.refs_0_, bf16[2,2,96,256]{3,2,1,0:T(8,128)(2,1)S(1)} %collective-permute-done.15.refs_1_, bf16[2,2,96,256]{3,2,1,0:T(8,128)(2,1)S(1)} %collective-permute-done.19.refs_2_, ...), custom_call_target="tpu_custom_call" | custom-call | tf_op jit(solution)/shard_map/expert_in/pallas_call | solution.py:43
  63.4 1.2 %expert_out.1 = (bf16[4,2,96,256]{3,2,1,0:T(8,128)(2,1)S(1)}, bf16[4,2,96,256]{3,2,1,0:T(8,128)(2,1)S(1)}, bf16[4,2,96,256]{3,2,1,0:T(8,128)(2,1)S(1)}, bf16[4,2,96,256]{3,2,1,0:T(8,128)(2,1)S(1)}) custom-call(s32[1]{0:T(128)} %bitcast.me_ref, f32[384,1024]{1,0:T(8,128)S(1)} %get-tuple-element.79.pre_ref, f32[384,1]{1,0:T(8,128)S(1)} %get-tuple-element.76.sq_ref, ...), custom_call_target="tpu_custom_call" | custom-call | tf_op jit(solution)/shard_map/expert_out/pallas_call | solution.py:43
  64.7 0.6 collective-permute-start.22
  65.3 1.3 %collective-permute-done.22.b_ref = bf16[4,2,96,256]{3,2,1,0:T(8,128)(2,1)S(1)} collective-permute-done((bf16[4,2,96,256]{3,2,1,0:T(8,128)(2,1)S(1)}, bf16[4,2,96,256]{3,2,1,0:T(8,128)(2,1)S(1)}, u32[]{:S(2)}, u32[]{:S(2)}) %collective-permute-start.22) | collective-permute-done | bytes 393248 | tf_op jit(solution)/shard_map/ppermute | solution.py:57
  66.7 1.3 %collective-permute-start.23 = (bf16[2,2,96,256]{3,2,1,0:T(8,128)(2,1)S(1)}, bf16[2,2,96,256]{3,2,1,0:T(8,128)(2,1)S(1)}, u32[]{:S(2)}, u32[]{:S(2)}) collective-permute-start(bf16[2,2,96,256]{3,2,1,0:T(8,128)(2,1)S(1)} %get-tuple-element.84), channel_id=1, source_target_pairs={{0,2},{1,3},{2,0},{3,1},{4,6},{5,7},{6,4},{7,5},{8,10},{9,11},{10,... | collective-permute-start | bytes 589832 | tf_op jit(solution)/shard_map/ppermute | solution.py:57
  68.1 1.0 %collective-permute-start.27 = (bf16[2,2,96,256]{3,2,1,0:T(8,128)(2,1)S(1)}, bf16[2,2,96,256]{3,2,1,0:T(8,128)(2,1)S(1)}, u32[]{:S(2)}, u32[]{:S(2)}) collective-permute-start(bf16[2,2,96,256]{3,2,1,0:T(8,128)(2,1)S(1)} %get-tuple-element.92), channel_id=1, source_target_pairs={{0,4},{1,5},{2,6},{3,7},{4,0},{5,1},{6,2},{7,3},{8,12},{9,13},{10,... | collective-permute-start | bytes 589832 | tf_op jit(solution)/shard_map/ppermute | solution.py:57
  69.1 4.9 %collective-permute-done.23.b_ref = bf16[2,2,96,256]{3,2,1,0:T(8,128)(2,1)S(1)} collective-permute-done((bf16[2,2,96,256]{3,2,1,0:T(8,128)(2,1)S(1)}, bf16[2,2,96,256]{3,2,1,0:T(8,128)(2,1)S(1)}, u32[]{:S(2)}, u32[]{:S(2)}) %collective-permute-start.23) | collective-permute-done | bytes 196640 | tf_op jit(solution)/shard_map/ppermute | solution.py:57
  74.0 1.5 %collective-permute-start.24 = (bf16[1,2,96,256]{3,2,1,0:T(8,128)(2,1)S(1)}, bf16[1,2,96,256]{3,2,1,0:T(8,128)(2,1)S(1)}, u32[]{:S(2)}, u32[]{:S(2)}) collective-permute-start(bf16[1,2,96,256]{3,2,1,0:T(8,128)(2,1)S(1)} %get-tuple-element.86), channel_id=1, source_target_pairs={{0,4},{1,5},{2,6},{3,7},{4,0},{5,1},{6,2},{7,3},{8,12},{9,13},{10,... | collective-permute-start | bytes 294920 | tf_op jit(solution)/shard_map/ppermute | solution.py:57
  75.6 0.7 collective-permute-start.28
  76.3 2.4 %collective-permute-done.24.b_ref = bf16[1,2,96,256]{3,2,1,0:T(8,128)(2,1)S(1)} collective-permute-done((bf16[1,2,96,256]{3,2,1,0:T(8,128)(2,1)S(1)}, bf16[1,2,96,256]{3,2,1,0:T(8,128)(2,1)S(1)}, u32[]{:S(2)}, u32[]{:S(2)}) %collective-permute-start.24) | collective-permute-done | bytes 98336 | tf_op jit(solution)/shard_map/ppermute | solution.py:57
  78.8 1.5 %collective-permute-done.28.b_ref = bf16[1,2,96,256]{3,2,1,0:T(8,128)(2,1)S(1)} collective-permute-done((bf16[1,2,96,256]{3,2,1,0:T(8,128)(2,1)S(1)}, bf16[1,2,96,256]{3,2,1,0:T(8,128)(2,1)S(1)}, u32[]{:S(2)}, u32[]{:S(2)}) %collective-permute-start.28) | collective-permute-done | bytes 98336 | tf_op jit(solution)/shard_map/ppermute | solution.py:57
  80.3 0.9 %collective-permute-start.29 = (bf16[96,256]{1,0:T(8,128)(2,1)S(1)}, bf16[96,256]{1,0:T(8,128)(2,1)S(1)}, u32[]{:S(2)}, u32[]{:S(2)}) collective-permute-start(bf16[96,256]{1,0:T(8,128)(2,1)S(1)} %get-tuple-element.95), channel_id=1, source_target_pairs={{0,16},{8,24},{16,0},{24,8},{1,17},{9,25},{17,1},{25,9},{2,18},{10... | collective-permute-start | bytes 147464 | tf_op jit(solution)/shard_map/ppermute | solution.py:57
  81.2 2.1 %collective-permute-start.30 = (bf16[96,256]{1,0:T(8,128)(2,1)S(1)}, bf16[96,256]{1,0:T(8,128)(2,1)S(1)}, u32[]{:S(2)}, u32[]{:S(2)}) collective-permute-start(bf16[96,256]{1,0:T(8,128)(2,1)S(1)} %get-tuple-element.96), channel_id=1, source_target_pairs={{0,24},{8,16},{16,8},{24,0},{1,25},{9,17},{17,9},{25,1},{2,26},{10... | collective-permute-start | bytes 147464 | tf_op jit(solution)/shard_map/ppermute | solution.py:57
  83.6 2.3 %collective-permute-done.29 = bf16[96,256]{1,0:T(8,128)(2,1)S(1)} collective-permute-done((bf16[96,256]{1,0:T(8,128)(2,1)S(1)}, bf16[96,256]{1,0:T(8,128)(2,1)S(1)}, u32[]{:S(2)}, u32[]{:S(2)}) %collective-permute-start.29) | collective-permute-done | bytes 49184 | tf_op jit(solution)/shard_map/ppermute | solution.py:57
  85.9 1.2 %collective-permute-done.30 = bf16[96,256]{1,0:T(8,128)(2,1)S(1)} collective-permute-done((bf16[96,256]{1,0:T(8,128)(2,1)S(1)}, bf16[96,256]{1,0:T(8,128)(2,1)S(1)}, u32[]{:S(2)}, u32[]{:S(2)}) %collective-permute-start.30) | collective-permute-done | bytes 49184 | tf_op jit(solution)/shard_map/ppermute | solution.py:57
  87.1 0.7 add_convert_fusion
  (56 shorter events, 2.7 us)
Async XLA Ops:
  0.6 6.7 %collective-permute-start = (bf16[96,256]{1,0:T(8,128)(2,1)}, bf16[96,256]{1,0:T(8,128)(2,1)S(1)}, u32[]{:S(2)}, u32[]{:S(2)}) collective-permute-start(bf16[96,256]{1,0:T(8,128)(2,1)} %bitcast.42), channel_id=1, source_target_pairs={{0,1},{1,0},{2,3},{3,2},{4,5},{5,4},{6,7},{7,6},{8,9},{9,8},{10,11... | collective-permute-start | bytes 147464 | tf_op jit(solution)/shard_map/ppermute | solution.py:57
  4.3 7.1 %copy-start = (f32[128]{0:T(128)S(1)}, f32[128]{0:T(128)}, u32[]{:S(2)}) copy-start(f32[128]{0:T(128)} %param.33) | copy-start | bytes 1540
  7.4 8.3 %collective-permute-start.1 = (bf16[2,96,256]{2,1,0:T(8,128)(2,1)S(1)}, bf16[2,96,256]{2,1,0:T(8,128)(2,1)S(1)}, u32[]{:S(2)}, u32[]{:S(2)}) collective-permute-start(bf16[2,96,256]{2,1,0:T(8,128)(2,1)S(1)} %stack.25.refs_4_.refs_0_), channel_id=1, source_target_pairs={{0,2},{1,3},{2,0},{3,1},{4,6},{5,7},{6,4},{7,5},{8,10},{9,11},{10,... | collective-permute-start | bytes 294920 | tf_op jit(solution)/shard_map/ppermute | solution.py:57
  9.9 6.1 %collective-permute-start.2 = (bf16[2,96,256]{2,1,0:T(8,128)(2,1)S(1)}, bf16[2,96,256]{2,1,0:T(8,128)(2,1)S(1)}, u32[]{:S(2)}, u32[]{:S(2)}) collective-permute-start(bf16[2,96,256]{2,1,0:T(8,128)(2,1)S(1)} %stack.25.refs_4_.refs_0_), channel_id=1, source_target_pairs={{0,4},{1,5},{2,6},{3,7},{4,0},{5,1},{6,2},{7,3},{8,12},{9,13},{10,... | collective-permute-start | bytes 294920 | tf_op jit(solution)/shard_map/ppermute | solution.py:57
  11.5 5.5 %collective-permute-start.3 = (bf16[2,96,256]{2,1,0:T(8,128)(2,1)S(1)}, bf16[2,96,256]{2,1,0:T(8,128)(2,1)S(1)}, u32[]{:S(2)}, u32[]{:S(2)}) collective-permute-start(bf16[2,96,256]{2,1,0:T(8,128)(2,1)S(1)} %stack.25.refs_4_.refs_0_), channel_id=1, source_target_pairs={{0,6},{1,7},{2,4},{3,5},{4,2},{5,3},{6,0},{7,1},{8,14},{9,15},{10,... | collective-permute-start | bytes 294920 | tf_op jit(solution)/shard_map/ppermute | solution.py:57
  22.7 1.5 %collective-permute-start.4 = (bf16[4,96,256]{2,1,0:T(8,128)(2,1)S(1)}, bf16[4,96,256]{2,1,0:T(8,128)(2,1)S(1)}, u32[]{:S(2)}, u32[]{:S(2)}) collective-permute-start(bf16[4,96,256]{2,1,0:T(8,128)(2,1)S(1)} %get-tuple-element.59), channel_id=1, source_target_pairs={{0,1},{1,0},{2,3},{3,2},{4,5},{5,4},{6,7},{7,6},{8,9},{9,8},{10,11... | collective-permute-start | bytes 589832 | tf_op jit(solution)/shard_map/ppermute | solution.py:57
  24.3 6.5 %collective-permute-start.5 = (bf16[96,256]{1,0:T(8,128)(2,1)S(1)}, bf16[96,256]{1,0:T(8,128)(2,1)S(1)}, u32[]{:S(2)}, u32[]{:S(2)}) collective-permute-start(bf16[96,256]{1,0:T(8,128)(2,1)S(1)} %get-tuple-element.100), channel_id=1, source_target_pairs={{0,2},{1,3},{2,0},{3,1},{4,6},{5,7},{6,4},{7,5},{8,10},{9,11},{10,... | collective-permute-start | bytes 147464 | tf_op jit(solution)/shard_map/ppermute | solution.py:57
  25.5 5.2 %collective-permute-start.6 = (bf16[96,256]{1,0:T(8,128)(2,1)S(1)}, bf16[96,256]{1,0:T(8,128)(2,1)S(1)}, u32[]{:S(2)}, u32[]{:S(2)}) collective-permute-start(bf16[96,256]{1,0:T(8,128)(2,1)S(1)} %get-tuple-element.99), channel_id=1, source_target_pairs={{0,4},{1,5},{2,6},{3,7},{4,0},{5,1},{6,2},{7,3},{8,12},{9,13},{10,... | collective-permute-start | bytes 147464 | tf_op jit(solution)/shard_map/ppermute | solution.py:57
  26.5 5.0 %collective-permute-start.7 = (bf16[96,256]{1,0:T(8,128)(2,1)S(1)}, bf16[96,256]{1,0:T(8,128)(2,1)S(1)}, u32[]{:S(2)}, u32[]{:S(2)}) collective-permute-start(bf16[96,256]{1,0:T(8,128)(2,1)S(1)} %get-tuple-element.98), channel_id=1, source_target_pairs={{0,6},{1,7},{2,4},{3,5},{4,2},{5,3},{6,0},{7,1},{8,14},{9,15},{10,... | collective-permute-start | bytes 147464 | tf_op jit(solution)/shard_map/ppermute | solution.py:57
  31.7 12.0 %collective-permute-start.8 = (bf16[96,1024]{1,0:T(8,128)(2,1)S(1)}, bf16[96,1024]{1,0:T(8,128)(2,1)S(1)}, u32[]{:S(2)}, u32[]{:S(2)}) collective-permute-start(bf16[96,1024]{1,0:T(8,128)(2,1)S(1)} %get-tuple-element.63.a_ref), channel_id=1, source_target_pairs={{0,2},{1,3},{2,0},{3,1},{4,6},{5,7},{6,4},{7,5},{8,10},{9,11},{10,... | collective-permute-start | bytes 589832 | tf_op jit(solution)/shard_map/ppermute | solution.py:57
  33.1 6.4 %collective-permute-start.16 = (bf16[112,256]{1,0:T(8,128)(2,1)S(1)}, bf16[112,256]{1,0:T(8,128)(2,1)S(1)}, u32[]{:S(2)}, u32[]{:S(2)}) collective-permute-start(bf16[112,256]{1,0:T(8,128)(2,1)S(1)} %get-tuple-element.70), channel_id=1, source_target_pairs={{0,16},{8,24},{16,0},{24,8},{1,17},{9,25},{17,1},{25,9},{2,18},{10... | collective-permute-start | bytes 172040 | tf_op jit(solution)/shard_map/ppermute | solution.py:57
  35.7 6.1 %collective-permute-start.17 = (bf16[112,256]{1,0:T(8,128)(2,1)S(1)}, bf16[112,256]{1,0:T(8,128)(2,1)S(1)}, u32[]{:S(2)}, u32[]{:S(2)}) collective-permute-start(bf16[112,256]{1,0:T(8,128)(2,1)S(1)} %get-tuple-element.71), channel_id=1, source_target_pairs={{0,24},{8,16},{16,8},{24,0},{1,25},{9,17},{17,9},{25,1},{2,26},{10... | collective-permute-start | bytes 172040 | tf_op jit(solution)/shard_map/ppermute | solution.py:57
  37.1 5.4 %collective-permute-start.11 = (bf16[112,256]{1,0:T(8,128)(2,1)S(1)}, bf16[112,256]{1,0:T(8,128)(2,1)S(1)}, u32[]{:S(2)}, u32[]{:S(2)}) collective-permute-start(bf16[112,256]{1,0:T(8,128)(2,1)S(1)} %get-tuple-element.65), channel_id=1, source_target_pairs={{0,8},{8,0},{16,24},{24,16},{1,9},{9,1},{17,25},{25,17},{2,10},{10... | collective-permute-start | bytes 172040 | tf_op jit(solution)/shard_map/ppermute | solution.py:57
  41.8 6.3 %collective-permute-start.18 = (bf16[1,2,96,256]{3,2,1,0:T(8,128)(2,1)S(1)}, bf16[1,2,96,256]{3,2,1,0:T(8,128)(2,1)S(1)}, u32[]{:S(2)}, u32[]{:S(2)}) collective-permute-start(bf16[1,2,96,256]{3,2,1,0:T(8,128)(2,1)S(1)} %bitcast.38), channel_id=1, source_target_pairs={{0,4},{1,5},{2,6},{3,7},{4,0},{5,1},{6,2},{7,3},{8,12},{9,13},{10,... | collective-permute-start | bytes 294920 | tf_op jit(solution)/shard_map/ppermute | solution.py:57
  42.4 6.6 %collective-permute-start.12 = (bf16[1,2,96,256]{3,2,1,0:T(8,128)(2,1)S(1)}, bf16[1,2,96,256]{3,2,1,0:T(8,128)(2,1)S(1)}, u32[]{:S(2)}, u32[]{:S(2)}) collective-permute-start(bf16[1,2,96,256]{3,2,1,0:T(8,128)(2,1)S(1)} %bitcast.36), channel_id=1, source_target_pairs={{0,2},{1,3},{2,0},{3,1},{4,6},{5,7},{6,4},{7,5},{8,10},{9,11},{10,... | collective-permute-start | bytes 294920 | tf_op jit(solution)/shard_map/ppermute | solution.py:57
  43.8 7.4 %collective-permute-start.9 = (bf16[96,1024]{1,0:T(8,128)(2,1)S(1)}, bf16[96,1024]{1,0:T(8,128)(2,1)S(1)}, u32[]{:S(2)}, u32[]{:S(2)}) collective-permute-start(bf16[96,1024]{1,0:T(8,128)(2,1)S(1)} %one_sum.4.a_ref.refs_1_), channel_id=1, source_target_pairs={{0,1},{1,0},{2,3},{3,2},{4,5},{5,4},{6,7},{7,6},{8,9},{9,8},{10,11... | collective-permute-start | bytes 589832 | tf_op jit(solution)/shard_map/ppermute | solution.py:57
  48.2 7.4 %collective-permute-start.20 = (bf16[2,2,96,256]{3,2,1,0:T(8,128)(2,1)S(1)}, bf16[2,2,96,256]{3,2,1,0:T(8,128)(2,1)S(1)}, u32[]{:S(2)}, u32[]{:S(2)}) collective-permute-start(bf16[2,2,96,256]{3,2,1,0:T(8,128)(2,1)S(1)} %stack.27.refs_1_.refs_2_), channel_id=1, source_target_pairs={{0,2},{1,3},{2,0},{3,1},{4,6},{5,7},{6,4},{7,5},{8,10},{9,11},{10,... | collective-permute-start | bytes 589832 | tf_op jit(solution)/shard_map/ppermute | solution.py:57
  49.1 7.8 %collective-permute-start.14 = (bf16[2,2,96,256]{3,2,1,0:T(8,128)(2,1)S(1)}, bf16[2,2,96,256]{3,2,1,0:T(8,128)(2,1)S(1)}, u32[]{:S(2)}, u32[]{:S(2)}) collective-permute-start(bf16[2,2,96,256]{3,2,1,0:T(8,128)(2,1)S(1)} %stack.26.refs_0_), channel_id=1, source_target_pairs={{0,4},{1,5},{2,6},{3,7},{4,0},{5,1},{6,2},{7,3},{8,12},{9,13},{10,... | collective-permute-start | bytes 589832 | tf_op jit(solution)/shard_map/ppermute | solution.py:57
  50.6 11.7 %collective-permute-start.19 = (bf16[2,2,96,256]{3,2,1,0:T(8,128)(2,1)S(1)}, bf16[2,2,96,256]{3,2,1,0:T(8,128)(2,1)S(1)}, u32[]{:S(2)}, u32[]{:S(2)}) collective-permute-start(bf16[2,2,96,256]{3,2,1,0:T(8,128)(2,1)S(1)} %stack.27.refs_1_.refs_2_), channel_id=1, source_target_pairs={{0,1},{1,0},{2,3},{3,2},{4,5},{5,4},{6,7},{7,6},{8,9},{9,8},{10,11... | collective-permute-start | bytes 589832 | tf_op jit(solution)/shard_map/ppermute | solution.py:57
  50.6 11.7 %collective-permute-start.13 = (bf16[2,2,96,256]{3,2,1,0:T(8,128)(2,1)S(1)}, bf16[2,2,96,256]{3,2,1,0:T(8,128)(2,1)S(1)}, u32[]{:S(2)}, u32[]{:S(2)}) collective-permute-start(bf16[2,2,96,256]{3,2,1,0:T(8,128)(2,1)S(1)} %stack.26.refs_0_), channel_id=1, source_target_pairs={{0,1},{1,0},{2,3},{3,2},{4,5},{5,4},{6,7},{7,6},{8,9},{9,8},{10,11... | collective-permute-start | bytes 589832 | tf_op jit(solution)/shard_map/ppermute | solution.py:57
  51.2 12.2 %collective-permute-start.10 = (bf16[96,1024]{1,0:T(8,128)(2,1)S(1)}, bf16[96,1024]{1,0:T(8,128)(2,1)S(1)}, u32[]{:S(2)}, u32[]{:S(2)}) collective-permute-start(bf16[96,1024]{1,0:T(8,128)(2,1)S(1)} %one_sum.5.refs_2_.a_ref), channel_id=1, source_target_pairs={{0,4},{1,5},{2,6},{3,7},{4,0},{5,1},{6,2},{7,3},{8,12},{9,13},{10,... | collective-permute-start | bytes 589832 | tf_op jit(solution)/shard_map/ppermute | solution.py:57
  55.5 6.8 %collective-permute-start.21 = (bf16[2,2,96,256]{3,2,1,0:T(8,128)(2,1)S(1)}, bf16[2,2,96,256]{3,2,1,0:T(8,128)(2,1)S(1)}, u32[]{:S(2)}, u32[]{:S(2)}) collective-permute-start(bf16[2,2,96,256]{3,2,1,0:T(8,128)(2,1)S(1)} %collective-permute-done.20.refs_3_), channel_id=1, source_target_pairs={{0,1},{1,0},{2,3},{3,2},{4,5},{5,4},{6,7},{7,6},{8,9},{9,8},{10,11... | collective-permute-start | bytes 589832 | tf_op jit(solution)/shard_map/ppermute | solution.py:57
  56.9 5.4 %collective-permute-start.15 = (bf16[2,2,96,256]{3,2,1,0:T(8,128)(2,1)S(1)}, bf16[2,2,96,256]{3,2,1,0:T(8,128)(2,1)S(1)}, u32[]{:S(2)}, u32[]{:S(2)}) collective-permute-start(bf16[2,2,96,256]{3,2,1,0:T(8,128)(2,1)S(1)} %collective-permute-done.14.refs_1_), channel_id=1, source_target_pairs={{0,1},{1,0},{2,3},{3,2},{4,5},{5,4},{6,7},{7,6},{8,9},{9,8},{10,11... | collective-permute-start | bytes 589832 | tf_op jit(solution)/shard_map/ppermute | solution.py:57
  64.7 1.9 %collective-permute-start.22 = (bf16[4,2,96,256]{3,2,1,0:T(8,128)(2,1)S(1)}, bf16[4,2,96,256]{3,2,1,0:T(8,128)(2,1)S(1)}, u32[]{:S(2)}, u32[]{:S(2)}) collective-permute-start(bf16[4,2,96,256]{3,2,1,0:T(8,128)(2,1)S(1)} %get-tuple-element.82), channel_id=1, source_target_pairs={{0,1},{1,0},{2,3},{3,2},{4,5},{5,4},{6,7},{7,6},{8,9},{9,8},{10,11... | collective-permute-start | bytes 1179656 | tf_op jit(solution)/shard_map/ppermute | solution.py:57
  65.3 2.7 %collective-permute-start.26 = (bf16[4,2,96,256]{3,2,1,0:T(8,128)(2,1)S(1)}, bf16[4,2,96,256]{3,2,1,0:T(8,128)(2,1)S(1)}, u32[]{:S(2)}, u32[]{:S(2)}) collective-permute-start(bf16[4,2,96,256]{3,2,1,0:T(8,128)(2,1)S(1)} %get-tuple-element.90), channel_id=1, source_target_pairs={{0,1},{1,0},{2,3},{3,2},{4,5},{5,4},{6,7},{7,6},{8,9},{9,8},{10,11... | collective-permute-start | bytes 1179656 | tf_op jit(solution)/shard_map/ppermute | solution.py:57
  66.7 7.2 %collective-permute-start.23 = (bf16[2,2,96,256]{3,2,1,0:T(8,128)(2,1)S(1)}, bf16[2,2,96,256]{3,2,1,0:T(8,128)(2,1)S(1)}, u32[]{:S(2)}, u32[]{:S(2)}) collective-permute-start(bf16[2,2,96,256]{3,2,1,0:T(8,128)(2,1)S(1)} %get-tuple-element.84), channel_id=1, source_target_pairs={{0,2},{1,3},{2,0},{3,1},{4,6},{5,7},{6,4},{7,5},{8,10},{9,11},{10,... | collective-permute-start | bytes 589832 | tf_op jit(solution)/shard_map/ppermute | solution.py:57
  68.1 7.5 %collective-permute-start.27 = (bf16[2,2,96,256]{3,2,1,0:T(8,128)(2,1)S(1)}, bf16[2,2,96,256]{3,2,1,0:T(8,128)(2,1)S(1)}, u32[]{:S(2)}, u32[]{:S(2)}) collective-permute-start(bf16[2,2,96,256]{3,2,1,0:T(8,128)(2,1)S(1)} %get-tuple-element.92), channel_id=1, source_target_pairs={{0,4},{1,5},{2,6},{3,7},{4,0},{5,1},{6,2},{7,3},{8,12},{9,13},{10,... | collective-permute-start | bytes 589832 | tf_op jit(solution)/shard_map/ppermute | solution.py:57
  74.0 4.7 %collective-permute-start.24 = (bf16[1,2,96,256]{3,2,1,0:T(8,128)(2,1)S(1)}, bf16[1,2,96,256]{3,2,1,0:T(8,128)(2,1)S(1)}, u32[]{:S(2)}, u32[]{:S(2)}) collective-permute-start(bf16[1,2,96,256]{3,2,1,0:T(8,128)(2,1)S(1)} %get-tuple-element.86), channel_id=1, source_target_pairs={{0,4},{1,5},{2,6},{3,7},{4,0},{5,1},{6,2},{7,3},{8,12},{9,13},{10,... | collective-permute-start | bytes 294920 | tf_op jit(solution)/shard_map/ppermute | solution.py:57
  75.6 4.7 %collective-permute-start.28 = (bf16[1,2,96,256]{3,2,1,0:T(8,128)(2,1)S(1)}, bf16[1,2,96,256]{3,2,1,0:T(8,128)(2,1)S(1)}, u32[]{:S(2)}, u32[]{:S(2)}) collective-permute-start(bf16[1,2,96,256]{3,2,1,0:T(8,128)(2,1)S(1)} %get-tuple-element.94), channel_id=1, source_target_pairs={{0,2},{1,3},{2,0},{3,1},{4,6},{5,7},{6,4},{7,5},{8,10},{9,11},{10,... | collective-permute-start | bytes 294920 | tf_op jit(solution)/shard_map/ppermute | solution.py:57
  78.7 4.8 %collective-permute-start.25 = (bf16[96,256]{1,0:T(8,128)(2,1)S(1)}, bf16[96,256]{1,0:T(8,128)(2,1)S(1)}, u32[]{:S(2)}, u32[]{:S(2)}) collective-permute-start(bf16[96,256]{1,0:T(8,128)(2,1)S(1)} %get-tuple-element.88), channel_id=1, source_target_pairs={{0,8},{8,0},{16,24},{24,16},{1,9},{9,1},{17,25},{25,17},{2,10},{10... | collective-permute-start | bytes 147464 | tf_op jit(solution)/shard_map/ppermute | solution.py:57
  80.3 5.6 %collective-permute-start.29 = (bf16[96,256]{1,0:T(8,128)(2,1)S(1)}, bf16[96,256]{1,0:T(8,128)(2,1)S(1)}, u32[]{:S(2)}, u32[]{:S(2)}) collective-permute-start(bf16[96,256]{1,0:T(8,128)(2,1)S(1)} %get-tuple-element.95), channel_id=1, source_target_pairs={{0,16},{8,24},{16,0},{24,8},{1,17},{9,25},{17,1},{25,9},{2,18},{10... | collective-permute-start | bytes 147464 | tf_op jit(solution)/shard_map/ppermute | solution.py:57
  81.2 5.9 %collective-permute-start.30 = (bf16[96,256]{1,0:T(8,128)(2,1)S(1)}, bf16[96,256]{1,0:T(8,128)(2,1)S(1)}, u32[]{:S(2)}, u32[]{:S(2)}) collective-permute-start(bf16[96,256]{1,0:T(8,128)(2,1)S(1)} %get-tuple-element.96), channel_id=1, source_target_pairs={{0,24},{8,16},{16,8},{24,0},{1,25},{9,17},{17,9},{25,1},{2,26},{10... | collective-permute-start | bytes 147464 | tf_op jit(solution)/shard_map/ppermute | solution.py:57

commit v3 on v2

--- a/solution.py
+++ b/solution.py
@@ -13,7 +13,7 @@
 SLOTS = 16
 F32 = jnp.float32
 BF16 = jnp.bfloat16
-VMEM_LIMIT = 16 * 1024 * 1024
+VMEM_LIMIT = 24 * 1024 * 1024
 
 
 def dot(a, b):
@@ -86,6 +86,62 @@
         (),
         (*(pltpu.with_memory_space_constraint(x, pltpu.HBM) for x in arrays), *after),
         [pltpu.SemaphoreType.DMA((len(arrays),))],
+    )
+
+
+def bring_kernel(count, seq_count, head_count, me_ref, seq_ref, *refs):
+    sources, (ids_hbm, chosen_hbm, gain_after_hbm) = refs[:count], refs[count : count + 3]
+    refs = refs[count + 4 :]
+    targets, (extra_ref, gain_mine_ref, gain_inv_ref) = refs[:count], refs[count : count + 3]
+    ids, chosen, gain_after, sems = refs[count + 3 :]
+    sources = (ids_hbm, chosen_hbm, gain_after_hbm, *sources)
+    targets = (ids, chosen, gain_after, *targets)
+    copies = [pltpu.make_async_copy(a, b, sems.at[n]) for n, (a, b) in enumerate(zip(sources, targets))]
+    for copy in copies:
+        copy.start()
+    for copy in copies[:3]:
+        copy.wait()
+    me, seq = me_ref[0], seq_ref[0]
+    gain_mine_ref[...] = gain_after[me]
+    gain_inv_ref[...] = 1.0 / gain_after[...]
+    top, steps, seqs = ids.shape
+    for z in range(seq_count):
+        target = (seq ^ z) * head_count + me
+        weight = jnp.zeros((steps, seqs), F32)
+        for n in range(top):
+            weight = weight + jnp.where(ids[n] == target, chosen[n], 0.0)
+        high = weight.astype(BF16).astype(F32)
+        both = jnp.concatenate([high, weight - high], axis=0)
+        rows, width = extra_ref.shape[1:]
+        both = jnp.concatenate([both, jnp.zeros((rows - 2 * steps, seqs), F32)], axis=0)
+        both = jnp.concatenate([both, jnp.zeros((rows, width - seqs), F32)], axis=1)
+        extra_ref[z] = both.astype(BF16)
+    for copy in copies[3:]:
+        copy.wait()
+
+
+def bring(me, seq, arrays, ids, chosen, gain_after, seq_count, after):
+    head_count, _, width = gain_after.shape
+    count = len(arrays)
+    hbm = (pltpu.with_memory_space_constraint(x, pltpu.HBM) for x in (*arrays, ids, chosen, gain_after))
+    return call(
+        functools.partial(bring_kernel, count, seq_count, head_count),
+        "bring",
+        [pltpu.VMEM(x.shape, x.dtype) for x in arrays]
+        + [
+            pltpu.VMEM((seq_count, 16, width), BF16),
+            pltpu.VMEM((1, width), F32),
+            pltpu.VMEM(gain_after.shape, F32),
+        ],
+        (me, seq),
+        (),
+        (*hbm, after),
+        [
+            pltpu.VMEM(ids.shape, jnp.int32),
+            pltpu.VMEM(chosen.shape, F32),
+            pltpu.VMEM(gain_after.shape, F32),
+            pltpu.SemaphoreType.DMA((count + 3,)),
+        ],
     )
 
 
@@ -104,16 +160,18 @@
         wk,
         wv,
         wz,
-        wo,
-        states,
-        _,
+        wo_hbm,
+        states_hbm,
         own_ref,
         sib_ref,
         keys_ref,
         delta_ref,
         total_ref,
+        wo,
+        states,
         left,
         recalls,
+        sems,
     ) = refs[head_count // 2 :]
     me = me_ref[0]
     _, rows, width = x_refs[0].shape
@@ -122,6 +180,16 @@
     value_heads = wv.shape[1] // DV
     group = value_heads // key_heads
     pair = group * DV
+
+    parts = sems.shape[0] - 1
+    part = seqs // parts
+    copies = []
+    for n in range(parts):
+        span = pl.ds(n * part, part)
+        copies.append(pltpu.make_async_copy(states_hbm.at[span], states.at[span], sems.at[n]))
+    copies.append(pltpu.make_async_copy(wo_hbm, wo, sems.at[parts]))
+    for copy in copies:
+        copy.start()
 
     squares = jnp.zeros((rows, 1), F32)
     for j in range(head_count):
@@ -189,7 +257,9 @@
                 recalls[i * group + u, pl.ds(base, SLOTS), :] = answer[:, u * DV : (u + 1) * DV]
         return carry
 
-    lax.fori_loop(0, seqs, one, 0, unroll=4)
+    for n in range(parts):
+        copies[n].wait()
+        lax.fori_loop(n * part, (n + 1) * part, one, 0, unroll=4)
 
     def wide(columns, t, i):
         return jnp.concatenate(
@@ -243,6 +313,7 @@
         m = m * lax.rsqrt(jnp.mean(m * m, axis=1, keepdims=True) + EPS)
         gated.append((m * pack_ref[2:3, :DV] * gates[:, h * DV : (h + 1) * DV]).astype(BF16))
     gated = jnp.concatenate(gated, axis=1)
+    copies[parts].wait()
     for c in range(head_count):
         piece = dot(gated, wo[:, c * width : (c + 1) * width]).astype(BF16)
         away = me ^ c
@@ -256,7 +327,7 @@
             sib_ref[away // 2] = piece
 
 
-def front(me, xs, gain, small, pack, wq, wk, wv, wz, wo, states, after, steps):
+def front(me, xs, gain, small, pack, wq, wk, wv, wz, wo, states, steps):
     _, rows, width = xs[0].shape
     head_count = 2 * len(xs)
     seqs = rows // steps
@@ -274,20 +345,23 @@
             pltpu.VMEM((key_heads, seqs, pair), F32),
         ],
         (me,),
-        (*xs, gain, small, pack, wq, wk, wv, wz, wo, states),
-        (after,),
+        (*xs, gain, small, pack, wq, wk, wv, wz),
+        [pltpu.with_memory_space_constraint(x, pltpu.HBM) for x in (wo, states)],
         [
+            pltpu.VMEM(wo.shape, BF16),
+            pltpu.VMEM(states.shape, F32),
             pltpu.VMEM((key_heads, seqs * SLOTS, DK), F32),
             pltpu.VMEM((value_heads, seqs * SLOTS, DV), F32),
+            pltpu.SemaphoreType.DMA((5,)),
         ],
     )
 
 
 def rows_kernel(pairs, *refs):
     merged_ref, received = refs[0], refs[1:pairs]
-    mine_ref, gain_ref, extra_ref, w_ref, _ = refs[pairs : pairs + 5]
-    resid_ref, x_ref, shared_ref = refs[pairs + 5 : pairs + 8]
-    messages = refs[pairs + 8 :]
+    mine_ref, gain_ref, extra_ref, _ = refs[pairs : pairs + 4]
+    resid_ref, x_ref = refs[pairs + 4 : pairs + 6]
+    messages = refs[pairs + 6 :]
     rows = mine_ref.shape[0]
     resid = mine_ref[...].astype(F32) + merged_ref[0].astype(F32)
     for ref in received:
@@ -298,10 +372,9 @@
     for z, ref in enumerate(messages):
         ref[:rows, :] = x
         ref[rows:, :] = extra_ref[z + 1]
-    shared_ref[...] = dot(x, w_ref[...]).astype(BF16)
-
-
-def make_rows(merged, received, mine, gain, extra, w, after):
+
+
+def make_rows(merged, received, mine, gain, extra, after):
     rows, width = mine.shape
     message = pltpu.VMEM((rows + extra.shape[1], width), BF16)
     return call(
@@ -310,23 +383,23 @@
         [
             pltpu.VMEM((rows, width), F32),
             pltpu.VMEM((rows, width), BF16),
-            pltpu.VMEM((rows, w.shape[1]), BF16),
             *([message] * (extra.shape[0] - 1)),
         ],
         (),
-        (merged, *received, mine, gain, extra, w),
+        (merged, *received, mine, gain, extra),
         after,
     )
 
 
-def slab_kernel(a_ref, b_ref, out_ref):
+def slab_kernel(a_ref, b_ref, *refs):
+    out_ref = refs[-1]
     rows = out_ref.shape[1]
     out_ref[0] = a_ref[:rows, :]
     out_ref[1] = b_ref[:rows, :]
 
 
-def slab_pair(a, b, rows):
-    [out] = call(slab_kernel, "slab", [pltpu.VMEM((2, rows, a.shape[1]), BF16)], (), (a, b))
+def slab_pair(a, b, rows, after):
+    [out] = call(slab_kernel, "slab", [pltpu.VMEM((2, rows, a.shape[1]), BF16)], (), (a, b), after)
     return out
 
 
@@ -466,9 +539,9 @@
     )
 
 
-def expert_out_kernel(orders, me_ref, pre_ref, sq_ref, extra_ref, w_ref, *refs):
+def expert_out_kernel(orders, steps, me_ref, pre_ref, sq_ref, extra_ref, w_ref, *refs):
     me = me_ref[0]
-    messages, outs = refs[:-4], refs[-4:]
+    messages, outs = refs[:-5], refs[-4:]
     features = w_ref.shape[2]
     hidden_width = w_ref.shape[1]
     start = 0
@@ -485,7 +558,9 @@
         for z in range(side * zs, (side + 1) * zs):
             extra = messages[z - 1][rows:, :] if z else extra_ref[0]
             columns = jnp.transpose(extra.astype(F32))
-            weight.append(columns[:rows, 0:1] + columns[:rows, 1:2])
+            for t in range(steps):
+                both = columns[:, t : t + 1] + columns[:, steps + t : steps + t + 1]
+                weight.append(both[: rows // steps])
         weight = jnp.concatenate(weight, axis=0)
         for odd, ref in ((1, sib), (0, own)):
             for n in range(count):
@@ -495,9 +570,9 @@
                 ref[n] = result.astype(BF16).reshape(zs, rows, width)
 
 
-def expert_out(me, pre, sq, extra, w, messages, orders, shapes, after):
+def expert_out(me, pre, sq, extra, w, messages, orders, shapes, steps, after):
     return call(
-        functools.partial(expert_out_kernel, orders),
+        functools.partial(expert_out_kernel, orders, steps),
         "expert_out",
         [pltpu.VMEM(shape, BF16) for shape in shapes],
         (me,),
@@ -515,16 +590,22 @@
     return (a.astype(F32) + b.astype(F32)).astype(BF16)
 
 
-def half_sum_kernel(a_ref, b_ref, keep_ref, send_ref):
+def half_sum_kernel(a_ref, b_ref, *refs):
+    keep_ref, send_ref = refs[-2:]
     half = a_ref.shape[0] // 2
     keep_ref[...] = add(a_ref[:half], b_ref[:half])
     send_ref[...] = add(a_ref[half:], b_ref[half:])
 
 
-def half_sum(a, b):
+def half_sum(a, b, after=()):
     shape = (a.shape[0] // 2, *a.shape[1:])
     return call(
-        half_sum_kernel, "half_sum", [pltpu.VMEM(shape, BF16), pltpu.VMEM(shape, BF16)], (), (a, b)
+        half_sum_kernel,
+        "half_sum",
+        [pltpu.VMEM(shape, BF16), pltpu.VMEM(shape, BF16)],
+        (),
+        (a, b),
+        after,
     )
 
 
@@ -547,22 +628,63 @@
     return out
 
 
-def shared_kernel(features, a_ref, b_ref, sq_ref, resid_ref, w_ref, out_ref):
+def shared_in_kernel(me_ref, x_ref, w_ref, *refs):
+    refs = refs[-2:]
+    half = w_ref.shape[1] // 2
+    part = half // 2
+    pre = dot(x_ref[...], w_ref[...]).astype(BF16)
+    odd = me_ref[0] % 2
+    for core in range(2):
+        for up in range(2):
+            piece = pre[:, up * half + core * part : up * half + (core + 1) * part]
+
+            @pl.when(odd == core)
+            def _():
+                refs[0][:, up * part : (up + 1) * part] = piece
+
+            @pl.when(odd != core)
+            def _():
+                refs[1][:, up * part : (up + 1) * part] = piece
+
+
+def shared_in(me, x, w, after):
+    shape = (x.shape[0], w.shape[1] // 2)
+    return call(
+        shared_in_kernel, "shared_in", [pltpu.VMEM(shape, BF16)] * 2, (me,), (x, w), after
+    )
+
+
+def shared_hidden_kernel(features, a_ref, b_ref, sq_ref, out_ref):
     rows = a_ref.shape[0]
     half = a_ref.shape[1] // 2
     inverse = lax.rsqrt(sq_ref[:rows, :] / features + EPS)
     pre = (a_ref[...].astype(F32) + b_ref[...].astype(F32)) * inverse
-    hidden = (silu(pre[:, :half]) * pre[:, half:]).astype(BF16)
-    out_ref[...] = resid_ref[...] + dot(hidden, w_ref[...])
-
-
-def shared_tail(features, a, b, sq, resid, w):
+    out_ref[...] = (silu(pre[:, :half]) * pre[:, half:]).astype(BF16)
+
+
+def shared_hidden(features, a, b, sq):
     [out] = call(
-        functools.partial(shared_kernel, features),
-        "shared",
-        [pltpu.VMEM(resid.shape, F32)],
+        functools.partial(shared_hidden_kernel, features),
+        "shared_hidden",
+        [pltpu.VMEM((a.shape[0], a.shape[1] // 2), BF16)],
         (),
-        (a, b, sq, resid, w),
+        (a, b, sq),
+    )
+    return out
+
+
+def shared_out_kernel(me_ref, a_ref, b_ref, resid_ref, w_ref, out_ref):
+    part = a_ref.shape[1]
+    odd = me_ref[0] % 2
+    total = resid_ref[...]
+    for core, ref in ((odd, a_ref), (1 - odd, b_ref)):
+        total = total + dot(ref[...], w_ref[pl.ds(pl.multiple_of(core * part, part), part), :])
+    out_ref[...] = total
+
+
+def shared_out(me, a, b, resid, w):
+    [out] = call(
+        shared_out_kernel, "shared_out", [pltpu.VMEM(resid.shape, F32)], (me,), (a, b, resid, w)
     )
     return out
 
@@ -602,28 +724,6 @@
 
     mine = jnp.transpose(tokens, (1, 0, 2)).reshape(rows, width)
     value_heads = w_beta.shape[1]
-    gain = input_gain.reshape(head_count, 1, width)
-    gain_after = post_gain.reshape(head_count, 1, width)
-
-    neighbour = exchange(mine, "head", 1)
-    mine, gain, gain_after, w_query, w_key, w_value, w_zgate = load(
-        (mine, gain, gain_after, w_query, w_key, w_value, w_zgate)
-    )
-    both = stack(mine, neighbour)
-    gathered = [both] + [exchange(both, "head", 2 * p) for p in range(1, pairs)]
-    states_here, w_out, w_shared_in, w_shared_out = load(
-        (states, w_out, w_shared_in, w_shared_out), (both,)
-    )
-
-    ids = jnp.transpose(router_ids, (1, 0, 2)).reshape(rows, -1)
-    chosen = jnp.transpose(router_weights, (1, 0, 2)).reshape(rows, -1)
-    targets = (seq_index ^ jnp.arange(seq_count, dtype=jnp.int32)) * head_count + head_index
-    named = ids[None] == targets[:, None, None]
-    weights = jnp.sum(jnp.where(named, chosen[None], 0.0), axis=2)
-    high, low = split(weights)
-    extra = jnp.stack([high, low], axis=1)
-    extra = jnp.pad(extra, ((0, 0), (0, 14), (0, width - rows)))
-
     small = jnp.concatenate([w_beta, w_alpha], axis=1)
     small = jnp.transpose(small.reshape(head_count, width, 2 * value_heads), (0, 2, 1))
     small = jnp.pad(small, ((0, 0), (0, -2 * value_heads % 16), (0, 0)))
@@ -635,69 +735,92 @@
         ]
     )
 
+    neighbour = exchange(mine, "head", 1)
+    [mine] = load((mine,))
+    both = stack(mine, neighbour)
+    gathered = [both] + [exchange(both, "head", 2 * p) for p in range(1, pairs)]
+    w_query, w_key, w_value, w_zgate, w_shared_in, w_shared_out, gain, extra, gain_mine, gain_inv = bring(
+        me,
+        seq_index.astype(jnp.int32).reshape(1),
+        (
+            w_query,
+            w_key,
+            w_value,
+            w_zgate,
+            w_shared_in,
+            w_shared_out,
+            input_gain.reshape(head_count, 1, width),
+        ),
+        jnp.transpose(router_ids, (2, 1, 0)),
+        jnp.transpose(router_weights, (2, 1, 0)),
+        post_gain.reshape(head_count, 1, width),
+        seq_count,
+        both,
+    )
     own, sib, keys, deltas, totals = front(
-        me, gathered, gain, small, pack, w_query, w_key, w_value, w_zgate, w_out, states_here, extra, steps
+        me, gathered, gain, small, pack, w_query, w_key, w_value, w_zgate, w_out, states, steps
     )
 
     merged = one_sum(own, exchange(sib, "head", 1))
     received = [exchange(merged[p], "head", 2 * p) for p in range(1, pairs)]
     w_in, w_down = load((w_expert_in, w_expert_out), (merged,))
-    gain_mine = lax.dynamic_index_in_dim(gain_after, head_index, 0, keepdims=False)
-    resid, x, shared_pre, *messages = make_rows(
-        merged, received, mine, gain_mine, extra, w_shared_in, (w_in,)
-    )
+    resid, x, *messages = make_rows(merged, received, mine, gain_mine, extra, (w_in,))
 
     half = seq_count // 2
     messages = [exchange(m, "seq", z + 1) for z, m in enumerate(messages)]
-    shared_pre = one_sum(shared_pre, exchange(shared_pre, "head", axes[0]))
-    shared_next = one_sum(shared_pre, exchange(shared_pre, "head", 1))
     slabs = [x] + messages
     natural, reverse = list(range(pairs)), bit_reversed(pairs)
     blocks = tuple(range(seqs // PER_BLOCK))
     cut = len(blocks) // 2
-    sides, siblings, tie = [], [], ()
+    shared_pre, sent = shared_in(me, x, w_shared_in, (messages[0],))
+    shared_pre = one_sum(shared_pre, exchange(sent, "head", 1))
+    shared_received = exchange(shared_pre, "head", axes[0])
+    sides, tie = [], ()
     for slab, bits in ((slabs[:half], axes), (slabs[half:], axes[::-1])):
         if half == 2:
-            side = slab_pair(*slab, rows)[None]
+            side = slab_pair(*slab, rows, tie)[None]
         else:
             side = jnp.stack([m[:rows] for m in slab])[None]
+        if not tie:
+            states_out, done_1 = update(keys, deltas, totals, states, blocks[:cut], (messages[0],))
+            tie = (done_1, shared_pre)
         for bit in bits[:-1]:
             received = exchange(side, "head", bit)
-            if not tie:
-                states_out, done_1 = update(keys, deltas, totals, states, blocks[:cut], (side, shared_pre))
-                tie = (done_1,)
             if side.shape[0] == 1:
-                side = stack(side[0], received[0], tie)
+                side = stack(side[0], received[0])
             else:
                 side = jnp.concatenate([side, received])
         sides.append([side, exchange(side, "head", bits[-1])])
-        siblings.append([exchange(piece, "head", 1) for piece in sides[-1]])
-    gain_inv = 1.0 / gain_after
+    siblings = [[exchange(piece, "head", 1) for piece in side] for side in sides]
     middle = pairs // 2
     orders = tuple((tuple(o[:middle]), tuple(o[middle:])) for o in (natural, reverse))
 
-    states_out, done_2 = update(
-        keys, deltas, totals, states, blocks[cut:], (sides[1][0], shared_next), states_out
-    )
-    pre = expert_in(me, sides, gain_inv, w_in, orders, 0, after=(done_2,))
+    pre = expert_in(me, sides, gain_inv, w_in, orders, 0, after=(done_1,))
     pre, squares = expert_in(me, siblings, gain_inv, w_in, orders, 1, pre)
-    shared_pre, shared_received = shared_next, None
-    for bit in axes[1:]:
-        if shared_received is not None:
-            shared_pre = one_sum(shared_pre, shared_received)
-        shared_received = exchange(shared_pre, "head", bit)
     shape = (pairs, half, rows, width)
     a_own, a_sib, b_own, b_sib = expert_out(
-        me, pre, squares, extra, w_down, messages, (reverse, natural), (shape,) * 4, (shared_received,)
-    )
-    base = shared_tail(features, shared_pre, shared_received, squares, resid, w_shared_out)
+        me, pre, squares, extra, w_down, messages, (reverse, natural), (shape,) * 4, steps, (shared_received,)
+    )
+    owns = [a_own, b_own]
+    received = [exchange(sib, "head", 1) for sib in (a_sib, b_sib)]
+    tie = ()
+    for n, bits in enumerate(zip(axes, axes[::-1])):
+        for side, bit in enumerate(bits):
+            owns[side], sent = half_sum(owns[side], received[side], tie)
+            received[side] = exchange(sent, "head", bit)
+        if n == 0:
+            states_out, done_2 = update(
+                keys, deltas, totals, states, blocks[cut:], tuple(owns), states_out
+            )
+            tie = (done_2,)
+        else:
+            shared_pre = one_sum(shared_pre, shared_received, (owns[1],))
+            shared_received = exchange(shared_pre, "head", axes[n])
+    hidden = shared_hidden(features, shared_pre, shared_received, squares)
+    base = shared_out(me, hidden, exchange(hidden, "head", 1), resid, w_shared_out)
     slabs = []
-    for own, sib, bits in ((a_own, a_sib, axes), (b_own, b_sib, axes[::-1])):
-        received = exchange(sib, "head", 1)
-        for bit in bits:
-            own, sent = half_sum(own, received)
-            received = exchange(sent, "head", bit)
-        slabs += last_sum(own, received)
+    for side in range(2):
+        slabs += last_sum(owns[side], received[side])
     result = base + slabs[0].astype(F32)
     for z in range(1, seq_count):
         result = result + exchange(slabs[z], "seq", z).astype(F32)

time: 88.1 us -> 87.1 us (0.989)
  local copies, waits for them, and re-layouts: 2.31 us -> 0.7 us
  Pallas kernels: 28.7 us -> 27.4 us
  starting transfers between devices: 27.6 us -> 28.7 us
    pallas_call x25 -> x27, Pallas kernels: 28.7 us -> 27.4 us  [call(): pl.pallas_call(body, out_shape=tuple(out_shapes), in_specs=[SMEM_SPEC] *...]
    ppermute x31 -> x32, starting transfers between devices: 27.6 us -> 28.7 us  [exchange(): return lax.ppermute(x, axis, [(i, i ^ bit) for i in range(size)])]
    ppermute x31 -> x32, waiting for transfers between devices: 26.6 us -> 26.9 us  [exchange(): return lax.ppermute(x, axis, [(i, i ^ bit) for i in range(size)])]
  transfers between devices with their start and end apart: 31 -> 32, of which waited for: 14 -> 16; matrix products, arithmetic and copies ran while one was open for 4% -> 2% of each run, Pallas kernels for 25% -> 21%
where the time goes in v3:
time: 87.1 us; the launch traced here: 86.7 us
  starting transfers between devices  28.7 us (33%)
  Pallas kernels  27.4 us (31%)
  waiting for transfers between devices  26.9 us (31%)
  other arithmetic  2.07 us (2%)
  between operations  0.93 us (1%)
    ppermute x32, starting transfers between devices, exchange(): return lax.ppermute(x, axis, [(i, i ^ bit) for i in range(size)])  28.7 us
    pallas_call x27, Pallas kernels, call(): pl.pallas_call(body, out_shape=tuple(out_shapes), in_specs=[SMEM_SPEC] *...  27.4 us
    ppermute x32, waiting for transfers between devices, exchange(): return lax.ppermute(x, axis, [(i, i ^ bit) for i in range(size)])  26.9 us
  transfers between devices with their start and end apart: 32, of which 16 were waited for; matrix products, arithmetic and copies ran while one was open for 2% of the time, Pallas kernels for 21%

profile of v3, /device:TPU:0, one launch (start us, length us, event | category | flops | bytes accessed | tf_op | source)
XLA Modules:
  0.0 86.7 jit_solution(12342066348825792173)
XLA Ops:
  1.1 0.8 pad_maximum_fusion
  1.9 0.7 pad_bitcast_fusion
  2.6 0.8 load.2.a_ref.refs_4_
  3.4 2.6 %collective-permute-start.1 = (bf16[2,96,256]{2,1,0:T(8,128)(2,1)S(1)}, bf16[2,96,256]{2,1,0:T(8,128)(2,1)S(1)}, u32[]{:S(2)}, u32[]{:S(2)}) collective-permute-start(bf16[2,96,256]{2,1,0:T(8,128)(2,1)S(1)} %stack.19.refs_10_.refs_0_), channel_id=1, source_target_pairs={{0,2},{1,3},{2,0},{3,1},{4,6},{5,7},{6,4},{7,5},{8,10},{9,11},{10,... | collective-permute-start | bytes 294920 | tf_op jit(solution)/shard_map/ppermute | solution.py:57
  6.0 1.5 %collective-permute-start.2 = (bf16[2,96,256]{2,1,0:T(8,128)(2,1)S(1)}, bf16[2,96,256]{2,1,0:T(8,128)(2,1)S(1)}, u32[]{:S(2)}, u32[]{:S(2)}) collective-permute-start(bf16[2,96,256]{2,1,0:T(8,128)(2,1)S(1)} %stack.19.refs_10_.refs_0_), channel_id=1, source_target_pairs={{0,4},{1,5},{2,6},{3,7},{4,0},{5,1},{6,2},{7,3},{8,12},{9,13},{10,... | collective-permute-start | bytes 294920 | tf_op jit(solution)/shard_map/ppermute | solution.py:57
  7.6 0.7 pad_maximum_fusion.1.refs_6_
  8.2 3.1 %bring.1 = (bf16[2048,256]{1,0:T(8,128)(2,1)S(1)}, bf16[2048,256]{1,0:T(8,128)(2,1)S(1)}, bf16[2048,512]{1,0:T(8,128)(2,1)S(1)}, bf16[2048,512]{1,0:T(8,128)(2,1...) custom-call(s32[1]{0:T(128)} %bitcast.me_ref, ...), custom_call_target="tpu_custom_call" | custom-call | tf_op jit(solution)/shard_map/bring/pallas_call | solution.py:43
  11.3 0.7 collective-permute-done.2.refs_2_
  12.1 1.0 %collective-permute-done.3.refs_3_ = bf16[2,96,256]{2,1,0:T(8,128)(2,1)S(1)} collective-permute-done((bf16[2,96,256]{2,1,0:T(8,128)(2,1)S(1)}, bf16[2,96,256]{2,1,0:T(8,128)(2,1)S(1)}, u32[]{:S(2)}, u32[]{:S(2)}) %collective-permute-start.3) | collective-permute-done | bytes 98336 | tf_op jit(solution)/shard_map/ppermute | solution.py:57
  13.1 7.5 %front.1 = (bf16[4,96,256]{2,1,0:T(8,128)(2,1)S(1)}, bf16[4,96,256]{2,1,0:T(8,128)(2,1)S(1)}, f32[2,96,128]{2,1,0:T(8,128)S(1)}, f32[2,3,32,256]{3,2,1,0:T(8,128)S(1)}, f32[2,32,256]{2,1,0:T(8,128)S(1)}) custom-call(s32[1]{0:T(128)} %bitcast.me_ref, bf16[2,96,256]{2,1,0:T(8,128)(2,1)S(1)} %stack.19.refs_10_.refs_0_, ...), custom_call_target="tpu_custom_call" | custom-call | tf_op jit(solution)/shard_map/front/pallas_call | solution.py:43
  20.7 1.4 %collective-permute-done.4.b_ref = bf16[4,96,256]{2,1,0:T(8,128)(2,1)S(1)} collective-permute-done((bf16[4,96,256]{2,1,0:T(8,128)(2,1)S(1)}, bf16[4,96,256]{2,1,0:T(8,128)(2,1)S(1)}, u32[]{:S(2)}, u32[]{:S(2)}) %collective-permute-start.4) | collective-permute-done | bytes 196640 | tf_op jit(solution)/shard_map/ppermute | solution.py:57
  22.2 1.3 %collective-permute-start.5 = (bf16[96,256]{1,0:T(8,128)(2,1)S(1)}, bf16[96,256]{1,0:T(8,128)(2,1)S(1)}, u32[]{:S(2)}, u32[]{:S(2)}) collective-permute-start(bf16[96,256]{1,0:T(8,128)(2,1)S(1)} %get-tuple-element.100), channel_id=1, source_target_pairs={{0,2},{1,3},{2,0},{3,1},{4,6},{5,7},{6,4},{7,5},{8,10},{9,11},{10,... | collective-permute-start | bytes 147464 | tf_op jit(solution)/shard_map/ppermute | solution.py:57
  23.4 0.8 collective-permute-start.6
  24.3 1.5 %collective-permute-start.7 = (bf16[96,256]{1,0:T(8,128)(2,1)S(1)}, bf16[96,256]{1,0:T(8,128)(2,1)S(1)}, u32[]{:S(2)}, u32[]{:S(2)}) collective-permute-start(bf16[96,256]{1,0:T(8,128)(2,1)S(1)} %get-tuple-element.98), channel_id=1, source_target_pairs={{0,6},{1,7},{2,4},{3,5},{4,2},{5,3},{6,0},{7,1},{8,14},{9,15},{10,... | collective-permute-start | bytes 147464 | tf_op jit(solution)/shard_map/ppermute | solution.py:57
  25.7 2.9 %load.3 = (bf16[1,2048,1024]{2,1,0:T(8,128)(2,1)S(1)}, bf16[1,512,2048]{2,1,0:T(8,128)(2,1)S(1)}) custom-call(bf16[1,2048,1024]{2,1,0:T(8,128)(2,1)} %refs_0_.3, bf16[1,512,2048]{2,1,0:T(8,128)(2,1)} %refs_1_.3, bf16[4,96,256]{2,1,0:T(8,128)(2,1)S(1)} %one_sum.3.refs_2_.refs_0_), custom_call_target="tpu_custom_call" | custom-call | tf_op jit(solution)/shard_map/load/pallas_call | solution.py:43
  28.6 0.6 collective-permute-done.7.refs_3_
  29.3 1.6 %collective-permute-start.8 = (bf16[112,256]{1,0:T(8,128)(2,1)S(1)}, bf16[112,256]{1,0:T(8,128)(2,1)S(1)}, u32[]{:S(2)}, u32[]{:S(2)}) collective-permute-start(bf16[112,256]{1,0:T(8,128)(2,1)S(1)} %get-tuple-element.62), channel_id=1, source_target_pairs={{0,8},{8,0},{16,24},{24,16},{1,9},{9,1},{17,25},{25,17},{2,10},{10... | collective-permute-start | bytes 172040 | tf_op jit(solution)/shard_map/ppermute | solution.py:57
  30.9 2.6 %collective-permute-done.8.refs_0_.b_ref = bf16[112,256]{1,0:T(8,128)(2,1)S(1)} collective-permute-done((bf16[112,256]{1,0:T(8,128)(2,1)S(1)}, bf16[112,256]{1,0:T(8,128)(2,1)S(1)}, u32[]{:S(2)}, u32[]{:S(2)}) %collective-permute-start.8) | collective-permute-done | bytes 57376 | tf_op jit(solution)/shard_map/ppermute | solution.py:57
  33.9 2.7 %collective-permute-start.15 = (bf16[112,256]{1,0:T(8,128)(2,1)S(1)}, bf16[112,256]{1,0:T(8,128)(2,1)S(1)}, u32[]{:S(2)}, u32[]{:S(2)}) collective-permute-start(bf16[112,256]{1,0:T(8,128)(2,1)S(1)} %get-tuple-element.65), channel_id=1, source_target_pairs={{0,16},{8,24},{16,0},{24,8},{1,17},{9,25},{17,1},{25,9},{2,18},{10... | collective-permute-start | bytes 172040 | tf_op jit(solution)/shard_map/ppermute | solution.py:57
  36.5 1.3 %collective-permute-start.16 = (bf16[112,256]{1,0:T(8,128)(2,1)S(1)}, bf16[112,256]{1,0:T(8,128)(2,1)S(1)}, u32[]{:S(2)}, u32[]{:S(2)}) collective-permute-start(bf16[112,256]{1,0:T(8,128)(2,1)S(1)} %get-tuple-element.66), channel_id=1, source_target_pairs={{0,24},{8,16},{16,8},{24,0},{1,25},{9,17},{17,9},{25,1},{2,26},{10... | collective-permute-start | bytes 172040 | tf_op jit(solution)/shard_map/ppermute | solution.py:57
  37.9 1.6 %collective-permute-start.11 = (bf16[1,2,96,256]{3,2,1,0:T(8,128)(2,1)S(1)}, bf16[1,2,96,256]{3,2,1,0:T(8,128)(2,1)S(1)}, u32[]{:S(2)}, u32[]{:S(2)}) collective-permute-start(bf16[1,2,96,256]{3,2,1,0:T(8,128)(2,1)S(1)} %bitcast.31), channel_id=1, source_target_pairs={{0,2},{1,3},{2,0},{3,1},{4,6},{5,7},{6,4},{7,5},{8,10},{9,11},{10,... | collective-permute-start | bytes 294920 | tf_op jit(solution)/shard_map/ppermute | solution.py:57
  39.4 4.3 %update.2 = (f32[32,4,128,128]{3,2,1,0:T(8,128)}, f32[8,128]{1,0:T(8,128)S(1)}) custom-call(f32[2,96,128]{2,1,0:T(8,128)S(1)} %get-tuple-element.67.keys_ref, f32[2,3,32,256]{3,2,1,0:T(8,128)S(1)} %get-tuple-element.68.delta_ref, f32[2,32,256]{2,1,0:T(8,128)S(1)} %get-tuple-element.69.total_ref, f32[32,4,128,128]{3,2,1,0:T(8,128)} %states_ref.3, ...), custom_call_target="tpu_custom_call" | custom-call | tf_op jit(solution)/shard_map/update/pallas_call | solution.py:43
  43.8 0.6 collective-permute-start.17
  44.4 1.5 %collective-permute-start.13 = (bf16[2,2,96,256]{3,2,1,0:T(8,128)(2,1)S(1)}, bf16[2,2,96,256]{3,2,1,0:T(8,128)(2,1)S(1)}, u32[]{:S(2)}, u32[]{:S(2)}) collective-permute-start(bf16[2,2,96,256]{3,2,1,0:T(8,128)(2,1)S(1)} %stack.20.refs_0_), channel_id=1, source_target_pairs={{0,4},{1,5},{2,6},{3,7},{4,0},{5,1},{6,2},{7,3},{8,12},{9,13},{10,... | collective-permute-start | bytes 589832 | tf_op jit(solution)/shard_map/ppermute | solution.py:57
  46.0 3.6 %collective-permute-done.17 = bf16[1,2,96,256]{3,2,1,0:T(8,128)(2,1)S(1)} collective-permute-done((bf16[1,2,96,256]{3,2,1,0:T(8,128)(2,1)S(1)}, bf16[1,2,96,256]{3,2,1,0:T(8,128)(2,1)S(1)}, u32[]{:S(2)}, u32[]{:S(2)}) %collective-permute-start.17) | collective-permute-done | bytes 98336 | tf_op jit(solution)/shard_map/ppermute | solution.py:57
  49.6 0.6 collective-permute-start.19
  50.7 1.7 %collective-permute-done.13.refs_1_ = bf16[2,2,96,256]{3,2,1,0:T(8,128)(2,1)S(1)} collective-permute-done((bf16[2,2,96,256]{3,2,1,0:T(8,128)(2,1)S(1)}, bf16[2,2,96,256]{3,2,1,0:T(8,128)(2,1)S(1)}, u32[]{:S(2)}, u32[]{:S(2)}) %collective-permute-start.13) | collective-permute-done | bytes 196640 | tf_op jit(solution)/shard_map/ppermute | solution.py:57
  52.4 2.9 %collective-permute-done.19.refs_3_ = bf16[2,2,96,256]{3,2,1,0:T(8,128)(2,1)S(1)} collective-permute-done((bf16[2,2,96,256]{3,2,1,0:T(8,128)(2,1)S(1)}, bf16[2,2,96,256]{3,2,1,0:T(8,128)(2,1)S(1)}, u32[]{:S(2)}, u32[]{:S(2)}) %collective-permute-start.19) | collective-permute-done | bytes 196640 | tf_op jit(solution)/shard_map/ppermute | solution.py:57
  55.3 0.5 collective-permute-start.10
  55.9 1.1 %expert_in.2 = (f32[384,1024]{1,0:T(8,128)S(1)}, f32[384,1]{1,0:T(8,128)S(1)}) custom-call(s32[1]{0:T(128)} %bitcast.me_ref, bf16[2,2,96,256]{3,2,1,0:T(8,128)(2,1)S(1)} %stack.20.refs_0_, bf16[2,2,96,256]{3,2,1,0:T(8,128)(2,1)S(1)} %collective-permute-done.13.refs_1_, bf16[2,2,96,256]{3,2,1,0:T(8,128)(2,1)S(1)} %stack.21.refs_2_, ...), custom_call_target="tpu_custom_call" | custom-call | tf_op jit(solution)/shard_map/expert_in/pallas_call | solution.py:43
  57.0 1.1 %expert_in.3 = (f32[384,1024]{1,0:T(8,128)S(1)}, f32[384,1]{1,0:T(8,128)S(1)}) custom-call(s32[1]{0:T(128)} %bitcast.me_ref, bf16[2,2,96,256]{3,2,1,0:T(8,128)(2,1)S(1)} %collective-permute-done.12.refs_0_, bf16[2,2,96,256]{3,2,1,0:T(8,128)(2,1)S(1)} %collective-permute-done.14.refs_1_, bf16[2,2,96,256]{3,2,1,0:T(8,128)(2,1)S(1)} %collective-permute-done.18.refs_2_, ...), custom_call_target="tpu_custom_call" | custom-call | tf_op jit(solution)/shard_map/expert_in/pallas_call | solution.py:43
  58.1 2.4 %collective-permute-done.10.refs_3_.b_ref = bf16[96,512]{1,0:T(8,128)(2,1)S(1)} collective-permute-done((bf16[96,512]{1,0:T(8,128)(2,1)S(1)}, bf16[96,512]{1,0:T(8,128)(2,1)S(1)}, u32[]{:S(2)}, u32[]{:S(2)}) %collective-permute-start.10) | collective-permute-done | bytes 98336 | tf_op jit(solution)/shard_map/ppermute | solution.py:57
  60.5 1.2 %expert_out.1 = (bf16[4,2,96,256]{3,2,1,0:T(8,128)(2,1)S(1)}, bf16[4,2,96,256]{3,2,1,0:T(8,128)(2,1)S(1)}, bf16[4,2,96,256]{3,2,1,0:T(8,128)(2,1)S(1)}, bf16[4,2,96,256]{3,2,1,0:T(8,128)(2,1)S(1)}) custom-call(s32[1]{0:T(128)} %bitcast.me_ref, f32[384,1024]{1,0:T(8,128)S(1)} %get-tuple-element.74.pre_ref, f32[384,1]{1,0:T(8,128)S(1)} %get-tuple-element.75.sq_ref, ...), custom_call_target="tpu_custom_call" | custom-call | tf_op jit(solution)/shard_map/expert_out/pallas_call | solution.py:43
  62.4 1.2 %collective-permute-done.21.b_ref = bf16[4,2,96,256]{3,2,1,0:T(8,128)(2,1)S(1)} collective-permute-done((bf16[4,2,96,256]{3,2,1,0:T(8,128)(2,1)S(1)}, bf16[4,2,96,256]{3,2,1,0:T(8,128)(2,1)S(1)}, u32[]{:S(2)}, u32[]{:S(2)}) %collective-permute-start.21) | collective-permute-done | bytes 393248 | tf_op jit(solution)/shard_map/ppermute | solution.py:57
  63.7 0.6 collective-permute-start.22
  64.3 1.3 %collective-permute-start.26 = (bf16[2,2,96,256]{3,2,1,0:T(8,128)(2,1)S(1)}, bf16[2,2,96,256]{3,2,1,0:T(8,128)(2,1)S(1)}, u32[]{:S(2)}, u32[]{:S(2)}) collective-permute-start(bf16[2,2,96,256]{3,2,1,0:T(8,128)(2,1)S(1)} %get-tuple-element.89), channel_id=1, source_target_pairs={{0,2},{1,3},{2,0},{3,1},{4,6},{5,7},{6,4},{7,5},{8,10},{9,11},{10,... | collective-permute-start | bytes 589832 | tf_op jit(solution)/shard_map/ppermute | solution.py:57
  65.6 4.3 %update.3 = (f32[32,4,128,128]{3,2,1,0:T(8,128)}, f32[8,128]{1,0:T(8,128)S(1)}) custom-call(f32[2,96,128]{2,1,0:T(8,128)S(1)} %get-tuple-element.67.keys_ref, f32[2,3,32,256]{3,2,1,0:T(8,128)S(1)} %get-tuple-element.68.delta_ref, f32[2,32,256]{2,1,0:T(8,128)S(1)} %get-tuple-element.69.total_ref, ...), custom_call_target="tpu_custom_call", output_to_operand_aliasing={{0}: (4, {})} | custom-call | tf_op jit(solution)/shard_map/update/pallas_call | solution.py:43
  69.9 0.8 collective-permute-done.22.b_ref
  70.8 0.6 collective-permute-start.24
  71.4 1.6 %collective-permute-start.27 = (bf16[1,2,96,256]{3,2,1,0:T(8,128)(2,1)S(1)}, bf16[1,2,96,256]{3,2,1,0:T(8,128)(2,1)S(1)}, u32[]{:S(2)}, u32[]{:S(2)}) collective-permute-start(bf16[1,2,96,256]{3,2,1,0:T(8,128)(2,1)S(1)} %get-tuple-element.91), channel_id=1, source_target_pairs={{0,4},{1,5},{2,6},{3,7},{4,0},{5,1},{6,2},{7,3},{8,12},{9,13},{10,... | collective-permute-start | bytes 294920 | tf_op jit(solution)/shard_map/ppermute | solution.py:57
  73.0 0.5 collective-permute-start.29
  73.5 2.4 %collective-permute-done.24.b_ref = bf16[96,512]{1,0:T(8,128)(2,1)S(1)} collective-permute-done((bf16[96,512]{1,0:T(8,128)(2,1)S(1)}, bf16[96,512]{1,0:T(8,128)(2,1)S(1)}, u32[]{:S(2)}, u32[]{:S(2)}) %collective-permute-start.24) | collective-permute-done | bytes 98336 | tf_op jit(solution)/shard_map/ppermute | solution.py:57
  76.1 0.9 collective-permute-done.27.b_ref
  77.6 2.6 %collective-permute-start.30 = (bf16[96,256]{1,0:T(8,128)(2,1)S(1)}, bf16[96,256]{1,0:T(8,128)(2,1)S(1)}, u32[]{:S(2)}, u32[]{:S(2)}) collective-permute-start(bf16[96,256]{1,0:T(8,128)(2,1)S(1)} %get-tuple-element.95), channel_id=1, source_target_pairs={{0,16},{8,24},{16,0},{24,8},{1,17},{9,25},{17,1},{25,9},{2,18},{10... | collective-permute-start | bytes 147464 | tf_op jit(solution)/shard_map/ppermute | solution.py:57
  80.2 1.3 %collective-permute-start.31 = (bf16[96,256]{1,0:T(8,128)(2,1)S(1)}, bf16[96,256]{1,0:T(8,128)(2,1)S(1)}, u32[]{:S(2)}, u32[]{:S(2)}) collective-permute-start(bf16[96,256]{1,0:T(8,128)(2,1)S(1)} %get-tuple-element.96), channel_id=1, source_target_pairs={{0,24},{8,16},{16,8},{24,0},{1,25},{9,17},{17,9},{25,1},{2,26},{10... | collective-permute-start | bytes 147464 | tf_op jit(solution)/shard_map/ppermute | solution.py:57
  81.7 1.4 %collective-permute-done.30 = bf16[96,256]{1,0:T(8,128)(2,1)S(1)} collective-permute-done((bf16[96,256]{1,0:T(8,128)(2,1)S(1)}, bf16[96,256]{1,0:T(8,128)(2,1)S(1)}, u32[]{:S(2)}, u32[]{:S(2)}) %collective-permute-start.30) | collective-permute-done | bytes 49184 | tf_op jit(solution)/shard_map/ppermute | solution.py:57
  83.2 2.9 %collective-permute-done.31 = bf16[96,256]{1,0:T(8,128)(2,1)S(1)} collective-permute-done((bf16[96,256]{1,0:T(8,128)(2,1)S(1)}, bf16[96,256]{1,0:T(8,128)(2,1)S(1)}, u32[]{:S(2)}, u32[]{:S(2)}) %collective-permute-start.31) | collective-permute-done | bytes 49184 | tf_op jit(solution)/shard_map/ppermute | solution.py:57
  86.1 0.7 add_convert_fusion
  (49 shorter events, 3.6 us)
Async XLA Ops:
  0.6 2.8 %collective-permute-start = (bf16[96,256]{1,0:T(8,128)(2,1)}, bf16[96,256]{1,0:T(8,128)(2,1)S(1)}, u32[]{:S(2)}, u32[]{:S(2)}) collective-permute-start(bf16[96,256]{1,0:T(8,128)(2,1)} %bitcast.35), channel_id=1, source_target_pairs={{0,1},{1,0},{2,3},{3,2},{4,5},{5,4},{6,7},{7,6},{8,9},{9,8},{10,11... | collective-permute-start | bytes 147464 | tf_op jit(solution)/shard_map/ppermute | solution.py:57
  3.4 7.9 %collective-permute-start.1 = (bf16[2,96,256]{2,1,0:T(8,128)(2,1)S(1)}, bf16[2,96,256]{2,1,0:T(8,128)(2,1)S(1)}, u32[]{:S(2)}, u32[]{:S(2)}) collective-permute-start(bf16[2,96,256]{2,1,0:T(8,128)(2,1)S(1)} %stack.19.refs_10_.refs_0_), channel_id=1, source_target_pairs={{0,2},{1,3},{2,0},{3,1},{4,6},{5,7},{6,4},{7,5},{8,10},{9,11},{10,... | collective-permute-start | bytes 294920 | tf_op jit(solution)/shard_map/ppermute | solution.py:57
  6.0 6.1 %collective-permute-start.2 = (bf16[2,96,256]{2,1,0:T(8,128)(2,1)S(1)}, bf16[2,96,256]{2,1,0:T(8,128)(2,1)S(1)}, u32[]{:S(2)}, u32[]{:S(2)}) collective-permute-start(bf16[2,96,256]{2,1,0:T(8,128)(2,1)S(1)} %stack.19.refs_10_.refs_0_), channel_id=1, source_target_pairs={{0,4},{1,5},{2,6},{3,7},{4,0},{5,1},{6,2},{7,3},{8,12},{9,13},{10,... | collective-permute-start | bytes 294920 | tf_op jit(solution)/shard_map/ppermute | solution.py:57
  7.5 5.5 %collective-permute-start.3 = (bf16[2,96,256]{2,1,0:T(8,128)(2,1)S(1)}, bf16[2,96,256]{2,1,0:T(8,128)(2,1)S(1)}, u32[]{:S(2)}, u32[]{:S(2)}) collective-permute-start(bf16[2,96,256]{2,1,0:T(8,128)(2,1)S(1)} %stack.19.refs_10_.refs_0_), channel_id=1, source_target_pairs={{0,6},{1,7},{2,4},{3,5},{4,2},{5,3},{6,0},{7,1},{8,14},{9,15},{10,... | collective-permute-start | bytes 294920 | tf_op jit(solution)/shard_map/ppermute | solution.py:57
  20.6 1.5 %collective-permute-start.4 = (bf16[4,96,256]{2,1,0:T(8,128)(2,1)S(1)}, bf16[4,96,256]{2,1,0:T(8,128)(2,1)S(1)}, u32[]{:S(2)}, u32[]{:S(2)}) collective-permute-start(bf16[4,96,256]{2,1,0:T(8,128)(2,1)S(1)} %get-tuple-element.56), channel_id=1, source_target_pairs={{0,1},{1,0},{2,3},{3,2},{4,5},{5,4},{6,7},{7,6},{8,9},{9,8},{10,11... | collective-permute-start | bytes 589832 | tf_op jit(solution)/shard_map/ppermute | solution.py:57
  22.2 6.4 %collective-permute-start.5 = (bf16[96,256]{1,0:T(8,128)(2,1)S(1)}, bf16[96,256]{1,0:T(8,128)(2,1)S(1)}, u32[]{:S(2)}, u32[]{:S(2)}) collective-permute-start(bf16[96,256]{1,0:T(8,128)(2,1)S(1)} %get-tuple-element.100), channel_id=1, source_target_pairs={{0,2},{1,3},{2,0},{3,1},{4,6},{5,7},{6,4},{7,5},{8,10},{9,11},{10,... | collective-permute-start | bytes 147464 | tf_op jit(solution)/shard_map/ppermute | solution.py:57
  23.4 5.2 %collective-permute-start.6 = (bf16[96,256]{1,0:T(8,128)(2,1)S(1)}, bf16[96,256]{1,0:T(8,128)(2,1)S(1)}, u32[]{:S(2)}, u32[]{:S(2)}) collective-permute-start(bf16[96,256]{1,0:T(8,128)(2,1)S(1)} %get-tuple-element.99), channel_id=1, source_target_pairs={{0,4},{1,5},{2,6},{3,7},{4,0},{5,1},{6,2},{7,3},{8,12},{9,13},{10,... | collective-permute-start | bytes 147464 | tf_op jit(solution)/shard_map/ppermute | solution.py:57
  24.3 5.0 %collective-permute-start.7 = (bf16[96,256]{1,0:T(8,128)(2,1)S(1)}, bf16[96,256]{1,0:T(8,128)(2,1)S(1)}, u32[]{:S(2)}, u32[]{:S(2)}) collective-permute-start(bf16[96,256]{1,0:T(8,128)(2,1)S(1)} %get-tuple-element.98), channel_id=1, source_target_pairs={{0,6},{1,7},{2,4},{3,5},{4,2},{5,3},{6,0},{7,1},{8,14},{9,15},{10,... | collective-permute-start | bytes 147464 | tf_op jit(solution)/shard_map/ppermute | solution.py:57
  29.3 4.2 %collective-permute-start.8 = (bf16[112,256]{1,0:T(8,128)(2,1)S(1)}, bf16[112,256]{1,0:T(8,128)(2,1)S(1)}, u32[]{:S(2)}, u32[]{:S(2)}) collective-permute-start(bf16[112,256]{1,0:T(8,128)(2,1)S(1)} %get-tuple-element.62), channel_id=1, source_target_pairs={{0,8},{8,0},{16,24},{24,16},{1,9},{9,1},{17,25},{25,17},{2,10},{10... | collective-permute-start | bytes 172040 | tf_op jit(solution)/shard_map/ppermute | solution.py:57
  33.8 9.9 %collective-permute-start.9 = (bf16[96,512]{1,0:T(8,128)(2,1)S(1)}, bf16[96,512]{1,0:T(8,128)(2,1)S(1)}, u32[]{:S(2)}, u32[]{:S(2)}) collective-permute-start(bf16[96,512]{1,0:T(8,128)(2,1)S(1)} %get-tuple-element.64), channel_id=1, source_target_pairs={{0,1},{1,0},{2,3},{3,2},{4,5},{5,4},{6,7},{7,6},{8,9},{9,8},{10,11... | collective-permute-start | bytes 294920 | tf_op jit(solution)/shard_map/ppermute | solution.py:57
  33.9 9.9 %collective-permute-start.15 = (bf16[112,256]{1,0:T(8,128)(2,1)S(1)}, bf16[112,256]{1,0:T(8,128)(2,1)S(1)}, u32[]{:S(2)}, u32[]{:S(2)}) collective-permute-start(bf16[112,256]{1,0:T(8,128)(2,1)S(1)} %get-tuple-element.65), channel_id=1, source_target_pairs={{0,16},{8,24},{16,0},{24,8},{1,17},{9,25},{17,1},{25,9},{2,18},{10... | collective-permute-start | bytes 172040 | tf_op jit(solution)/shard_map/ppermute | solution.py:57
  36.5 7.2 %collective-permute-start.16 = (bf16[112,256]{1,0:T(8,128)(2,1)S(1)}, bf16[112,256]{1,0:T(8,128)(2,1)S(1)}, u32[]{:S(2)}, u32[]{:S(2)}) collective-permute-start(bf16[112,256]{1,0:T(8,128)(2,1)S(1)} %get-tuple-element.66), channel_id=1, source_target_pairs={{0,24},{8,16},{16,8},{24,0},{1,25},{9,17},{17,9},{25,1},{2,26},{10... | collective-permute-start | bytes 172040 | tf_op jit(solution)/shard_map/ppermute | solution.py:57
  37.9 6.5 %collective-permute-start.11 = (bf16[1,2,96,256]{3,2,1,0:T(8,128)(2,1)S(1)}, bf16[1,2,96,256]{3,2,1,0:T(8,128)(2,1)S(1)}, u32[]{:S(2)}, u32[]{:S(2)}) collective-permute-start(bf16[1,2,96,256]{3,2,1,0:T(8,128)(2,1)S(1)} %bitcast.31), channel_id=1, source_target_pairs={{0,2},{1,3},{2,0},{3,1},{4,6},{5,7},{6,4},{7,5},{8,10},{9,11},{10,... | collective-permute-start | bytes 294920 | tf_op jit(solution)/shard_map/ppermute | solution.py:57
  43.8 5.8 %collective-permute-start.17 = (bf16[1,2,96,256]{3,2,1,0:T(8,128)(2,1)S(1)}, bf16[1,2,96,256]{3,2,1,0:T(8,128)(2,1)S(1)}, u32[]{:S(2)}, u32[]{:S(2)}) collective-permute-start(bf16[1,2,96,256]{3,2,1,0:T(8,128)(2,1)S(1)} %bitcast.30), channel_id=1, source_target_pairs={{0,4},{1,5},{2,6},{3,7},{4,0},{5,1},{6,2},{7,3},{8,12},{9,13},{10,... | collective-permute-start | bytes 294920 | tf_op jit(solution)/shard_map/ppermute | solution.py:57
  44.4 8.0 %collective-permute-start.13 = (bf16[2,2,96,256]{3,2,1,0:T(8,128)(2,1)S(1)}, bf16[2,2,96,256]{3,2,1,0:T(8,128)(2,1)S(1)}, u32[]{:S(2)}, u32[]{:S(2)}) collective-permute-start(bf16[2,2,96,256]{3,2,1,0:T(8,128)(2,1)S(1)} %stack.20.refs_0_), channel_id=1, source_target_pairs={{0,4},{1,5},{2,6},{3,7},{4,0},{5,1},{6,2},{7,3},{8,12},{9,13},{10,... | collective-permute-start | bytes 589832 | tf_op jit(solution)/shard_map/ppermute | solution.py:57
  49.6 5.7 %collective-permute-start.19 = (bf16[2,2,96,256]{3,2,1,0:T(8,128)(2,1)S(1)}, bf16[2,2,96,256]{3,2,1,0:T(8,128)(2,1)S(1)}, u32[]{:S(2)}, u32[]{:S(2)}) collective-permute-start(bf16[2,2,96,256]{3,2,1,0:T(8,128)(2,1)S(1)} %stack.21.refs_2_), channel_id=1, source_target_pairs={{0,2},{1,3},{2,0},{3,1},{4,6},{5,7},{6,4},{7,5},{8,10},{9,11},{10,... | collective-permute-start | bytes 589832 | tf_op jit(solution)/shard_map/ppermute | solution.py:57
  50.2 6.8 %collective-permute-start.12 = (bf16[2,2,96,256]{3,2,1,0:T(8,128)(2,1)S(1)}, bf16[2,2,96,256]{3,2,1,0:T(8,128)(2,1)S(1)}, u32[]{:S(2)}, u32[]{:S(2)}) collective-permute-start(bf16[2,2,96,256]{3,2,1,0:T(8,128)(2,1)S(1)} %stack.20.refs_0_), channel_id=1, source_target_pairs={{0,1},{1,0},{2,3},{3,2},{4,5},{5,4},{6,7},{7,6},{8,9},{9,8},{10,11... | collective-permute-start | bytes 589832 | tf_op jit(solution)/shard_map/ppermute | solution.py:57
  50.2 6.8 %collective-permute-start.18 = (bf16[2,2,96,256]{3,2,1,0:T(8,128)(2,1)S(1)}, bf16[2,2,96,256]{3,2,1,0:T(8,128)(2,1)S(1)}, u32[]{:S(2)}, u32[]{:S(2)}) collective-permute-start(bf16[2,2,96,256]{3,2,1,0:T(8,128)(2,1)S(1)} %stack.21.refs_2_), channel_id=1, source_target_pairs={{0,1},{1,0},{2,3},{3,2},{4,5},{5,4},{6,7},{7,6},{8,9},{9,8},{10,11... | collective-permute-start | bytes 589832 | tf_op jit(solution)/shard_map/ppermute | solution.py:57
  52.4 4.6 %collective-permute-start.14 = (bf16[2,2,96,256]{3,2,1,0:T(8,128)(2,1)S(1)}, bf16[2,2,96,256]{3,2,1,0:T(8,128)(2,1)S(1)}, u32[]{:S(2)}, u32[]{:S(2)}) collective-permute-start(bf16[2,2,96,256]{3,2,1,0:T(8,128)(2,1)S(1)} %collective-permute-done.13.refs_1_), channel_id=1, source_target_pairs={{0,1},{1,0},{2,3},{3,2},{4,5},{5,4},{6,7},{7,6},{8,9},{9,8},{10,11... | collective-permute-start | bytes 589832 | tf_op jit(solution)/shard_map/ppermute | solution.py:57
  55.3 1.7 %collective-permute-start.20 = (bf16[2,2,96,256]{3,2,1,0:T(8,128)(2,1)S(1)}, bf16[2,2,96,256]{3,2,1,0:T(8,128)(2,1)S(1)}, u32[]{:S(2)}, u32[]{:S(2)}) collective-permute-start(bf16[2,2,96,256]{3,2,1,0:T(8,128)(2,1)S(1)} %collective-permute-done.19.refs_3_), channel_id=1, source_target_pairs={{0,1},{1,0},{2,3},{3,2},{4,5},{5,4},{6,7},{7,6},{8,9},{9,8},{10,11... | collective-permute-start | bytes 589832 | tf_op jit(solution)/shard_map/ppermute | solution.py:57
  55.3 5.2 %collective-permute-start.10 = (bf16[96,512]{1,0:T(8,128)(2,1)S(1)}, bf16[96,512]{1,0:T(8,128)(2,1)S(1)}, u32[]{:S(2)}, u32[]{:S(2)}) collective-permute-start(bf16[96,512]{1,0:T(8,128)(2,1)S(1)} %one_sum.4.refs_1_.a_ref), channel_id=1, source_target_pairs={{0,2},{1,3},{2,0},{3,1},{4,6},{5,7},{6,4},{7,5},{8,10},{9,11},{10,... | collective-permute-start | bytes 294920 | tf_op jit(solution)/shard_map/ppermute | solution.py:57
  61.8 1.8 %collective-permute-start.21 = (bf16[4,2,96,256]{3,2,1,0:T(8,128)(2,1)S(1)}, bf16[4,2,96,256]{3,2,1,0:T(8,128)(2,1)S(1)}, u32[]{:S(2)}, u32[]{:S(2)}) collective-permute-start(bf16[4,2,96,256]{3,2,1,0:T(8,128)(2,1)S(1)} %get-tuple-element.78), channel_id=1, source_target_pairs={{0,1},{1,0},{2,3},{3,2},{4,5},{5,4},{6,7},{7,6},{8,9},{9,8},{10,11... | collective-permute-start | bytes 1179656 | tf_op jit(solution)/shard_map/ppermute | solution.py:57
  61.9 2.4 %collective-permute-start.23 = (bf16[4,2,96,256]{3,2,1,0:T(8,128)(2,1)S(1)}, bf16[4,2,96,256]{3,2,1,0:T(8,128)(2,1)S(1)}, u32[]{:S(2)}, u32[]{:S(2)}) collective-permute-start(bf16[4,2,96,256]{3,2,1,0:T(8,128)(2,1)S(1)} %get-tuple-element.83), channel_id=1, source_target_pairs={{0,1},{1,0},{2,3},{3,2},{4,5},{5,4},{6,7},{7,6},{8,9},{9,8},{10,11... | collective-permute-start | bytes 1179656 | tf_op jit(solution)/shard_map/ppermute | solution.py:57
  63.7 7.0 %collective-permute-start.22 = (bf16[2,2,96,256]{3,2,1,0:T(8,128)(2,1)S(1)}, bf16[2,2,96,256]{3,2,1,0:T(8,128)(2,1)S(1)}, u32[]{:S(2)}, u32[]{:S(2)}) collective-permute-start(bf16[2,2,96,256]{3,2,1,0:T(8,128)(2,1)S(1)} %get-tuple-element.80), channel_id=1, source_target_pairs={{0,4},{1,5},{2,6},{3,7},{4,0},{5,1},{6,2},{7,3},{8,12},{9,13},{10,... | collective-permute-start | bytes 589832 | tf_op jit(solution)/shard_map/ppermute | solution.py:57
  64.3 7.0 %collective-permute-start.26 = (bf16[2,2,96,256]{3,2,1,0:T(8,128)(2,1)S(1)}, bf16[2,2,96,256]{3,2,1,0:T(8,128)(2,1)S(1)}, u32[]{:S(2)}, u32[]{:S(2)}) collective-permute-start(bf16[2,2,96,256]{3,2,1,0:T(8,128)(2,1)S(1)} %get-tuple-element.89), channel_id=1, source_target_pairs={{0,2},{1,3},{2,0},{3,1},{4,6},{5,7},{6,4},{7,5},{8,10},{9,11},{10,... | collective-permute-start | bytes 589832 | tf_op jit(solution)/shard_map/ppermute | solution.py:57
  70.8 5.1 %collective-permute-start.24 = (bf16[96,512]{1,0:T(8,128)(2,1)S(1)}, bf16[96,512]{1,0:T(8,128)(2,1)S(1)}, u32[]{:S(2)}, u32[]{:S(2)}) collective-permute-start(bf16[96,512]{1,0:T(8,128)(2,1)S(1)} %one_sum.5.a_ref), channel_id=1, source_target_pairs={{0,4},{1,5},{2,6},{3,7},{4,0},{5,1},{6,2},{7,3},{8,12},{9,13},{10,... | collective-permute-start | bytes 294920 | tf_op jit(solution)/shard_map/ppermute | solution.py:57
  71.4 5.6 %collective-permute-start.27 = (bf16[1,2,96,256]{3,2,1,0:T(8,128)(2,1)S(1)}, bf16[1,2,96,256]{3,2,1,0:T(8,128)(2,1)S(1)}, u32[]{:S(2)}, u32[]{:S(2)}) collective-permute-start(bf16[1,2,96,256]{3,2,1,0:T(8,128)(2,1)S(1)} %get-tuple-element.91), channel_id=1, source_target_pairs={{0,4},{1,5},{2,6},{3,7},{4,0},{5,1},{6,2},{7,3},{8,12},{9,13},{10,... | collective-permute-start | bytes 294920 | tf_op jit(solution)/shard_map/ppermute | solution.py:57
  73.0 4.6 %collective-permute-start.29 = (bf16[1,2,96,256]{3,2,1,0:T(8,128)(2,1)S(1)}, bf16[1,2,96,256]{3,2,1,0:T(8,128)(2,1)S(1)}, u32[]{:S(2)}, u32[]{:S(2)}) collective-permute-start(bf16[1,2,96,256]{3,2,1,0:T(8,128)(2,1)S(1)} %get-tuple-element.94), channel_id=1, source_target_pairs={{0,2},{1,3},{2,0},{3,1},{4,6},{5,7},{6,4},{7,5},{8,10},{9,11},{10,... | collective-permute-start | bytes 294920 | tf_op jit(solution)/shard_map/ppermute | solution.py:57
  76.0 5.5 %collective-permute-start.25 = (bf16[96,256]{1,0:T(8,128)(2,1)S(1)}, bf16[96,256]{1,0:T(8,128)(2,1)S(1)}, u32[]{:S(2)}, u32[]{:S(2)}) collective-permute-start(bf16[96,256]{1,0:T(8,128)(2,1)S(1)} %shared_hidden.1.a_ref), channel_id=1, source_target_pairs={{0,1},{1,0},{2,3},{3,2},{4,5},{5,4},{6,7},{7,6},{8,9},{9,8},{10,11... | collective-permute-start | bytes 147464 | tf_op jit(solution)/shard_map/ppermute | solution.py:57
  77.0 4.7 %collective-permute-start.28 = (bf16[96,256]{1,0:T(8,128)(2,1)S(1)}, bf16[96,256]{1,0:T(8,128)(2,1)S(1)}, u32[]{:S(2)}, u32[]{:S(2)}) collective-permute-start(bf16[96,256]{1,0:T(8,128)(2,1)S(1)} %get-tuple-element.93), channel_id=1, source_target_pairs={{0,8},{8,0},{16,24},{24,16},{1,9},{9,1},{17,25},{25,17},{2,10},{10... | collective-permute-start | bytes 147464 | tf_op jit(solution)/shard_map/ppermute | solution.py:57
  77.6 5.5 %collective-permute-start.30 = (bf16[96,256]{1,0:T(8,128)(2,1)S(1)}, bf16[96,256]{1,0:T(8,128)(2,1)S(1)}, u32[]{:S(2)}, u32[]{:S(2)}) collective-permute-start(bf16[96,256]{1,0:T(8,128)(2,1)S(1)} %get-tuple-element.95), channel_id=1, source_target_pairs={{0,16},{8,24},{16,0},{24,8},{1,17},{9,25},{17,1},{25,9},{2,18},{10... | collective-permute-start | bytes 147464 | tf_op jit(solution)/shard_map/ppermute | solution.py:57
  80.2 5.9 %collective-permute-start.31 = (bf16[96,256]{1,0:T(8,128)(2,1)S(1)}, bf16[96,256]{1,0:T(8,128)(2,1)S(1)}, u32[]{:S(2)}, u32[]{:S(2)}) collective-permute-start(bf16[96,256]{1,0:T(8,128)(2,1)S(1)} %get-tuple-element.96), channel_id=1, source_target_pairs={{0,24},{8,16},{16,8},{24,0},{1,25},{9,17},{17,9},{25,1},{2,26},{10... | collective-permute-start | bytes 147464 | tf_op jit(solution)/shard_map/ppermute | solution.py:57

commit v4 on v3

--- a/solution.py
+++ b/solution.py
@@ -57,14 +57,14 @@
     return lax.ppermute(x, axis, [(i, i ^ bit) for i in range(size)])
 
 
-def stack_kernel(a_ref, b_ref, *refs):
-    out_ref = refs[-1]
-    out_ref[0] = a_ref[...]
-    out_ref[1] = b_ref[...]
-
-
-def stack(a, b, after=()):
-    [out] = call(stack_kernel, "stack", [pltpu.VMEM((2, *a.shape), a.dtype)], (), (a, b), after)
+def stack_kernel(*refs):
+    for n, ref in enumerate(refs[:-1]):
+        refs[-1][n] = ref[...]
+
+
+def stack(*arrays):
+    shape = (len(arrays), *arrays[0].shape)
+    [out] = call(stack_kernel, "stack", [pltpu.VMEM(shape, arrays[0].dtype)], (), arrays)
     return out
 
 
@@ -89,18 +89,20 @@
     )
 
 
-def bring_kernel(count, seq_count, head_count, me_ref, seq_ref, *refs):
-    sources, (ids_hbm, chosen_hbm, gain_after_hbm) = refs[:count], refs[count : count + 3]
-    refs = refs[count + 4 :]
-    targets, (extra_ref, gain_mine_ref, gain_inv_ref) = refs[:count], refs[count : count + 3]
-    ids, chosen, gain_after, sems = refs[count + 3 :]
-    sources = (ids_hbm, chosen_hbm, gain_after_hbm, *sources)
-    targets = (ids, chosen, gain_after, *targets)
+def bring_kernel(count, vectors, seq_count, head_count, me_ref, seq_ref, *refs):
+    small = 3 + vectors
+    sources, refs = refs[: small + count], refs[small + count :]
+    targets, (pack_ref, extra_ref, gain_mine_ref, gain_inv_ref) = refs[:count], refs[count : count + 4]
+    scratch, sems = refs[count + 4 : -1], refs[-1]
+    ids, chosen, gain_after = scratch[:3]
+    targets = (*scratch, *targets)
     copies = [pltpu.make_async_copy(a, b, sems.at[n]) for n, (a, b) in enumerate(zip(sources, targets))]
     for copy in copies:
         copy.start()
-    for copy in copies[:3]:
+    for copy in copies[:small]:
         copy.wait()
+    for n, ref in enumerate(scratch[3:]):
+        pack_ref[n : n + 1, : ref.shape[1]] = ref[...]
     me, seq = me_ref[0], seq_ref[0]
     gain_mine_ref[...] = gain_after[me]
     gain_inv_ref[...] = 1.0 / gain_after[...]
@@ -116,32 +118,28 @@
         both = jnp.concatenate([both, jnp.zeros((rows - 2 * steps, seqs), F32)], axis=0)
         both = jnp.concatenate([both, jnp.zeros((rows, width - seqs), F32)], axis=1)
         extra_ref[z] = both.astype(BF16)
-    for copy in copies[3:]:
+    for copy in copies[small:]:
         copy.wait()
 
 
-def bring(me, seq, arrays, ids, chosen, gain_after, seq_count, after):
+def bring(me, seq, arrays, vectors, ids, chosen, gain_after, seq_count):
     head_count, _, width = gain_after.shape
-    count = len(arrays)
-    hbm = (pltpu.with_memory_space_constraint(x, pltpu.HBM) for x in (*arrays, ids, chosen, gain_after))
+    small = (ids, chosen, gain_after, *vectors)
     return call(
-        functools.partial(bring_kernel, count, seq_count, head_count),
+        functools.partial(bring_kernel, len(arrays), len(vectors), seq_count, head_count),
         "bring",
         [pltpu.VMEM(x.shape, x.dtype) for x in arrays]
         + [
+            pltpu.VMEM((8, 128), F32),
             pltpu.VMEM((seq_count, 16, width), BF16),
             pltpu.VMEM((1, width), F32),
             pltpu.VMEM(gain_after.shape, F32),
         ],
         (me, seq),
         (),
-        (*hbm, after),
-        [
-            pltpu.VMEM(ids.shape, jnp.int32),
-            pltpu.VMEM(chosen.shape, F32),
-            pltpu.VMEM(gain_after.shape, F32),
-            pltpu.SemaphoreType.DMA((count + 3,)),
-        ],
+        [pltpu.with_memory_space_constraint(x, pltpu.HBM) for x in (*small, *arrays)],
+        [pltpu.VMEM(x.shape, x.dtype) for x in small]
+        + [pltpu.SemaphoreType.DMA((len(small) + len(arrays),))],
     )
 
 
@@ -151,7 +149,7 @@
     me_ref,
     *refs,
 ):
-    x_refs = refs[: head_count // 2]
+    x_refs = refs[:2]
     (
         gain_ref,
         small_ref,
@@ -172,7 +170,7 @@
         left,
         recalls,
         sems,
-    ) = refs[head_count // 2 :]
+    ) = refs[2:]
     me = me_ref[0]
     _, rows, width = x_refs[0].shape
     seqs = rows // steps
@@ -193,14 +191,14 @@
 
     squares = jnp.zeros((rows, 1), F32)
     for j in range(head_count):
-        xj = x_refs[j // 2][j % 2].astype(F32)
+        xj = x_refs[j % 2][j // 2].astype(F32)
         squares = squares + jnp.sum(xj * xj, axis=1, keepdims=True)
     inverse = lax.rsqrt(squares / (head_count * width) + EPS)
     normed = []
     spans = []
     for j in range(head_count):
         block = me ^ j
-        normed.append((x_refs[j // 2][j % 2].astype(F32) * inverse * gain_ref[block]).astype(BF16))
+        normed.append((x_refs[j % 2][j // 2].astype(F32) * inverse * gain_ref[block]).astype(BF16))
         spans.append(pl.ds(pl.multiple_of(block * width, width), width))
 
     def project(w_ref):
@@ -328,8 +326,8 @@
 
 
 def front(me, xs, gain, small, pack, wq, wk, wv, wz, wo, states, steps):
-    _, rows, width = xs[0].shape
-    head_count = 2 * len(xs)
+    pairs, rows, width = xs[0].shape
+    head_count = 2 * pairs
     seqs = rows // steps
     key_heads = wq.shape[1] // DK
     value_heads = wv.shape[1] // DV
@@ -484,99 +482,103 @@
     )
 
 
-def expert_in_kernel(orders, odd, first, me_ref, *refs):
-    pieces = refs[: sum(map(len, orders))]
-    refs = refs[len(pieces) :]
-    gain_inv_ref, w_ref = refs[:2]
-    if first:
-        pre_ref, sq_ref = refs[-2:]
-    else:
-        pre_in, sq_in = refs[2:4]
-        pre_ref, sq_ref = refs[-2:]
-    me = me_ref[0]
-    start, at = 0, 0
-    for order in orders:
-        blocks, xs = [], []
-        for part in order:
-            ref = pieces[at]
-            at += 1
-            _, zs, rows, width = ref.shape
-            for n, place in enumerate(part):
-                xs.append(ref[n].reshape(zs * rows, width))
-                blocks.append(me ^ (2 * place + odd))
-        spans = [pl.ds(pl.multiple_of(b * width, width), width) for b in blocks]
-        span = slice(start, start + zs * rows)
-        start += zs * rows
-        for c in range(0, w_ref.shape[2], 256):
-            columns = slice(c, c + 256)
-            total = None if first else pre_in[span, columns]
-            for x, where in zip(xs, spans):
-                term = dot(x, w_ref[0, where, columns])
-                total = term if total is None else total + term
-            pre_ref[span, columns] = total
-        squares = None
-        for x, block in zip(xs, blocks):
-            plain = x.astype(F32) * gain_inv_ref[block]
-            plain = plain * plain
-            for c in range(0, width, 128):
-                part = plain[:, c : c + 128]
-                squares = part if squares is None else squares + part
-        squares = jnp.sum(squares, axis=1, keepdims=True)
-        sq_ref[span, :] = squares if first else squares + sq_in[span, :]
-
-
-def expert_in(me, sides, gain_inv, w, orders, odd, before=(), after=()):
-    pieces = [piece for side in sides for piece in side]
-    rows = pieces[0].shape[2]
-    total = sum(side[0].shape[1] for side in sides) * rows
+def blocks_of(pieces, order, odd, me):
+    xs, places = [], []
+    for ref, part in zip(pieces, order):
+        _, zs, rows, width = ref.shape
+        for n, place in enumerate(part):
+            xs.append(ref[n].reshape(zs * rows, width))
+            places.append(me ^ (2 * place + odd))
+    return xs, places
+
+
+def rows_squares(xs, places, gain_inv_ref):
+    squares = None
+    for x, place in zip(xs, places):
+        plain = x.astype(F32) * gain_inv_ref[place]
+        plain = plain * plain
+        for c in range(0, x.shape[1], 128):
+            part = plain[:, c : c + 128]
+            squares = part if squares is None else squares + part
+    return jnp.sum(squares, axis=1, keepdims=True)
+
+
+def columns_sum(total, xs, places, w_ref, columns):
+    for x, place in zip(xs, places):
+        width = x.shape[1]
+        term = dot(x, w_ref[0, pl.ds(pl.multiple_of(place * width, width), width), columns])
+        total = term if total is None else total + term
+    return total
+
+
+def expert_first_kernel(order, me_ref, *refs):
+    pieces, (gain_inv_ref, w_ref) = refs[: len(order)], refs[len(order) : len(order) + 2]
+    pre_ref, sq_ref = refs[-2:]
+    xs, places = blocks_of(pieces, order, 0, me_ref[0])
+    for c in range(0, w_ref.shape[2], 256):
+        columns = slice(c, c + 256)
+        pre_ref[:, columns] = columns_sum(None, xs, places, w_ref, columns)
+    sq_ref[...] = rows_squares(xs, places, gain_inv_ref)
+
+
+def expert_first(me, pieces, gain_inv, w, order, after=()):
+    total = pieces[0].shape[1] * pieces[0].shape[2]
     return call(
-        functools.partial(expert_in_kernel, orders, odd, not before),
-        "expert_in",
+        functools.partial(expert_first_kernel, order),
+        "expert_first",
         [pltpu.VMEM((total, w.shape[2]), F32), pltpu.VMEM((total, 1), F32)],
         (me,),
-        (*pieces, gain_inv, w, *before),
+        (*pieces, gain_inv, w),
         after,
     )
 
 
-def expert_out_kernel(orders, steps, me_ref, pre_ref, sq_ref, extra_ref, w_ref, *refs):
+def expert_rest_kernel(order, order_out, steps, whole, me_ref, *refs):
+    pieces, refs = refs[: len(order)], refs[len(order) :]
+    gain_inv_ref, w_ref, pre_ref, sq_ref, down_ref = refs[:5]
+    own, sib, sq_out = refs[-3:]
     me = me_ref[0]
-    messages, outs = refs[:-5], refs[-4:]
-    features = w_ref.shape[2]
-    hidden_width = w_ref.shape[1]
-    start = 0
-    for side, order in enumerate(orders):
-        own, sib = outs[2 * side : 2 * side + 2]
-        count, zs, rows, width = own.shape
-        span = slice(start, start + zs * rows)
-        start += zs * rows
-        inverse = lax.rsqrt(sq_ref[span, :] / features + EPS)
-        gate = pre_ref[span, :hidden_width] * inverse
-        up = pre_ref[span, hidden_width:] * inverse
-        hidden = (silu(gate) * up).astype(BF16)
-        weight = []
-        for z in range(side * zs, (side + 1) * zs):
-            extra = messages[z - 1][rows:, :] if z else extra_ref[0]
-            columns = jnp.transpose(extra.astype(F32))
-            for t in range(steps):
-                both = columns[:, t : t + 1] + columns[:, steps + t : steps + t + 1]
-                weight.append(both[: rows // steps])
-        weight = jnp.concatenate(weight, axis=0)
-        for odd, ref in ((1, sib), (0, own)):
-            for n in range(count):
-                block = me ^ (2 * order[n] + odd)
-                columns = pl.ds(pl.multiple_of(block * width, width), width)
-                result = dot(hidden, w_ref[0, :, columns]) * weight
-                ref[n] = result.astype(BF16).reshape(zs, rows, width)
-
-
-def expert_out(me, pre, sq, extra, w, messages, orders, shapes, steps, after):
+    features = down_ref.shape[2]
+    hidden_width = down_ref.shape[1]
+    count, zs, rows, width = own.shape
+    xs, places = blocks_of(pieces, order, 1, me)
+    squares = sq_ref[...] + rows_squares(xs, places, gain_inv_ref)
+    sq_out[...] = squares
+    inverse = lax.rsqrt(squares / features + EPS)
+    hidden = []
+    for c in range(0, hidden_width, 256):
+        parts = []
+        for at in (c, hidden_width + c):
+            columns = slice(at, at + 256)
+            parts.append(columns_sum(pre_ref[:, columns], xs, places, w_ref, columns) * inverse)
+        hidden.append((silu(parts[0]) * parts[1]).astype(BF16))
+    hidden = jnp.concatenate(hidden, axis=1)
+    weight = []
+    for z in range(zs):
+        ref = refs[5 + z]
+        extra = ref[0] if z == 0 and whole else ref[rows:, :]
+        columns = jnp.transpose(extra.astype(F32))
+        for t in range(steps):
+            both = columns[:, t : t + 1] + columns[:, steps + t : steps + t + 1]
+            weight.append(both[: rows // steps])
+    weight = jnp.concatenate(weight, axis=0)
+    for odd, ref in ((1, sib), (0, own)):
+        for n in range(count):
+            block = me ^ (2 * order_out[n] + odd)
+            columns = pl.ds(pl.multiple_of(block * width, width), width)
+            result = dot(hidden, down_ref[0, :, columns]) * weight
+            ref[n] = result.astype(BF16).reshape(zs, rows, width)
+
+
+def expert_rest(me, pieces, gain_inv, w, pre, sq, down, weights, order, order_out, steps, whole, after):
+    count = 2 * pieces[0].shape[0]
+    shape = (count, *pieces[0].shape[1:])
     return call(
-        functools.partial(expert_out_kernel, orders, steps),
-        "expert_out",
-        [pltpu.VMEM(shape, BF16) for shape in shapes],
+        functools.partial(expert_rest_kernel, order, order_out, steps, whole),
+        "expert_rest",
+        [pltpu.VMEM(shape, BF16), pltpu.VMEM(shape, BF16), pltpu.VMEM(sq.shape, F32)],
         (me,),
-        (pre, sq, extra, w, *messages),
+        (*pieces, gain_inv, w, pre, sq, down, *weights),
         after,
     )
 
@@ -727,36 +729,29 @@
     small = jnp.concatenate([w_beta, w_alpha], axis=1)
     small = jnp.transpose(small.reshape(head_count, width, 2 * value_heads), (0, 2, 1))
     small = jnp.pad(small, ((0, 0), (0, -2 * value_heads % 16), (0, 0)))
-    pack = jnp.stack(
-        [
-            jnp.pad(decay_scale, (0, DV - value_heads)),
-            jnp.pad(dt_bias, (0, DV - value_heads)),
-            gated_gain,
-        ]
-    )
-
-    neighbour = exchange(mine, "head", 1)
-    [mine] = load((mine,))
-    both = stack(mine, neighbour)
-    gathered = [both] + [exchange(both, "head", 2 * p) for p in range(1, pairs)]
-    w_query, w_key, w_value, w_zgate, w_shared_in, w_shared_out, gain, extra, gain_mine, gain_inv = bring(
+
+    others = [exchange(mine, "head", 2 * p) for p in range(1, pairs)]
+    mine, w_query, w_key, w_shared_in, w_shared_out, gain, pack, extra, gain_mine, gain_inv = bring(
         me,
         seq_index.astype(jnp.int32).reshape(1),
         (
+            mine,
             w_query,
             w_key,
-            w_value,
-            w_zgate,
             w_shared_in,
             w_shared_out,
             input_gain.reshape(head_count, 1, width),
         ),
+        [v.reshape(1, -1) for v in (decay_scale, dt_bias, gated_gain)],
         jnp.transpose(router_ids, (2, 1, 0)),
         jnp.transpose(router_weights, (2, 1, 0)),
         post_gain.reshape(head_count, 1, width),
         seq_count,
-        both,
-    )
+    )
+    own_tokens = stack(mine, *others)
+    sib_tokens = exchange(own_tokens, "head", 1)
+    w_value, w_zgate = load((w_value, w_zgate), (own_tokens,))
+    gathered = (own_tokens, sib_tokens)
     own, sib, keys, deltas, totals = front(
         me, gathered, gain, small, pack, w_query, w_key, w_value, w_zgate, w_out, states, steps
     )
@@ -772,7 +767,7 @@
     natural, reverse = list(range(pairs)), bit_reversed(pairs)
     blocks = tuple(range(seqs // PER_BLOCK))
     cut = len(blocks) // 2
-    shared_pre, sent = shared_in(me, x, w_shared_in, (messages[0],))
+    shared_pre, sent = shared_in(me, x, w_shared_in, ())
     shared_pre = one_sum(shared_pre, exchange(sent, "head", 1))
     shared_received = exchange(shared_pre, "head", axes[0])
     sides, tie = [], ()
@@ -795,14 +790,31 @@
     middle = pairs // 2
     orders = tuple((tuple(o[:middle]), tuple(o[middle:])) for o in (natural, reverse))
 
-    pre = expert_in(me, sides, gain_inv, w_in, orders, 0, after=(done_1,))
-    pre, squares = expert_in(me, siblings, gain_inv, w_in, orders, 1, pre)
-    shape = (pairs, half, rows, width)
-    a_own, a_sib, b_own, b_sib = expert_out(
-        me, pre, squares, extra, w_down, messages, (reverse, natural), (shape,) * 4, steps, (shared_received,)
-    )
-    owns = [a_own, b_own]
-    received = [exchange(sib, "head", 1) for sib in (a_sib, b_sib)]
+    firsts = [
+        expert_first(me, side, gain_inv, w_in, order, (done_1,)) for side, order in zip(sides, orders)
+    ]
+    owns, sibs, squares = [], [], []
+    weights = (extra, *messages)
+    ties = ((), (shared_received,))
+    for n, order_out in enumerate((reverse, natural)):
+        own, sib, square = expert_rest(
+            me,
+            siblings[n],
+            gain_inv,
+            w_in,
+            *firsts[n],
+            w_down,
+            weights[n * half : (n + 1) * half],
+            orders[n],
+            order_out,
+            steps,
+            n == 0,
+            ties[n],
+        )
+        owns.append(own)
+        sibs.append(sib)
+        squares.append(square)
+    received = [exchange(sib, "head", 1) for sib in sibs]
     tie = ()
     for n, bits in enumerate(zip(axes, axes[::-1])):
         for side, bit in enumerate(bits):
@@ -816,7 +828,7 @@
         else:
             shared_pre = one_sum(shared_pre, shared_received, (owns[1],))
             shared_received = exchange(shared_pre, "head", axes[n])
-    hidden = shared_hidden(features, shared_pre, shared_received, squares)
+    hidden = shared_hidden(features, shared_pre, shared_received, squares[0])
     base = shared_out(me, hidden, exchange(hidden, "head", 1), resid, w_shared_out)
     slabs = []
     for side in range(2):

time: 87.1 us -> 82.2 us (0.944)
  waiting for transfers between devices: 26.9 us -> 20.2 us
  starting transfers between devices: 28.7 us -> 31.9 us
  other arithmetic: 2.07 us -> 0.68 us
    ppermute x32, waiting for transfers between devices: 26.9 us -> 20.2 us  [exchange(): return lax.ppermute(x, axis, [(i, i ^ bit) for i in range(size)])]
    ppermute x32, starting transfers between devices: 28.7 us -> 31.9 us  [exchange(): return lax.ppermute(x, axis, [(i, i ^ bit) for i in range(size)])]
    pallas_call x27 -> x28, Pallas kernels: 27.4 us -> 28.2 us  [call(): pl.pallas_call(body, out_shape=tuple(out_shapes), in_specs=[SMEM_SPEC] *...]
  transfers between devices with their start and end apart: 32 -> 32, of which waited for: 16 -> 12; matrix products, arithmetic and copies ran while one was open for 2% -> 0% of each run, Pallas kernels for 21% -> 25%
where the time goes in v4:
time: 82.2 us; the launch traced here: 82 us
  starting transfers between devices  31.9 us (39%)
  Pallas kernels  28.2 us (34%)
  waiting for transfers between devices  20.2 us (25%)
  between operations  0.97 us (1%)
    ppermute x32, starting transfers between devices, exchange(): return lax.ppermute(x, axis, [(i, i ^ bit) for i in range(size)])  31.9 us
    pallas_call x28, Pallas kernels, call(): pl.pallas_call(body, out_shape=tuple(out_shapes), in_specs=[SMEM_SPEC] *...  28.2 us
    ppermute x32, waiting for transfers between devices, exchange(): return lax.ppermute(x, axis, [(i, i ^ bit) for i in range(size)])  20.2 us
  transfers between devices with their start and end apart: 32, of which 12 were waited for; matrix products, arithmetic and copies ran while one was open for 0% of the time, Pallas kernels for 25%

profile of v4, /device:TPU:0, one launch (start us, length us, event | category | flops | bytes accessed | tf_op | source)
XLA Modules:
  0.0 82.0 jit_solution(2614507369924451341)
XLA Ops:
  0.7 3.0 %collective-permute-start = (bf16[96,256]{1,0:T(8,128)(2,1)}, bf16[96,256]{1,0:T(8,128)(2,1)S(1)}, u32[]{:S(2)}, u32[]{:S(2)}) collective-permute-start(bf16[96,256]{1,0:T(8,128)(2,1)} %bitcast.34), channel_id=1, source_target_pairs={{0,2},{1,3},{2,0},{3,1},{4,6},{5,7},{6,4},{7,5},{8,10},{9,11},{10,... | collective-permute-start | bytes 147464 | tf_op jit(solution)/shard_map/ppermute | solution.py:57
  3.7 1.5 %collective-permute-start.1 = (bf16[96,256]{1,0:T(8,128)(2,1)}, bf16[96,256]{1,0:T(8,128)(2,1)S(1)}, u32[]{:S(2)}, u32[]{:S(2)}) collective-permute-start(bf16[96,256]{1,0:T(8,128)(2,1)} %bitcast.35), channel_id=1, source_target_pairs={{0,4},{1,5},{2,6},{3,7},{4,0},{5,1},{6,2},{7,3},{8,12},{9,13},{10,... | collective-permute-start | bytes 147464 | tf_op jit(solution)/shard_map/ppermute | solution.py:57
  5.2 2.0 %bring.1 = (bf16[96,256]{1,0:T(8,128)(2,1)S(1)}, bf16[2048,256]{1,0:T(8,128)(2,1)S(1)}, bf16[2048,256]{1,0:T(8,128)(2,1)S(1)}, bf16[256,1024]{1,0:T(8,128)(2,1)S...) custom-call(s32[1]{0:T(128)} %bitcast.me_ref, ...), custom_call_target="tpu_custom_call" | custom-call | tf_op jit(solution)/shard_map/bring/pallas_call | solution.py:43
  7.2 0.8 collective-permute-done.1.refs_2_
  8.0 2.4 %collective-permute-done.2.refs_3_ = bf16[96,256]{1,0:T(8,128)(2,1)S(1)} collective-permute-done((bf16[96,256]{1,0:T(8,128)(2,1)}, bf16[96,256]{1,0:T(8,128)(2,1)S(1)}, u32[]{:S(2)}, u32[]{:S(2)}) %collective-permute-start.2) | collective-permute-done | bytes 49184 | tf_op jit(solution)/shard_map/ppermute | solution.py:57
  10.5 2.2 %load.2 = (bf16[2048,512]{1,0:T(8,128)(2,1)S(1)}, bf16[2048,512]{1,0:T(8,128)(2,1)S(1)}) custom-call(bf16[2048,512]{1,0:T(8,128)(2,1)} %refs_0_.2, bf16[2048,512]{1,0:T(8,128)(2,1)} %refs_1_.2, bf16[4,96,256]{2,1,0:T(8,128)(2,1)S(1)} %stack.3.refs_2_.refs_0_), custom_call_target="tpu_custom_call" | custom-call | tf_op jit(solution)/shard_map/load/pallas_call | solution.py:43
  12.8 7.5 %front.1 = (bf16[4,96,256]{2,1,0:T(8,128)(2,1)S(1)}, bf16[4,96,256]{2,1,0:T(8,128)(2,1)S(1)}, f32[2,96,128]{2,1,0:T(8,128)S(1)}, f32[2,3,32,256]{3,2,1,0:T(8,128)S(1)}, f32[2,32,256]{2,1,0:T(8,128)S(1)}) custom-call(s32[1]{0:T(128)} %bitcast.me_ref, bf16[4,96,256]{2,1,0:T(8,128)(2,1)S(1)} %stack.3.refs_2_.refs_0_, ...), custom_call_target="tpu_custom_call" | custom-call | tf_op jit(solution)/shard_map/front/pallas_call | solution.py:43
  20.3 0.5 collective-permute-start.4
  20.9 1.1 %collective-permute-done.4.b_ref = bf16[4,96,256]{2,1,0:T(8,128)(2,1)S(1)} collective-permute-done((bf16[4,96,256]{2,1,0:T(8,128)(2,1)S(1)}, bf16[4,96,256]{2,1,0:T(8,128)(2,1)S(1)}, u32[]{:S(2)}, u32[]{:S(2)}) %collective-permute-start.4) | collective-permute-done | bytes 196640 | tf_op jit(solution)/shard_map/ppermute | solution.py:57
  22.0 0.6 collective-permute-start.5
  22.7 2.9 %collective-permute-start.7 = (bf16[96,256]{1,0:T(8,128)(2,1)S(1)}, bf16[96,256]{1,0:T(8,128)(2,1)S(1)}, u32[]{:S(2)}, u32[]{:S(2)}) collective-permute-start(bf16[96,256]{1,0:T(8,128)(2,1)S(1)} %get-tuple-element.104), channel_id=1, source_target_pairs={{0,6},{1,7},{2,4},{3,5},{4,2},{5,3},{6,0},{7,1},{8,14},{9,15},{10,... | collective-permute-start | bytes 147464 | tf_op jit(solution)/shard_map/ppermute | solution.py:57
  25.6 2.9 %load.3 = (bf16[1,2048,1024]{2,1,0:T(8,128)(2,1)S(1)}, bf16[1,512,2048]{2,1,0:T(8,128)(2,1)S(1)}) custom-call(bf16[1,2048,1024]{2,1,0:T(8,128)(2,1)} %refs_0_.3, bf16[1,512,2048]{2,1,0:T(8,128)(2,1)} %refs_1_.3, bf16[4,96,256]{2,1,0:T(8,128)(2,1)S(1)} %one_sum.3.refs_2_.refs_0_), custom_call_target="tpu_custom_call" | custom-call | tf_op jit(solution)/shard_map/load/pallas_call | solution.py:43
  28.5 0.3 shared_in.1
  28.9 1.6 %collective-permute-start.12 = (bf16[112,256]{1,0:T(8,128)(2,1)S(1)}, bf16[112,256]{1,0:T(8,128)(2,1)S(1)}, u32[]{:S(2)}, u32[]{:S(2)}) collective-permute-start(bf16[112,256]{1,0:T(8,128)(2,1)S(1)} %get-tuple-element.74), channel_id=1, source_target_pairs={{0,8},{8,0},{16,24},{24,16},{1,9},{9,1},{17,25},{25,17},{2,10},{10... | collective-permute-start | bytes 172040 | tf_op jit(solution)/shard_map/ppermute | solution.py:57
  30.5 2.6 %collective-permute-start.10 = (bf16[112,256]{1,0:T(8,128)(2,1)S(1)}, bf16[112,256]{1,0:T(8,128)(2,1)S(1)}, u32[]{:S(2)}, u32[]{:S(2)}) collective-permute-start(bf16[112,256]{1,0:T(8,128)(2,1)S(1)} %get-tuple-element.69), channel_id=1, source_target_pairs={{0,16},{8,24},{16,0},{24,8},{1,17},{9,25},{17,1},{25,9},{2,18},{10... | collective-permute-start | bytes 172040 | tf_op jit(solution)/shard_map/ppermute | solution.py:57
  33.1 0.2 collective-permute-start.11
  33.3 1.2 %collective-permute-start.19 = (bf16[1,2,96,256]{3,2,1,0:T(8,128)(2,1)S(1)}, bf16[1,2,96,256]{3,2,1,0:T(8,128)(2,1)S(1)}, u32[]{:S(2)}, u32[]{:S(2)}) collective-permute-start(bf16[1,2,96,256]{3,2,1,0:T(8,128)(2,1)S(1)} %bitcast.29), channel_id=1, source_target_pairs={{0,2},{1,3},{2,0},{3,1},{4,6},{5,7},{6,4},{7,5},{8,10},{9,11},{10,... | collective-permute-start | bytes 294920 | tf_op jit(solution)/shard_map/ppermute | solution.py:57
  34.5 4.3 %update.2 = (f32[32,4,128,128]{3,2,1,0:T(8,128)}, f32[8,128]{1,0:T(8,128)S(1)}) custom-call(f32[2,96,128]{2,1,0:T(8,128)S(1)} %get-tuple-element.71.keys_ref, f32[2,3,32,256]{3,2,1,0:T(8,128)S(1)} %get-tuple-element.72.delta_ref, f32[2,32,256]{2,1,0:T(8,128)S(1)} %get-tuple-element.73.total_ref, f32[32,4,128,128]{3,2,1,0:T(8,128)} %states_ref.3, ...), custom_call_target="tpu_custom_call" | custom-call | tf_op jit(solution)/shard_map/update/pallas_call | solution.py:43
  38.8 0.3 collective-permute-done.11.b_ref.refs_8_
  39.2 1.3 %collective-permute-start.13 = (bf16[1,2,96,256]{3,2,1,0:T(8,128)(2,1)S(1)}, bf16[1,2,96,256]{3,2,1,0:T(8,128)(2,1)S(1)}, u32[]{:S(2)}, u32[]{:S(2)}) collective-permute-start(bf16[1,2,96,256]{3,2,1,0:T(8,128)(2,1)S(1)} %bitcast.28), channel_id=1, source_target_pairs={{0,4},{1,5},{2,6},{3,7},{4,0},{5,1},{6,2},{7,3},{8,12},{9,13},{10,... | collective-permute-start | bytes 294920 | tf_op jit(solution)/shard_map/ppermute | solution.py:57
  40.5 0.9 %collective-permute-start.21 = (bf16[2,2,96,256]{3,2,1,0:T(8,128)(2,1)S(1)}, bf16[2,2,96,256]{3,2,1,0:T(8,128)(2,1)S(1)}, u32[]{:S(2)}, u32[]{:S(2)}) collective-permute-start(bf16[2,2,96,256]{3,2,1,0:T(8,128)(2,1)S(1)} %stack.5.refs_0_), channel_id=1, source_target_pairs={{0,4},{1,5},{2,6},{3,7},{4,0},{5,1},{6,2},{7,3},{8,12},{9,13},{10,... | collective-permute-start | bytes 589832 | tf_op jit(solution)/shard_map/ppermute | solution.py:57
  41.3 3.5 %collective-permute-done.13 = bf16[1,2,96,256]{3,2,1,0:T(8,128)(2,1)S(1)} collective-permute-done((bf16[1,2,96,256]{3,2,1,0:T(8,128)(2,1)S(1)}, bf16[1,2,96,256]{3,2,1,0:T(8,128)(2,1)S(1)}, u32[]{:S(2)}, u32[]{:S(2)}) %collective-permute-start.13) | collective-permute-done | bytes 98336 | tf_op jit(solution)/shard_map/ppermute | solution.py:57
  44.8 1.2 %collective-permute-start.15 = (bf16[2,2,96,256]{3,2,1,0:T(8,128)(2,1)S(1)}, bf16[2,2,96,256]{3,2,1,0:T(8,128)(2,1)S(1)}, u32[]{:S(2)}, u32[]{:S(2)}) collective-permute-start(bf16[2,2,96,256]{3,2,1,0:T(8,128)(2,1)S(1)} %stack.4.refs_0_), channel_id=1, source_target_pairs={{0,2},{1,3},{2,0},{3,1},{4,6},{5,7},{6,4},{7,5},{8,10},{9,11},{10,... | collective-permute-start | bytes 589832 | tf_op jit(solution)/shard_map/ppermute | solution.py:57
  46.1 1.5 %collective-permute-done.21.refs_1_ = bf16[2,2,96,256]{3,2,1,0:T(8,128)(2,1)S(1)} collective-permute-done((bf16[2,2,96,256]{3,2,1,0:T(8,128)(2,1)S(1)}, bf16[2,2,96,256]{3,2,1,0:T(8,128)(2,1)S(1)}, u32[]{:S(2)}, u32[]{:S(2)}) %collective-permute-start.21) | collective-permute-done | bytes 196640 | tf_op jit(solution)/shard_map/ppermute | solution.py:57
  47.5 0.5 collective-permute-start.14
  48.0 2.5 %collective-permute-done.15.refs_1_ = bf16[2,2,96,256]{3,2,1,0:T(8,128)(2,1)S(1)} collective-permute-done((bf16[2,2,96,256]{3,2,1,0:T(8,128)(2,1)S(1)}, bf16[2,2,96,256]{3,2,1,0:T(8,128)(2,1)S(1)}, u32[]{:S(2)}, u32[]{:S(2)}) %collective-permute-start.15) | collective-permute-done | bytes 196640 | tf_op jit(solution)/shard_map/ppermute | solution.py:57
  50.6 1.2 %collective-permute-start.9 = (bf16[96,512]{1,0:T(8,128)(2,1)S(1)}, bf16[96,512]{1,0:T(8,128)(2,1)S(1)}, u32[]{:S(2)}, u32[]{:S(2)}) collective-permute-start(bf16[96,512]{1,0:T(8,128)(2,1)S(1)} %one_sum.4.refs_1_.a_ref), channel_id=1, source_target_pairs={{0,2},{1,3},{2,0},{3,1},{4,6},{5,7},{6,4},{7,5},{8,10},{9,11},{10,... | collective-permute-start | bytes 294920 | tf_op jit(solution)/shard_map/ppermute | solution.py:57
  51.7 0.6 expert_first.3
  52.4 0.6 expert_first.2
  53.0 1.2 %expert_rest.3 = (bf16[4,2,96,256]{3,2,1,0:T(8,128)(2,1)S(1)}, bf16[4,2,96,256]{3,2,1,0:T(8,128)(2,1)S(1)}, f32[192,1]{1,0:T(8,128)S(1)}) custom-call(s32[1]{0:T(128)} %bitcast.me_ref, bf16[2,2,96,256]{3,2,1,0:T(8,128)(2,1)S(1)} %collective-permute-done.20.refs_0_, bf16[2,2,96,256]{3,2,1,0:T(8,128)(2,1)S(1)} %collective-permute-done.22.refs_1_, ...), custom_call_target="tpu_custom_call" | custom-call | tf_op jit(solution)/shard_map/expert_rest/pallas_call | solution.py:43
  54.2 0.3 collective-permute-start.23
  54.5 1.3 %collective-permute-done.9.refs_9_.b_ref = bf16[96,512]{1,0:T(8,128)(2,1)S(1)} collective-permute-done((bf16[96,512]{1,0:T(8,128)(2,1)S(1)}, bf16[96,512]{1,0:T(8,128)(2,1)S(1)}, u32[]{:S(2)}, u32[]{:S(2)}) %collective-permute-start.9) | collective-permute-done | bytes 98336 | tf_op jit(solution)/shard_map/ppermute | solution.py:57
  55.8 1.5 %expert_rest.2 = (bf16[4,2,96,256]{3,2,1,0:T(8,128)(2,1)S(1)}, bf16[4,2,96,256]{3,2,1,0:T(8,128)(2,1)S(1)}, f32[192,1]{1,0:T(8,128)}) custom-call(s32[1]{0:T(128)} %bitcast.me_ref, bf16[2,2,96,256]{3,2,1,0:T(8,128)(2,1)S(1)} %collective-permute-done.14.refs_0_, bf16[2,2,96,256]{3,2,1,0:T(8,128)(2,1)S(1)} %collective-permute-done.16.refs_1_, ...), custom_call_target="tpu_custom_call" | custom-call | tf_op jit(solution)/shard_map/expert_rest/pallas_call | solution.py:43
  57.4 1.2 %collective-permute-start.26 = (bf16[2,2,96,256]{3,2,1,0:T(8,128)(2,1)S(1)}, bf16[2,2,96,256]{3,2,1,0:T(8,128)(2,1)S(1)}, u32[]{:S(2)}, u32[]{:S(2)}) collective-permute-start(bf16[2,2,96,256]{3,2,1,0:T(8,128)(2,1)S(1)} %get-tuple-element.95), channel_id=1, source_target_pairs={{0,2},{1,3},{2,0},{3,1},{4,6},{5,7},{6,4},{7,5},{8,10},{9,11},{10,... | collective-permute-start | bytes 589832 | tf_op jit(solution)/shard_map/ppermute | solution.py:57
  58.6 0.4 collective-permute-done.17.b_ref
  59.1 1.4 %collective-permute-start.18 = (bf16[2,2,96,256]{3,2,1,0:T(8,128)(2,1)S(1)}, bf16[2,2,96,256]{3,2,1,0:T(8,128)(2,1)S(1)}, u32[]{:S(2)}, u32[]{:S(2)}) collective-permute-start(bf16[2,2,96,256]{3,2,1,0:T(8,128)(2,1)S(1)} %get-tuple-element.83), channel_id=1, source_target_pairs={{0,4},{1,5},{2,6},{3,7},{4,0},{5,1},{6,2},{7,3},{8,12},{9,13},{10,... | collective-permute-start | bytes 589832 | tf_op jit(solution)/shard_map/ppermute | solution.py:57
  60.6 4.3 %update.3 = (f32[32,4,128,128]{3,2,1,0:T(8,128)}, f32[8,128]{1,0:T(8,128)S(1)}) custom-call(f32[2,96,128]{2,1,0:T(8,128)S(1)} %get-tuple-element.71.keys_ref, f32[2,3,32,256]{3,2,1,0:T(8,128)S(1)} %get-tuple-element.72.delta_ref, f32[2,32,256]{2,1,0:T(8,128)S(1)} %get-tuple-element.73.total_ref, ...), custom_call_target="tpu_custom_call", output_to_operand_aliasing={{0}: (4, {})} | custom-call | tf_op jit(solution)/shard_map/update/pallas_call | solution.py:43
  64.9 1.4 %collective-permute-start.27 = (bf16[1,2,96,256]{3,2,1,0:T(8,128)(2,1)S(1)}, bf16[1,2,96,256]{3,2,1,0:T(8,128)(2,1)S(1)}, u32[]{:S(2)}, u32[]{:S(2)}) collective-permute-start(bf16[1,2,96,256]{3,2,1,0:T(8,128)(2,1)S(1)} %get-tuple-element.97), channel_id=1, source_target_pairs={{0,4},{1,5},{2,6},{3,7},{4,0},{5,1},{6,2},{7,3},{8,12},{9,13},{10,... | collective-permute-start | bytes 294920 | tf_op jit(solution)/shard_map/ppermute | solution.py:57
  66.4 1.3 %collective-permute-start.24 = (bf16[96,512]{1,0:T(8,128)(2,1)S(1)}, bf16[96,512]{1,0:T(8,128)(2,1)S(1)}, u32[]{:S(2)}, u32[]{:S(2)}) collective-permute-start(bf16[96,512]{1,0:T(8,128)(2,1)S(1)} %one_sum.5.a_ref), channel_id=1, source_target_pairs={{0,4},{1,5},{2,6},{3,7},{4,0},{5,1},{6,2},{7,3},{8,12},{9,13},{10,... | collective-permute-start | bytes 294920 | tf_op jit(solution)/shard_map/ppermute | solution.py:57
  67.7 1.3 %collective-permute-start.29 = (bf16[1,2,96,256]{3,2,1,0:T(8,128)(2,1)S(1)}, bf16[1,2,96,256]{3,2,1,0:T(8,128)(2,1)S(1)}, u32[]{:S(2)}, u32[]{:S(2)}) collective-permute-start(bf16[1,2,96,256]{3,2,1,0:T(8,128)(2,1)S(1)} %get-tuple-element.100), channel_id=1, source_target_pairs={{0,2},{1,3},{2,0},{3,1},{4,6},{5,7},{6,4},{7,5},{8,10},{9,11},{10,... | collective-permute-start | bytes 294920 | tf_op jit(solution)/shard_map/ppermute | solution.py:57
  69.0 1.6 %collective-permute-done.27.b_ref = bf16[1,2,96,256]{3,2,1,0:T(8,128)(2,1)S(1)} collective-permute-done((bf16[1,2,96,256]{3,2,1,0:T(8,128)(2,1)S(1)}, bf16[1,2,96,256]{3,2,1,0:T(8,128)(2,1)S(1)}, u32[]{:S(2)}, u32[]{:S(2)}) %collective-permute-start.27) | collective-permute-done | bytes 98336 | tf_op jit(solution)/shard_map/ppermute | solution.py:57
  70.6 1.5 %collective-permute-start.28 = (bf16[96,256]{1,0:T(8,128)(2,1)S(1)}, bf16[96,256]{1,0:T(8,128)(2,1)S(1)}, u32[]{:S(2)}, u32[]{:S(2)}) collective-permute-start(bf16[96,256]{1,0:T(8,128)(2,1)S(1)} %get-tuple-element.99), channel_id=1, source_target_pairs={{0,8},{8,0},{16,24},{24,16},{1,9},{9,1},{17,25},{25,17},{2,10},{10... | collective-permute-start | bytes 147464 | tf_op jit(solution)/shard_map/ppermute | solution.py:57
  72.1 0.1 shared_hidden.1.a_ref
  72.4 4.0 %collective-permute-start.31 = (bf16[96,256]{1,0:T(8,128)(2,1)S(1)}, bf16[96,256]{1,0:T(8,128)(2,1)S(1)}, u32[]{:S(2)}, u32[]{:S(2)}) collective-permute-start(bf16[96,256]{1,0:T(8,128)(2,1)S(1)} %get-tuple-element.102), channel_id=1, source_target_pairs={{0,24},{8,16},{16,8},{24,0},{1,25},{9,17},{17,9},{25,1},{2,26},{10... | collective-permute-start | bytes 147464 | tf_op jit(solution)/shard_map/ppermute | solution.py:57
  76.4 0.2 shared_out.1
  76.6 1.9 %collective-permute-done.31 = bf16[96,256]{1,0:T(8,128)(2,1)S(1)} collective-permute-done((bf16[96,256]{1,0:T(8,128)(2,1)S(1)}, bf16[96,256]{1,0:T(8,128)(2,1)S(1)}, u32[]{:S(2)}, u32[]{:S(2)}) %collective-permute-start.31) | collective-permute-done | bytes 49184 | tf_op jit(solution)/shard_map/ppermute | solution.py:57
  78.5 2.9 %collective-permute-done.30 = bf16[96,256]{1,0:T(8,128)(2,1)S(1)} collective-permute-done((bf16[96,256]{1,0:T(8,128)(2,1)S(1)}, bf16[96,256]{1,0:T(8,128)(2,1)S(1)}, u32[]{:S(2)}, u32[]{:S(2)}) %collective-permute-start.30) | collective-permute-done | bytes 49184 | tf_op jit(solution)/shard_map/ppermute | solution.py:57
  81.4 0.7 add_convert_fusion
  (52 shorter events, 1.0 us)
Async XLA Ops:
  0.6 9.8 %copy-start = (bf16[2048,4]{0,1:T(4,128)(2,1)S(1)}, bf16[2048,4]{0,1:T(4,128)(2,1)}, u32[]{:S(2)}) copy-start(bf16[2048,4]{0,1:T(4,128)(2,1)} %param.30) | copy-start | bytes 49156
  0.6 9.8 %copy-start.1 = (bf16[2048,4]{0,1:T(4,128)(2,1)S(1)}, bf16[2048,4]{0,1:T(4,128)(2,1)}, u32[]{:S(2)}) copy-start(bf16[2048,4]{0,1:T(4,128)(2,1)} %param.29) | copy-start | bytes 49156
  0.7 6.5 %collective-permute-start = (bf16[96,256]{1,0:T(8,128)(2,1)}, bf16[96,256]{1,0:T(8,128)(2,1)S(1)}, u32[]{:S(2)}, u32[]{:S(2)}) collective-permute-start(bf16[96,256]{1,0:T(8,128)(2,1)} %bitcast.34), channel_id=1, source_target_pairs={{0,2},{1,3},{2,0},{3,1},{4,6},{5,7},{6,4},{7,5},{8,10},{9,11},{10,... | collective-permute-start | bytes 147464 | tf_op jit(solution)/shard_map/ppermute | solution.py:57
  3.7 4.3 %collective-permute-start.1 = (bf16[96,256]{1,0:T(8,128)(2,1)}, bf16[96,256]{1,0:T(8,128)(2,1)S(1)}, u32[]{:S(2)}, u32[]{:S(2)}) collective-permute-start(bf16[96,256]{1,0:T(8,128)(2,1)} %bitcast.35), channel_id=1, source_target_pairs={{0,4},{1,5},{2,6},{3,7},{4,0},{5,1},{6,2},{7,3},{8,12},{9,13},{10,... | collective-permute-start | bytes 147464 | tf_op jit(solution)/shard_map/ppermute | solution.py:57
  5.2 5.2 %collective-permute-start.2 = (bf16[96,256]{1,0:T(8,128)(2,1)}, bf16[96,256]{1,0:T(8,128)(2,1)S(1)}, u32[]{:S(2)}, u32[]{:S(2)}) collective-permute-start(bf16[96,256]{1,0:T(8,128)(2,1)} %bitcast.36), channel_id=1, source_target_pairs={{0,6},{1,7},{2,4},{3,5},{4,2},{5,3},{6,0},{7,1},{8,14},{9,15},{10,... | collective-permute-start | bytes 147464 | tf_op jit(solution)/shard_map/ppermute | solution.py:57
  10.4 2.4 %collective-permute-start.3 = (bf16[4,96,256]{2,1,0:T(8,128)(2,1)S(1)}, bf16[4,96,256]{2,1,0:T(8,128)(2,1)S(1)}, u32[]{:S(2)}, u32[]{:S(2)}) collective-permute-start(bf16[4,96,256]{2,1,0:T(8,128)(2,1)S(1)} %stack.3.refs_2_.refs_0_), channel_id=1, source_target_pairs={{0,1},{1,0},{2,3},{3,2},{4,5},{5,4},{6,7},{7,6},{8,9},{9,8},{10,11... | collective-permute-start | bytes 589832 | tf_op jit(solution)/shard_map/ppermute | solution.py:57
  20.3 1.6 %collective-permute-start.4 = (bf16[4,96,256]{2,1,0:T(8,128)(2,1)S(1)}, bf16[4,96,256]{2,1,0:T(8,128)(2,1)S(1)}, u32[]{:S(2)}, u32[]{:S(2)}) collective-permute-start(bf16[4,96,256]{2,1,0:T(8,128)(2,1)S(1)} %get-tuple-element.61), channel_id=1, source_target_pairs={{0,1},{1,0},{2,3},{3,2},{4,5},{5,4},{6,7},{7,6},{8,9},{9,8},{10,11... | collective-permute-start | bytes 589832 | tf_op jit(solution)/shard_map/ppermute | solution.py:57
  22.0 6.5 %collective-permute-start.5 = (bf16[96,256]{1,0:T(8,128)(2,1)S(1)}, bf16[96,256]{1,0:T(8,128)(2,1)S(1)}, u32[]{:S(2)}, u32[]{:S(2)}) collective-permute-start(bf16[96,256]{1,0:T(8,128)(2,1)S(1)} %get-tuple-element.106), channel_id=1, source_target_pairs={{0,2},{1,3},{2,0},{3,1},{4,6},{5,7},{6,4},{7,5},{8,10},{9,11},{10,... | collective-permute-start | bytes 147464 | tf_op jit(solution)/shard_map/ppermute | solution.py:57
  22.6 5.9 %collective-permute-start.6 = (bf16[96,256]{1,0:T(8,128)(2,1)S(1)}, bf16[96,256]{1,0:T(8,128)(2,1)S(1)}, u32[]{:S(2)}, u32[]{:S(2)}) collective-permute-start(bf16[96,256]{1,0:T(8,128)(2,1)S(1)} %get-tuple-element.105), channel_id=1, source_target_pairs={{0,4},{1,5},{2,6},{3,7},{4,0},{5,1},{6,2},{7,3},{8,12},{9,13},{10,... | collective-permute-start | bytes 147464 | tf_op jit(solution)/shard_map/ppermute | solution.py:57
  22.7 5.8 %collective-permute-start.7 = (bf16[96,256]{1,0:T(8,128)(2,1)S(1)}, bf16[96,256]{1,0:T(8,128)(2,1)S(1)}, u32[]{:S(2)}, u32[]{:S(2)}) collective-permute-start(bf16[96,256]{1,0:T(8,128)(2,1)S(1)} %get-tuple-element.104), channel_id=1, source_target_pairs={{0,6},{1,7},{2,4},{3,5},{4,2},{5,3},{6,0},{7,1},{8,14},{9,15},{10,... | collective-permute-start | bytes 147464 | tf_op jit(solution)/shard_map/ppermute | solution.py:57
  28.8 10.0 %collective-permute-start.8 = (bf16[96,512]{1,0:T(8,128)(2,1)S(1)}, bf16[96,512]{1,0:T(8,128)(2,1)S(1)}, u32[]{:S(2)}, u32[]{:S(2)}) collective-permute-start(bf16[96,512]{1,0:T(8,128)(2,1)S(1)} %get-tuple-element.68), channel_id=1, source_target_pairs={{0,1},{1,0},{2,3},{3,2},{4,5},{5,4},{6,7},{7,6},{8,9},{9,8},{10,11... | collective-permute-start | bytes 294920 | tf_op jit(solution)/shard_map/ppermute | solution.py:57
  28.9 4.5 %collective-permute-start.12 = (bf16[112,256]{1,0:T(8,128)(2,1)S(1)}, bf16[112,256]{1,0:T(8,128)(2,1)S(1)}, u32[]{:S(2)}, u32[]{:S(2)}) collective-permute-start(bf16[112,256]{1,0:T(8,128)(2,1)S(1)} %get-tuple-element.74), channel_id=1, source_target_pairs={{0,8},{8,0},{16,24},{24,16},{1,9},{9,1},{17,25},{25,17},{2,10},{10... | collective-permute-start | bytes 172040 | tf_op jit(solution)/shard_map/ppermute | solution.py:57
  30.5 8.3 %collective-permute-start.10 = (bf16[112,256]{1,0:T(8,128)(2,1)S(1)}, bf16[112,256]{1,0:T(8,128)(2,1)S(1)}, u32[]{:S(2)}, u32[]{:S(2)}) collective-permute-start(bf16[112,256]{1,0:T(8,128)(2,1)S(1)} %get-tuple-element.69), channel_id=1, source_target_pairs={{0,16},{8,24},{16,0},{24,8},{1,17},{9,25},{17,1},{25,9},{2,18},{10... | collective-permute-start | bytes 172040 | tf_op jit(solution)/shard_map/ppermute | solution.py:57
  33.1 6.0 %collective-permute-start.11 = (bf16[112,256]{1,0:T(8,128)(2,1)S(1)}, bf16[112,256]{1,0:T(8,128)(2,1)S(1)}, u32[]{:S(2)}, u32[]{:S(2)}) collective-permute-start(bf16[112,256]{1,0:T(8,128)(2,1)S(1)} %get-tuple-element.70), channel_id=1, source_target_pairs={{0,24},{8,16},{16,8},{24,0},{1,25},{9,17},{17,9},{25,1},{2,26},{10... | collective-permute-start | bytes 172040 | tf_op jit(solution)/shard_map/ppermute | solution.py:57
  33.3 7.1 %collective-permute-start.19 = (bf16[1,2,96,256]{3,2,1,0:T(8,128)(2,1)S(1)}, bf16[1,2,96,256]{3,2,1,0:T(8,128)(2,1)S(1)}, u32[]{:S(2)}, u32[]{:S(2)}) collective-permute-start(bf16[1,2,96,256]{3,2,1,0:T(8,128)(2,1)S(1)} %bitcast.29), channel_id=1, source_target_pairs={{0,2},{1,3},{2,0},{3,1},{4,6},{5,7},{6,4},{7,5},{8,10},{9,11},{10,... | collective-permute-start | bytes 294920 | tf_op jit(solution)/shard_map/ppermute | solution.py:57
  39.2 5.7 %collective-permute-start.13 = (bf16[1,2,96,256]{3,2,1,0:T(8,128)(2,1)S(1)}, bf16[1,2,96,256]{3,2,1,0:T(8,128)(2,1)S(1)}, u32[]{:S(2)}, u32[]{:S(2)}) collective-permute-start(bf16[1,2,96,256]{3,2,1,0:T(8,128)(2,1)S(1)} %bitcast.28), channel_id=1, source_target_pairs={{0,4},{1,5},{2,6},{3,7},{4,0},{5,1},{6,2},{7,3},{8,12},{9,13},{10,... | collective-permute-start | bytes 294920 | tf_op jit(solution)/shard_map/ppermute | solution.py:57
  40.5 7.0 %collective-permute-start.21 = (bf16[2,2,96,256]{3,2,1,0:T(8,128)(2,1)S(1)}, bf16[2,2,96,256]{3,2,1,0:T(8,128)(2,1)S(1)}, u32[]{:S(2)}, u32[]{:S(2)}) collective-permute-start(bf16[2,2,96,256]{3,2,1,0:T(8,128)(2,1)S(1)} %stack.5.refs_0_), channel_id=1, source_target_pairs={{0,4},{1,5},{2,6},{3,7},{4,0},{5,1},{6,2},{7,3},{8,12},{9,13},{10,... | collective-permute-start | bytes 589832 | tf_op jit(solution)/shard_map/ppermute | solution.py:57
  44.8 5.7 %collective-permute-start.15 = (bf16[2,2,96,256]{3,2,1,0:T(8,128)(2,1)S(1)}, bf16[2,2,96,256]{3,2,1,0:T(8,128)(2,1)S(1)}, u32[]{:S(2)}, u32[]{:S(2)}) collective-permute-start(bf16[2,2,96,256]{3,2,1,0:T(8,128)(2,1)S(1)} %stack.4.refs_0_), channel_id=1, source_target_pairs={{0,2},{1,3},{2,0},{3,1},{4,6},{5,7},{6,4},{7,5},{8,10},{9,11},{10,... | collective-permute-start | bytes 589832 | tf_op jit(solution)/shard_map/ppermute | solution.py:57
  46.1 6.9 %collective-permute-start.20 = (bf16[2,2,96,256]{3,2,1,0:T(8,128)(2,1)S(1)}, bf16[2,2,96,256]{3,2,1,0:T(8,128)(2,1)S(1)}, u32[]{:S(2)}, u32[]{:S(2)}) collective-permute-start(bf16[2,2,96,256]{3,2,1,0:T(8,128)(2,1)S(1)} %stack.5.refs_0_), channel_id=1, source_target_pairs={{0,1},{1,0},{2,3},{3,2},{4,5},{5,4},{6,7},{7,6},{8,9},{9,8},{10,11... | collective-permute-start | bytes 589832 | tf_op jit(solution)/shard_map/ppermute | solution.py:57
  47.5 5.5 %collective-permute-start.22 = (bf16[2,2,96,256]{3,2,1,0:T(8,128)(2,1)S(1)}, bf16[2,2,96,256]{3,2,1,0:T(8,128)(2,1)S(1)}, u32[]{:S(2)}, u32[]{:S(2)}) collective-permute-start(bf16[2,2,96,256]{3,2,1,0:T(8,128)(2,1)S(1)} %collective-permute-done.21.refs_1_), channel_id=1, source_target_pairs={{0,1},{1,0},{2,3},{3,2},{4,5},{5,4},{6,7},{7,6},{8,9},{9,8},{10,11... | collective-permute-start | bytes 589832 | tf_op jit(solution)/shard_map/ppermute | solution.py:57
  47.5 8.3 %collective-permute-start.14 = (bf16[2,2,96,256]{3,2,1,0:T(8,128)(2,1)S(1)}, bf16[2,2,96,256]{3,2,1,0:T(8,128)(2,1)S(1)}, u32[]{:S(2)}, u32[]{:S(2)}) collective-permute-start(bf16[2,2,96,256]{3,2,1,0:T(8,128)(2,1)S(1)} %stack.4.refs_0_), channel_id=1, source_target_pairs={{0,1},{1,0},{2,3},{3,2},{4,5},{5,4},{6,7},{7,6},{8,9},{9,8},{10,11... | collective-permute-start | bytes 589832 | tf_op jit(solution)/shard_map/ppermute | solution.py:57
  50.6 5.2 %collective-permute-start.16 = (bf16[2,2,96,256]{3,2,1,0:T(8,128)(2,1)S(1)}, bf16[2,2,96,256]{3,2,1,0:T(8,128)(2,1)S(1)}, u32[]{:S(2)}, u32[]{:S(2)}) collective-permute-start(bf16[2,2,96,256]{3,2,1,0:T(8,128)(2,1)S(1)} %collective-permute-done.15.refs_1_), channel_id=1, source_target_pairs={{0,1},{1,0},{2,3},{3,2},{4,5},{5,4},{6,7},{7,6},{8,9},{9,8},{10,11... | collective-permute-start | bytes 589832 | tf_op jit(solution)/shard_map/ppermute | solution.py:57
  50.6 5.2 %collective-permute-start.9 = (bf16[96,512]{1,0:T(8,128)(2,1)S(1)}, bf16[96,512]{1,0:T(8,128)(2,1)S(1)}, u32[]{:S(2)}, u32[]{:S(2)}) collective-permute-start(bf16[96,512]{1,0:T(8,128)(2,1)S(1)} %one_sum.4.refs_1_.a_ref), channel_id=1, source_target_pairs={{0,2},{1,3},{2,0},{3,1},{4,6},{5,7},{6,4},{7,5},{8,10},{9,11},{10,... | collective-permute-start | bytes 294920 | tf_op jit(solution)/shard_map/ppermute | solution.py:57
  54.2 3.1 %collective-permute-start.23 = (bf16[4,2,96,256]{3,2,1,0:T(8,128)(2,1)S(1)}, bf16[4,2,96,256]{3,2,1,0:T(8,128)(2,1)S(1)}, u32[]{:S(2)}, u32[]{:S(2)}) collective-permute-start(bf16[4,2,96,256]{3,2,1,0:T(8,128)(2,1)S(1)} %get-tuple-element.88), channel_id=1, source_target_pairs={{0,1},{1,0},{2,3},{3,2},{4,5},{5,4},{6,7},{7,6},{8,9},{9,8},{10,11... | collective-permute-start | bytes 1179656 | tf_op jit(solution)/shard_map/ppermute | solution.py:57
  57.3 1.7 %collective-permute-start.17 = (bf16[4,2,96,256]{3,2,1,0:T(8,128)(2,1)S(1)}, bf16[4,2,96,256]{3,2,1,0:T(8,128)(2,1)S(1)}, u32[]{:S(2)}, u32[]{:S(2)}) collective-permute-start(bf16[4,2,96,256]{3,2,1,0:T(8,128)(2,1)S(1)} %get-tuple-element.81), channel_id=1, source_target_pairs={{0,1},{1,0},{2,3},{3,2},{4,5},{5,4},{6,7},{7,6},{8,9},{9,8},{10,11... | collective-permute-start | bytes 1179656 | tf_op jit(solution)/shard_map/ppermute | solution.py:57
  57.4 7.4 %collective-permute-start.26 = (bf16[2,2,96,256]{3,2,1,0:T(8,128)(2,1)S(1)}, bf16[2,2,96,256]{3,2,1,0:T(8,128)(2,1)S(1)}, u32[]{:S(2)}, u32[]{:S(2)}) collective-permute-start(bf16[2,2,96,256]{3,2,1,0:T(8,128)(2,1)S(1)} %get-tuple-element.95), channel_id=1, source_target_pairs={{0,2},{1,3},{2,0},{3,1},{4,6},{5,7},{6,4},{7,5},{8,10},{9,11},{10,... | collective-permute-start | bytes 589832 | tf_op jit(solution)/shard_map/ppermute | solution.py:57
  59.1 7.1 %collective-permute-start.18 = (bf16[2,2,96,256]{3,2,1,0:T(8,128)(2,1)S(1)}, bf16[2,2,96,256]{3,2,1,0:T(8,128)(2,1)S(1)}, u32[]{:S(2)}, u32[]{:S(2)}) collective-permute-start(bf16[2,2,96,256]{3,2,1,0:T(8,128)(2,1)S(1)} %get-tuple-element.83), channel_id=1, source_target_pairs={{0,4},{1,5},{2,6},{3,7},{4,0},{5,1},{6,2},{7,3},{8,12},{9,13},{10,... | collective-permute-start | bytes 589832 | tf_op jit(solution)/shard_map/ppermute | solution.py:57
  64.9 5.7 %collective-permute-start.27 = (bf16[1,2,96,256]{3,2,1,0:T(8,128)(2,1)S(1)}, bf16[1,2,96,256]{3,2,1,0:T(8,128)(2,1)S(1)}, u32[]{:S(2)}, u32[]{:S(2)}) collective-permute-start(bf16[1,2,96,256]{3,2,1,0:T(8,128)(2,1)S(1)} %get-tuple-element.97), channel_id=1, source_target_pairs={{0,4},{1,5},{2,6},{3,7},{4,0},{5,1},{6,2},{7,3},{8,12},{9,13},{10,... | collective-permute-start | bytes 294920 | tf_op jit(solution)/shard_map/ppermute | solution.py:57
  66.4 5.8 %collective-permute-start.24 = (bf16[96,512]{1,0:T(8,128)(2,1)S(1)}, bf16[96,512]{1,0:T(8,128)(2,1)S(1)}, u32[]{:S(2)}, u32[]{:S(2)}) collective-permute-start(bf16[96,512]{1,0:T(8,128)(2,1)S(1)} %one_sum.5.a_ref), channel_id=1, source_target_pairs={{0,4},{1,5},{2,6},{3,7},{4,0},{5,1},{6,2},{7,3},{8,12},{9,13},{10,... | collective-permute-start | bytes 294920 | tf_op jit(solution)/shard_map/ppermute | solution.py:57
  67.7 4.7 %collective-permute-start.29 = (bf16[1,2,96,256]{3,2,1,0:T(8,128)(2,1)S(1)}, bf16[1,2,96,256]{3,2,1,0:T(8,128)(2,1)S(1)}, u32[]{:S(2)}, u32[]{:S(2)}) collective-permute-start(bf16[1,2,96,256]{3,2,1,0:T(8,128)(2,1)S(1)} %get-tuple-element.100), channel_id=1, source_target_pairs={{0,2},{1,3},{2,0},{3,1},{4,6},{5,7},{6,4},{7,5},{8,10},{9,11},{10,... | collective-permute-start | bytes 294920 | tf_op jit(solution)/shard_map/ppermute | solution.py:57
  70.6 6.0 %collective-permute-start.28 = (bf16[96,256]{1,0:T(8,128)(2,1)S(1)}, bf16[96,256]{1,0:T(8,128)(2,1)S(1)}, u32[]{:S(2)}, u32[]{:S(2)}) collective-permute-start(bf16[96,256]{1,0:T(8,128)(2,1)S(1)} %get-tuple-element.99), channel_id=1, source_target_pairs={{0,8},{8,0},{16,24},{24,16},{1,9},{9,1},{17,25},{25,17},{2,10},{10... | collective-permute-start | bytes 147464 | tf_op jit(solution)/shard_map/ppermute | solution.py:57
  72.3 4.1 %collective-permute-start.25 = (bf16[96,256]{1,0:T(8,128)(2,1)S(1)}, bf16[96,256]{1,0:T(8,128)(2,1)S(1)}, u32[]{:S(2)}, u32[]{:S(2)}) collective-permute-start(bf16[96,256]{1,0:T(8,128)(2,1)S(1)} %shared_hidden.1.a_ref), channel_id=1, source_target_pairs={{0,1},{1,0},{2,3},{3,2},{4,5},{5,4},{6,7},{7,6},{8,9},{9,8},{10,11... | collective-permute-start | bytes 147464 | tf_op jit(solution)/shard_map/ppermute | solution.py:57
  72.4 6.1 %collective-permute-start.31 = (bf16[96,256]{1,0:T(8,128)(2,1)S(1)}, bf16[96,256]{1,0:T(8,128)(2,1)S(1)}, u32[]{:S(2)}, u32[]{:S(2)}) collective-permute-start(bf16[96,256]{1,0:T(8,128)(2,1)S(1)} %get-tuple-element.102), channel_id=1, source_target_pairs={{0,24},{8,16},{16,8},{24,0},{1,25},{9,17},{17,9},{25,1},{2,26},{10... | collective-permute-start | bytes 147464 | tf_op jit(solution)/shard_map/ppermute | solution.py:57
  76.4 5.0 %collective-permute-start.30 = (bf16[96,256]{1,0:T(8,128)(2,1)S(1)}, bf16[96,256]{1,0:T(8,128)(2,1)S(1)}, u32[]{:S(2)}, u32[]{:S(2)}) collective-permute-start(bf16[96,256]{1,0:T(8,128)(2,1)S(1)} %get-tuple-element.101), channel_id=1, source_target_pairs={{0,16},{8,24},{16,0},{24,8},{1,17},{9,25},{17,1},{25,9},{2,18},{10... | collective-permute-start | bytes 147464 | tf_op jit(solution)/shard_map/ppermute | solution.py:57

commit v5 on v4

--- a/solution.py
+++ b/solution.py
@@ -57,14 +57,15 @@
     return lax.ppermute(x, axis, [(i, i ^ bit) for i in range(size)])
 
 
-def stack_kernel(*refs):
-    for n, ref in enumerate(refs[:-1]):
+def stack_kernel(count, *refs):
+    for n, ref in enumerate(refs[:count]):
         refs[-1][n] = ref[...]
 
 
-def stack(*arrays):
+def stack(arrays, after=()):
     shape = (len(arrays), *arrays[0].shape)
-    [out] = call(stack_kernel, "stack", [pltpu.VMEM(shape, arrays[0].dtype)], (), arrays)
+    body = functools.partial(stack_kernel, len(arrays))
+    [out] = call(body, "stack", [pltpu.VMEM(shape, arrays[0].dtype)], (), arrays, after)
     return out
 
 
@@ -405,15 +406,22 @@
 
 
 def update_kernel(steps, blocks, keys_ref, delta_ref, total_ref, states_ref, *refs):
-    out_ref, done_ref, left, right, olds, buffers, old_sems, sems = refs[-8:]
-    loads = []
+    out_ref, done_ref, left, right, olds, news, old_sems, sems = refs[-8:]
+    half = PER_BLOCK // 2
+    loads, stores = [], []
     for n, block in enumerate(blocks):
-        span = pl.ds(block * PER_BLOCK, PER_BLOCK)
-        loads.append(pltpu.make_async_copy(states_ref.at[span], olds.at[n], old_sems.at[n]))
-        loads[-1].start()
+        for part in range(2):
+            whole = pl.ds(block * PER_BLOCK + part * half, half)
+            here = pl.ds(part * half, half)
+            at = 2 * n + part
+            loads.append(
+                pltpu.make_async_copy(states_ref.at[whole], olds.at[n, here], old_sems.at[at])
+            )
+            stores.append(pltpu.make_async_copy(news.at[n, here], out_ref.at[whole], sems.at[at]))
+            loads[-1].start()
     key_heads, rows, _ = keys_ref.shape
     seqs = rows // steps
-    group = states_ref.shape[1] // key_heads
+    group = olds.shape[2] // key_heads
     first, count = blocks[0] * PER_BLOCK, len(blocks) * PER_BLOCK
     for i in range(key_heads):
         for at in range(SLOTS):
@@ -429,30 +437,30 @@
                 d = d - d_high if steps <= at < 2 * steps else d_high
                 right[i * group + u, rows_at, :] = d if at < 3 * steps else jnp.zeros_like(d)
     slot_of = lax.broadcasted_iota(jnp.int32, (DK, DK), 1) // SLOTS
-    copies = []
     for n, block in enumerate(blocks):
-        if n >= 2:
-            copies[n - 2].wait()
-        loads[n].wait()
-        buffer = buffers.at[n % 2]
         span = slice(n * DK, (n + 1) * DK)
-        for i in range(key_heads):
-            lhs = jnp.transpose(left[i, span, :])
-            rhs = jnp.concatenate([right[i * group + u, span, :] for u in range(group)], axis=1)
-            rhs = rhs.astype(BF16)
-            for m in range(PER_BLOCK):
-                s = block * PER_BLOCK + m
-                masked = jnp.where(slot_of == m, lhs, 0.0).astype(BF16)
-                change = dot(masked, rhs)
+        lhs = [jnp.transpose(left[i, span, :]) for i in range(key_heads)]
+        rhs = [
+            jnp.concatenate(
+                [right[i * group + u, span, :] for u in range(group)], axis=1
+            ).astype(BF16)
+            for i in range(key_heads)
+        ]
+        for m in range(PER_BLOCK):
+            if m % half == 0:
+                loads[2 * n + m // half].wait()
+            s = block * PER_BLOCK + m
+            for i in range(key_heads):
+                masked = jnp.where(slot_of == m, lhs[i], 0.0).astype(BF16)
+                change = dot(masked, rhs[i])
                 for u in range(group):
                     columns = slice(u * DV, (u + 1) * DV)
                     h = i * group + u
                     total = total_ref[i, s : s + 1, columns]
-                    buffer[m, h] = olds[n, m, h] * total + change[:, columns]
-        span = pl.ds(block * PER_BLOCK, PER_BLOCK)
-        copies.append(pltpu.make_async_copy(buffer, out_ref.at[span], sems.at[n % 2]))
-        copies[-1].start()
-    for copy in copies[-2:]:
+                    news[n, m, h] = olds[n, m, h] * total + change[:, columns]
+            if m % half == half - 1:
+                stores[2 * n + m // half].start()
+    for copy in stores:
         copy.wait()
     done_ref[...] = jnp.zeros_like(done_ref)
 
@@ -462,6 +470,7 @@
     rows = len(blocks) * DK
     value_heads = states.shape[1]
     loose = after if before is None else (before, *after)
+    buffers = pltpu.VMEM((len(blocks), PER_BLOCK, *states.shape[1:]), F32)
     return call(
         functools.partial(update_kernel, steps, blocks),
         "update",
@@ -472,10 +481,10 @@
         [
             pltpu.VMEM((key_heads, rows, DK), F32),
             pltpu.VMEM((value_heads, rows, DV), F32),
-            pltpu.VMEM((len(blocks), PER_BLOCK, *states.shape[1:]), F32),
-            pltpu.VMEM((2, PER_BLOCK, *states.shape[1:]), F32),
-            pltpu.SemaphoreType.DMA((len(blocks),)),
-            pltpu.SemaphoreType.DMA((2,)),
+            buffers,
+            buffers,
+            pltpu.SemaphoreType.DMA((2 * len(blocks),)),
+            pltpu.SemaphoreType.DMA((2 * len(blocks),)),
         ],
         None if before is None else {4: 0},
         [ANY_SPEC, VMEM_SPEC],
@@ -630,6 +639,26 @@
     return out
 
 
+def finish_kernel(count, *refs):
+    total = refs[0][...]
+    for ref in refs[1:count]:
+        total = total + ref[...].astype(F32)
+    refs[-1][...] = total.astype(BF16)
+
+
+def finish(base, slab, received, after):
+    arrays = (base, slab, *received)
+    [out] = call(
+        functools.partial(finish_kernel, len(arrays)),
+        "finish",
+        [jax.ShapeDtypeStruct(base.shape, BF16)],
+        (),
+        arrays,
+        after,
+    )
+    return out
+
+
 def shared_in_kernel(me_ref, x_ref, w_ref, *refs):
     refs = refs[-2:]
     half = w_ref.shape[1] // 2
@@ -656,7 +685,8 @@
     )
 
 
-def shared_hidden_kernel(features, a_ref, b_ref, sq_ref, out_ref):
+def shared_hidden_kernel(features, a_ref, b_ref, sq_ref, *refs):
+    out_ref = refs[-1]
     rows = a_ref.shape[0]
     half = a_ref.shape[1] // 2
     inverse = lax.rsqrt(sq_ref[:rows, :] / features + EPS)
@@ -664,13 +694,14 @@
     out_ref[...] = (silu(pre[:, :half]) * pre[:, half:]).astype(BF16)
 
 
-def shared_hidden(features, a, b, sq):
+def shared_hidden(features, a, b, sq, after):
     [out] = call(
         functools.partial(shared_hidden_kernel, features),
         "shared_hidden",
         [pltpu.VMEM((a.shape[0], a.shape[1] // 2), BF16)],
         (),
         (a, b, sq),
+        after,
     )
     return out
 
@@ -731,13 +762,14 @@
     small = jnp.pad(small, ((0, 0), (0, -2 * value_heads % 16), (0, 0)))
 
     others = [exchange(mine, "head", 2 * p) for p in range(1, pairs)]
-    mine, w_query, w_key, w_shared_in, w_shared_out, gain, pack, extra, gain_mine, gain_inv = bring(
+    mine, w_query, w_key, w_value, w_shared_in, w_shared_out, gain, pack, extra, gain_mine, gain_inv = bring(
         me,
         seq_index.astype(jnp.int32).reshape(1),
         (
             mine,
             w_query,
             w_key,
+            w_value,
             w_shared_in,
             w_shared_out,
             input_gain.reshape(head_count, 1, width),
@@ -748,9 +780,9 @@
         post_gain.reshape(head_count, 1, width),
         seq_count,
     )
-    own_tokens = stack(mine, *others)
+    own_tokens = stack((mine, *others))
     sib_tokens = exchange(own_tokens, "head", 1)
-    w_value, w_zgate = load((w_value, w_zgate), (own_tokens,))
+    [w_zgate] = load((w_zgate,), (own_tokens,))
     gathered = (own_tokens, sib_tokens)
     own, sib, keys, deltas, totals = front(
         me, gathered, gain, small, pack, w_query, w_key, w_value, w_zgate, w_out, states, steps
@@ -766,32 +798,39 @@
     slabs = [x] + messages
     natural, reverse = list(range(pairs)), bit_reversed(pairs)
     blocks = tuple(range(seqs // PER_BLOCK))
-    cut = len(blocks) // 2
+    quarters = [blocks[len(blocks) * n // 4 : len(blocks) * (n + 1) // 4] for n in range(4)]
     shared_pre, sent = shared_in(me, x, w_shared_in, ())
     shared_pre = one_sum(shared_pre, exchange(sent, "head", 1))
     shared_received = exchange(shared_pre, "head", axes[0])
     sides, tie = [], ()
     for slab, bits in ((slabs[:half], axes), (slabs[half:], axes[::-1])):
         if half == 2:
-            side = slab_pair(*slab, rows, tie)[None]
+            side = slab_pair(*slab, rows, tie[:2])[None]
         else:
             side = jnp.stack([m[:rows] for m in slab])[None]
-        if not tie:
-            states_out, done_1 = update(keys, deltas, totals, states, blocks[:cut], (messages[0],))
-            tie = (done_1, shared_pre)
+        if not sides:
+            states_out, done = update(keys, deltas, totals, states, quarters[0], (side,))
+            tie = (done, shared_pre)
         for bit in bits[:-1]:
             received = exchange(side, "head", bit)
             if side.shape[0] == 1:
-                side = stack(side[0], received[0])
+                side = stack((side[0], received[0]), tie if sides else ())
             else:
                 side = jnp.concatenate([side, received])
+        if not sides:
+            states_out, done = update(keys, deltas, totals, states, quarters[1], (side,), states_out)
+            tie = (*tie, done, shared_received)
         sides.append([side, exchange(side, "head", bits[-1])])
     siblings = [[exchange(piece, "head", 1) for piece in side] for side in sides]
     middle = pairs // 2
     orders = tuple((tuple(o[:middle]), tuple(o[middle:])) for o in (natural, reverse))
 
+    shared_pre = one_sum(shared_pre, shared_received, (sides[0][1], sides[1][1]))
+    for bit in axes[1:-1]:
+        shared_pre = one_sum(shared_pre, exchange(shared_pre, "head", bit))
+    shared_received = exchange(shared_pre, "head", axes[-1])
     firsts = [
-        expert_first(me, side, gain_inv, w_in, order, (done_1,)) for side, order in zip(sides, orders)
+        expert_first(me, side, gain_inv, w_in, order, (done,)) for side, order in zip(sides, orders)
     ]
     owns, sibs, squares = [], [], []
     weights = (extra, *messages)
@@ -821,22 +860,20 @@
             owns[side], sent = half_sum(owns[side], received[side], tie)
             received[side] = exchange(sent, "head", bit)
         if n == 0:
-            states_out, done_2 = update(
-                keys, deltas, totals, states, blocks[cut:], tuple(owns), states_out
+            states_out, done = update(
+                keys, deltas, totals, states, quarters[2], tuple(owns), states_out
             )
-            tie = (done_2,)
-        else:
-            shared_pre = one_sum(shared_pre, shared_received, (owns[1],))
-            shared_received = exchange(shared_pre, "head", axes[n])
-    hidden = shared_hidden(features, shared_pre, shared_received, squares[0])
-    base = shared_out(me, hidden, exchange(hidden, "head", 1), resid, w_shared_out)
+            hidden = shared_hidden(features, shared_pre, shared_received, squares[0], tuple(owns))
+            hidden_received = exchange(hidden, "head", 1)
+            tie = (done, hidden_received)
+    base = shared_out(me, hidden, hidden_received, resid, w_shared_out)
     slabs = []
     for side in range(2):
         slabs += last_sum(owns[side], received[side])
-    result = base + slabs[0].astype(F32)
-    for z in range(1, seq_count):
-        result = result + exchange(slabs[z], "seq", z).astype(F32)
-    layer_out = jnp.transpose(result.astype(BF16).reshape(steps, seqs, width), (1, 0, 2))
+    states_out, done = update(keys, deltas, totals, states, quarters[3], (slabs[-1],), states_out)
+    received = [exchange(slabs[z], "seq", z) for z in range(1, seq_count)]
+    result = finish(base, slabs[0], received, (done,))
+    layer_out = jnp.transpose(result.reshape(steps, seqs, width), (1, 0, 2))
     return (layer_out, states_out)
 
 

time: 82.2 us -> 79.8 us (0.971)
  Pallas kernels: 28.2 us -> 32.3 us
  waiting for transfers between devices: 20.2 us -> 16.2 us
  starting transfers between devices: 31.9 us -> 30 us
    pallas_call x28 -> x31, Pallas kernels: 28.2 us -> 32.3 us  [call(): pl.pallas_call(body, out_shape=tuple(out_shapes), in_specs=[SMEM_SPEC] *...]
    ppermute x32, waiting for transfers between devices: 20.2 us -> 16.2 us  [exchange(): return lax.ppermute(x, axis, [(i, i ^ bit) for i in range(size)])]
    ppermute x32, starting transfers between devices: 31.9 us -> 30 us  [exchange(): return lax.ppermute(x, axis, [(i, i ^ bit) for i in range(size)])]
  transfers between devices with their start and end apart: 32 -> 32, of which waited for: 12 -> 12; matrix products, arithmetic and copies ran while one was open for 0% -> 0% of each run, Pallas kernels for 25% -> 30%
where the time goes in v5:
time: 79.8 us; the launch traced here: 79.6 us
  Pallas kernels  32.3 us (40%)
  starting transfers between devices  30 us (38%)
  waiting for transfers between devices  16.2 us (20%)
  between operations  1 us (1%)
    pallas_call x31, Pallas kernels, call(): pl.pallas_call(body, out_shape=tuple(out_shapes), in_specs=[SMEM_SPEC] *...  32.3 us
    ppermute x32, starting transfers between devices, exchange(): return lax.ppermute(x, axis, [(i, i ^ bit) for i in range(size)])  30 us
    ppermute x32, waiting for transfers between devices, exchange(): return lax.ppermute(x, axis, [(i, i ^ bit) for i in range(size)])  16.2 us
  transfers between devices with their start and end apart: 32, of which 12 were waited for; matrix products, arithmetic and copies ran while one was open for 0% of the time, Pallas kernels for 30%

profile of v5, /device:TPU:0, one launch (start us, length us, event | category | flops | bytes accessed | tf_op | source)
XLA Modules:
  0.0 79.6 jit_solution(10324957267145033391)
XLA Ops:
  0.7 3.0 %collective-permute-start = (bf16[96,256]{1,0:T(8,128)(2,1)}, bf16[96,256]{1,0:T(8,128)(2,1)S(1)}, u32[]{:S(2)}, u32[]{:S(2)}) collective-permute-start(bf16[96,256]{1,0:T(8,128)(2,1)} %bitcast.34), channel_id=1, source_target_pairs={{0,2},{1,3},{2,0},{3,1},{4,6},{5,7},{6,4},{7,5},{8,10},{9,11},{10,... | collective-permute-start | bytes 147464 | tf_op jit(solution)/shard_map/ppermute | solution.py:57
  3.7 1.5 %collective-permute-start.1 = (bf16[96,256]{1,0:T(8,128)(2,1)}, bf16[96,256]{1,0:T(8,128)(2,1)S(1)}, u32[]{:S(2)}, u32[]{:S(2)}) collective-permute-start(bf16[96,256]{1,0:T(8,128)(2,1)} %bitcast.35), channel_id=1, source_target_pairs={{0,4},{1,5},{2,6},{3,7},{4,0},{5,1},{6,2},{7,3},{8,12},{9,13},{10,... | collective-permute-start | bytes 147464 | tf_op jit(solution)/shard_map/ppermute | solution.py:57
  5.2 2.6 %bring.1 = (bf16[96,256]{1,0:T(8,128)(2,1)S(1)}, bf16[2048,256]{1,0:T(8,128)(2,1)S(1)}, bf16[2048,256]{1,0:T(8,128)(2,1)S(1)}, bf16[2048,512]{1,0:T(8,128)(2,1)S...) custom-call(s32[1]{0:T(128)} %bitcast.me_ref, ...), custom_call_target="tpu_custom_call" | custom-call | tf_op jit(solution)/shard_map/bring/pallas_call | solution.py:43
  8.0 2.4 %collective-permute-done.2.refs_3_ = bf16[96,256]{1,0:T(8,128)(2,1)S(1)} collective-permute-done((bf16[96,256]{1,0:T(8,128)(2,1)}, bf16[96,256]{1,0:T(8,128)(2,1)S(1)}, u32[]{:S(2)}, u32[]{:S(2)}) %collective-permute-start.2) | collective-permute-done | bytes 49184 | tf_op jit(solution)/shard_map/ppermute | solution.py:57
  10.5 1.6 %load.2.refs_8_ = bf16[2048,512]{1,0:T(8,128)(2,1)S(1)} custom-call(bf16[2048,512]{1,0:T(8,128)(2,1)} %refs_0_.2, bf16[4,96,256]{2,1,0:T(8,128)(2,1)S(1)} %stack.3.refs_1_.refs_0_), custom_call_target="tpu_custom_call" | custom-call | tf_op jit(solution)/shard_map/load/pallas_call | solution.py:43
  12.2 7.5 %front.1 = (bf16[4,96,256]{2,1,0:T(8,128)(2,1)S(1)}, bf16[4,96,256]{2,1,0:T(8,128)(2,1)S(1)}, f32[2,96,128]{2,1,0:T(8,128)S(1)}, f32[2,3,32,256]{3,2,1,0:T(8,128)S(1)}, f32[2,32,256]{2,1,0:T(8,128)S(1)}) custom-call(s32[1]{0:T(128)} %bitcast.me_ref, bf16[4,96,256]{2,1,0:T(8,128)(2,1)S(1)} %stack.3.refs_1_.refs_0_, ...), custom_call_target="tpu_custom_call" | custom-call | tf_op jit(solution)/shard_map/front/pallas_call | solution.py:43
  19.7 0.5 collective-permute-start.4
  20.2 1.1 %collective-permute-done.4.b_ref = bf16[4,96,256]{2,1,0:T(8,128)(2,1)S(1)} collective-permute-done((bf16[4,96,256]{2,1,0:T(8,128)(2,1)S(1)}, bf16[4,96,256]{2,1,0:T(8,128)(2,1)S(1)}, u32[]{:S(2)}, u32[]{:S(2)}) %collective-permute-start.4) | collective-permute-done | bytes 196640 | tf_op jit(solution)/shard_map/ppermute | solution.py:57
  21.4 0.6 collective-permute-start.5
  22.0 0.4 collective-permute-start.6
  22.4 2.5 %collective-permute-start.7 = (bf16[96,256]{1,0:T(8,128)(2,1)S(1)}, bf16[96,256]{1,0:T(8,128)(2,1)S(1)}, u32[]{:S(2)}, u32[]{:S(2)}) collective-permute-start(bf16[96,256]{1,0:T(8,128)(2,1)S(1)} %get-tuple-element.110), channel_id=1, source_target_pairs={{0,6},{1,7},{2,4},{3,5},{4,2},{5,3},{6,0},{7,1},{8,14},{9,15},{10,... | collective-permute-start | bytes 147464 | tf_op jit(solution)/shard_map/ppermute | solution.py:57
  24.9 2.9 %load.3 = (bf16[1,2048,1024]{2,1,0:T(8,128)(2,1)S(1)}, bf16[1,512,2048]{2,1,0:T(8,128)(2,1)S(1)}) custom-call(bf16[1,2048,1024]{2,1,0:T(8,128)(2,1)} %refs_0_.3, bf16[1,512,2048]{2,1,0:T(8,128)(2,1)} %refs_1_.1, bf16[4,96,256]{2,1,0:T(8,128)(2,1)S(1)} %one_sum.3.refs_2_.refs_0_), custom_call_target="tpu_custom_call" | custom-call | tf_op jit(solution)/shard_map/load/pallas_call | solution.py:43
  27.9 0.4 shared_in.1
  28.4 1.6 %collective-permute-start.10 = (bf16[112,256]{1,0:T(8,128)(2,1)S(1)}, bf16[112,256]{1,0:T(8,128)(2,1)S(1)}, u32[]{:S(2)}, u32[]{:S(2)}) collective-permute-start(bf16[112,256]{1,0:T(8,128)(2,1)S(1)} %get-tuple-element.71), channel_id=1, source_target_pairs={{0,8},{8,0},{16,24},{24,16},{1,9},{9,1},{17,25},{25,17},{2,10},{10... | collective-permute-start | bytes 172040 | tf_op jit(solution)/shard_map/ppermute | solution.py:57
  30.1 2.6 %collective-permute-start.13 = (bf16[112,256]{1,0:T(8,128)(2,1)S(1)}, bf16[112,256]{1,0:T(8,128)(2,1)S(1)}, u32[]{:S(2)}, u32[]{:S(2)}) collective-permute-start(bf16[112,256]{1,0:T(8,128)(2,1)S(1)} %get-tuple-element.72), channel_id=1, source_target_pairs={{0,16},{8,24},{16,0},{24,8},{1,17},{9,25},{17,1},{25,9},{2,18},{10... | collective-permute-start | bytes 172040 | tf_op jit(solution)/shard_map/ppermute | solution.py:57
  32.9 1.2 %collective-permute-start.11 = (bf16[1,2,96,256]{3,2,1,0:T(8,128)(2,1)S(1)}, bf16[1,2,96,256]{3,2,1,0:T(8,128)(2,1)S(1)}, u32[]{:S(2)}, u32[]{:S(2)}) collective-permute-start(bf16[1,2,96,256]{3,2,1,0:T(8,128)(2,1)S(1)} %bitcast.28), channel_id=1, source_target_pairs={{0,2},{1,3},{2,0},{3,1},{4,6},{5,7},{6,4},{7,5},{8,10},{9,11},{10,... | collective-permute-start | bytes 294920 | tf_op jit(solution)/shard_map/ppermute | solution.py:57
  34.1 3.0 %update.4 = (f32[32,4,128,128]{3,2,1,0:T(8,128)}, f32[8,128]{1,0:T(8,128)S(1)}) custom-call(f32[2,96,128]{2,1,0:T(8,128)S(1)} %get-tuple-element.74.keys_ref, f32[2,3,32,256]{3,2,1,0:T(8,128)S(1)} %get-tuple-element.75.delta_ref, f32[2,32,256]{2,1,0:T(8,128)S(1)} %get-tuple-element.76.total_ref, f32[32,4,128,128]{3,2,1,0:T(8,128)} %states_ref.7, ...), custom_call_target="tpu_custom_call" | custom-call | tf_op jit(solution)/shard_map/update/pallas_call | solution.py:43
  37.1 1.6 %collective-permute-done.14.b_ref.refs_8_ = bf16[112,256]{1,0:T(8,128)(2,1)S(1)} collective-permute-done((bf16[112,256]{1,0:T(8,128)(2,1)S(1)}, bf16[112,256]{1,0:T(8,128)(2,1)S(1)}, u32[]{:S(2)}, u32[]{:S(2)}) %collective-permute-start.14) | collective-permute-done | bytes 57376 | tf_op jit(solution)/shard_map/ppermute | solution.py:57
  38.7 1.2 %collective-permute-start.15 = (bf16[1,2,96,256]{3,2,1,0:T(8,128)(2,1)S(1)}, bf16[1,2,96,256]{3,2,1,0:T(8,128)(2,1)S(1)}, u32[]{:S(2)}, u32[]{:S(2)}) collective-permute-start(bf16[1,2,96,256]{3,2,1,0:T(8,128)(2,1)S(1)} %bitcast.30), channel_id=1, source_target_pairs={{0,4},{1,5},{2,6},{3,7},{4,0},{5,1},{6,2},{7,3},{8,12},{9,13},{10,... | collective-permute-start | bytes 294920 | tf_op jit(solution)/shard_map/ppermute | solution.py:57
  39.9 1.5 %collective-permute-start.9 = (bf16[96,512]{1,0:T(8,128)(2,1)S(1)}, bf16[96,512]{1,0:T(8,128)(2,1)S(1)}, u32[]{:S(2)}, u32[]{:S(2)}) collective-permute-start(bf16[96,512]{1,0:T(8,128)(2,1)S(1)} %one_sum.4.refs_1_.refs_3_.a_ref), channel_id=1, source_target_pairs={{0,2},{1,3},{2,0},{3,1},{4,6},{5,7},{6,4},{7,5},{8,10},{9,11},{10,... | collective-permute-start | bytes 294920 | tf_op jit(solution)/shard_map/ppermute | solution.py:57
  41.4 0.6 collective-permute-start.12
  42.0 3.0 %update.5 = (f32[32,4,128,128]{3,2,1,0:T(8,128)}, f32[8,128]{1,0:T(8,128)S(1)}) custom-call(f32[2,96,128]{2,1,0:T(8,128)S(1)} %get-tuple-element.74.keys_ref, f32[2,3,32,256]{3,2,1,0:T(8,128)S(1)} %get-tuple-element.75.delta_ref, f32[2,32,256]{2,1,0:T(8,128)S(1)} %get-tuple-element.76.total_ref, ...), custom_call_target="tpu_custom_call", output_to_operand_aliasing={{0}: (4, {})} | custom-call | tf_op jit(solution)/shard_map/update/pallas_call | solution.py:43
  45.0 1.1 %collective-permute-start.16 = (bf16[2,2,96,256]{3,2,1,0:T(8,128)(2,1)S(1)}, bf16[2,2,96,256]{3,2,1,0:T(8,128)(2,1)S(1)}, u32[]{:S(2)}, u32[]{:S(2)}) collective-permute-start(bf16[2,2,96,256]{3,2,1,0:T(8,128)(2,1)S(1)} %stack.5.refs_0_), channel_id=1, source_target_pairs={{0,2},{1,3},{2,0},{3,1},{4,6},{5,7},{6,4},{7,5},{8,10},{9,11},{10,... | collective-permute-start | bytes 589832 | tf_op jit(solution)/shard_map/ppermute | solution.py:57
  46.1 1.5 %collective-permute-done.12.refs_0_.refs_1_ = bf16[2,2,96,256]{3,2,1,0:T(8,128)(2,1)S(1)} collective-permute-done((bf16[2,2,96,256]{3,2,1,0:T(8,128)(2,1)S(1)}, bf16[2,2,96,256]{3,2,1,0:T(8,128)(2,1)S(1)}, u32[]{:S(2)}, u32[]{:S(2)}) %collective-permute-start.12) | collective-permute-done | bytes 196640 | tf_op jit(solution)/shard_map/ppermute | solution.py:57
  47.6 0.5 collective-permute-start.21
  48.1 2.7 %collective-permute-done.16.refs_1_ = bf16[2,2,96,256]{3,2,1,0:T(8,128)(2,1)S(1)} collective-permute-done((bf16[2,2,96,256]{3,2,1,0:T(8,128)(2,1)S(1)}, bf16[2,2,96,256]{3,2,1,0:T(8,128)(2,1)S(1)}, u32[]{:S(2)}, u32[]{:S(2)}) %collective-permute-start.16) | collective-permute-done | bytes 196640 | tf_op jit(solution)/shard_map/ppermute | solution.py:57
  50.8 1.6 %collective-permute-start.17 = (bf16[96,512]{1,0:T(8,128)(2,1)S(1)}, bf16[96,512]{1,0:T(8,128)(2,1)S(1)}, u32[]{:S(2)}, u32[]{:S(2)}) collective-permute-start(bf16[96,512]{1,0:T(8,128)(2,1)S(1)} %one_sum.5.a_ref), channel_id=1, source_target_pairs={{0,4},{1,5},{2,6},{3,7},{4,0},{5,1},{6,2},{7,3},{8,12},{9,13},{10,... | collective-permute-start | bytes 294920 | tf_op jit(solution)/shard_map/ppermute | solution.py:57
  52.3 0.6 expert_first.2
  52.9 0.6 expert_first.3
  53.6 1.2 %expert_rest.2 = (bf16[4,2,96,256]{3,2,1,0:T(8,128)(2,1)S(1)}, bf16[4,2,96,256]{3,2,1,0:T(8,128)(2,1)S(1)}, f32[192,1]{1,0:T(8,128)S(1)}) custom-call(s32[1]{0:T(128)} %bitcast.me_ref, bf16[2,2,96,256]{3,2,1,0:T(8,128)(2,1)S(1)} %collective-permute-done.18.refs_0_, bf16[2,2,96,256]{3,2,1,0:T(8,128)(2,1)S(1)} %collective-permute-done.19.refs_1_, ...), custom_call_target="tpu_custom_call" | custom-call | tf_op jit(solution)/shard_map/expert_rest/pallas_call | solution.py:43
  54.8 0.3 collective-permute-start.20
  55.1 0.9 %collective-permute-done.17.refs_9_.b_ref = bf16[96,512]{1,0:T(8,128)(2,1)S(1)} collective-permute-done((bf16[96,512]{1,0:T(8,128)(2,1)S(1)}, bf16[96,512]{1,0:T(8,128)(2,1)S(1)}, u32[]{:S(2)}, u32[]{:S(2)}) %collective-permute-start.17) | collective-permute-done | bytes 98336 | tf_op jit(solution)/shard_map/ppermute | solution.py:57
  56.0 1.5 %expert_rest.3 = (bf16[4,2,96,256]{3,2,1,0:T(8,128)(2,1)S(1)}, bf16[4,2,96,256]{3,2,1,0:T(8,128)(2,1)S(1)}, f32[192,1]{1,0:T(8,128)}) custom-call(s32[1]{0:T(128)} %bitcast.me_ref, bf16[2,2,96,256]{3,2,1,0:T(8,128)(2,1)S(1)} %collective-permute-done.21.refs_0_, bf16[2,2,96,256]{3,2,1,0:T(8,128)(2,1)S(1)} %collective-permute-done.22.refs_1_, ...), custom_call_target="tpu_custom_call" | custom-call | tf_op jit(solution)/shard_map/expert_rest/pallas_call | solution.py:43
  57.7 1.1 %collective-permute-start.25 = (bf16[2,2,96,256]{3,2,1,0:T(8,128)(2,1)S(1)}, bf16[2,2,96,256]{3,2,1,0:T(8,128)(2,1)S(1)}, u32[]{:S(2)}, u32[]{:S(2)}) collective-permute-start(bf16[2,2,96,256]{3,2,1,0:T(8,128)(2,1)S(1)} %get-tuple-element.95), channel_id=1, source_target_pairs={{0,2},{1,3},{2,0},{3,1},{4,6},{5,7},{6,4},{7,5},{8,10},{9,11},{10,... | collective-permute-start | bytes 589832 | tf_op jit(solution)/shard_map/ppermute | solution.py:57
  58.8 0.5 collective-permute-done.23.b_ref
  59.4 1.6 %collective-permute-start.28 = (bf16[2,2,96,256]{3,2,1,0:T(8,128)(2,1)S(1)}, bf16[2,2,96,256]{3,2,1,0:T(8,128)(2,1)S(1)}, u32[]{:S(2)}, u32[]{:S(2)}) collective-permute-start(bf16[2,2,96,256]{3,2,1,0:T(8,128)(2,1)S(1)} %get-tuple-element.102), channel_id=1, source_target_pairs={{0,4},{1,5},{2,6},{3,7},{4,0},{5,1},{6,2},{7,3},{8,12},{9,13},{10,... | collective-permute-start | bytes 589832 | tf_op jit(solution)/shard_map/ppermute | solution.py:57
  61.2 3.0 %update.6 = (f32[32,4,128,128]{3,2,1,0:T(8,128)}, f32[8,128]{1,0:T(8,128)S(1)}) custom-call(f32[2,96,128]{2,1,0:T(8,128)S(1)} %get-tuple-element.74.keys_ref, f32[2,3,32,256]{3,2,1,0:T(8,128)S(1)} %get-tuple-element.75.delta_ref, f32[2,32,256]{2,1,0:T(8,128)S(1)} %get-tuple-element.76.total_ref, ...), custom_call_target="tpu_custom_call", output_to_operand_aliasing={{0}: (4, {})} | custom-call | tf_op jit(solution)/shard_map/update/pallas_call | solution.py:43
  64.2 0.9 %collective-permute-done.25.b_ref = bf16[2,2,96,256]{3,2,1,0:T(8,128)(2,1)S(1)} collective-permute-done((bf16[2,2,96,256]{3,2,1,0:T(8,128)(2,1)S(1)}, bf16[2,2,96,256]{3,2,1,0:T(8,128)(2,1)S(1)}, u32[]{:S(2)}, u32[]{:S(2)}) %collective-permute-start.25) | collective-permute-done | bytes 196640 | tf_op jit(solution)/shard_map/ppermute | solution.py:57
  65.1 1.6 %collective-permute-start.26 = (bf16[1,2,96,256]{3,2,1,0:T(8,128)(2,1)S(1)}, bf16[1,2,96,256]{3,2,1,0:T(8,128)(2,1)S(1)}, u32[]{:S(2)}, u32[]{:S(2)}) collective-permute-start(bf16[1,2,96,256]{3,2,1,0:T(8,128)(2,1)S(1)} %get-tuple-element.99), channel_id=1, source_target_pairs={{0,4},{1,5},{2,6},{3,7},{4,0},{5,1},{6,2},{7,3},{8,12},{9,13},{10,... | collective-permute-start | bytes 294920 | tf_op jit(solution)/shard_map/ppermute | solution.py:57
  66.7 0.8 %collective-permute-start.29 = (bf16[1,2,96,256]{3,2,1,0:T(8,128)(2,1)S(1)}, bf16[1,2,96,256]{3,2,1,0:T(8,128)(2,1)S(1)}, u32[]{:S(2)}, u32[]{:S(2)}) collective-permute-start(bf16[1,2,96,256]{3,2,1,0:T(8,128)(2,1)S(1)} %get-tuple-element.104), channel_id=1, source_target_pairs={{0,2},{1,3},{2,0},{3,1},{4,6},{5,7},{6,4},{7,5},{8,10},{9,11},{10,... | collective-permute-start | bytes 294920 | tf_op jit(solution)/shard_map/ppermute | solution.py:57
  67.5 2.3 %collective-permute-done.26.b_ref = bf16[1,2,96,256]{3,2,1,0:T(8,128)(2,1)S(1)} collective-permute-done((bf16[1,2,96,256]{3,2,1,0:T(8,128)(2,1)S(1)}, bf16[1,2,96,256]{3,2,1,0:T(8,128)(2,1)S(1)}, u32[]{:S(2)}, u32[]{:S(2)}) %collective-permute-start.26) | collective-permute-done | bytes 98336 | tf_op jit(solution)/shard_map/ppermute | solution.py:57
  69.8 0.7 collective-permute-start.27
  70.5 0.9 %collective-permute-done.29.b_ref = bf16[1,2,96,256]{3,2,1,0:T(8,128)(2,1)S(1)} collective-permute-done((bf16[1,2,96,256]{3,2,1,0:T(8,128)(2,1)S(1)}, bf16[1,2,96,256]{3,2,1,0:T(8,128)(2,1)S(1)}, u32[]{:S(2)}, u32[]{:S(2)}) %collective-permute-start.29) | collective-permute-done | bytes 98336 | tf_op jit(solution)/shard_map/ppermute | solution.py:57
  71.4 1.6 %collective-permute-start.30 = (bf16[96,256]{1,0:T(8,128)(2,1)S(1)}, bf16[96,256]{1,0:T(8,128)(2,1)S(1)}, u32[]{:S(2)}, u32[]{:S(2)}) collective-permute-start(bf16[96,256]{1,0:T(8,128)(2,1)S(1)} %get-tuple-element.105), channel_id=1, source_target_pairs={{0,16},{8,24},{16,0},{24,8},{1,17},{9,25},{17,1},{25,9},{2,18},{10... | collective-permute-start | bytes 147464 | tf_op jit(solution)/shard_map/ppermute | solution.py:57
  73.0 1.4 %collective-permute-start.31 = (bf16[96,256]{1,0:T(8,128)(2,1)S(1)}, bf16[96,256]{1,0:T(8,128)(2,1)S(1)}, u32[]{:S(2)}, u32[]{:S(2)}) collective-permute-start(bf16[96,256]{1,0:T(8,128)(2,1)S(1)} %get-tuple-element.106.refs_1_), channel_id=1, source_target_pairs={{0,24},{8,16},{16,8},{24,0},{1,25},{9,17},{17,9},{25,1},{2,26},{10... | collective-permute-start | bytes 147464 | tf_op jit(solution)/shard_map/ppermute | solution.py:57
  74.7 2.9 %update.7 = (f32[32,4,128,128]{3,2,1,0:T(8,128)}, f32[8,128]{1,0:T(8,128)S(1)}) custom-call(f32[2,96,128]{2,1,0:T(8,128)S(1)} %get-tuple-element.74.keys_ref, f32[2,3,32,256]{3,2,1,0:T(8,128)S(1)} %get-tuple-element.75.delta_ref, f32[2,32,256]{2,1,0:T(8,128)S(1)} %get-tuple-element.76.total_ref, ...), custom_call_target="tpu_custom_call", output_to_operand_aliasing={{0}: (4, {})} | custom-call | tf_op jit(solution)/shard_map/update/pallas_call | solution.py:43
  77.6 1.3 %collective-permute-done.31.refs_4_ = bf16[96,256]{1,0:T(8,128)(2,1)S(1)} collective-permute-done((bf16[96,256]{1,0:T(8,128)(2,1)S(1)}, bf16[96,256]{1,0:T(8,128)(2,1)S(1)}, u32[]{:S(2)}, u32[]{:S(2)}) %collective-permute-start.31) | collective-permute-done | bytes 49184 | tf_op jit(solution)/shard_map/ppermute | solution.py:57
  78.9 0.7 finish.1
  (54 shorter events, 1.6 us)
Async XLA Ops:
  0.6 9.8 %copy-start.1 = (bf16[2048,4]{0,1:T(4,128)(2,1)S(1)}, bf16[2048,4]{0,1:T(4,128)(2,1)}, u32[]{:S(2)}) copy-start(bf16[2048,4]{0,1:T(4,128)(2,1)} %param.29) | copy-start | bytes 49156
  0.6 9.8 %copy-start = (bf16[2048,4]{0,1:T(4,128)(2,1)S(1)}, bf16[2048,4]{0,1:T(4,128)(2,1)}, u32[]{:S(2)}) copy-start(bf16[2048,4]{0,1:T(4,128)(2,1)} %param.30) | copy-start | bytes 49156
  0.7 7.2 %collective-permute-start = (bf16[96,256]{1,0:T(8,128)(2,1)}, bf16[96,256]{1,0:T(8,128)(2,1)S(1)}, u32[]{:S(2)}, u32[]{:S(2)}) collective-permute-start(bf16[96,256]{1,0:T(8,128)(2,1)} %bitcast.34), channel_id=1, source_target_pairs={{0,2},{1,3},{2,0},{3,1},{4,6},{5,7},{6,4},{7,5},{8,10},{9,11},{10,... | collective-permute-start | bytes 147464 | tf_op jit(solution)/shard_map/ppermute | solution.py:57
  3.7 4.3 %collective-permute-start.1 = (bf16[96,256]{1,0:T(8,128)(2,1)}, bf16[96,256]{1,0:T(8,128)(2,1)S(1)}, u32[]{:S(2)}, u32[]{:S(2)}) collective-permute-start(bf16[96,256]{1,0:T(8,128)(2,1)} %bitcast.35), channel_id=1, source_target_pairs={{0,4},{1,5},{2,6},{3,7},{4,0},{5,1},{6,2},{7,3},{8,12},{9,13},{10,... | collective-permute-start | bytes 147464 | tf_op jit(solution)/shard_map/ppermute | solution.py:57
  5.2 5.2 %collective-permute-start.2 = (bf16[96,256]{1,0:T(8,128)(2,1)}, bf16[96,256]{1,0:T(8,128)(2,1)S(1)}, u32[]{:S(2)}, u32[]{:S(2)}) collective-permute-start(bf16[96,256]{1,0:T(8,128)(2,1)} %bitcast.36), channel_id=1, source_target_pairs={{0,6},{1,7},{2,4},{3,5},{4,2},{5,3},{6,0},{7,1},{8,14},{9,15},{10,... | collective-permute-start | bytes 147464 | tf_op jit(solution)/shard_map/ppermute | solution.py:57
  10.4 1.8 %collective-permute-start.3 = (bf16[4,96,256]{2,1,0:T(8,128)(2,1)S(1)}, bf16[4,96,256]{2,1,0:T(8,128)(2,1)S(1)}, u32[]{:S(2)}, u32[]{:S(2)}) collective-permute-start(bf16[4,96,256]{2,1,0:T(8,128)(2,1)S(1)} %stack.3.refs_1_.refs_0_), channel_id=1, source_target_pairs={{0,1},{1,0},{2,3},{3,2},{4,5},{5,4},{6,7},{7,6},{8,9},{9,8},{10,11... | collective-permute-start | bytes 589832 | tf_op jit(solution)/shard_map/ppermute | solution.py:57
  19.7 1.6 %collective-permute-start.4 = (bf16[4,96,256]{2,1,0:T(8,128)(2,1)S(1)}, bf16[4,96,256]{2,1,0:T(8,128)(2,1)S(1)}, u32[]{:S(2)}, u32[]{:S(2)}) collective-permute-start(bf16[4,96,256]{2,1,0:T(8,128)(2,1)S(1)} %get-tuple-element.63), channel_id=1, source_target_pairs={{0,1},{1,0},{2,3},{3,2},{4,5},{5,4},{6,7},{7,6},{8,9},{9,8},{10,11... | collective-permute-start | bytes 589832 | tf_op jit(solution)/shard_map/ppermute | solution.py:57
  21.4 6.5 %collective-permute-start.5 = (bf16[96,256]{1,0:T(8,128)(2,1)S(1)}, bf16[96,256]{1,0:T(8,128)(2,1)S(1)}, u32[]{:S(2)}, u32[]{:S(2)}) collective-permute-start(bf16[96,256]{1,0:T(8,128)(2,1)S(1)} %get-tuple-element.112), channel_id=1, source_target_pairs={{0,2},{1,3},{2,0},{3,1},{4,6},{5,7},{6,4},{7,5},{8,10},{9,11},{10,... | collective-permute-start | bytes 147464 | tf_op jit(solution)/shard_map/ppermute | solution.py:57
  22.0 5.9 %collective-permute-start.6 = (bf16[96,256]{1,0:T(8,128)(2,1)S(1)}, bf16[96,256]{1,0:T(8,128)(2,1)S(1)}, u32[]{:S(2)}, u32[]{:S(2)}) collective-permute-start(bf16[96,256]{1,0:T(8,128)(2,1)S(1)} %get-tuple-element.111), channel_id=1, source_target_pairs={{0,4},{1,5},{2,6},{3,7},{4,0},{5,1},{6,2},{7,3},{8,12},{9,13},{10,... | collective-permute-start | bytes 147464 | tf_op jit(solution)/shard_map/ppermute | solution.py:57
  22.4 5.5 %collective-permute-start.7 = (bf16[96,256]{1,0:T(8,128)(2,1)S(1)}, bf16[96,256]{1,0:T(8,128)(2,1)S(1)}, u32[]{:S(2)}, u32[]{:S(2)}) collective-permute-start(bf16[96,256]{1,0:T(8,128)(2,1)S(1)} %get-tuple-element.110), channel_id=1, source_target_pairs={{0,6},{1,7},{2,4},{3,5},{4,2},{5,3},{6,0},{7,1},{8,14},{9,15},{10,... | collective-permute-start | bytes 147464 | tf_op jit(solution)/shard_map/ppermute | solution.py:57
  28.3 8.7 %collective-permute-start.8 = (bf16[96,512]{1,0:T(8,128)(2,1)S(1)}, bf16[96,512]{1,0:T(8,128)(2,1)S(1)}, u32[]{:S(2)}, u32[]{:S(2)}) collective-permute-start(bf16[96,512]{1,0:T(8,128)(2,1)S(1)} %get-tuple-element.70), channel_id=1, source_target_pairs={{0,1},{1,0},{2,3},{3,2},{4,5},{5,4},{6,7},{7,6},{8,9},{9,8},{10,11... | collective-permute-start | bytes 294920 | tf_op jit(solution)/shard_map/ppermute | solution.py:57
  28.4 4.5 %collective-permute-start.10 = (bf16[112,256]{1,0:T(8,128)(2,1)S(1)}, bf16[112,256]{1,0:T(8,128)(2,1)S(1)}, u32[]{:S(2)}, u32[]{:S(2)}) collective-permute-start(bf16[112,256]{1,0:T(8,128)(2,1)S(1)} %get-tuple-element.71), channel_id=1, source_target_pairs={{0,8},{8,0},{16,24},{24,16},{1,9},{9,1},{17,25},{25,17},{2,10},{10... | collective-permute-start | bytes 172040 | tf_op jit(solution)/shard_map/ppermute | solution.py:57
  30.1 7.0 %collective-permute-start.13 = (bf16[112,256]{1,0:T(8,128)(2,1)S(1)}, bf16[112,256]{1,0:T(8,128)(2,1)S(1)}, u32[]{:S(2)}, u32[]{:S(2)}) collective-permute-start(bf16[112,256]{1,0:T(8,128)(2,1)S(1)} %get-tuple-element.72), channel_id=1, source_target_pairs={{0,16},{8,24},{16,0},{24,8},{1,17},{9,25},{17,1},{25,9},{2,18},{10... | collective-permute-start | bytes 172040 | tf_op jit(solution)/shard_map/ppermute | solution.py:57
  32.6 6.0 %collective-permute-start.14 = (bf16[112,256]{1,0:T(8,128)(2,1)S(1)}, bf16[112,256]{1,0:T(8,128)(2,1)S(1)}, u32[]{:S(2)}, u32[]{:S(2)}) collective-permute-start(bf16[112,256]{1,0:T(8,128)(2,1)S(1)} %get-tuple-element.73), channel_id=1, source_target_pairs={{0,24},{8,16},{16,8},{24,0},{1,25},{9,17},{17,9},{25,1},{2,26},{10... | collective-permute-start | bytes 172040 | tf_op jit(solution)/shard_map/ppermute | solution.py:57
  32.9 8.5 %collective-permute-start.11 = (bf16[1,2,96,256]{3,2,1,0:T(8,128)(2,1)S(1)}, bf16[1,2,96,256]{3,2,1,0:T(8,128)(2,1)S(1)}, u32[]{:S(2)}, u32[]{:S(2)}) collective-permute-start(bf16[1,2,96,256]{3,2,1,0:T(8,128)(2,1)S(1)} %bitcast.28), channel_id=1, source_target_pairs={{0,2},{1,3},{2,0},{3,1},{4,6},{5,7},{6,4},{7,5},{8,10},{9,11},{10,... | collective-permute-start | bytes 294920 | tf_op jit(solution)/shard_map/ppermute | solution.py:57
  38.7 6.3 %collective-permute-start.15 = (bf16[1,2,96,256]{3,2,1,0:T(8,128)(2,1)S(1)}, bf16[1,2,96,256]{3,2,1,0:T(8,128)(2,1)S(1)}, u32[]{:S(2)}, u32[]{:S(2)}) collective-permute-start(bf16[1,2,96,256]{3,2,1,0:T(8,128)(2,1)S(1)} %bitcast.30), channel_id=1, source_target_pairs={{0,4},{1,5},{2,6},{3,7},{4,0},{5,1},{6,2},{7,3},{8,12},{9,13},{10,... | collective-permute-start | bytes 294920 | tf_op jit(solution)/shard_map/ppermute | solution.py:57
  39.9 5.1 %collective-permute-start.9 = (bf16[96,512]{1,0:T(8,128)(2,1)S(1)}, bf16[96,512]{1,0:T(8,128)(2,1)S(1)}, u32[]{:S(2)}, u32[]{:S(2)}) collective-permute-start(bf16[96,512]{1,0:T(8,128)(2,1)S(1)} %one_sum.4.refs_1_.refs_3_.a_ref), channel_id=1, source_target_pairs={{0,2},{1,3},{2,0},{3,1},{4,6},{5,7},{6,4},{7,5},{8,10},{9,11},{10,... | collective-permute-start | bytes 294920 | tf_op jit(solution)/shard_map/ppermute | solution.py:57
  41.4 6.1 %collective-permute-start.12 = (bf16[2,2,96,256]{3,2,1,0:T(8,128)(2,1)S(1)}, bf16[2,2,96,256]{3,2,1,0:T(8,128)(2,1)S(1)}, u32[]{:S(2)}, u32[]{:S(2)}) collective-permute-start(bf16[2,2,96,256]{3,2,1,0:T(8,128)(2,1)S(1)} %stack.4.refs_1_.refs_0_), channel_id=1, source_target_pairs={{0,4},{1,5},{2,6},{3,7},{4,0},{5,1},{6,2},{7,3},{8,12},{9,13},{10,... | collective-permute-start | bytes 589832 | tf_op jit(solution)/shard_map/ppermute | solution.py:57
  45.0 5.7 %collective-permute-start.16 = (bf16[2,2,96,256]{3,2,1,0:T(8,128)(2,1)S(1)}, bf16[2,2,96,256]{3,2,1,0:T(8,128)(2,1)S(1)}, u32[]{:S(2)}, u32[]{:S(2)}) collective-permute-start(bf16[2,2,96,256]{3,2,1,0:T(8,128)(2,1)S(1)} %stack.5.refs_0_), channel_id=1, source_target_pairs={{0,2},{1,3},{2,0},{3,1},{4,6},{5,7},{6,4},{7,5},{8,10},{9,11},{10,... | collective-permute-start | bytes 589832 | tf_op jit(solution)/shard_map/ppermute | solution.py:57
  46.1 7.5 %collective-permute-start.18 = (bf16[2,2,96,256]{3,2,1,0:T(8,128)(2,1)S(1)}, bf16[2,2,96,256]{3,2,1,0:T(8,128)(2,1)S(1)}, u32[]{:S(2)}, u32[]{:S(2)}) collective-permute-start(bf16[2,2,96,256]{3,2,1,0:T(8,128)(2,1)S(1)} %stack.4.refs_1_.refs_0_), channel_id=1, source_target_pairs={{0,1},{1,0},{2,3},{3,2},{4,5},{5,4},{6,7},{7,6},{8,9},{9,8},{10,11... | collective-permute-start | bytes 589832 | tf_op jit(solution)/shard_map/ppermute | solution.py:57
  47.6 6.0 %collective-permute-start.19 = (bf16[2,2,96,256]{3,2,1,0:T(8,128)(2,1)S(1)}, bf16[2,2,96,256]{3,2,1,0:T(8,128)(2,1)S(1)}, u32[]{:S(2)}, u32[]{:S(2)}) collective-permute-start(bf16[2,2,96,256]{3,2,1,0:T(8,128)(2,1)S(1)} %collective-permute-done.12.refs_0_.refs_1_), channel_id=1, source_target_pairs={{0,1},{1,0},{2,3},{3,2},{4,5},{5,4},{6,7},{7,6},{8,9},{9,8},{10,11... | collective-permute-start | bytes 589832 | tf_op jit(solution)/shard_map/ppermute | solution.py:57
  47.6 7.5 %collective-permute-start.21 = (bf16[2,2,96,256]{3,2,1,0:T(8,128)(2,1)S(1)}, bf16[2,2,96,256]{3,2,1,0:T(8,128)(2,1)S(1)}, u32[]{:S(2)}, u32[]{:S(2)}) collective-permute-start(bf16[2,2,96,256]{3,2,1,0:T(8,128)(2,1)S(1)} %stack.5.refs_0_), channel_id=1, source_target_pairs={{0,1},{1,0},{2,3},{3,2},{4,5},{5,4},{6,7},{7,6},{8,9},{9,8},{10,11... | collective-permute-start | bytes 589832 | tf_op jit(solution)/shard_map/ppermute | solution.py:57
  50.7 5.3 %collective-permute-start.22 = (bf16[2,2,96,256]{3,2,1,0:T(8,128)(2,1)S(1)}, bf16[2,2,96,256]{3,2,1,0:T(8,128)(2,1)S(1)}, u32[]{:S(2)}, u32[]{:S(2)}) collective-permute-start(bf16[2,2,96,256]{3,2,1,0:T(8,128)(2,1)S(1)} %collective-permute-done.16.refs_1_), channel_id=1, source_target_pairs={{0,1},{1,0},{2,3},{3,2},{4,5},{5,4},{6,7},{7,6},{8,9},{9,8},{10,11... | collective-permute-start | bytes 589832 | tf_op jit(solution)/shard_map/ppermute | solution.py:57
  50.8 5.3 %collective-permute-start.17 = (bf16[96,512]{1,0:T(8,128)(2,1)S(1)}, bf16[96,512]{1,0:T(8,128)(2,1)S(1)}, u32[]{:S(2)}, u32[]{:S(2)}) collective-permute-start(bf16[96,512]{1,0:T(8,128)(2,1)S(1)} %one_sum.5.a_ref), channel_id=1, source_target_pairs={{0,4},{1,5},{2,6},{3,7},{4,0},{5,1},{6,2},{7,3},{8,12},{9,13},{10,... | collective-permute-start | bytes 294920 | tf_op jit(solution)/shard_map/ppermute | solution.py:57
  54.8 2.8 %collective-permute-start.20 = (bf16[4,2,96,256]{3,2,1,0:T(8,128)(2,1)S(1)}, bf16[4,2,96,256]{3,2,1,0:T(8,128)(2,1)S(1)}, u32[]{:S(2)}, u32[]{:S(2)}) collective-permute-start(bf16[4,2,96,256]{3,2,1,0:T(8,128)(2,1)S(1)} %get-tuple-element.86), channel_id=1, source_target_pairs={{0,1},{1,0},{2,3},{3,2},{4,5},{5,4},{6,7},{7,6},{8,9},{9,8},{10,11... | collective-permute-start | bytes 1179656 | tf_op jit(solution)/shard_map/ppermute | solution.py:57
  57.6 1.7 %collective-permute-start.23 = (bf16[4,2,96,256]{3,2,1,0:T(8,128)(2,1)S(1)}, bf16[4,2,96,256]{3,2,1,0:T(8,128)(2,1)S(1)}, u32[]{:S(2)}, u32[]{:S(2)}) collective-permute-start(bf16[4,2,96,256]{3,2,1,0:T(8,128)(2,1)S(1)} %get-tuple-element.91), channel_id=1, source_target_pairs={{0,1},{1,0},{2,3},{3,2},{4,5},{5,4},{6,7},{7,6},{8,9},{9,8},{10,11... | collective-permute-start | bytes 1179656 | tf_op jit(solution)/shard_map/ppermute | solution.py:57
  57.7 7.4 %collective-permute-start.25 = (bf16[2,2,96,256]{3,2,1,0:T(8,128)(2,1)S(1)}, bf16[2,2,96,256]{3,2,1,0:T(8,128)(2,1)S(1)}, u32[]{:S(2)}, u32[]{:S(2)}) collective-permute-start(bf16[2,2,96,256]{3,2,1,0:T(8,128)(2,1)S(1)} %get-tuple-element.95), channel_id=1, source_target_pairs={{0,2},{1,3},{2,0},{3,1},{4,6},{5,7},{6,4},{7,5},{8,10},{9,11},{10,... | collective-permute-start | bytes 589832 | tf_op jit(solution)/shard_map/ppermute | solution.py:57
  59.4 7.3 %collective-permute-start.28 = (bf16[2,2,96,256]{3,2,1,0:T(8,128)(2,1)S(1)}, bf16[2,2,96,256]{3,2,1,0:T(8,128)(2,1)S(1)}, u32[]{:S(2)}, u32[]{:S(2)}) collective-permute-start(bf16[2,2,96,256]{3,2,1,0:T(8,128)(2,1)S(1)} %get-tuple-element.102), channel_id=1, source_target_pairs={{0,4},{1,5},{2,6},{3,7},{4,0},{5,1},{6,2},{7,3},{8,12},{9,13},{10,... | collective-permute-start | bytes 589832 | tf_op jit(solution)/shard_map/ppermute | solution.py:57
  61.1 3.1 %collective-permute-start.24 = (bf16[96,256]{1,0:T(8,128)(2,1)S(1)}, bf16[96,256]{1,0:T(8,128)(2,1)S(1)}, u32[]{:S(2)}, u32[]{:S(2)}) collective-permute-start(bf16[96,256]{1,0:T(8,128)(2,1)S(1)} %shared_hidden.1.a_ref), channel_id=1, source_target_pairs={{0,1},{1,0},{2,3},{3,2},{4,5},{5,4},{6,7},{7,6},{8,9},{9,8},{10,11... | collective-permute-start | bytes 147464 | tf_op jit(solution)/shard_map/ppermute | solution.py:57
  65.1 4.7 %collective-permute-start.26 = (bf16[1,2,96,256]{3,2,1,0:T(8,128)(2,1)S(1)}, bf16[1,2,96,256]{3,2,1,0:T(8,128)(2,1)S(1)}, u32[]{:S(2)}, u32[]{:S(2)}) collective-permute-start(bf16[1,2,96,256]{3,2,1,0:T(8,128)(2,1)S(1)} %get-tuple-element.99), channel_id=1, source_target_pairs={{0,4},{1,5},{2,6},{3,7},{4,0},{5,1},{6,2},{7,3},{8,12},{9,13},{10,... | collective-permute-start | bytes 294920 | tf_op jit(solution)/shard_map/ppermute | solution.py:57
  66.7 4.7 %collective-permute-start.29 = (bf16[1,2,96,256]{3,2,1,0:T(8,128)(2,1)S(1)}, bf16[1,2,96,256]{3,2,1,0:T(8,128)(2,1)S(1)}, u32[]{:S(2)}, u32[]{:S(2)}) collective-permute-start(bf16[1,2,96,256]{3,2,1,0:T(8,128)(2,1)S(1)} %get-tuple-element.104), channel_id=1, source_target_pairs={{0,2},{1,3},{2,0},{3,1},{4,6},{5,7},{6,4},{7,5},{8,10},{9,11},{10,... | collective-permute-start | bytes 294920 | tf_op jit(solution)/shard_map/ppermute | solution.py:57
  69.8 7.8 %collective-permute-start.27 = (bf16[96,256]{1,0:T(8,128)(2,1)S(1)}, bf16[96,256]{1,0:T(8,128)(2,1)S(1)}, u32[]{:S(2)}, u32[]{:S(2)}) collective-permute-start(bf16[96,256]{1,0:T(8,128)(2,1)S(1)} %get-tuple-element.101), channel_id=1, source_target_pairs={{0,8},{8,0},{16,24},{24,16},{1,9},{9,1},{17,25},{25,17},{2,10},{10... | collective-permute-start | bytes 147464 | tf_op jit(solution)/shard_map/ppermute | solution.py:57
  71.4 6.2 %collective-permute-start.30 = (bf16[96,256]{1,0:T(8,128)(2,1)S(1)}, bf16[96,256]{1,0:T(8,128)(2,1)S(1)}, u32[]{:S(2)}, u32[]{:S(2)}) collective-permute-start(bf16[96,256]{1,0:T(8,128)(2,1)S(1)} %get-tuple-element.105), channel_id=1, source_target_pairs={{0,16},{8,24},{16,0},{24,8},{1,17},{9,25},{17,1},{25,9},{2,18},{10... | collective-permute-start | bytes 147464 | tf_op jit(solution)/shard_map/ppermute | solution.py:57
  73.0 5.9 %collective-permute-start.31 = (bf16[96,256]{1,0:T(8,128)(2,1)S(1)}, bf16[96,256]{1,0:T(8,128)(2,1)S(1)}, u32[]{:S(2)}, u32[]{:S(2)}) collective-permute-start(bf16[96,256]{1,0:T(8,128)(2,1)S(1)} %get-tuple-element.106.refs_1_), channel_id=1, source_target_pairs={{0,24},{8,16},{16,8},{24,0},{1,25},{9,17},{17,9},{25,1},{2,26},{10... | collective-permute-start | bytes 147464 | tf_op jit(solution)/shard_map/ppermute | solution.py:57

commit v6 on v5

--- a/solution.py
+++ b/solution.py
@@ -351,7 +351,7 @@
             pltpu.VMEM(states.shape, F32),
             pltpu.VMEM((key_heads, seqs * SLOTS, DK), F32),
             pltpu.VMEM((value_heads, seqs * SLOTS, DV), F32),
-            pltpu.SemaphoreType.DMA((5,)),
+            pltpu.SemaphoreType.DMA((9,)),
         ],
     )
 
@@ -388,6 +388,15 @@
         (merged, *received, mine, gain, extra),
         after,
     )
+
+
+def keep_kernel(x_ref, *refs):
+    refs[-1][...] = x_ref[...]
+
+
+def keep(x, after):
+    [out] = call(keep_kernel, "keep", [pltpu.VMEM(x.shape, x.dtype)], (), (x,), after)
+    return out
 
 
 def slab_kernel(a_ref, b_ref, *refs):
@@ -790,7 +799,7 @@
 
     merged = one_sum(own, exchange(sib, "head", 1))
     received = [exchange(merged[p], "head", 2 * p) for p in range(1, pairs)]
-    w_in, w_down = load((w_expert_in, w_expert_out), (merged,))
+    [w_in] = load((w_expert_in,), (merged,))
     resid, x, *messages = make_rows(merged, received, mine, gain_mine, extra, (w_in,))
 
     half = seq_count // 2
@@ -818,10 +827,15 @@
             else:
                 side = jnp.concatenate([side, received])
         if not sides:
-            states_out, done = update(keys, deltas, totals, states, quarters[1], (side,), states_out)
-            tie = (*tie, done, shared_received)
+            [w_down] = load((w_expert_out,), (side,))
+            tie = (*tie, w_down)
         sides.append([side, exchange(side, "head", bits[-1])])
-    siblings = [[exchange(piece, "head", 1) for piece in side] for side in sides]
+    states_out, done = update(
+        keys, deltas, totals, states, quarters[1] + quarters[2], (sides[0][0], sides[1][0]), states_out
+    )
+    siblings = [
+        [exchange(side[0], "head", 1), exchange(keep(side[1], (done, shared_received)), "head", 1)] for side in sides
+    ]
     middle = pairs // 2
     orders = tuple((tuple(o[:middle]), tuple(o[middle:])) for o in (natural, reverse))
 
@@ -861,7 +875,7 @@
             received[side] = exchange(sent, "head", bit)
         if n == 0:
             states_out, done = update(
-                keys, deltas, totals, states, quarters[2], tuple(owns), states_out
+                keys, deltas, totals, states, quarters[3], tuple(owns), states_out
             )
             hidden = shared_hidden(features, shared_pre, shared_received, squares[0], tuple(owns))
             hidden_received = exchange(hidden, "head", 1)
@@ -870,9 +884,8 @@
     slabs = []
     for side in range(2):
         slabs += last_sum(owns[side], received[side])
-    states_out, done = update(keys, deltas, totals, states, quarters[3], (slabs[-1],), states_out)
     received = [exchange(slabs[z], "seq", z) for z in range(1, seq_count)]
-    result = finish(base, slabs[0], received, (done,))
+    result = finish(base, slabs[0], received, ())
     layer_out = jnp.transpose(result.reshape(steps, seqs, width), (1, 0, 2))
     return (layer_out, states_out)
 

time: 79.8 us -> 80.7 us (1.011)
  starting transfers between devices: 30 us -> 31.6 us
  Pallas kernels: 32.3 us -> 30.8 us
    ppermute x32, starting transfers between devices: 30 us -> 31.6 us  [exchange(): return lax.ppermute(x, axis, [(i, i ^ bit) for i in range(size)])]
    pallas_call x31 -> x33, Pallas kernels: 32.3 us -> 30.8 us  [call(): pl.pallas_call(body, out_shape=tuple(out_shapes), in_specs=[SMEM_SPEC] *...]
  transfers between devices with their start and end apart: 32 -> 32, of which waited for: 12 -> 14; matrix products, arithmetic and copies ran while one was open for 0% -> 0% of each run, Pallas kernels for 30% -> 28%
where the time goes in v6:
time: 80.7 us; the launch traced here: 80.4 us
  starting transfers between devices  31.6 us (39%)
  Pallas kernels  30.8 us (38%)
  waiting for transfers between devices  17 us (21%)
  between operations  0.96 us (1%)
    ppermute x32, starting transfers between devices, exchange(): return lax.ppermute(x, axis, [(i, i ^ bit) for i in range(size)])  31.6 us
    pallas_call x33, Pallas kernels, call(): pl.pallas_call(body, out_shape=tuple(out_shapes), in_specs=[SMEM_SPEC] *...  30.8 us
    ppermute x32, waiting for transfers between devices, exchange(): return lax.ppermute(x, axis, [(i, i ^ bit) for i in range(size)])  17 us
  transfers between devices with their start and end apart: 32, of which 14 were waited for; matrix products, arithmetic and copies ran while one was open for 0% of the time, Pallas kernels for 28%

profile of v6, /device:TPU:0, one launch (start us, length us, event | category | flops | bytes accessed | tf_op | source)
XLA Modules:
  0.0 80.4 jit_solution(13773089353277360545)
XLA Ops:
  0.6 3.0 %collective-permute-start = (bf16[96,256]{1,0:T(8,128)(2,1)}, bf16[96,256]{1,0:T(8,128)(2,1)S(1)}, u32[]{:S(2)}, u32[]{:S(2)}) collective-permute-start(bf16[96,256]{1,0:T(8,128)(2,1)} %bitcast.34), channel_id=1, source_target_pairs={{0,2},{1,3},{2,0},{3,1},{4,6},{5,7},{6,4},{7,5},{8,10},{9,11},{10,... | collective-permute-start | bytes 147464 | tf_op jit(solution)/shard_map/ppermute | solution.py:57
  3.6 1.5 %collective-permute-start.1 = (bf16[96,256]{1,0:T(8,128)(2,1)}, bf16[96,256]{1,0:T(8,128)(2,1)S(1)}, u32[]{:S(2)}, u32[]{:S(2)}) collective-permute-start(bf16[96,256]{1,0:T(8,128)(2,1)} %bitcast.35), channel_id=1, source_target_pairs={{0,4},{1,5},{2,6},{3,7},{4,0},{5,1},{6,2},{7,3},{8,12},{9,13},{10,... | collective-permute-start | bytes 147464 | tf_op jit(solution)/shard_map/ppermute | solution.py:57
  5.2 2.6 %bring.1 = (bf16[96,256]{1,0:T(8,128)(2,1)S(1)}, bf16[2048,256]{1,0:T(8,128)(2,1)S(1)}, bf16[2048,256]{1,0:T(8,128)(2,1)S(1)}, bf16[2048,512]{1,0:T(8,128)(2,1)S...) custom-call(s32[1]{0:T(128)} %bitcast.me_ref, ...), custom_call_target="tpu_custom_call" | custom-call | tf_op jit(solution)/shard_map/bring/pallas_call | solution.py:43
  7.9 2.4 %collective-permute-done.2.refs_3_ = bf16[96,256]{1,0:T(8,128)(2,1)S(1)} collective-permute-done((bf16[96,256]{1,0:T(8,128)(2,1)}, bf16[96,256]{1,0:T(8,128)(2,1)S(1)}, u32[]{:S(2)}, u32[]{:S(2)}) %collective-permute-start.2) | collective-permute-done | bytes 49184 | tf_op jit(solution)/shard_map/ppermute | solution.py:57
  10.5 1.6 %load.3.refs_8_ = bf16[2048,512]{1,0:T(8,128)(2,1)S(1)} custom-call(bf16[2048,512]{1,0:T(8,128)(2,1)} %refs_0_.3, bf16[4,96,256]{2,1,0:T(8,128)(2,1)S(1)} %stack.3.refs_1_.refs_0_), custom_call_target="tpu_custom_call" | custom-call | tf_op jit(solution)/shard_map/load/pallas_call | solution.py:43
  12.1 7.1 %front.1 = (bf16[4,96,256]{2,1,0:T(8,128)(2,1)S(1)}, bf16[4,96,256]{2,1,0:T(8,128)(2,1)S(1)}, f32[2,96,128]{2,1,0:T(8,128)S(1)}, f32[2,3,32,256]{3,2,1,0:T(8,128)S(1)}, f32[2,32,256]{2,1,0:T(8,128)S(1)}) custom-call(s32[1]{0:T(128)} %bitcast.me_ref, bf16[4,96,256]{2,1,0:T(8,128)(2,1)S(1)} %stack.3.refs_1_.refs_0_, ...), custom_call_target="tpu_custom_call" | custom-call | tf_op jit(solution)/shard_map/front/pallas_call | solution.py:43
  19.3 0.5 collective-permute-start.4
  19.8 1.1 %collective-permute-done.4.b_ref = bf16[4,96,256]{2,1,0:T(8,128)(2,1)S(1)} collective-permute-done((bf16[4,96,256]{2,1,0:T(8,128)(2,1)S(1)}, bf16[4,96,256]{2,1,0:T(8,128)(2,1)S(1)}, u32[]{:S(2)}, u32[]{:S(2)}) %collective-permute-start.4) | collective-permute-done | bytes 196640 | tf_op jit(solution)/shard_map/ppermute | solution.py:57
  21.0 0.6 collective-permute-start.5
  21.6 0.4 collective-permute-start.6
  22.0 2.5 %collective-permute-start.7 = (bf16[96,256]{1,0:T(8,128)(2,1)S(1)}, bf16[96,256]{1,0:T(8,128)(2,1)S(1)}, u32[]{:S(2)}, u32[]{:S(2)}) collective-permute-start(bf16[96,256]{1,0:T(8,128)(2,1)S(1)} %get-tuple-element.102), channel_id=1, source_target_pairs={{0,6},{1,7},{2,4},{3,5},{4,2},{5,3},{6,0},{7,1},{8,14},{9,15},{10,... | collective-permute-start | bytes 147464 | tf_op jit(solution)/shard_map/ppermute | solution.py:57
  24.5 2.2 %load.4.refs_7_.refs_3_ = bf16[1,2048,1024]{2,1,0:T(8,128)(2,1)S(1)} custom-call(bf16[1,2048,1024]{2,1,0:T(8,128)(2,1)} %refs_0_.4, bf16[4,96,256]{2,1,0:T(8,128)(2,1)S(1)} %one_sum.3.refs_1_.refs_0_), custom_call_target="tpu_custom_call" | custom-call | tf_op jit(solution)/shard_map/load/pallas_call | solution.py:43
  26.8 0.2 collective-permute-done.7.refs_3_
  27.0 0.4 shared_in.1
  27.6 1.7 %collective-permute-start.10 = (bf16[112,256]{1,0:T(8,128)(2,1)S(1)}, bf16[112,256]{1,0:T(8,128)(2,1)S(1)}, u32[]{:S(2)}, u32[]{:S(2)}) collective-permute-start(bf16[112,256]{1,0:T(8,128)(2,1)S(1)} %get-tuple-element.66), channel_id=1, source_target_pairs={{0,8},{8,0},{16,24},{24,16},{1,9},{9,1},{17,25},{25,17},{2,10},{10... | collective-permute-start | bytes 172040 | tf_op jit(solution)/shard_map/ppermute | solution.py:57
  29.3 2.6 %collective-permute-start.13 = (bf16[112,256]{1,0:T(8,128)(2,1)S(1)}, bf16[112,256]{1,0:T(8,128)(2,1)S(1)}, u32[]{:S(2)}, u32[]{:S(2)}) collective-permute-start(bf16[112,256]{1,0:T(8,128)(2,1)S(1)} %get-tuple-element.67), channel_id=1, source_target_pairs={{0,16},{8,24},{16,0},{24,8},{1,17},{9,25},{17,1},{25,9},{2,18},{10... | collective-permute-start | bytes 172040 | tf_op jit(solution)/shard_map/ppermute | solution.py:57
  32.0 1.6 %collective-permute-start.11 = (bf16[1,2,96,256]{3,2,1,0:T(8,128)(2,1)S(1)}, bf16[1,2,96,256]{3,2,1,0:T(8,128)(2,1)S(1)}, u32[]{:S(2)}, u32[]{:S(2)}) collective-permute-start(bf16[1,2,96,256]{3,2,1,0:T(8,128)(2,1)S(1)} %bitcast.28), channel_id=1, source_target_pairs={{0,2},{1,3},{2,0},{3,1},{4,6},{5,7},{6,4},{7,5},{8,10},{9,11},{10,... | collective-permute-start | bytes 294920 | tf_op jit(solution)/shard_map/ppermute | solution.py:57
  33.7 3.0 %update.3 = (f32[32,4,128,128]{3,2,1,0:T(8,128)}, f32[8,128]{1,0:T(8,128)S(1)}) custom-call(f32[2,96,128]{2,1,0:T(8,128)S(1)} %get-tuple-element.69.keys_ref, f32[2,3,32,256]{3,2,1,0:T(8,128)S(1)} %get-tuple-element.70.delta_ref, f32[2,32,256]{2,1,0:T(8,128)S(1)} %get-tuple-element.71.total_ref, f32[32,4,128,128]{3,2,1,0:T(8,128)} %states_ref.5, ...), custom_call_target="tpu_custom_call" | custom-call | tf_op jit(solution)/shard_map/update/pallas_call | solution.py:43
  36.7 1.2 %collective-permute-done.14.b_ref.refs_8_ = bf16[112,256]{1,0:T(8,128)(2,1)S(1)} collective-permute-done((bf16[112,256]{1,0:T(8,128)(2,1)S(1)}, bf16[112,256]{1,0:T(8,128)(2,1)S(1)}, u32[]{:S(2)}, u32[]{:S(2)}) %collective-permute-start.14) | collective-permute-done | bytes 57376 | tf_op jit(solution)/shard_map/ppermute | solution.py:57
  37.9 1.6 %collective-permute-start.15 = (bf16[1,2,96,256]{3,2,1,0:T(8,128)(2,1)S(1)}, bf16[1,2,96,256]{3,2,1,0:T(8,128)(2,1)S(1)}, u32[]{:S(2)}, u32[]{:S(2)}) collective-permute-start(bf16[1,2,96,256]{3,2,1,0:T(8,128)(2,1)S(1)} %bitcast.30), channel_id=1, source_target_pairs={{0,4},{1,5},{2,6},{3,7},{4,0},{5,1},{6,2},{7,3},{8,12},{9,13},{10,... | collective-permute-start | bytes 294920 | tf_op jit(solution)/shard_map/ppermute | solution.py:57
  39.5 0.6 collective-permute-start.12
  40.1 1.6 %load.5.refs_4_.refs_6_ = bf16[1,512,2048]{2,1,0:T(8,128)(2,1)S(1)} custom-call(bf16[1,512,2048]{2,1,0:T(8,128)(2,1)} %refs_0_.5, bf16[2,2,96,256]{3,2,1,0:T(8,128)(2,1)S(1)} %stack.4.refs_1_.refs_0_), custom_call_target="tpu_custom_call" | custom-call | tf_op jit(solution)/shard_map/load/pallas_call | solution.py:43
  41.7 1.9 %collective-permute-done.15 = bf16[1,2,96,256]{3,2,1,0:T(8,128)(2,1)S(1)} collective-permute-done((bf16[1,2,96,256]{3,2,1,0:T(8,128)(2,1)S(1)}, bf16[1,2,96,256]{3,2,1,0:T(8,128)(2,1)S(1)}, u32[]{:S(2)}, u32[]{:S(2)}) %collective-permute-start.15) | collective-permute-done | bytes 98336 | tf_op jit(solution)/shard_map/ppermute | solution.py:57
  43.6 1.6 %collective-permute-start.16 = (bf16[2,2,96,256]{3,2,1,0:T(8,128)(2,1)S(1)}, bf16[2,2,96,256]{3,2,1,0:T(8,128)(2,1)S(1)}, u32[]{:S(2)}, u32[]{:S(2)}) collective-permute-start(bf16[2,2,96,256]{3,2,1,0:T(8,128)(2,1)S(1)} %stack.5.refs_2_.refs_0_), channel_id=1, source_target_pairs={{0,2},{1,3},{2,0},{3,1},{4,6},{5,7},{6,4},{7,5},{8,10},{9,11},{10,... | collective-permute-start | bytes 589832 | tf_op jit(solution)/shard_map/ppermute | solution.py:57
  45.2 0.5 collective-permute-start.9
  45.7 3.8 %update.4 = (f32[32,4,128,128]{3,2,1,0:T(8,128)}, f32[8,128]{1,0:T(8,128)S(1)}) custom-call(f32[2,96,128]{2,1,0:T(8,128)S(1)} %get-tuple-element.69.keys_ref, f32[2,3,32,256]{3,2,1,0:T(8,128)S(1)} %get-tuple-element.70.delta_ref, f32[2,32,256]{2,1,0:T(8,128)S(1)} %get-tuple-element.71.total_ref, ...), custom_call_target="tpu_custom_call", output_to_operand_aliasing={{0}: (4, {})} | custom-call | tf_op jit(solution)/shard_map/update/pallas_call | solution.py:43
  49.6 0.9 %collective-permute-done.9.b_ref.refs_1_ = bf16[96,512]{1,0:T(8,128)(2,1)S(1)} collective-permute-done((bf16[96,512]{1,0:T(8,128)(2,1)S(1)}, bf16[96,512]{1,0:T(8,128)(2,1)S(1)}, u32[]{:S(2)}, u32[]{:S(2)}) %collective-permute-start.9) | collective-permute-done | bytes 98336 | tf_op jit(solution)/shard_map/ppermute | solution.py:57
  50.5 0.5 collective-permute-start.21
  51.2 1.5 %collective-permute-start.17 = (bf16[96,512]{1,0:T(8,128)(2,1)S(1)}, bf16[96,512]{1,0:T(8,128)(2,1)S(1)}, u32[]{:S(2)}, u32[]{:S(2)}) collective-permute-start(bf16[96,512]{1,0:T(8,128)(2,1)S(1)} %one_sum.5.a_ref), channel_id=1, source_target_pairs={{0,4},{1,5},{2,6},{3,7},{4,0},{5,1},{6,2},{7,3},{8,12},{9,13},{10,... | collective-permute-start | bytes 294920 | tf_op jit(solution)/shard_map/ppermute | solution.py:57
  52.8 0.6 expert_first.2
  53.4 0.6 expert_first.3
  54.0 1.2 %expert_rest.2 = (bf16[4,2,96,256]{3,2,1,0:T(8,128)(2,1)S(1)}, bf16[4,2,96,256]{3,2,1,0:T(8,128)(2,1)S(1)}, f32[192,1]{1,0:T(8,128)S(1)}) custom-call(s32[1]{0:T(128)} %bitcast.me_ref, bf16[2,2,96,256]{3,2,1,0:T(8,128)(2,1)S(1)} %collective-permute-done.18.refs_0_, bf16[2,2,96,256]{3,2,1,0:T(8,128)(2,1)S(1)} %collective-permute-done.19.refs_1_, ...), custom_call_target="tpu_custom_call" | custom-call | tf_op jit(solution)/shard_map/expert_rest/pallas_call | solution.py:43
  55.4 1.0 %collective-permute-done.17.refs_9_.b_ref = bf16[96,512]{1,0:T(8,128)(2,1)S(1)} collective-permute-done((bf16[96,512]{1,0:T(8,128)(2,1)S(1)}, bf16[96,512]{1,0:T(8,128)(2,1)S(1)}, u32[]{:S(2)}, u32[]{:S(2)}) %collective-permute-start.17) | collective-permute-done | bytes 98336 | tf_op jit(solution)/shard_map/ppermute | solution.py:57
  56.4 1.6 %expert_rest.3 = (bf16[4,2,96,256]{3,2,1,0:T(8,128)(2,1)S(1)}, bf16[4,2,96,256]{3,2,1,0:T(8,128)(2,1)S(1)}, f32[192,1]{1,0:T(8,128)}) custom-call(s32[1]{0:T(128)} %bitcast.me_ref, bf16[2,2,96,256]{3,2,1,0:T(8,128)(2,1)S(1)} %collective-permute-done.21.refs_0_, bf16[2,2,96,256]{3,2,1,0:T(8,128)(2,1)S(1)} %collective-permute-done.22.refs_1_, ...), custom_call_target="tpu_custom_call" | custom-call | tf_op jit(solution)/shard_map/expert_rest/pallas_call | solution.py:43
  58.1 1.5 %collective-permute-start.25 = (bf16[2,2,96,256]{3,2,1,0:T(8,128)(2,1)S(1)}, bf16[2,2,96,256]{3,2,1,0:T(8,128)(2,1)S(1)}, u32[]{:S(2)}, u32[]{:S(2)}) collective-permute-start(bf16[2,2,96,256]{3,2,1,0:T(8,128)(2,1)S(1)} %get-tuple-element.89), channel_id=1, source_target_pairs={{0,2},{1,3},{2,0},{3,1},{4,6},{5,7},{6,4},{7,5},{8,10},{9,11},{10,... | collective-permute-start | bytes 589832 | tf_op jit(solution)/shard_map/ppermute | solution.py:57
  59.8 1.5 %collective-permute-start.28 = (bf16[2,2,96,256]{3,2,1,0:T(8,128)(2,1)S(1)}, bf16[2,2,96,256]{3,2,1,0:T(8,128)(2,1)S(1)}, u32[]{:S(2)}, u32[]{:S(2)}) collective-permute-start(bf16[2,2,96,256]{3,2,1,0:T(8,128)(2,1)S(1)} %get-tuple-element.96), channel_id=1, source_target_pairs={{0,4},{1,5},{2,6},{3,7},{4,0},{5,1},{6,2},{7,3},{8,12},{9,13},{10,... | collective-permute-start | bytes 589832 | tf_op jit(solution)/shard_map/ppermute | solution.py:57
  61.5 2.9 %update.5 = (f32[32,4,128,128]{3,2,1,0:T(8,128)}, f32[8,128]{1,0:T(8,128)S(1)}) custom-call(f32[2,96,128]{2,1,0:T(8,128)S(1)} %get-tuple-element.69.keys_ref, f32[2,3,32,256]{3,2,1,0:T(8,128)S(1)} %get-tuple-element.70.delta_ref, f32[2,32,256]{2,1,0:T(8,128)S(1)} %get-tuple-element.71.total_ref, ...), custom_call_target="tpu_custom_call", output_to_operand_aliasing={{0}: (4, {})} | custom-call | tf_op jit(solution)/shard_map/update/pallas_call | solution.py:43
  64.5 1.0 %collective-permute-done.25.b_ref = bf16[2,2,96,256]{3,2,1,0:T(8,128)(2,1)S(1)} collective-permute-done((bf16[2,2,96,256]{3,2,1,0:T(8,128)(2,1)S(1)}, bf16[2,2,96,256]{3,2,1,0:T(8,128)(2,1)S(1)}, u32[]{:S(2)}, u32[]{:S(2)}) %collective-permute-start.25) | collective-permute-done | bytes 196640 | tf_op jit(solution)/shard_map/ppermute | solution.py:57
  65.5 1.5 %collective-permute-start.26 = (bf16[1,2,96,256]{3,2,1,0:T(8,128)(2,1)S(1)}, bf16[1,2,96,256]{3,2,1,0:T(8,128)(2,1)S(1)}, u32[]{:S(2)}, u32[]{:S(2)}) collective-permute-start(bf16[1,2,96,256]{3,2,1,0:T(8,128)(2,1)S(1)} %get-tuple-element.93), channel_id=1, source_target_pairs={{0,4},{1,5},{2,6},{3,7},{4,0},{5,1},{6,2},{7,3},{8,12},{9,13},{10,... | collective-permute-start | bytes 294920 | tf_op jit(solution)/shard_map/ppermute | solution.py:57
  67.1 1.6 %collective-permute-start.29 = (bf16[1,2,96,256]{3,2,1,0:T(8,128)(2,1)S(1)}, bf16[1,2,96,256]{3,2,1,0:T(8,128)(2,1)S(1)}, u32[]{:S(2)}, u32[]{:S(2)}) collective-permute-start(bf16[1,2,96,256]{3,2,1,0:T(8,128)(2,1)S(1)} %get-tuple-element.98), channel_id=1, source_target_pairs={{0,2},{1,3},{2,0},{3,1},{4,6},{5,7},{6,4},{7,5},{8,10},{9,11},{10,... | collective-permute-start | bytes 294920 | tf_op jit(solution)/shard_map/ppermute | solution.py:57
  68.7 1.6 %collective-permute-done.26.b_ref = bf16[1,2,96,256]{3,2,1,0:T(8,128)(2,1)S(1)} collective-permute-done((bf16[1,2,96,256]{3,2,1,0:T(8,128)(2,1)S(1)}, bf16[1,2,96,256]{3,2,1,0:T(8,128)(2,1)S(1)}, u32[]{:S(2)}, u32[]{:S(2)}) %collective-permute-start.26) | collective-permute-done | bytes 98336 | tf_op jit(solution)/shard_map/ppermute | solution.py:57
  70.3 0.6 collective-permute-start.27
  70.9 0.9 %collective-permute-done.29.b_ref = bf16[1,2,96,256]{3,2,1,0:T(8,128)(2,1)S(1)} collective-permute-done((bf16[1,2,96,256]{3,2,1,0:T(8,128)(2,1)S(1)}, bf16[1,2,96,256]{3,2,1,0:T(8,128)(2,1)S(1)}, u32[]{:S(2)}, u32[]{:S(2)}) %collective-permute-start.29) | collective-permute-done | bytes 98336 | tf_op jit(solution)/shard_map/ppermute | solution.py:57
  71.8 2.1 %collective-permute-start.30 = (bf16[96,256]{1,0:T(8,128)(2,1)S(1)}, bf16[96,256]{1,0:T(8,128)(2,1)S(1)}, u32[]{:S(2)}, u32[]{:S(2)}) collective-permute-start(bf16[96,256]{1,0:T(8,128)(2,1)S(1)} %get-tuple-element.99), channel_id=1, source_target_pairs={{0,16},{8,24},{16,0},{24,8},{1,17},{9,25},{17,1},{25,9},{2,18},{10... | collective-permute-start | bytes 147464 | tf_op jit(solution)/shard_map/ppermute | solution.py:57
  73.9 1.1 %collective-permute-start.31 = (bf16[96,256]{1,0:T(8,128)(2,1)S(1)}, bf16[96,256]{1,0:T(8,128)(2,1)S(1)}, u32[]{:S(2)}, u32[]{:S(2)}) collective-permute-start(bf16[96,256]{1,0:T(8,128)(2,1)S(1)} %get-tuple-element.100), channel_id=1, source_target_pairs={{0,24},{8,16},{16,8},{24,0},{1,25},{9,17},{17,9},{25,1},{2,26},{10... | collective-permute-start | bytes 147464 | tf_op jit(solution)/shard_map/ppermute | solution.py:57
  75.2 2.7 %collective-permute-done.30.refs_3_ = bf16[96,256]{1,0:T(8,128)(2,1)S(1)} collective-permute-done((bf16[96,256]{1,0:T(8,128)(2,1)S(1)}, bf16[96,256]{1,0:T(8,128)(2,1)S(1)}, u32[]{:S(2)}, u32[]{:S(2)}) %collective-permute-start.30) | collective-permute-done | bytes 49184 | tf_op jit(solution)/shard_map/ppermute | solution.py:57
  77.9 1.9 %collective-permute-done.31.refs_4_ = bf16[96,256]{1,0:T(8,128)(2,1)S(1)} collective-permute-done((bf16[96,256]{1,0:T(8,128)(2,1)S(1)}, bf16[96,256]{1,0:T(8,128)(2,1)S(1)}, u32[]{:S(2)}, u32[]{:S(2)}) %collective-permute-start.31) | collective-permute-done | bytes 49184 | tf_op jit(solution)/shard_map/ppermute | solution.py:57
  79.8 0.7 finish.1
  (56 shorter events, 2.0 us)
Async XLA Ops:
  0.6 7.2 %collective-permute-start = (bf16[96,256]{1,0:T(8,128)(2,1)}, bf16[96,256]{1,0:T(8,128)(2,1)S(1)}, u32[]{:S(2)}, u32[]{:S(2)}) collective-permute-start(bf16[96,256]{1,0:T(8,128)(2,1)} %bitcast.34), channel_id=1, source_target_pairs={{0,2},{1,3},{2,0},{3,1},{4,6},{5,7},{6,4},{7,5},{8,10},{9,11},{10,... | collective-permute-start | bytes 147464 | tf_op jit(solution)/shard_map/ppermute | solution.py:57
  3.6 4.3 %collective-permute-start.1 = (bf16[96,256]{1,0:T(8,128)(2,1)}, bf16[96,256]{1,0:T(8,128)(2,1)S(1)}, u32[]{:S(2)}, u32[]{:S(2)}) collective-permute-start(bf16[96,256]{1,0:T(8,128)(2,1)} %bitcast.35), channel_id=1, source_target_pairs={{0,4},{1,5},{2,6},{3,7},{4,0},{5,1},{6,2},{7,3},{8,12},{9,13},{10,... | collective-permute-start | bytes 147464 | tf_op jit(solution)/shard_map/ppermute | solution.py:57
  5.2 5.2 %collective-permute-start.2 = (bf16[96,256]{1,0:T(8,128)(2,1)}, bf16[96,256]{1,0:T(8,128)(2,1)S(1)}, u32[]{:S(2)}, u32[]{:S(2)}) collective-permute-start(bf16[96,256]{1,0:T(8,128)(2,1)} %bitcast.36), channel_id=1, source_target_pairs={{0,6},{1,7},{2,4},{3,5},{4,2},{5,3},{6,0},{7,1},{8,14},{9,15},{10,... | collective-permute-start | bytes 147464 | tf_op jit(solution)/shard_map/ppermute | solution.py:57
  5.2 5.3 %copy-start = (bf16[2048,4]{0,1:T(4,128)(2,1)S(1)}, bf16[2048,4]{0,1:T(4,128)(2,1)}, u32[]{:S(2)}) copy-start(bf16[2048,4]{0,1:T(4,128)(2,1)} %param.30) | copy-start | bytes 49156
  5.2 5.3 %copy-start.1 = (bf16[2048,4]{0,1:T(4,128)(2,1)S(1)}, bf16[2048,4]{0,1:T(4,128)(2,1)}, u32[]{:S(2)}) copy-start(bf16[2048,4]{0,1:T(4,128)(2,1)} %param.29) | copy-start | bytes 49156
  10.4 1.8 %collective-permute-start.3 = (bf16[4,96,256]{2,1,0:T(8,128)(2,1)S(1)}, bf16[4,96,256]{2,1,0:T(8,128)(2,1)S(1)}, u32[]{:S(2)}, u32[]{:S(2)}) collective-permute-start(bf16[4,96,256]{2,1,0:T(8,128)(2,1)S(1)} %stack.3.refs_1_.refs_0_), channel_id=1, source_target_pairs={{0,1},{1,0},{2,3},{3,2},{4,5},{5,4},{6,7},{7,6},{8,9},{9,8},{10,11... | collective-permute-start | bytes 589832 | tf_op jit(solution)/shard_map/ppermute | solution.py:57
  19.3 1.6 %collective-permute-start.4 = (bf16[4,96,256]{2,1,0:T(8,128)(2,1)S(1)}, bf16[4,96,256]{2,1,0:T(8,128)(2,1)S(1)}, u32[]{:S(2)}, u32[]{:S(2)}) collective-permute-start(bf16[4,96,256]{2,1,0:T(8,128)(2,1)S(1)} %get-tuple-element.59), channel_id=1, source_target_pairs={{0,1},{1,0},{2,3},{3,2},{4,5},{5,4},{6,7},{7,6},{8,9},{9,8},{10,11... | collective-permute-start | bytes 589832 | tf_op jit(solution)/shard_map/ppermute | solution.py:57
  21.0 5.8 %collective-permute-start.5 = (bf16[96,256]{1,0:T(8,128)(2,1)S(1)}, bf16[96,256]{1,0:T(8,128)(2,1)S(1)}, u32[]{:S(2)}, u32[]{:S(2)}) collective-permute-start(bf16[96,256]{1,0:T(8,128)(2,1)S(1)} %get-tuple-element.104), channel_id=1, source_target_pairs={{0,2},{1,3},{2,0},{3,1},{4,6},{5,7},{6,4},{7,5},{8,10},{9,11},{10,... | collective-permute-start | bytes 147464 | tf_op jit(solution)/shard_map/ppermute | solution.py:57
  21.6 5.2 %collective-permute-start.6 = (bf16[96,256]{1,0:T(8,128)(2,1)S(1)}, bf16[96,256]{1,0:T(8,128)(2,1)S(1)}, u32[]{:S(2)}, u32[]{:S(2)}) collective-permute-start(bf16[96,256]{1,0:T(8,128)(2,1)S(1)} %get-tuple-element.103), channel_id=1, source_target_pairs={{0,4},{1,5},{2,6},{3,7},{4,0},{5,1},{6,2},{7,3},{8,12},{9,13},{10,... | collective-permute-start | bytes 147464 | tf_op jit(solution)/shard_map/ppermute | solution.py:57
  22.0 5.0 %collective-permute-start.7 = (bf16[96,256]{1,0:T(8,128)(2,1)S(1)}, bf16[96,256]{1,0:T(8,128)(2,1)S(1)}, u32[]{:S(2)}, u32[]{:S(2)}) collective-permute-start(bf16[96,256]{1,0:T(8,128)(2,1)S(1)} %get-tuple-element.102), channel_id=1, source_target_pairs={{0,6},{1,7},{2,4},{3,5},{4,2},{5,3},{6,0},{7,1},{8,14},{9,15},{10,... | collective-permute-start | bytes 147464 | tf_op jit(solution)/shard_map/ppermute | solution.py:57
  27.5 9.2 %collective-permute-start.8 = (bf16[96,512]{1,0:T(8,128)(2,1)S(1)}, bf16[96,512]{1,0:T(8,128)(2,1)S(1)}, u32[]{:S(2)}, u32[]{:S(2)}) collective-permute-start(bf16[96,512]{1,0:T(8,128)(2,1)S(1)} %get-tuple-element.65), channel_id=1, source_target_pairs={{0,1},{1,0},{2,3},{3,2},{4,5},{5,4},{6,7},{7,6},{8,9},{9,8},{10,11... | collective-permute-start | bytes 294920 | tf_op jit(solution)/shard_map/ppermute | solution.py:57
  27.6 4.5 %collective-permute-start.10 = (bf16[112,256]{1,0:T(8,128)(2,1)S(1)}, bf16[112,256]{1,0:T(8,128)(2,1)S(1)}, u32[]{:S(2)}, u32[]{:S(2)}) collective-permute-start(bf16[112,256]{1,0:T(8,128)(2,1)S(1)} %get-tuple-element.66), channel_id=1, source_target_pairs={{0,8},{8,0},{16,24},{24,16},{1,9},{9,1},{17,25},{25,17},{2,10},{10... | collective-permute-start | bytes 172040 | tf_op jit(solution)/shard_map/ppermute | solution.py:57
  29.3 7.4 %collective-permute-start.13 = (bf16[112,256]{1,0:T(8,128)(2,1)S(1)}, bf16[112,256]{1,0:T(8,128)(2,1)S(1)}, u32[]{:S(2)}, u32[]{:S(2)}) collective-permute-start(bf16[112,256]{1,0:T(8,128)(2,1)S(1)} %get-tuple-element.67), channel_id=1, source_target_pairs={{0,16},{8,24},{16,0},{24,8},{1,17},{9,25},{17,1},{25,9},{2,18},{10... | collective-permute-start | bytes 172040 | tf_op jit(solution)/shard_map/ppermute | solution.py:57
  31.9 6.0 %collective-permute-start.14 = (bf16[112,256]{1,0:T(8,128)(2,1)S(1)}, bf16[112,256]{1,0:T(8,128)(2,1)S(1)}, u32[]{:S(2)}, u32[]{:S(2)}) collective-permute-start(bf16[112,256]{1,0:T(8,128)(2,1)S(1)} %get-tuple-element.68), channel_id=1, source_target_pairs={{0,24},{8,16},{16,8},{24,0},{1,25},{9,17},{17,9},{25,1},{2,26},{10... | collective-permute-start | bytes 172040 | tf_op jit(solution)/shard_map/ppermute | solution.py:57
  32.0 7.5 %collective-permute-start.11 = (bf16[1,2,96,256]{3,2,1,0:T(8,128)(2,1)S(1)}, bf16[1,2,96,256]{3,2,1,0:T(8,128)(2,1)S(1)}, u32[]{:S(2)}, u32[]{:S(2)}) collective-permute-start(bf16[1,2,96,256]{3,2,1,0:T(8,128)(2,1)S(1)} %bitcast.28), channel_id=1, source_target_pairs={{0,2},{1,3},{2,0},{3,1},{4,6},{5,7},{6,4},{7,5},{8,10},{9,11},{10,... | collective-permute-start | bytes 294920 | tf_op jit(solution)/shard_map/ppermute | solution.py:57
  37.9 5.7 %collective-permute-start.15 = (bf16[1,2,96,256]{3,2,1,0:T(8,128)(2,1)S(1)}, bf16[1,2,96,256]{3,2,1,0:T(8,128)(2,1)S(1)}, u32[]{:S(2)}, u32[]{:S(2)}) collective-permute-start(bf16[1,2,96,256]{3,2,1,0:T(8,128)(2,1)S(1)} %bitcast.30), channel_id=1, source_target_pairs={{0,4},{1,5},{2,6},{3,7},{4,0},{5,1},{6,2},{7,3},{8,12},{9,13},{10,... | collective-permute-start | bytes 294920 | tf_op jit(solution)/shard_map/ppermute | solution.py:57
  39.5 10.9 %collective-permute-start.12 = (bf16[2,2,96,256]{3,2,1,0:T(8,128)(2,1)S(1)}, bf16[2,2,96,256]{3,2,1,0:T(8,128)(2,1)S(1)}, u32[]{:S(2)}, u32[]{:S(2)}) collective-permute-start(bf16[2,2,96,256]{3,2,1,0:T(8,128)(2,1)S(1)} %stack.4.refs_1_.refs_0_), channel_id=1, source_target_pairs={{0,4},{1,5},{2,6},{3,7},{4,0},{5,1},{6,2},{7,3},{8,12},{9,13},{10,... | collective-permute-start | bytes 589832 | tf_op jit(solution)/shard_map/ppermute | solution.py:57
  43.6 7.4 %collective-permute-start.16 = (bf16[2,2,96,256]{3,2,1,0:T(8,128)(2,1)S(1)}, bf16[2,2,96,256]{3,2,1,0:T(8,128)(2,1)S(1)}, u32[]{:S(2)}, u32[]{:S(2)}) collective-permute-start(bf16[2,2,96,256]{3,2,1,0:T(8,128)(2,1)S(1)} %stack.5.refs_2_.refs_0_), channel_id=1, source_target_pairs={{0,2},{1,3},{2,0},{3,1},{4,6},{5,7},{6,4},{7,5},{8,10},{9,11},{10,... | collective-permute-start | bytes 589832 | tf_op jit(solution)/shard_map/ppermute | solution.py:57
  45.2 5.2 %collective-permute-start.9 = (bf16[96,512]{1,0:T(8,128)(2,1)S(1)}, bf16[96,512]{1,0:T(8,128)(2,1)S(1)}, u32[]{:S(2)}, u32[]{:S(2)}) collective-permute-start(bf16[96,512]{1,0:T(8,128)(2,1)S(1)} %one_sum.4.refs_1_.refs_3_.a_ref), channel_id=1, source_target_pairs={{0,2},{1,3},{2,0},{3,1},{4,6},{5,7},{6,4},{7,5},{8,10},{9,11},{10,... | collective-permute-start | bytes 294920 | tf_op jit(solution)/shard_map/ppermute | solution.py:57
  45.7 8.2 %collective-permute-start.18 = (bf16[2,2,96,256]{3,2,1,0:T(8,128)(2,1)S(1)}, bf16[2,2,96,256]{3,2,1,0:T(8,128)(2,1)S(1)}, u32[]{:S(2)}, u32[]{:S(2)}) collective-permute-start(bf16[2,2,96,256]{3,2,1,0:T(8,128)(2,1)S(1)} %stack.4.refs_1_.refs_0_), channel_id=1, source_target_pairs={{0,1},{1,0},{2,3},{3,2},{4,5},{5,4},{6,7},{7,6},{8,9},{9,8},{10,11... | collective-permute-start | bytes 589832 | tf_op jit(solution)/shard_map/ppermute | solution.py:57
  50.5 3.5 %collective-permute-start.19 = (bf16[2,2,96,256]{3,2,1,0:T(8,128)(2,1)S(1)}, bf16[2,2,96,256]{3,2,1,0:T(8,128)(2,1)S(1)}, u32[]{:S(2)}, u32[]{:S(2)}) collective-permute-start(bf16[2,2,96,256]{3,2,1,0:T(8,128)(2,1)S(1)} %keep.2), channel_id=1, source_target_pairs={{0,1},{1,0},{2,3},{3,2},{4,5},{5,4},{6,7},{7,6},{8,9},{9,8},{10,11... | collective-permute-start | bytes 589832 | tf_op jit(solution)/shard_map/ppermute | solution.py:57
  50.5 4.9 %collective-permute-start.21 = (bf16[2,2,96,256]{3,2,1,0:T(8,128)(2,1)S(1)}, bf16[2,2,96,256]{3,2,1,0:T(8,128)(2,1)S(1)}, u32[]{:S(2)}, u32[]{:S(2)}) collective-permute-start(bf16[2,2,96,256]{3,2,1,0:T(8,128)(2,1)S(1)} %stack.5.refs_2_.refs_0_), channel_id=1, source_target_pairs={{0,1},{1,0},{2,3},{3,2},{4,5},{5,4},{6,7},{7,6},{8,9},{9,8},{10,11... | collective-permute-start | bytes 589832 | tf_op jit(solution)/shard_map/ppermute | solution.py:57
  51.1 5.4 %collective-permute-start.22 = (bf16[2,2,96,256]{3,2,1,0:T(8,128)(2,1)S(1)}, bf16[2,2,96,256]{3,2,1,0:T(8,128)(2,1)S(1)}, u32[]{:S(2)}, u32[]{:S(2)}) collective-permute-start(bf16[2,2,96,256]{3,2,1,0:T(8,128)(2,1)S(1)} %keep.3), channel_id=1, source_target_pairs={{0,1},{1,0},{2,3},{3,2},{4,5},{5,4},{6,7},{7,6},{8,9},{9,8},{10,11... | collective-permute-start | bytes 589832 | tf_op jit(solution)/shard_map/ppermute | solution.py:57
  51.2 5.2 %collective-permute-start.17 = (bf16[96,512]{1,0:T(8,128)(2,1)S(1)}, bf16[96,512]{1,0:T(8,128)(2,1)S(1)}, u32[]{:S(2)}, u32[]{:S(2)}) collective-permute-start(bf16[96,512]{1,0:T(8,128)(2,1)S(1)} %one_sum.5.a_ref), channel_id=1, source_target_pairs={{0,4},{1,5},{2,6},{3,7},{4,0},{5,1},{6,2},{7,3},{8,12},{9,13},{10,... | collective-permute-start | bytes 294920 | tf_op jit(solution)/shard_map/ppermute | solution.py:57
  55.2 2.8 %collective-permute-start.20 = (bf16[4,2,96,256]{3,2,1,0:T(8,128)(2,1)S(1)}, bf16[4,2,96,256]{3,2,1,0:T(8,128)(2,1)S(1)}, u32[]{:S(2)}, u32[]{:S(2)}) collective-permute-start(bf16[4,2,96,256]{3,2,1,0:T(8,128)(2,1)S(1)} %get-tuple-element.80), channel_id=1, source_target_pairs={{0,1},{1,0},{2,3},{3,2},{4,5},{5,4},{6,7},{7,6},{8,9},{9,8},{10,11... | collective-permute-start | bytes 1179656 | tf_op jit(solution)/shard_map/ppermute | solution.py:57
  58.0 1.7 %collective-permute-start.23 = (bf16[4,2,96,256]{3,2,1,0:T(8,128)(2,1)S(1)}, bf16[4,2,96,256]{3,2,1,0:T(8,128)(2,1)S(1)}, u32[]{:S(2)}, u32[]{:S(2)}) collective-permute-start(bf16[4,2,96,256]{3,2,1,0:T(8,128)(2,1)S(1)} %get-tuple-element.85), channel_id=1, source_target_pairs={{0,1},{1,0},{2,3},{3,2},{4,5},{5,4},{6,7},{7,6},{8,9},{9,8},{10,11... | collective-permute-start | bytes 1179656 | tf_op jit(solution)/shard_map/ppermute | solution.py:57
  58.1 7.4 %collective-permute-start.25 = (bf16[2,2,96,256]{3,2,1,0:T(8,128)(2,1)S(1)}, bf16[2,2,96,256]{3,2,1,0:T(8,128)(2,1)S(1)}, u32[]{:S(2)}, u32[]{:S(2)}) collective-permute-start(bf16[2,2,96,256]{3,2,1,0:T(8,128)(2,1)S(1)} %get-tuple-element.89), channel_id=1, source_target_pairs={{0,2},{1,3},{2,0},{3,1},{4,6},{5,7},{6,4},{7,5},{8,10},{9,11},{10,... | collective-permute-start | bytes 589832 | tf_op jit(solution)/shard_map/ppermute | solution.py:57
  59.8 7.2 %collective-permute-start.28 = (bf16[2,2,96,256]{3,2,1,0:T(8,128)(2,1)S(1)}, bf16[2,2,96,256]{3,2,1,0:T(8,128)(2,1)S(1)}, u32[]{:S(2)}, u32[]{:S(2)}) collective-permute-start(bf16[2,2,96,256]{3,2,1,0:T(8,128)(2,1)S(1)} %get-tuple-element.96), channel_id=1, source_target_pairs={{0,4},{1,5},{2,6},{3,7},{4,0},{5,1},{6,2},{7,3},{8,12},{9,13},{10,... | collective-permute-start | bytes 589832 | tf_op jit(solution)/shard_map/ppermute | solution.py:57
  61.5 3.0 %collective-permute-start.24 = (bf16[96,256]{1,0:T(8,128)(2,1)S(1)}, bf16[96,256]{1,0:T(8,128)(2,1)S(1)}, u32[]{:S(2)}, u32[]{:S(2)}) collective-permute-start(bf16[96,256]{1,0:T(8,128)(2,1)S(1)} %shared_hidden.1.a_ref), channel_id=1, source_target_pairs={{0,1},{1,0},{2,3},{3,2},{4,5},{5,4},{6,7},{7,6},{8,9},{9,8},{10,11... | collective-permute-start | bytes 147464 | tf_op jit(solution)/shard_map/ppermute | solution.py:57
  65.5 4.7 %collective-permute-start.26 = (bf16[1,2,96,256]{3,2,1,0:T(8,128)(2,1)S(1)}, bf16[1,2,96,256]{3,2,1,0:T(8,128)(2,1)S(1)}, u32[]{:S(2)}, u32[]{:S(2)}) collective-permute-start(bf16[1,2,96,256]{3,2,1,0:T(8,128)(2,1)S(1)} %get-tuple-element.93), channel_id=1, source_target_pairs={{0,4},{1,5},{2,6},{3,7},{4,0},{5,1},{6,2},{7,3},{8,12},{9,13},{10,... | collective-permute-start | bytes 294920 | tf_op jit(solution)/shard_map/ppermute | solution.py:57
  67.1 4.7 %collective-permute-start.29 = (bf16[1,2,96,256]{3,2,1,0:T(8,128)(2,1)S(1)}, bf16[1,2,96,256]{3,2,1,0:T(8,128)(2,1)S(1)}, u32[]{:S(2)}, u32[]{:S(2)}) collective-permute-start(bf16[1,2,96,256]{3,2,1,0:T(8,128)(2,1)S(1)} %get-tuple-element.98), channel_id=1, source_target_pairs={{0,2},{1,3},{2,0},{3,1},{4,6},{5,7},{6,4},{7,5},{8,10},{9,11},{10,... | collective-permute-start | bytes 294920 | tf_op jit(solution)/shard_map/ppermute | solution.py:57
  70.3 5.0 %collective-permute-start.27 = (bf16[96,256]{1,0:T(8,128)(2,1)S(1)}, bf16[96,256]{1,0:T(8,128)(2,1)S(1)}, u32[]{:S(2)}, u32[]{:S(2)}) collective-permute-start(bf16[96,256]{1,0:T(8,128)(2,1)S(1)} %get-tuple-element.95), channel_id=1, source_target_pairs={{0,8},{8,0},{16,24},{24,16},{1,9},{9,1},{17,25},{25,17},{2,10},{10... | collective-permute-start | bytes 147464 | tf_op jit(solution)/shard_map/ppermute | solution.py:57
  71.8 6.1 %collective-permute-start.30 = (bf16[96,256]{1,0:T(8,128)(2,1)S(1)}, bf16[96,256]{1,0:T(8,128)(2,1)S(1)}, u32[]{:S(2)}, u32[]{:S(2)}) collective-permute-start(bf16[96,256]{1,0:T(8,128)(2,1)S(1)} %get-tuple-element.99), channel_id=1, source_target_pairs={{0,16},{8,24},{16,0},{24,8},{1,17},{9,25},{17,1},{25,9},{2,18},{10... | collective-permute-start | bytes 147464 | tf_op jit(solution)/shard_map/ppermute | solution.py:57
  73.9 5.9 %collective-permute-start.31 = (bf16[96,256]{1,0:T(8,128)(2,1)S(1)}, bf16[96,256]{1,0:T(8,128)(2,1)S(1)}, u32[]{:S(2)}, u32[]{:S(2)}) collective-permute-start(bf16[96,256]{1,0:T(8,128)(2,1)S(1)} %get-tuple-element.100), channel_id=1, source_target_pairs={{0,24},{8,16},{16,8},{24,0},{1,25},{9,17},{17,9},{25,1},{2,26},{10... | collective-permute-start | bytes 147464 | tf_op jit(solution)/shard_map/ppermute | solution.py:57

commit v7 on v5

--- a/solution.py
+++ b/solution.py
@@ -351,7 +351,7 @@
             pltpu.VMEM(states.shape, F32),
             pltpu.VMEM((key_heads, seqs * SLOTS, DK), F32),
             pltpu.VMEM((value_heads, seqs * SLOTS, DV), F32),
-            pltpu.SemaphoreType.DMA((5,)),
+            pltpu.SemaphoreType.DMA((9,)),
         ],
     )
 
@@ -580,7 +580,7 @@
 
 
 def expert_rest(me, pieces, gain_inv, w, pre, sq, down, weights, order, order_out, steps, whole, after):
-    count = 2 * pieces[0].shape[0]
+    count = len(order_out)
     shape = (count, *pieces[0].shape[1:])
     return call(
         functools.partial(expert_rest_kernel, order, order_out, steps, whole),
@@ -661,44 +661,81 @@
 
 def shared_in_kernel(me_ref, x_ref, w_ref, *refs):
     refs = refs[-2:]
+    chunks, _, width = refs[0].shape
     half = w_ref.shape[1] // 2
     part = half // 2
     pre = dot(x_ref[...], w_ref[...]).astype(BF16)
     odd = me_ref[0] % 2
     for core in range(2):
-        for up in range(2):
-            piece = pre[:, up * half + core * part : up * half + (core + 1) * part]
+        for n in range(chunks):
+            up, at = divmod(n * width, part)
+            start = up * half + core * part + at
+            piece = pre[:, start : start + width]
 
             @pl.when(odd == core)
             def _():
-                refs[0][:, up * part : (up + 1) * part] = piece
+                refs[0][n] = piece
 
             @pl.when(odd != core)
             def _():
-                refs[1][:, up * part : (up + 1) * part] = piece
+                refs[1][n] = piece
 
 
 def shared_in(me, x, w, after):
-    shape = (x.shape[0], w.shape[1] // 2)
+    rows, width = x.shape
+    shape = (w.shape[1] // 2 // width, rows, width)
     return call(
         shared_in_kernel, "shared_in", [pltpu.VMEM(shape, BF16)] * 2, (me,), (x, w), after
     )
 
 
+def open_kernel(a_ref, b_ref, keep_ref, received_ref, *refs):
+    out_ref = refs[-1]
+    rows = out_ref.shape[2]
+    out_ref[0, 0] = a_ref[:rows, :]
+    out_ref[0, 1] = b_ref[:rows, :]
+    out_ref[1] = add(keep_ref[...], received_ref[...])
+
+
+def open_side(a, b, keep, received, after):
+    shape = (2, *keep.shape)
+    [out] = call(open_kernel, "open", [pltpu.VMEM(shape, BF16)], (), (a, b, keep, received), after)
+    return out
+
+
+def grow_kernel(mine_ref, received_ref, *refs):
+    out_ref = refs[-1]
+    count = mine_ref.shape[0] - 1
+    out_ref[:count] = mine_ref[:count]
+    out_ref[count : 2 * count] = received_ref[:count]
+    out_ref[2 * count] = add(mine_ref[count], received_ref[count])
+
+
+def grow(mine, received, after):
+    shape = (2 * mine.shape[0] - 1, *mine.shape[1:])
+    [out] = call(grow_kernel, "grow", [pltpu.VMEM(shape, BF16)], (), (mine, received), after)
+    return out
+
+
 def shared_hidden_kernel(features, a_ref, b_ref, sq_ref, *refs):
     out_ref = refs[-1]
-    rows = a_ref.shape[0]
-    half = a_ref.shape[1] // 2
+    last, chunks, rows, width = a_ref.shape
     inverse = lax.rsqrt(sq_ref[:rows, :] / features + EPS)
-    pre = (a_ref[...].astype(F32) + b_ref[...].astype(F32)) * inverse
-    out_ref[...] = (silu(pre[:, :half]) * pre[:, half:]).astype(BF16)
+    pre = [
+        (a_ref[last - 1, n].astype(F32) + b_ref[last - 1, n].astype(F32)) * inverse
+        for n in range(chunks)
+    ]
+    for n in range(chunks // 2):
+        columns = slice(n * width, (n + 1) * width)
+        out_ref[:, columns] = (silu(pre[n]) * pre[chunks // 2 + n]).astype(BF16)
 
 
 def shared_hidden(features, a, b, sq, after):
+    _, chunks, rows, width = a.shape
     [out] = call(
         functools.partial(shared_hidden_kernel, features),
         "shared_hidden",
-        [pltpu.VMEM((a.shape[0], a.shape[1] // 2), BF16)],
+        [pltpu.VMEM((rows, chunks // 2 * width), BF16)],
         (),
         (a, b, sq),
         after,
@@ -790,7 +827,7 @@
 
     merged = one_sum(own, exchange(sib, "head", 1))
     received = [exchange(merged[p], "head", 2 * p) for p in range(1, pairs)]
-    w_in, w_down = load((w_expert_in, w_expert_out), (merged,))
+    [w_in] = load((w_expert_in,), (merged,))
     resid, x, *messages = make_rows(merged, received, mine, gain_mine, extra, (w_in,))
 
     half = seq_count // 2
@@ -799,42 +836,41 @@
     natural, reverse = list(range(pairs)), bit_reversed(pairs)
     blocks = tuple(range(seqs // PER_BLOCK))
     quarters = [blocks[len(blocks) * n // 4 : len(blocks) * (n + 1) // 4] for n in range(4)]
-    shared_pre, sent = shared_in(me, x, w_shared_in, ())
-    shared_pre = one_sum(shared_pre, exchange(sent, "head", 1))
-    shared_received = exchange(shared_pre, "head", axes[0])
-    sides, tie = [], ()
-    for slab, bits in ((slabs[:half], axes), (slabs[half:], axes[::-1])):
-        if half == 2:
-            side = slab_pair(*slab, rows, tie[:2])[None]
+    shared_keep, sent = shared_in(me, x, w_shared_in, ())
+    shared_received = exchange(sent, "head", 1)
+    [w_down] = load((w_expert_out,), (shared_keep,))
+    if half == 2:
+        side = open_side(*slabs[:2], shared_keep, shared_received, (*slabs[2:], w_down))
+    else:
+        rows_only = jnp.stack([m[:rows] for m in slabs[:half]])
+        side = jnp.stack([rows_only, add(shared_keep, shared_received)])
+    if half == 2:
+        other = slab_pair(*slabs[2:], rows, ())[None]
+    else:
+        other = jnp.stack([m[:rows] for m in slabs[half:]])[None]
+    states_out, done = update(
+        keys, deltas, totals, states, quarters[0] + quarters[1], (side, other)
+    )
+    for bit in axes[:0:-1]:
+        received = exchange(other, "head", bit)
+        if other.shape[0] == 1:
+            other = stack((other[0], received[0]), (done,))
         else:
-            side = jnp.stack([m[:rows] for m in slab])[None]
-        if not sides:
-            states_out, done = update(keys, deltas, totals, states, quarters[0], (side,))
-            tie = (done, shared_pre)
-        for bit in bits[:-1]:
-            received = exchange(side, "head", bit)
-            if side.shape[0] == 1:
-                side = stack((side[0], received[0]), tie if sides else ())
-            else:
-                side = jnp.concatenate([side, received])
-        if not sides:
-            states_out, done = update(keys, deltas, totals, states, quarters[1], (side,), states_out)
-            tie = (*tie, done, shared_received)
-        sides.append([side, exchange(side, "head", bits[-1])])
+            other = jnp.concatenate([other, received])
+    for bit in axes[:-1]:
+        side = grow(side, exchange(side, "head", bit), (done, other))
+    sides = [[side, exchange(side, "head", axes[-1])]]
+    sides.append([other, exchange(other, "head", axes[0])])
     siblings = [[exchange(piece, "head", 1) for piece in side] for side in sides]
     middle = pairs // 2
     orders = tuple((tuple(o[:middle]), tuple(o[middle:])) for o in (natural, reverse))
 
-    shared_pre = one_sum(shared_pre, shared_received, (sides[0][1], sides[1][1]))
-    for bit in axes[1:-1]:
-        shared_pre = one_sum(shared_pre, exchange(shared_pre, "head", bit))
-    shared_received = exchange(shared_pre, "head", axes[-1])
-    firsts = [
-        expert_first(me, side, gain_inv, w_in, order, (done,)) for side, order in zip(sides, orders)
-    ]
+    firsts = []
+    for side, order in zip(sides, orders):
+        firsts.append(expert_first(me, side, gain_inv, w_in, order, (done,)))
+        done = firsts[-1][1]
     owns, sibs, squares = [], [], []
     weights = (extra, *messages)
-    ties = ((), (shared_received,))
     for n, order_out in enumerate((reverse, natural)):
         own, sib, square = expert_rest(
             me,
@@ -848,7 +884,7 @@
             order_out,
             steps,
             n == 0,
-            ties[n],
+            tuple(owns),
         )
         owns.append(own)
         sibs.append(sib)
@@ -863,7 +899,7 @@
             states_out, done = update(
                 keys, deltas, totals, states, quarters[2], tuple(owns), states_out
             )
-            hidden = shared_hidden(features, shared_pre, shared_received, squares[0], tuple(owns))
+            hidden = shared_hidden(features, *sides[0], squares[0], tuple(owns))
             hidden_received = exchange(hidden, "head", 1)
             tie = (done, hidden_received)
     base = shared_out(me, hidden, hidden_received, resid, w_shared_out)

time: 79.8 us -> 79.6 us (level)
  waiting for transfers between devices: 16.2 us -> 21.2 us
  starting transfers between devices: 30 us -> 26.3 us
  Pallas kernels: 32.3 us -> 30.8 us
    ppermute x32 -> x30, waiting for transfers between devices: 16.2 us -> 21.2 us  [exchange(): return lax.ppermute(x, axis, [(i, i ^ bit) for i in range(size)])]
    ppermute x32 -> x30, starting transfers between devices: 30 us -> 26.3 us  [exchange(): return lax.ppermute(x, axis, [(i, i ^ bit) for i in range(size)])]
    pallas_call x31 -> x29, Pallas kernels: 32.3 us -> 30.8 us  [call(): pl.pallas_call(body, out_shape=tuple(out_shapes), in_specs=[SMEM_SPEC] *...]
  transfers between devices with their start and end apart: 32 -> 30, of which waited for: 12 -> 13; matrix products, arithmetic and copies ran while one was open for 0% -> 0% of each run, Pallas kernels for 30% -> 28%
where the time goes in v7:
time: 79.6 us; the launch traced here: 79.3 us
  Pallas kernels  30.8 us (39%)
  starting transfers between devices  26.3 us (33%)
  waiting for transfers between devices  21.2 us (27%)
  between operations  0.95 us (1%)
    pallas_call x29, Pallas kernels, call(): pl.pallas_call(body, out_shape=tuple(out_shapes), in_specs=[SMEM_SPEC] *...  30.8 us
    ppermute x30, starting transfers between devices, exchange(): return lax.ppermute(x, axis, [(i, i ^ bit) for i in range(size)])  26.3 us
    ppermute x30, waiting for transfers between devices, exchange(): return lax.ppermute(x, axis, [(i, i ^ bit) for i in range(size)])  21.2 us
  transfers between devices with their start and end apart: 30, of which 13 were waited for; matrix products, arithmetic and copies ran while one was open for 0% of the time, Pallas kernels for 28%

profile of v7, /device:TPU:0, one launch (start us, length us, event | category | flops | bytes accessed | tf_op | source)
XLA Modules:
  0.0 79.3 jit_solution(11155846146292750205)
XLA Ops:
  0.6 3.0 %collective-permute-start = (bf16[96,256]{1,0:T(8,128)(2,1)}, bf16[96,256]{1,0:T(8,128)(2,1)S(1)}, u32[]{:S(2)}, u32[]{:S(2)}) collective-permute-start(bf16[96,256]{1,0:T(8,128)(2,1)} %bitcast.30), channel_id=1, source_target_pairs={{0,2},{1,3},{2,0},{3,1},{4,6},{5,7},{6,4},{7,5},{8,10},{9,11},{10,... | collective-permute-start | bytes 147464 | tf_op jit(solution)/shard_map/ppermute | solution.py:57
  3.6 1.5 %collective-permute-start.1 = (bf16[96,256]{1,0:T(8,128)(2,1)}, bf16[96,256]{1,0:T(8,128)(2,1)S(1)}, u32[]{:S(2)}, u32[]{:S(2)}) collective-permute-start(bf16[96,256]{1,0:T(8,128)(2,1)} %bitcast.31), channel_id=1, source_target_pairs={{0,4},{1,5},{2,6},{3,7},{4,0},{5,1},{6,2},{7,3},{8,12},{9,13},{10,... | collective-permute-start | bytes 147464 | tf_op jit(solution)/shard_map/ppermute | solution.py:57
  5.2 2.6 %bring.1 = (bf16[96,256]{1,0:T(8,128)(2,1)S(1)}, bf16[2048,256]{1,0:T(8,128)(2,1)S(1)}, bf16[2048,256]{1,0:T(8,128)(2,1)S(1)}, bf16[2048,512]{1,0:T(8,128)(2,1)S...) custom-call(s32[1]{0:T(128)} %bitcast.me_ref, ...), custom_call_target="tpu_custom_call" | custom-call | tf_op jit(solution)/shard_map/bring/pallas_call | solution.py:43
  7.9 2.4 %collective-permute-done.2.refs_3_ = bf16[96,256]{1,0:T(8,128)(2,1)S(1)} collective-permute-done((bf16[96,256]{1,0:T(8,128)(2,1)}, bf16[96,256]{1,0:T(8,128)(2,1)S(1)}, u32[]{:S(2)}, u32[]{:S(2)}) %collective-permute-start.2) | collective-permute-done | bytes 49184 | tf_op jit(solution)/shard_map/ppermute | solution.py:57
  10.5 1.6 %load.3.refs_8_ = bf16[2048,512]{1,0:T(8,128)(2,1)S(1)} custom-call(bf16[2048,512]{1,0:T(8,128)(2,1)} %refs_0_.3, bf16[4,96,256]{2,1,0:T(8,128)(2,1)S(1)} %stack.2.refs_1_.refs_0_), custom_call_target="tpu_custom_call" | custom-call | tf_op jit(solution)/shard_map/load/pallas_call | solution.py:43
  12.1 7.1 %front.1 = (bf16[4,96,256]{2,1,0:T(8,128)(2,1)S(1)}, bf16[4,96,256]{2,1,0:T(8,128)(2,1)S(1)}, f32[2,96,128]{2,1,0:T(8,128)S(1)}, f32[2,3,32,256]{3,2,1,0:T(8,128)S(1)}, f32[2,32,256]{2,1,0:T(8,128)S(1)}) custom-call(s32[1]{0:T(128)} %bitcast.me_ref, bf16[4,96,256]{2,1,0:T(8,128)(2,1)S(1)} %stack.2.refs_1_.refs_0_, ...), custom_call_target="tpu_custom_call" | custom-call | tf_op jit(solution)/shard_map/front/pallas_call | solution.py:43
  19.3 0.5 collective-permute-start.4
  19.8 1.1 %collective-permute-done.4.b_ref = bf16[4,96,256]{2,1,0:T(8,128)(2,1)S(1)} collective-permute-done((bf16[4,96,256]{2,1,0:T(8,128)(2,1)S(1)}, bf16[4,96,256]{2,1,0:T(8,128)(2,1)S(1)}, u32[]{:S(2)}, u32[]{:S(2)}) %collective-permute-start.4) | collective-permute-done | bytes 196640 | tf_op jit(solution)/shard_map/ppermute | solution.py:57
  21.0 0.6 collective-permute-start.5
  21.6 0.4 collective-permute-start.6
  22.0 2.5 %collective-permute-start.7 = (bf16[96,256]{1,0:T(8,128)(2,1)S(1)}, bf16[96,256]{1,0:T(8,128)(2,1)S(1)}, u32[]{:S(2)}, u32[]{:S(2)}) collective-permute-start(bf16[96,256]{1,0:T(8,128)(2,1)S(1)} %get-tuple-element.102), channel_id=1, source_target_pairs={{0,6},{1,7},{2,4},{3,5},{4,2},{5,3},{6,0},{7,1},{8,14},{9,15},{10,... | collective-permute-start | bytes 147464 | tf_op jit(solution)/shard_map/ppermute | solution.py:57
  24.5 2.2 %load.4.refs_7_.refs_3_ = bf16[1,2048,1024]{2,1,0:T(8,128)(2,1)S(1)} custom-call(bf16[1,2048,1024]{2,1,0:T(8,128)(2,1)} %refs_0_.4, bf16[4,96,256]{2,1,0:T(8,128)(2,1)S(1)} %one_sum.1.refs_1_.refs_0_), custom_call_target="tpu_custom_call" | custom-call | tf_op jit(solution)/shard_map/load/pallas_call | solution.py:43
  26.8 0.2 collective-permute-done.7.refs_3_
  27.0 0.4 shared_in.1
  27.6 1.7 %collective-permute-start.8 = (bf16[112,256]{1,0:T(8,128)(2,1)S(1)}, bf16[112,256]{1,0:T(8,128)(2,1)S(1)}, u32[]{:S(2)}, u32[]{:S(2)}) collective-permute-start(bf16[112,256]{1,0:T(8,128)(2,1)S(1)} %get-tuple-element.63), channel_id=1, source_target_pairs={{0,8},{8,0},{16,24},{24,16},{1,9},{9,1},{17,25},{25,17},{2,10},{10... | collective-permute-start | bytes 172040 | tf_op jit(solution)/shard_map/ppermute | solution.py:57
  29.3 2.6 %collective-permute-start.10 = (bf16[112,256]{1,0:T(8,128)(2,1)S(1)}, bf16[112,256]{1,0:T(8,128)(2,1)S(1)}, u32[]{:S(2)}, u32[]{:S(2)}) collective-permute-start(bf16[112,256]{1,0:T(8,128)(2,1)S(1)} %get-tuple-element.67), channel_id=1, source_target_pairs={{0,16},{8,24},{16,0},{24,8},{1,17},{9,25},{17,1},{25,9},{2,18},{10... | collective-permute-start | bytes 172040 | tf_op jit(solution)/shard_map/ppermute | solution.py:57
  32.0 1.6 %load.5.refs_2_.refs_6_ = bf16[1,512,2048]{2,1,0:T(8,128)(2,1)S(1)} custom-call(bf16[1,512,2048]{2,1,0:T(8,128)(2,1)} %refs_0_.5, bf16[2,96,256]{2,1,0:T(8,128)(2,1)S(1)} %get-tuple-element.65.refs_1_.keep_ref), custom_call_target="tpu_custom_call" | custom-call | tf_op jit(solution)/shard_map/load/pallas_call | solution.py:43
  33.6 2.2 %collective-permute-done.10.refs_0_.a_ref.refs_7_ = bf16[112,256]{1,0:T(8,128)(2,1)S(1)} collective-permute-done((bf16[112,256]{1,0:T(8,128)(2,1)S(1)}, bf16[112,256]{1,0:T(8,128)(2,1)S(1)}, u32[]{:S(2)}, u32[]{:S(2)}) %collective-permute-start.10) | collective-permute-done | bytes 57376 | tf_op jit(solution)/shard_map/ppermute | solution.py:57
  35.9 2.1 %collective-permute-done.11.refs_1_.b_ref.refs_8_ = bf16[112,256]{1,0:T(8,128)(2,1)S(1)} collective-permute-done((bf16[112,256]{1,0:T(8,128)(2,1)S(1)}, bf16[112,256]{1,0:T(8,128)(2,1)S(1)}, u32[]{:S(2)}, u32[]{:S(2)}) %collective-permute-start.11) | collective-permute-done | bytes 57376 | tf_op jit(solution)/shard_map/ppermute | solution.py:57
  38.0 1.6 %collective-permute-start.12 = (bf16[2,2,96,256]{3,2,1,0:T(8,128)(2,1)S(1)}, bf16[2,2,96,256]{3,2,1,0:T(8,128)(2,1)S(1)}, u32[]{:S(2)}, u32[]{:S(2)}) collective-permute-start(bf16[2,2,96,256]{3,2,1,0:T(8,128)(2,1)S(1)} %open.1.refs_0_.mine_ref), channel_id=1, source_target_pairs={{0,2},{1,3},{2,0},{3,1},{4,6},{5,7},{6,4},{7,5},{8,10},{9,11},{10,... | collective-permute-start | bytes 589832 | tf_op jit(solution)/shard_map/ppermute | solution.py:57
  39.5 1.6 %collective-permute-start.13 = (bf16[1,2,96,256]{3,2,1,0:T(8,128)(2,1)S(1)}, bf16[1,2,96,256]{3,2,1,0:T(8,128)(2,1)S(1)}, u32[]{:S(2)}, u32[]{:S(2)}) collective-permute-start(bf16[1,2,96,256]{3,2,1,0:T(8,128)(2,1)S(1)} %bitcast.26), channel_id=1, source_target_pairs={{0,4},{1,5},{2,6},{3,7},{4,0},{5,1},{6,2},{7,3},{8,12},{9,13},{10,... | collective-permute-start | bytes 294920 | tf_op jit(solution)/shard_map/ppermute | solution.py:57
  41.1 3.8 %update.3 = (f32[32,4,128,128]{3,2,1,0:T(8,128)}, f32[8,128]{1,0:T(8,128)S(1)}) custom-call(f32[2,96,128]{2,1,0:T(8,128)S(1)} %get-tuple-element.69.keys_ref, f32[2,3,32,256]{3,2,1,0:T(8,128)S(1)} %get-tuple-element.70.delta_ref, f32[2,32,256]{2,1,0:T(8,128)S(1)} %get-tuple-element.71.total_ref, f32[32,4,128,128]{3,2,1,0:T(8,128)} %states_ref.5, ...), custom_call_target="tpu_custom_call" | custom-call | tf_op jit(solution)/shard_map/update/pallas_call | solution.py:43
  45.0 0.9 %collective-permute-start.14 = (bf16[3,2,96,256]{3,2,1,0:T(8,128)(2,1)S(1)}, bf16[3,2,96,256]{3,2,1,0:T(8,128)(2,1)S(1)}, u32[]{:S(2)}, u32[]{:S(2)}) collective-permute-start(bf16[3,2,96,256]{3,2,1,0:T(8,128)(2,1)S(1)} %grow.1.refs_0_.a_ref), channel_id=1, source_target_pairs={{0,4},{1,5},{2,6},{3,7},{4,0},{5,1},{6,2},{7,3},{8,12},{9,13},{10,... | collective-permute-start | bytes 884744 | tf_op jit(solution)/shard_map/ppermute | solution.py:57
  45.9 0.9 %collective-permute-start.19 = (bf16[2,2,96,256]{3,2,1,0:T(8,128)(2,1)S(1)}, bf16[2,2,96,256]{3,2,1,0:T(8,128)(2,1)S(1)}, u32[]{:S(2)}, u32[]{:S(2)}) collective-permute-start(bf16[2,2,96,256]{3,2,1,0:T(8,128)(2,1)S(1)} %stack.3.refs_1_.refs_0_), channel_id=1, source_target_pairs={{0,2},{1,3},{2,0},{3,1},{4,6},{5,7},{6,4},{7,5},{8,10},{9,11},{10,... | collective-permute-start | bytes 589832 | tf_op jit(solution)/shard_map/ppermute | solution.py:57
  46.8 5.4 %collective-permute-done.14.refs_1_.b_ref = bf16[3,2,96,256]{3,2,1,0:T(8,128)(2,1)S(1)} collective-permute-done((bf16[3,2,96,256]{3,2,1,0:T(8,128)(2,1)S(1)}, bf16[3,2,96,256]{3,2,1,0:T(8,128)(2,1)S(1)}, u32[]{:S(2)}, u32[]{:S(2)}) %collective-permute-start.14) | collective-permute-done | bytes 294944 | tf_op jit(solution)/shard_map/ppermute | solution.py:57
  52.2 0.5 collective-permute-start.18
  52.7 0.6 expert_first.2
  53.4 0.6 expert_first.3
  54.0 1.2 %expert_rest.2 = (bf16[4,2,96,256]{3,2,1,0:T(8,128)(2,1)S(1)}, bf16[4,2,96,256]{3,2,1,0:T(8,128)(2,1)S(1)}, f32[192,1]{1,0:T(8,128)S(1)}) custom-call(s32[1]{0:T(128)} %bitcast.me_ref, bf16[3,2,96,256]{3,2,1,0:T(8,128)(2,1)S(1)} %collective-permute-done.15.refs_0_, bf16[3,2,96,256]{3,2,1,0:T(8,128)(2,1)S(1)} %collective-permute-done.16.refs_1_, ...), custom_call_target="tpu_custom_call" | custom-call | tf_op jit(solution)/shard_map/expert_rest/pallas_call | solution.py:43
  55.2 0.5 collective-permute-start.17
  55.7 1.5 %expert_rest.3 = (bf16[4,2,96,256]{3,2,1,0:T(8,128)(2,1)S(1)}, bf16[4,2,96,256]{3,2,1,0:T(8,128)(2,1)S(1)}, f32[192,1]{1,0:T(8,128)}) custom-call(s32[1]{0:T(128)} %bitcast.me_ref, bf16[2,2,96,256]{3,2,1,0:T(8,128)(2,1)S(1)} %collective-permute-done.18.refs_0_, bf16[2,2,96,256]{3,2,1,0:T(8,128)(2,1)S(1)} %collective-permute-done.20.refs_1_, ...), custom_call_target="tpu_custom_call" | custom-call | tf_op jit(solution)/shard_map/expert_rest/pallas_call | solution.py:43
  57.4 0.6 collective-permute-start.23
  58.1 1.0 %collective-permute-done.21.b_ref = bf16[4,2,96,256]{3,2,1,0:T(8,128)(2,1)S(1)} collective-permute-done((bf16[4,2,96,256]{3,2,1,0:T(8,128)(2,1)S(1)}, bf16[4,2,96,256]{3,2,1,0:T(8,128)(2,1)S(1)}, u32[]{:S(2)}, u32[]{:S(2)}) %collective-permute-start.21) | collective-permute-done | bytes 393248 | tf_op jit(solution)/shard_map/ppermute | solution.py:57
  59.1 0.6 collective-permute-start.26
  59.9 3.0 %update.4 = (f32[32,4,128,128]{3,2,1,0:T(8,128)}, f32[8,128]{1,0:T(8,128)S(1)}) custom-call(f32[2,96,128]{2,1,0:T(8,128)S(1)} %get-tuple-element.69.keys_ref, f32[2,3,32,256]{3,2,1,0:T(8,128)S(1)} %get-tuple-element.70.delta_ref, f32[2,32,256]{2,1,0:T(8,128)S(1)} %get-tuple-element.71.total_ref, ...), custom_call_target="tpu_custom_call", output_to_operand_aliasing={{0}: (4, {})} | custom-call | tf_op jit(solution)/shard_map/update/pallas_call | solution.py:43
  62.9 1.8 %collective-permute-done.23.b_ref = bf16[2,2,96,256]{3,2,1,0:T(8,128)(2,1)S(1)} collective-permute-done((bf16[2,2,96,256]{3,2,1,0:T(8,128)(2,1)S(1)}, bf16[2,2,96,256]{3,2,1,0:T(8,128)(2,1)S(1)}, u32[]{:S(2)}, u32[]{:S(2)}) %collective-permute-start.23) | collective-permute-done | bytes 196640 | tf_op jit(solution)/shard_map/ppermute | solution.py:57
  64.8 0.6 collective-permute-start.24
  65.4 0.7 collective-permute-done.26.b_ref
  66.2 0.6 collective-permute-start.27
  66.8 2.7 %collective-permute-done.24.b_ref = bf16[1,2,96,256]{3,2,1,0:T(8,128)(2,1)S(1)} collective-permute-done((bf16[1,2,96,256]{3,2,1,0:T(8,128)(2,1)S(1)}, bf16[1,2,96,256]{3,2,1,0:T(8,128)(2,1)S(1)}, u32[]{:S(2)}, u32[]{:S(2)}) %collective-permute-start.24) | collective-permute-done | bytes 98336 | tf_op jit(solution)/shard_map/ppermute | solution.py:57
  69.5 1.0 %collective-permute-start.25 = (bf16[96,256]{1,0:T(8,128)(2,1)S(1)}, bf16[96,256]{1,0:T(8,128)(2,1)S(1)}, u32[]{:S(2)}, u32[]{:S(2)}) collective-permute-start(bf16[96,256]{1,0:T(8,128)(2,1)S(1)} %get-tuple-element.93), channel_id=1, source_target_pairs={{0,8},{8,0},{16,24},{24,16},{1,9},{9,1},{17,25},{25,17},{2,10},{10... | collective-permute-start | bytes 147464 | tf_op jit(solution)/shard_map/ppermute | solution.py:57
  70.6 0.3 collective-permute-done.27.b_ref
  70.9 1.8 %collective-permute-start.28 = (bf16[96,256]{1,0:T(8,128)(2,1)S(1)}, bf16[96,256]{1,0:T(8,128)(2,1)S(1)}, u32[]{:S(2)}, u32[]{:S(2)}) collective-permute-start(bf16[96,256]{1,0:T(8,128)(2,1)S(1)} %get-tuple-element.97), channel_id=1, source_target_pairs={{0,16},{8,24},{16,0},{24,8},{1,17},{9,25},{17,1},{25,9},{2,18},{10... | collective-permute-start | bytes 147464 | tf_op jit(solution)/shard_map/ppermute | solution.py:57
  72.7 1.6 %collective-permute-start.29 = (bf16[96,256]{1,0:T(8,128)(2,1)S(1)}, bf16[96,256]{1,0:T(8,128)(2,1)S(1)}, u32[]{:S(2)}, u32[]{:S(2)}) collective-permute-start(bf16[96,256]{1,0:T(8,128)(2,1)S(1)} %get-tuple-element.98.refs_1_), channel_id=1, source_target_pairs={{0,24},{8,16},{16,8},{24,0},{1,25},{9,17},{17,9},{25,1},{2,26},{10... | collective-permute-start | bytes 147464 | tf_op jit(solution)/shard_map/ppermute | solution.py:57
  74.3 0.2 shared_out.1.refs_0_
  74.5 2.9 %update.5 = (f32[32,4,128,128]{3,2,1,0:T(8,128)}, f32[8,128]{1,0:T(8,128)S(1)}) custom-call(f32[2,96,128]{2,1,0:T(8,128)S(1)} %get-tuple-element.69.keys_ref, f32[2,3,32,256]{3,2,1,0:T(8,128)S(1)} %get-tuple-element.70.delta_ref, f32[2,32,256]{2,1,0:T(8,128)S(1)} %get-tuple-element.71.total_ref, ...), custom_call_target="tpu_custom_call", output_to_operand_aliasing={{0}: (4, {})} | custom-call | tf_op jit(solution)/shard_map/update/pallas_call | solution.py:43
  77.5 1.2 %collective-permute-done.29.refs_4_ = bf16[96,256]{1,0:T(8,128)(2,1)S(1)} collective-permute-done((bf16[96,256]{1,0:T(8,128)(2,1)S(1)}, bf16[96,256]{1,0:T(8,128)(2,1)S(1)}, u32[]{:S(2)}, u32[]{:S(2)}) %collective-permute-start.29) | collective-permute-done | bytes 49184 | tf_op jit(solution)/shard_map/ppermute | solution.py:57
  78.6 0.7 finish.1
  (48 shorter events, 1.3 us)
Async XLA Ops:
  0.6 7.2 %collective-permute-start = (bf16[96,256]{1,0:T(8,128)(2,1)}, bf16[96,256]{1,0:T(8,128)(2,1)S(1)}, u32[]{:S(2)}, u32[]{:S(2)}) collective-permute-start(bf16[96,256]{1,0:T(8,128)(2,1)} %bitcast.30), channel_id=1, source_target_pairs={{0,2},{1,3},{2,0},{3,1},{4,6},{5,7},{6,4},{7,5},{8,10},{9,11},{10,... | collective-permute-start | bytes 147464 | tf_op jit(solution)/shard_map/ppermute | solution.py:57
  3.6 4.3 %collective-permute-start.1 = (bf16[96,256]{1,0:T(8,128)(2,1)}, bf16[96,256]{1,0:T(8,128)(2,1)S(1)}, u32[]{:S(2)}, u32[]{:S(2)}) collective-permute-start(bf16[96,256]{1,0:T(8,128)(2,1)} %bitcast.31), channel_id=1, source_target_pairs={{0,4},{1,5},{2,6},{3,7},{4,0},{5,1},{6,2},{7,3},{8,12},{9,13},{10,... | collective-permute-start | bytes 147464 | tf_op jit(solution)/shard_map/ppermute | solution.py:57
  5.2 5.2 %collective-permute-start.2 = (bf16[96,256]{1,0:T(8,128)(2,1)}, bf16[96,256]{1,0:T(8,128)(2,1)S(1)}, u32[]{:S(2)}, u32[]{:S(2)}) collective-permute-start(bf16[96,256]{1,0:T(8,128)(2,1)} %bitcast.32), channel_id=1, source_target_pairs={{0,6},{1,7},{2,4},{3,5},{4,2},{5,3},{6,0},{7,1},{8,14},{9,15},{10,... | collective-permute-start | bytes 147464 | tf_op jit(solution)/shard_map/ppermute | solution.py:57
  5.2 5.3 %copy-start = (bf16[2048,4]{0,1:T(4,128)(2,1)S(1)}, bf16[2048,4]{0,1:T(4,128)(2,1)}, u32[]{:S(2)}) copy-start(bf16[2048,4]{0,1:T(4,128)(2,1)} %param.30) | copy-start | bytes 49156
  5.2 5.3 %copy-start.1 = (bf16[2048,4]{0,1:T(4,128)(2,1)S(1)}, bf16[2048,4]{0,1:T(4,128)(2,1)}, u32[]{:S(2)}) copy-start(bf16[2048,4]{0,1:T(4,128)(2,1)} %param.29) | copy-start | bytes 49156
  10.4 1.8 %collective-permute-start.3 = (bf16[4,96,256]{2,1,0:T(8,128)(2,1)S(1)}, bf16[4,96,256]{2,1,0:T(8,128)(2,1)S(1)}, u32[]{:S(2)}, u32[]{:S(2)}) collective-permute-start(bf16[4,96,256]{2,1,0:T(8,128)(2,1)S(1)} %stack.2.refs_1_.refs_0_), channel_id=1, source_target_pairs={{0,1},{1,0},{2,3},{3,2},{4,5},{5,4},{6,7},{7,6},{8,9},{9,8},{10,11... | collective-permute-start | bytes 589832 | tf_op jit(solution)/shard_map/ppermute | solution.py:57
  19.3 1.6 %collective-permute-start.4 = (bf16[4,96,256]{2,1,0:T(8,128)(2,1)S(1)}, bf16[4,96,256]{2,1,0:T(8,128)(2,1)S(1)}, u32[]{:S(2)}, u32[]{:S(2)}) collective-permute-start(bf16[4,96,256]{2,1,0:T(8,128)(2,1)S(1)} %get-tuple-element.59), channel_id=1, source_target_pairs={{0,1},{1,0},{2,3},{3,2},{4,5},{5,4},{6,7},{7,6},{8,9},{9,8},{10,11... | collective-permute-start | bytes 589832 | tf_op jit(solution)/shard_map/ppermute | solution.py:57
  21.0 5.8 %collective-permute-start.5 = (bf16[96,256]{1,0:T(8,128)(2,1)S(1)}, bf16[96,256]{1,0:T(8,128)(2,1)S(1)}, u32[]{:S(2)}, u32[]{:S(2)}) collective-permute-start(bf16[96,256]{1,0:T(8,128)(2,1)S(1)} %get-tuple-element.104), channel_id=1, source_target_pairs={{0,2},{1,3},{2,0},{3,1},{4,6},{5,7},{6,4},{7,5},{8,10},{9,11},{10,... | collective-permute-start | bytes 147464 | tf_op jit(solution)/shard_map/ppermute | solution.py:57
  21.6 5.2 %collective-permute-start.6 = (bf16[96,256]{1,0:T(8,128)(2,1)S(1)}, bf16[96,256]{1,0:T(8,128)(2,1)S(1)}, u32[]{:S(2)}, u32[]{:S(2)}) collective-permute-start(bf16[96,256]{1,0:T(8,128)(2,1)S(1)} %get-tuple-element.103), channel_id=1, source_target_pairs={{0,4},{1,5},{2,6},{3,7},{4,0},{5,1},{6,2},{7,3},{8,12},{9,13},{10,... | collective-permute-start | bytes 147464 | tf_op jit(solution)/shard_map/ppermute | solution.py:57
  22.0 5.0 %collective-permute-start.7 = (bf16[96,256]{1,0:T(8,128)(2,1)S(1)}, bf16[96,256]{1,0:T(8,128)(2,1)S(1)}, u32[]{:S(2)}, u32[]{:S(2)}) collective-permute-start(bf16[96,256]{1,0:T(8,128)(2,1)S(1)} %get-tuple-element.102), channel_id=1, source_target_pairs={{0,6},{1,7},{2,4},{3,5},{4,2},{5,3},{6,0},{7,1},{8,14},{9,15},{10,... | collective-permute-start | bytes 147464 | tf_op jit(solution)/shard_map/ppermute | solution.py:57
  27.5 10.4 %collective-permute-start.9 = (bf16[2,96,256]{2,1,0:T(8,128)(2,1)S(1)}, bf16[2,96,256]{2,1,0:T(8,128)(2,1)S(1)}, u32[]{:S(2)}, u32[]{:S(2)}) collective-permute-start(bf16[2,96,256]{2,1,0:T(8,128)(2,1)S(1)} %get-tuple-element.66), channel_id=1, source_target_pairs={{0,1},{1,0},{2,3},{3,2},{4,5},{5,4},{6,7},{7,6},{8,9},{9,8},{10,11... | collective-permute-start | bytes 294920 | tf_op jit(solution)/shard_map/ppermute | solution.py:57
  27.6 6.1 %collective-permute-start.8 = (bf16[112,256]{1,0:T(8,128)(2,1)S(1)}, bf16[112,256]{1,0:T(8,128)(2,1)S(1)}, u32[]{:S(2)}, u32[]{:S(2)}) collective-permute-start(bf16[112,256]{1,0:T(8,128)(2,1)S(1)} %get-tuple-element.63), channel_id=1, source_target_pairs={{0,8},{8,0},{16,24},{24,16},{1,9},{9,1},{17,25},{25,17},{2,10},{10... | collective-permute-start | bytes 172040 | tf_op jit(solution)/shard_map/ppermute | solution.py:57
  29.3 6.6 %collective-permute-start.10 = (bf16[112,256]{1,0:T(8,128)(2,1)S(1)}, bf16[112,256]{1,0:T(8,128)(2,1)S(1)}, u32[]{:S(2)}, u32[]{:S(2)}) collective-permute-start(bf16[112,256]{1,0:T(8,128)(2,1)S(1)} %get-tuple-element.67), channel_id=1, source_target_pairs={{0,16},{8,24},{16,0},{24,8},{1,17},{9,25},{17,1},{25,9},{2,18},{10... | collective-permute-start | bytes 172040 | tf_op jit(solution)/shard_map/ppermute | solution.py:57
  31.9 6.0 %collective-permute-start.11 = (bf16[112,256]{1,0:T(8,128)(2,1)S(1)}, bf16[112,256]{1,0:T(8,128)(2,1)S(1)}, u32[]{:S(2)}, u32[]{:S(2)}) collective-permute-start(bf16[112,256]{1,0:T(8,128)(2,1)S(1)} %get-tuple-element.68), channel_id=1, source_target_pairs={{0,24},{8,16},{16,8},{24,0},{1,25},{9,17},{17,9},{25,1},{2,26},{10... | collective-permute-start | bytes 172040 | tf_op jit(solution)/shard_map/ppermute | solution.py:57
  38.0 7.0 %collective-permute-start.12 = (bf16[2,2,96,256]{3,2,1,0:T(8,128)(2,1)S(1)}, bf16[2,2,96,256]{3,2,1,0:T(8,128)(2,1)S(1)}, u32[]{:S(2)}, u32[]{:S(2)}) collective-permute-start(bf16[2,2,96,256]{3,2,1,0:T(8,128)(2,1)S(1)} %open.1.refs_0_.mine_ref), channel_id=1, source_target_pairs={{0,2},{1,3},{2,0},{3,1},{4,6},{5,7},{6,4},{7,5},{8,10},{9,11},{10,... | collective-permute-start | bytes 589832 | tf_op jit(solution)/shard_map/ppermute | solution.py:57
  39.5 5.4 %collective-permute-start.13 = (bf16[1,2,96,256]{3,2,1,0:T(8,128)(2,1)S(1)}, bf16[1,2,96,256]{3,2,1,0:T(8,128)(2,1)S(1)}, u32[]{:S(2)}, u32[]{:S(2)}) collective-permute-start(bf16[1,2,96,256]{3,2,1,0:T(8,128)(2,1)S(1)} %bitcast.26), channel_id=1, source_target_pairs={{0,4},{1,5},{2,6},{3,7},{4,0},{5,1},{6,2},{7,3},{8,12},{9,13},{10,... | collective-permute-start | bytes 294920 | tf_op jit(solution)/shard_map/ppermute | solution.py:57
  45.0 7.2 %collective-permute-start.14 = (bf16[3,2,96,256]{3,2,1,0:T(8,128)(2,1)S(1)}, bf16[3,2,96,256]{3,2,1,0:T(8,128)(2,1)S(1)}, u32[]{:S(2)}, u32[]{:S(2)}) collective-permute-start(bf16[3,2,96,256]{3,2,1,0:T(8,128)(2,1)S(1)} %grow.1.refs_0_.a_ref), channel_id=1, source_target_pairs={{0,4},{1,5},{2,6},{3,7},{4,0},{5,1},{6,2},{7,3},{8,12},{9,13},{10,... | collective-permute-start | bytes 884744 | tf_op jit(solution)/shard_map/ppermute | solution.py:57
  45.9 6.9 %collective-permute-start.19 = (bf16[2,2,96,256]{3,2,1,0:T(8,128)(2,1)S(1)}, bf16[2,2,96,256]{3,2,1,0:T(8,128)(2,1)S(1)}, u32[]{:S(2)}, u32[]{:S(2)}) collective-permute-start(bf16[2,2,96,256]{3,2,1,0:T(8,128)(2,1)S(1)} %stack.3.refs_1_.refs_0_), channel_id=1, source_target_pairs={{0,2},{1,3},{2,0},{3,1},{4,6},{5,7},{6,4},{7,5},{8,10},{9,11},{10,... | collective-permute-start | bytes 589832 | tf_op jit(solution)/shard_map/ppermute | solution.py:57
  46.8 7.2 %collective-permute-start.15 = (bf16[3,2,96,256]{3,2,1,0:T(8,128)(2,1)S(1)}, bf16[3,2,96,256]{3,2,1,0:T(8,128)(2,1)S(1)}, u32[]{:S(2)}, u32[]{:S(2)}) collective-permute-start(bf16[3,2,96,256]{3,2,1,0:T(8,128)(2,1)S(1)} %grow.1.refs_0_.a_ref), channel_id=1, source_target_pairs={{0,1},{1,0},{2,3},{3,2},{4,5},{5,4},{6,7},{7,6},{8,9},{9,8},{10,11... | collective-permute-start | bytes 884744 | tf_op jit(solution)/shard_map/ppermute | solution.py:57
  52.2 1.8 %collective-permute-start.16 = (bf16[3,2,96,256]{3,2,1,0:T(8,128)(2,1)S(1)}, bf16[3,2,96,256]{3,2,1,0:T(8,128)(2,1)S(1)}, u32[]{:S(2)}, u32[]{:S(2)}) collective-permute-start(bf16[3,2,96,256]{3,2,1,0:T(8,128)(2,1)S(1)} %collective-permute-done.14.refs_1_.b_ref), channel_id=1, source_target_pairs={{0,1},{1,0},{2,3},{3,2},{4,5},{5,4},{6,7},{7,6},{8,9},{9,8},{10,11... | collective-permute-start | bytes 884744 | tf_op jit(solution)/shard_map/ppermute | solution.py:57
  52.2 3.5 %collective-permute-start.18 = (bf16[2,2,96,256]{3,2,1,0:T(8,128)(2,1)S(1)}, bf16[2,2,96,256]{3,2,1,0:T(8,128)(2,1)S(1)}, u32[]{:S(2)}, u32[]{:S(2)}) collective-permute-start(bf16[2,2,96,256]{3,2,1,0:T(8,128)(2,1)S(1)} %stack.3.refs_1_.refs_0_), channel_id=1, source_target_pairs={{0,1},{1,0},{2,3},{3,2},{4,5},{5,4},{6,7},{7,6},{8,9},{9,8},{10,11... | collective-permute-start | bytes 589832 | tf_op jit(solution)/shard_map/ppermute | solution.py:57
  52.7 3.0 %collective-permute-start.20 = (bf16[2,2,96,256]{3,2,1,0:T(8,128)(2,1)S(1)}, bf16[2,2,96,256]{3,2,1,0:T(8,128)(2,1)S(1)}, u32[]{:S(2)}, u32[]{:S(2)}) collective-permute-start(bf16[2,2,96,256]{3,2,1,0:T(8,128)(2,1)S(1)} %collective-permute-done.19.refs_1_), channel_id=1, source_target_pairs={{0,1},{1,0},{2,3},{3,2},{4,5},{5,4},{6,7},{7,6},{8,9},{9,8},{10,11... | collective-permute-start | bytes 589832 | tf_op jit(solution)/shard_map/ppermute | solution.py:57
  55.2 2.1 %collective-permute-start.17 = (bf16[4,2,96,256]{3,2,1,0:T(8,128)(2,1)S(1)}, bf16[4,2,96,256]{3,2,1,0:T(8,128)(2,1)S(1)}, u32[]{:S(2)}, u32[]{:S(2)}) collective-permute-start(bf16[4,2,96,256]{3,2,1,0:T(8,128)(2,1)S(1)} %get-tuple-element.78), channel_id=1, source_target_pairs={{0,1},{1,0},{2,3},{3,2},{4,5},{5,4},{6,7},{7,6},{8,9},{9,8},{10,11... | collective-permute-start | bytes 1179656 | tf_op jit(solution)/shard_map/ppermute | solution.py:57
  57.3 1.7 %collective-permute-start.21 = (bf16[4,2,96,256]{3,2,1,0:T(8,128)(2,1)S(1)}, bf16[4,2,96,256]{3,2,1,0:T(8,128)(2,1)S(1)}, u32[]{:S(2)}, u32[]{:S(2)}) collective-permute-start(bf16[4,2,96,256]{3,2,1,0:T(8,128)(2,1)S(1)} %get-tuple-element.83), channel_id=1, source_target_pairs={{0,1},{1,0},{2,3},{3,2},{4,5},{5,4},{6,7},{7,6},{8,9},{9,8},{10,11... | collective-permute-start | bytes 1179656 | tf_op jit(solution)/shard_map/ppermute | solution.py:57
  57.4 7.3 %collective-permute-start.23 = (bf16[2,2,96,256]{3,2,1,0:T(8,128)(2,1)S(1)}, bf16[2,2,96,256]{3,2,1,0:T(8,128)(2,1)S(1)}, u32[]{:S(2)}, u32[]{:S(2)}) collective-permute-start(bf16[2,2,96,256]{3,2,1,0:T(8,128)(2,1)S(1)} %get-tuple-element.87), channel_id=1, source_target_pairs={{0,2},{1,3},{2,0},{3,1},{4,6},{5,7},{6,4},{7,5},{8,10},{9,11},{10,... | collective-permute-start | bytes 589832 | tf_op jit(solution)/shard_map/ppermute | solution.py:57
  59.1 7.0 %collective-permute-start.26 = (bf16[2,2,96,256]{3,2,1,0:T(8,128)(2,1)S(1)}, bf16[2,2,96,256]{3,2,1,0:T(8,128)(2,1)S(1)}, u32[]{:S(2)}, u32[]{:S(2)}) collective-permute-start(bf16[2,2,96,256]{3,2,1,0:T(8,128)(2,1)S(1)} %get-tuple-element.94), channel_id=1, source_target_pairs={{0,4},{1,5},{2,6},{3,7},{4,0},{5,1},{6,2},{7,3},{8,12},{9,13},{10,... | collective-permute-start | bytes 589832 | tf_op jit(solution)/shard_map/ppermute | solution.py:57
  59.9 3.1 %collective-permute-start.22 = (bf16[96,256]{1,0:T(8,128)(2,1)S(1)}, bf16[96,256]{1,0:T(8,128)(2,1)S(1)}, u32[]{:S(2)}, u32[]{:S(2)}) collective-permute-start(bf16[96,256]{1,0:T(8,128)(2,1)S(1)} %shared_hidden.1.a_ref), channel_id=1, source_target_pairs={{0,1},{1,0},{2,3},{3,2},{4,5},{5,4},{6,7},{7,6},{8,9},{9,8},{10,11... | collective-permute-start | bytes 147464 | tf_op jit(solution)/shard_map/ppermute | solution.py:57
  64.8 4.7 %collective-permute-start.24 = (bf16[1,2,96,256]{3,2,1,0:T(8,128)(2,1)S(1)}, bf16[1,2,96,256]{3,2,1,0:T(8,128)(2,1)S(1)}, u32[]{:S(2)}, u32[]{:S(2)}) collective-permute-start(bf16[1,2,96,256]{3,2,1,0:T(8,128)(2,1)S(1)} %get-tuple-element.91), channel_id=1, source_target_pairs={{0,4},{1,5},{2,6},{3,7},{4,0},{5,1},{6,2},{7,3},{8,12},{9,13},{10,... | collective-permute-start | bytes 294920 | tf_op jit(solution)/shard_map/ppermute | solution.py:57
  66.2 4.7 %collective-permute-start.27 = (bf16[1,2,96,256]{3,2,1,0:T(8,128)(2,1)S(1)}, bf16[1,2,96,256]{3,2,1,0:T(8,128)(2,1)S(1)}, u32[]{:S(2)}, u32[]{:S(2)}) collective-permute-start(bf16[1,2,96,256]{3,2,1,0:T(8,128)(2,1)S(1)} %get-tuple-element.96), channel_id=1, source_target_pairs={{0,2},{1,3},{2,0},{3,1},{4,6},{5,7},{6,4},{7,5},{8,10},{9,11},{10,... | collective-permute-start | bytes 294920 | tf_op jit(solution)/shard_map/ppermute | solution.py:57
  69.5 7.9 %collective-permute-start.25 = (bf16[96,256]{1,0:T(8,128)(2,1)S(1)}, bf16[96,256]{1,0:T(8,128)(2,1)S(1)}, u32[]{:S(2)}, u32[]{:S(2)}) collective-permute-start(bf16[96,256]{1,0:T(8,128)(2,1)S(1)} %get-tuple-element.93), channel_id=1, source_target_pairs={{0,8},{8,0},{16,24},{24,16},{1,9},{9,1},{17,25},{25,17},{2,10},{10... | collective-permute-start | bytes 147464 | tf_op jit(solution)/shard_map/ppermute | solution.py:57
  70.9 6.6 %collective-permute-start.28 = (bf16[96,256]{1,0:T(8,128)(2,1)S(1)}, bf16[96,256]{1,0:T(8,128)(2,1)S(1)}, u32[]{:S(2)}, u32[]{:S(2)}) collective-permute-start(bf16[96,256]{1,0:T(8,128)(2,1)S(1)} %get-tuple-element.97), channel_id=1, source_target_pairs={{0,16},{8,24},{16,0},{24,8},{1,17},{9,25},{17,1},{25,9},{2,18},{10... | collective-permute-start | bytes 147464 | tf_op jit(solution)/shard_map/ppermute | solution.py:57
  72.7 5.9 %collective-permute-start.29 = (bf16[96,256]{1,0:T(8,128)(2,1)S(1)}, bf16[96,256]{1,0:T(8,128)(2,1)S(1)}, u32[]{:S(2)}, u32[]{:S(2)}) collective-permute-start(bf16[96,256]{1,0:T(8,128)(2,1)S(1)} %get-tuple-element.98.refs_1_), channel_id=1, source_target_pairs={{0,24},{8,16},{16,8},{24,0},{1,25},{9,17},{17,9},{25,1},{2,26},{10... | collective-permute-start | bytes 147464 | tf_op jit(solution)/shard_map/ppermute | solution.py:57

commit v8 on v7

--- a/solution.py
+++ b/solution.py
@@ -839,8 +839,9 @@
     shared_keep, sent = shared_in(me, x, w_shared_in, ())
     shared_received = exchange(sent, "head", 1)
     [w_down] = load((w_expert_out,), (shared_keep,))
+    states_out, done = update(keys, deltas, totals, states, quarters[3], (w_down,))
     if half == 2:
-        side = open_side(*slabs[:2], shared_keep, shared_received, (*slabs[2:], w_down))
+        side = open_side(*slabs[:2], shared_keep, shared_received, (*slabs[2:], done))
     else:
         rows_only = jnp.stack([m[:rows] for m in slabs[:half]])
         side = jnp.stack([rows_only, add(shared_keep, shared_received)])
@@ -849,7 +850,7 @@
     else:
         other = jnp.stack([m[:rows] for m in slabs[half:]])[None]
     states_out, done = update(
-        keys, deltas, totals, states, quarters[0] + quarters[1], (side, other)
+        keys, deltas, totals, states, quarters[0] + quarters[1], (side, other), states_out
     )
     for bit in axes[:0:-1]:
         received = exchange(other, "head", bit)
@@ -906,9 +907,8 @@
     slabs = []
     for side in range(2):
         slabs += last_sum(owns[side], received[side])
-    states_out, done = update(keys, deltas, totals, states, quarters[3], (slabs[-1],), states_out)
     received = [exchange(slabs[z], "seq", z) for z in range(1, seq_count)]
-    result = finish(base, slabs[0], received, (done,))
+    result = finish(base, slabs[0], received, ())
     layer_out = jnp.transpose(result.reshape(steps, seqs, width), (1, 0, 2))
     return (layer_out, states_out)
 

time: 79.6 us -> 80.2 us (level)
  starting transfers between devices: 26.3 us -> 28.9 us
  waiting for transfers between devices: 21.2 us -> 19.2 us
    ppermute x30, starting transfers between devices: 26.3 us -> 28.9 us  [exchange(): return lax.ppermute(x, axis, [(i, i ^ bit) for i in range(size)])]
    ppermute x30, waiting for transfers between devices: 21.2 us -> 19.2 us  [exchange(): return lax.ppermute(x, axis, [(i, i ^ bit) for i in range(size)])]
  transfers between devices with their start and end apart: 30 -> 30, of which waited for: 13 -> 11; matrix products, arithmetic and copies ran while one was open for 0% -> 0% of each run, Pallas kernels for 28% -> 26%
where the time goes in v8:
time: 80.2 us; the launch traced here: 80 us
  Pallas kernels  30.8 us (38%)
  starting transfers between devices  28.9 us (36%)
  waiting for transfers between devices  19.2 us (24%)
  between operations  0.95 us (1%)
    pallas_call x29, Pallas kernels, call(): pl.pallas_call(body, out_shape=tuple(out_shapes), in_specs=[SMEM_SPEC] *...  30.8 us
    ppermute x30, starting transfers between devices, exchange(): return lax.ppermute(x, axis, [(i, i ^ bit) for i in range(size)])  28.9 us
    ppermute x30, waiting for transfers between devices, exchange(): return lax.ppermute(x, axis, [(i, i ^ bit) for i in range(size)])  19.2 us
  transfers between devices with their start and end apart: 30, of which 11 were waited for; matrix products, arithmetic and copies ran while one was open for 0% of the time, Pallas kernels for 26%

profile of v8, /device:TPU:0, one launch (start us, length us, event | category | flops | bytes accessed | tf_op | source)
XLA Modules:
  0.0 80.0 jit_solution(11777056815751782203)
XLA Ops:
  0.6 3.0 %collective-permute-start = (bf16[96,256]{1,0:T(8,128)(2,1)}, bf16[96,256]{1,0:T(8,128)(2,1)S(1)}, u32[]{:S(2)}, u32[]{:S(2)}) collective-permute-start(bf16[96,256]{1,0:T(8,128)(2,1)} %bitcast.30), channel_id=1, source_target_pairs={{0,2},{1,3},{2,0},{3,1},{4,6},{5,7},{6,4},{7,5},{8,10},{9,11},{10,... | collective-permute-start | bytes 147464 | tf_op jit(solution)/shard_map/ppermute | solution.py:57
  3.6 1.5 %collective-permute-start.1 = (bf16[96,256]{1,0:T(8,128)(2,1)}, bf16[96,256]{1,0:T(8,128)(2,1)S(1)}, u32[]{:S(2)}, u32[]{:S(2)}) collective-permute-start(bf16[96,256]{1,0:T(8,128)(2,1)} %bitcast.31), channel_id=1, source_target_pairs={{0,4},{1,5},{2,6},{3,7},{4,0},{5,1},{6,2},{7,3},{8,12},{9,13},{10,... | collective-permute-start | bytes 147464 | tf_op jit(solution)/shard_map/ppermute | solution.py:57
  5.2 2.6 %bring.1 = (bf16[96,256]{1,0:T(8,128)(2,1)S(1)}, bf16[2048,256]{1,0:T(8,128)(2,1)S(1)}, bf16[2048,256]{1,0:T(8,128)(2,1)S(1)}, bf16[2048,512]{1,0:T(8,128)(2,1)S...) custom-call(s32[1]{0:T(128)} %bitcast.me_ref, ...), custom_call_target="tpu_custom_call" | custom-call | tf_op jit(solution)/shard_map/bring/pallas_call | solution.py:43
  7.9 2.4 %collective-permute-done.2.refs_3_ = bf16[96,256]{1,0:T(8,128)(2,1)S(1)} collective-permute-done((bf16[96,256]{1,0:T(8,128)(2,1)}, bf16[96,256]{1,0:T(8,128)(2,1)S(1)}, u32[]{:S(2)}, u32[]{:S(2)}) %collective-permute-start.2) | collective-permute-done | bytes 49184 | tf_op jit(solution)/shard_map/ppermute | solution.py:57
  10.5 1.6 %load.3.refs_8_ = bf16[2048,512]{1,0:T(8,128)(2,1)S(1)} custom-call(bf16[2048,512]{1,0:T(8,128)(2,1)} %refs_0_.3, bf16[4,96,256]{2,1,0:T(8,128)(2,1)S(1)} %stack.2.refs_1_.refs_0_), custom_call_target="tpu_custom_call" | custom-call | tf_op jit(solution)/shard_map/load/pallas_call | solution.py:43
  12.1 7.1 %front.1 = (bf16[4,96,256]{2,1,0:T(8,128)(2,1)S(1)}, bf16[4,96,256]{2,1,0:T(8,128)(2,1)S(1)}, f32[2,96,128]{2,1,0:T(8,128)S(1)}, f32[2,3,32,256]{3,2,1,0:T(8,128)S(1)}, f32[2,32,256]{2,1,0:T(8,128)S(1)}) custom-call(s32[1]{0:T(128)} %bitcast.me_ref, bf16[4,96,256]{2,1,0:T(8,128)(2,1)S(1)} %stack.2.refs_1_.refs_0_, ...), custom_call_target="tpu_custom_call" | custom-call | tf_op jit(solution)/shard_map/front/pallas_call | solution.py:43
  19.3 0.5 collective-permute-start.4
  19.8 1.1 %collective-permute-done.4.b_ref = bf16[4,96,256]{2,1,0:T(8,128)(2,1)S(1)} collective-permute-done((bf16[4,96,256]{2,1,0:T(8,128)(2,1)S(1)}, bf16[4,96,256]{2,1,0:T(8,128)(2,1)S(1)}, u32[]{:S(2)}, u32[]{:S(2)}) %collective-permute-start.4) | collective-permute-done | bytes 196640 | tf_op jit(solution)/shard_map/ppermute | solution.py:57
  21.0 0.6 collective-permute-start.5
  21.6 0.4 collective-permute-start.6
  22.0 2.5 %collective-permute-start.7 = (bf16[96,256]{1,0:T(8,128)(2,1)S(1)}, bf16[96,256]{1,0:T(8,128)(2,1)S(1)}, u32[]{:S(2)}, u32[]{:S(2)}) collective-permute-start(bf16[96,256]{1,0:T(8,128)(2,1)S(1)} %get-tuple-element.102), channel_id=1, source_target_pairs={{0,6},{1,7},{2,4},{3,5},{4,2},{5,3},{6,0},{7,1},{8,14},{9,15},{10,... | collective-permute-start | bytes 147464 | tf_op jit(solution)/shard_map/ppermute | solution.py:57
  24.5 2.2 %load.4.refs_7_.refs_3_ = bf16[1,2048,1024]{2,1,0:T(8,128)(2,1)S(1)} custom-call(bf16[1,2048,1024]{2,1,0:T(8,128)(2,1)} %refs_0_.4, bf16[4,96,256]{2,1,0:T(8,128)(2,1)S(1)} %one_sum.1.refs_1_.refs_0_), custom_call_target="tpu_custom_call" | custom-call | tf_op jit(solution)/shard_map/load/pallas_call | solution.py:43
  26.8 0.2 collective-permute-done.7.refs_3_
  27.0 0.4 shared_in.1
  27.6 2.7 %collective-permute-start.10 = (bf16[112,256]{1,0:T(8,128)(2,1)S(1)}, bf16[112,256]{1,0:T(8,128)(2,1)S(1)}, u32[]{:S(2)}, u32[]{:S(2)}) collective-permute-start(bf16[112,256]{1,0:T(8,128)(2,1)S(1)} %get-tuple-element.67), channel_id=1, source_target_pairs={{0,16},{8,24},{16,0},{24,8},{1,17},{9,25},{17,1},{25,9},{2,18},{10... | collective-permute-start | bytes 172040 | tf_op jit(solution)/shard_map/ppermute | solution.py:57
  30.3 1.3 %collective-permute-start.11 = (bf16[112,256]{1,0:T(8,128)(2,1)S(1)}, bf16[112,256]{1,0:T(8,128)(2,1)S(1)}, u32[]{:S(2)}, u32[]{:S(2)}) collective-permute-start(bf16[112,256]{1,0:T(8,128)(2,1)S(1)} %get-tuple-element.68), channel_id=1, source_target_pairs={{0,24},{8,16},{16,8},{24,0},{1,25},{9,17},{17,9},{25,1},{2,26},{10... | collective-permute-start | bytes 172040 | tf_op jit(solution)/shard_map/ppermute | solution.py:57
  31.6 0.2 collective-permute-start.8
  31.9 1.6 %load.5.refs_0_.refs_6_ = bf16[1,512,2048]{2,1,0:T(8,128)(2,1)S(1)} custom-call(bf16[1,512,2048]{2,1,0:T(8,128)(2,1)} %refs_0_.5, bf16[2,96,256]{2,1,0:T(8,128)(2,1)S(1)} %get-tuple-element.65.refs_1_.keep_ref), custom_call_target="tpu_custom_call" | custom-call | tf_op jit(solution)/shard_map/load/pallas_call | solution.py:43
  33.5 2.9 %update.3 = (f32[32,4,128,128]{3,2,1,0:T(8,128)}, f32[8,128]{1,0:T(8,128)S(1)}) custom-call(f32[2,96,128]{2,1,0:T(8,128)S(1)} %get-tuple-element.69.keys_ref, f32[2,3,32,256]{3,2,1,0:T(8,128)S(1)} %get-tuple-element.70.delta_ref, f32[2,32,256]{2,1,0:T(8,128)S(1)} %get-tuple-element.71.total_ref, f32[32,4,128,128]{3,2,1,0:T(8,128)} %states_ref.5, ...), custom_call_target="tpu_custom_call" | custom-call | tf_op jit(solution)/shard_map/update/pallas_call | solution.py:43
  36.4 0.3 collective-permute-done.11.refs_1_.b_ref.refs_8_
  36.8 1.6 %collective-permute-start.12 = (bf16[2,2,96,256]{3,2,1,0:T(8,128)(2,1)S(1)}, bf16[2,2,96,256]{3,2,1,0:T(8,128)(2,1)S(1)}, u32[]{:S(2)}, u32[]{:S(2)}) collective-permute-start(bf16[2,2,96,256]{3,2,1,0:T(8,128)(2,1)S(1)} %open.1.refs_1_.mine_ref), channel_id=1, source_target_pairs={{0,2},{1,3},{2,0},{3,1},{4,6},{5,7},{6,4},{7,5},{8,10},{9,11},{10,... | collective-permute-start | bytes 589832 | tf_op jit(solution)/shard_map/ppermute | solution.py:57
  38.3 1.6 %collective-permute-start.13 = (bf16[1,2,96,256]{3,2,1,0:T(8,128)(2,1)S(1)}, bf16[1,2,96,256]{3,2,1,0:T(8,128)(2,1)S(1)}, u32[]{:S(2)}, u32[]{:S(2)}) collective-permute-start(bf16[1,2,96,256]{3,2,1,0:T(8,128)(2,1)S(1)} %bitcast.26), channel_id=1, source_target_pairs={{0,4},{1,5},{2,6},{3,7},{4,0},{5,1},{6,2},{7,3},{8,12},{9,13},{10,... | collective-permute-start | bytes 294920 | tf_op jit(solution)/shard_map/ppermute | solution.py:57
  39.9 3.8 %update.4 = (f32[32,4,128,128]{3,2,1,0:T(8,128)}, f32[8,128]{1,0:T(8,128)S(1)}) custom-call(f32[2,96,128]{2,1,0:T(8,128)S(1)} %get-tuple-element.69.keys_ref, f32[2,3,32,256]{3,2,1,0:T(8,128)S(1)} %get-tuple-element.70.delta_ref, f32[2,32,256]{2,1,0:T(8,128)S(1)} %get-tuple-element.71.total_ref, ...), custom_call_target="tpu_custom_call", output_to_operand_aliasing={{0}: (4, {})} | custom-call | tf_op jit(solution)/shard_map/update/pallas_call | solution.py:43
  43.8 1.1 %collective-permute-start.14 = (bf16[3,2,96,256]{3,2,1,0:T(8,128)(2,1)S(1)}, bf16[3,2,96,256]{3,2,1,0:T(8,128)(2,1)S(1)}, u32[]{:S(2)}, u32[]{:S(2)}) collective-permute-start(bf16[3,2,96,256]{3,2,1,0:T(8,128)(2,1)S(1)} %grow.1.refs_0_.a_ref), channel_id=1, source_target_pairs={{0,4},{1,5},{2,6},{3,7},{4,0},{5,1},{6,2},{7,3},{8,12},{9,13},{10,... | collective-permute-start | bytes 884744 | tf_op jit(solution)/shard_map/ppermute | solution.py:57
  44.9 1.5 %collective-permute-start.19 = (bf16[2,2,96,256]{3,2,1,0:T(8,128)(2,1)S(1)}, bf16[2,2,96,256]{3,2,1,0:T(8,128)(2,1)S(1)}, u32[]{:S(2)}, u32[]{:S(2)}) collective-permute-start(bf16[2,2,96,256]{3,2,1,0:T(8,128)(2,1)S(1)} %stack.3.refs_1_.refs_0_), channel_id=1, source_target_pairs={{0,2},{1,3},{2,0},{3,1},{4,6},{5,7},{6,4},{7,5},{8,10},{9,11},{10,... | collective-permute-start | bytes 589832 | tf_op jit(solution)/shard_map/ppermute | solution.py:57
  46.4 5.5 %collective-permute-done.14.refs_1_.b_ref = bf16[3,2,96,256]{3,2,1,0:T(8,128)(2,1)S(1)} collective-permute-done((bf16[3,2,96,256]{3,2,1,0:T(8,128)(2,1)S(1)}, bf16[3,2,96,256]{3,2,1,0:T(8,128)(2,1)S(1)}, u32[]{:S(2)}, u32[]{:S(2)}) %collective-permute-start.14) | collective-permute-done | bytes 294944 | tf_op jit(solution)/shard_map/ppermute | solution.py:57
  51.9 0.5 collective-permute-start.18
  52.4 0.6 expert_first.2
  53.0 0.6 expert_first.3
  53.7 1.2 %expert_rest.2 = (bf16[4,2,96,256]{3,2,1,0:T(8,128)(2,1)S(1)}, bf16[4,2,96,256]{3,2,1,0:T(8,128)(2,1)S(1)}, f32[192,1]{1,0:T(8,128)S(1)}) custom-call(s32[1]{0:T(128)} %bitcast.me_ref, bf16[3,2,96,256]{3,2,1,0:T(8,128)(2,1)S(1)} %collective-permute-done.15.refs_0_, bf16[3,2,96,256]{3,2,1,0:T(8,128)(2,1)S(1)} %collective-permute-done.16.refs_1_, ...), custom_call_target="tpu_custom_call" | custom-call | tf_op jit(solution)/shard_map/expert_rest/pallas_call | solution.py:43
  54.9 1.5 %expert_rest.3 = (bf16[4,2,96,256]{3,2,1,0:T(8,128)(2,1)S(1)}, bf16[4,2,96,256]{3,2,1,0:T(8,128)(2,1)S(1)}, f32[192,1]{1,0:T(8,128)}) custom-call(s32[1]{0:T(128)} %bitcast.me_ref, bf16[2,2,96,256]{3,2,1,0:T(8,128)(2,1)S(1)} %collective-permute-done.18.refs_0_, bf16[2,2,96,256]{3,2,1,0:T(8,128)(2,1)S(1)} %collective-permute-done.20.refs_1_, ...), custom_call_target="tpu_custom_call" | custom-call | tf_op jit(solution)/shard_map/expert_rest/pallas_call | solution.py:43
  56.5 0.5 collective-permute-start.21
  57.0 1.3 %collective-permute-done.21.b_ref = bf16[4,2,96,256]{3,2,1,0:T(8,128)(2,1)S(1)} collective-permute-done((bf16[4,2,96,256]{3,2,1,0:T(8,128)(2,1)S(1)}, bf16[4,2,96,256]{3,2,1,0:T(8,128)(2,1)S(1)}, u32[]{:S(2)}, u32[]{:S(2)}) %collective-permute-start.21) | collective-permute-done | bytes 393248 | tf_op jit(solution)/shard_map/ppermute | solution.py:57
  58.4 0.8 %collective-permute-start.26 = (bf16[2,2,96,256]{3,2,1,0:T(8,128)(2,1)S(1)}, bf16[2,2,96,256]{3,2,1,0:T(8,128)(2,1)S(1)}, u32[]{:S(2)}, u32[]{:S(2)}) collective-permute-start(bf16[2,2,96,256]{3,2,1,0:T(8,128)(2,1)S(1)} %get-tuple-element.96), channel_id=1, source_target_pairs={{0,4},{1,5},{2,6},{3,7},{4,0},{5,1},{6,2},{7,3},{8,12},{9,13},{10,... | collective-permute-start | bytes 589832 | tf_op jit(solution)/shard_map/ppermute | solution.py:57
  59.3 1.5 %collective-permute-start.23 = (bf16[2,2,96,256]{3,2,1,0:T(8,128)(2,1)S(1)}, bf16[2,2,96,256]{3,2,1,0:T(8,128)(2,1)S(1)}, u32[]{:S(2)}, u32[]{:S(2)}) collective-permute-start(bf16[2,2,96,256]{3,2,1,0:T(8,128)(2,1)S(1)} %get-tuple-element.89), channel_id=1, source_target_pairs={{0,2},{1,3},{2,0},{3,1},{4,6},{5,7},{6,4},{7,5},{8,10},{9,11},{10,... | collective-permute-start | bytes 589832 | tf_op jit(solution)/shard_map/ppermute | solution.py:57
  60.8 0.1 shared_hidden.1.a_ref
  61.0 3.0 %update.5 = (f32[32,4,128,128]{3,2,1,0:T(8,128)}, f32[8,128]{1,0:T(8,128)S(1)}) custom-call(f32[2,96,128]{2,1,0:T(8,128)S(1)} %get-tuple-element.69.keys_ref, f32[2,3,32,256]{3,2,1,0:T(8,128)S(1)} %get-tuple-element.70.delta_ref, f32[2,32,256]{2,1,0:T(8,128)S(1)} %get-tuple-element.71.total_ref, ...), custom_call_target="tpu_custom_call", output_to_operand_aliasing={{0}: (4, {})} | custom-call | tf_op jit(solution)/shard_map/update/pallas_call | solution.py:43
  64.0 1.6 %collective-permute-done.26.b_ref = bf16[2,2,96,256]{3,2,1,0:T(8,128)(2,1)S(1)} collective-permute-done((bf16[2,2,96,256]{3,2,1,0:T(8,128)(2,1)S(1)}, bf16[2,2,96,256]{3,2,1,0:T(8,128)(2,1)S(1)}, u32[]{:S(2)}, u32[]{:S(2)}) %collective-permute-start.26) | collective-permute-done | bytes 196640 | tf_op jit(solution)/shard_map/ppermute | solution.py:57
  65.7 0.7 collective-permute-start.27
  66.5 1.6 %collective-permute-start.24 = (bf16[1,2,96,256]{3,2,1,0:T(8,128)(2,1)S(1)}, bf16[1,2,96,256]{3,2,1,0:T(8,128)(2,1)S(1)}, u32[]{:S(2)}, u32[]{:S(2)}) collective-permute-start(bf16[1,2,96,256]{3,2,1,0:T(8,128)(2,1)S(1)} %get-tuple-element.93), channel_id=1, source_target_pairs={{0,4},{1,5},{2,6},{3,7},{4,0},{5,1},{6,2},{7,3},{8,12},{9,13},{10,... | collective-permute-start | bytes 294920 | tf_op jit(solution)/shard_map/ppermute | solution.py:57
  68.1 2.3 %collective-permute-done.27.b_ref = bf16[1,2,96,256]{3,2,1,0:T(8,128)(2,1)S(1)} collective-permute-done((bf16[1,2,96,256]{3,2,1,0:T(8,128)(2,1)S(1)}, bf16[1,2,96,256]{3,2,1,0:T(8,128)(2,1)S(1)}, u32[]{:S(2)}, u32[]{:S(2)}) %collective-permute-start.27) | collective-permute-done | bytes 98336 | tf_op jit(solution)/shard_map/ppermute | solution.py:57
  70.4 3.0 %collective-permute-start.28 = (bf16[96,256]{1,0:T(8,128)(2,1)S(1)}, bf16[96,256]{1,0:T(8,128)(2,1)S(1)}, u32[]{:S(2)}, u32[]{:S(2)}) collective-permute-start(bf16[96,256]{1,0:T(8,128)(2,1)S(1)} %get-tuple-element.99), channel_id=1, source_target_pairs={{0,16},{8,24},{16,0},{24,8},{1,17},{9,25},{17,1},{25,9},{2,18},{10... | collective-permute-start | bytes 147464 | tf_op jit(solution)/shard_map/ppermute | solution.py:57
  73.4 1.0 %collective-permute-start.29 = (bf16[96,256]{1,0:T(8,128)(2,1)S(1)}, bf16[96,256]{1,0:T(8,128)(2,1)S(1)}, u32[]{:S(2)}, u32[]{:S(2)}) collective-permute-start(bf16[96,256]{1,0:T(8,128)(2,1)S(1)} %get-tuple-element.100), channel_id=1, source_target_pairs={{0,24},{8,16},{16,8},{24,0},{1,25},{9,17},{17,9},{25,1},{2,26},{10... | collective-permute-start | bytes 147464 | tf_op jit(solution)/shard_map/ppermute | solution.py:57
  74.4 0.4 collective-permute-start.25
  74.8 0.2 shared_out.1.refs_0_
  75.0 1.0 %collective-permute-done.28.refs_3_ = bf16[96,256]{1,0:T(8,128)(2,1)S(1)} collective-permute-done((bf16[96,256]{1,0:T(8,128)(2,1)S(1)}, bf16[96,256]{1,0:T(8,128)(2,1)S(1)}, u32[]{:S(2)}, u32[]{:S(2)}) %collective-permute-start.28) | collective-permute-done | bytes 49184 | tf_op jit(solution)/shard_map/ppermute | solution.py:57
  76.0 3.3 %collective-permute-done.29.refs_4_ = bf16[96,256]{1,0:T(8,128)(2,1)S(1)} collective-permute-done((bf16[96,256]{1,0:T(8,128)(2,1)S(1)}, bf16[96,256]{1,0:T(8,128)(2,1)S(1)}, u32[]{:S(2)}, u32[]{:S(2)}) %collective-permute-start.29) | collective-permute-done | bytes 49184 | tf_op jit(solution)/shard_map/ppermute | solution.py:57
  79.3 0.7 finish.1
  (48 shorter events, 1.0 us)
Async XLA Ops:
  0.6 7.2 %collective-permute-start = (bf16[96,256]{1,0:T(8,128)(2,1)}, bf16[96,256]{1,0:T(8,128)(2,1)S(1)}, u32[]{:S(2)}, u32[]{:S(2)}) collective-permute-start(bf16[96,256]{1,0:T(8,128)(2,1)} %bitcast.30), channel_id=1, source_target_pairs={{0,2},{1,3},{2,0},{3,1},{4,6},{5,7},{6,4},{7,5},{8,10},{9,11},{10,... | collective-permute-start | bytes 147464 | tf_op jit(solution)/shard_map/ppermute | solution.py:57
  3.6 4.3 %collective-permute-start.1 = (bf16[96,256]{1,0:T(8,128)(2,1)}, bf16[96,256]{1,0:T(8,128)(2,1)S(1)}, u32[]{:S(2)}, u32[]{:S(2)}) collective-permute-start(bf16[96,256]{1,0:T(8,128)(2,1)} %bitcast.31), channel_id=1, source_target_pairs={{0,4},{1,5},{2,6},{3,7},{4,0},{5,1},{6,2},{7,3},{8,12},{9,13},{10,... | collective-permute-start | bytes 147464 | tf_op jit(solution)/shard_map/ppermute | solution.py:57
  5.2 5.2 %collective-permute-start.2 = (bf16[96,256]{1,0:T(8,128)(2,1)}, bf16[96,256]{1,0:T(8,128)(2,1)S(1)}, u32[]{:S(2)}, u32[]{:S(2)}) collective-permute-start(bf16[96,256]{1,0:T(8,128)(2,1)} %bitcast.32), channel_id=1, source_target_pairs={{0,6},{1,7},{2,4},{3,5},{4,2},{5,3},{6,0},{7,1},{8,14},{9,15},{10,... | collective-permute-start | bytes 147464 | tf_op jit(solution)/shard_map/ppermute | solution.py:57
  5.2 5.3 %copy-start = (bf16[2048,4]{0,1:T(4,128)(2,1)S(1)}, bf16[2048,4]{0,1:T(4,128)(2,1)}, u32[]{:S(2)}) copy-start(bf16[2048,4]{0,1:T(4,128)(2,1)} %param.30) | copy-start | bytes 49156
  5.2 5.3 %copy-start.1 = (bf16[2048,4]{0,1:T(4,128)(2,1)S(1)}, bf16[2048,4]{0,1:T(4,128)(2,1)}, u32[]{:S(2)}) copy-start(bf16[2048,4]{0,1:T(4,128)(2,1)} %param.29) | copy-start | bytes 49156
  10.4 1.8 %collective-permute-start.3 = (bf16[4,96,256]{2,1,0:T(8,128)(2,1)S(1)}, bf16[4,96,256]{2,1,0:T(8,128)(2,1)S(1)}, u32[]{:S(2)}, u32[]{:S(2)}) collective-permute-start(bf16[4,96,256]{2,1,0:T(8,128)(2,1)S(1)} %stack.2.refs_1_.refs_0_), channel_id=1, source_target_pairs={{0,1},{1,0},{2,3},{3,2},{4,5},{5,4},{6,7},{7,6},{8,9},{9,8},{10,11... | collective-permute-start | bytes 589832 | tf_op jit(solution)/shard_map/ppermute | solution.py:57
  19.3 1.6 %collective-permute-start.4 = (bf16[4,96,256]{2,1,0:T(8,128)(2,1)S(1)}, bf16[4,96,256]{2,1,0:T(8,128)(2,1)S(1)}, u32[]{:S(2)}, u32[]{:S(2)}) collective-permute-start(bf16[4,96,256]{2,1,0:T(8,128)(2,1)S(1)} %get-tuple-element.59), channel_id=1, source_target_pairs={{0,1},{1,0},{2,3},{3,2},{4,5},{5,4},{6,7},{7,6},{8,9},{9,8},{10,11... | collective-permute-start | bytes 589832 | tf_op jit(solution)/shard_map/ppermute | solution.py:57
  21.0 5.8 %collective-permute-start.5 = (bf16[96,256]{1,0:T(8,128)(2,1)S(1)}, bf16[96,256]{1,0:T(8,128)(2,1)S(1)}, u32[]{:S(2)}, u32[]{:S(2)}) collective-permute-start(bf16[96,256]{1,0:T(8,128)(2,1)S(1)} %get-tuple-element.104), channel_id=1, source_target_pairs={{0,2},{1,3},{2,0},{3,1},{4,6},{5,7},{6,4},{7,5},{8,10},{9,11},{10,... | collective-permute-start | bytes 147464 | tf_op jit(solution)/shard_map/ppermute | solution.py:57
  21.6 5.2 %collective-permute-start.6 = (bf16[96,256]{1,0:T(8,128)(2,1)S(1)}, bf16[96,256]{1,0:T(8,128)(2,1)S(1)}, u32[]{:S(2)}, u32[]{:S(2)}) collective-permute-start(bf16[96,256]{1,0:T(8,128)(2,1)S(1)} %get-tuple-element.103), channel_id=1, source_target_pairs={{0,4},{1,5},{2,6},{3,7},{4,0},{5,1},{6,2},{7,3},{8,12},{9,13},{10,... | collective-permute-start | bytes 147464 | tf_op jit(solution)/shard_map/ppermute | solution.py:57
  22.0 5.0 %collective-permute-start.7 = (bf16[96,256]{1,0:T(8,128)(2,1)S(1)}, bf16[96,256]{1,0:T(8,128)(2,1)S(1)}, u32[]{:S(2)}, u32[]{:S(2)}) collective-permute-start(bf16[96,256]{1,0:T(8,128)(2,1)S(1)} %get-tuple-element.102), channel_id=1, source_target_pairs={{0,6},{1,7},{2,4},{3,5},{4,2},{5,3},{6,0},{7,1},{8,14},{9,15},{10,... | collective-permute-start | bytes 147464 | tf_op jit(solution)/shard_map/ppermute | solution.py:57
  27.5 9.2 %collective-permute-start.9 = (bf16[2,96,256]{2,1,0:T(8,128)(2,1)S(1)}, bf16[2,96,256]{2,1,0:T(8,128)(2,1)S(1)}, u32[]{:S(2)}, u32[]{:S(2)}) collective-permute-start(bf16[2,96,256]{2,1,0:T(8,128)(2,1)S(1)} %get-tuple-element.66), channel_id=1, source_target_pairs={{0,1},{1,0},{2,3},{3,2},{4,5},{5,4},{6,7},{7,6},{8,9},{9,8},{10,11... | collective-permute-start | bytes 294920 | tf_op jit(solution)/shard_map/ppermute | solution.py:57
  27.6 8.9 %collective-permute-start.10 = (bf16[112,256]{1,0:T(8,128)(2,1)S(1)}, bf16[112,256]{1,0:T(8,128)(2,1)S(1)}, u32[]{:S(2)}, u32[]{:S(2)}) collective-permute-start(bf16[112,256]{1,0:T(8,128)(2,1)S(1)} %get-tuple-element.67), channel_id=1, source_target_pairs={{0,16},{8,24},{16,0},{24,8},{1,17},{9,25},{17,1},{25,9},{2,18},{10... | collective-permute-start | bytes 172040 | tf_op jit(solution)/shard_map/ppermute | solution.py:57
  30.3 6.4 %collective-permute-start.11 = (bf16[112,256]{1,0:T(8,128)(2,1)S(1)}, bf16[112,256]{1,0:T(8,128)(2,1)S(1)}, u32[]{:S(2)}, u32[]{:S(2)}) collective-permute-start(bf16[112,256]{1,0:T(8,128)(2,1)S(1)} %get-tuple-element.68), channel_id=1, source_target_pairs={{0,24},{8,16},{16,8},{24,0},{1,25},{9,17},{17,9},{25,1},{2,26},{10... | collective-permute-start | bytes 172040 | tf_op jit(solution)/shard_map/ppermute | solution.py:57
  31.6 5.1 %collective-permute-start.8 = (bf16[112,256]{1,0:T(8,128)(2,1)S(1)}, bf16[112,256]{1,0:T(8,128)(2,1)S(1)}, u32[]{:S(2)}, u32[]{:S(2)}) collective-permute-start(bf16[112,256]{1,0:T(8,128)(2,1)S(1)} %get-tuple-element.63), channel_id=1, source_target_pairs={{0,8},{8,0},{16,24},{24,16},{1,9},{9,1},{17,25},{25,17},{2,10},{10... | collective-permute-start | bytes 172040 | tf_op jit(solution)/shard_map/ppermute | solution.py:57
  36.8 7.0 %collective-permute-start.12 = (bf16[2,2,96,256]{3,2,1,0:T(8,128)(2,1)S(1)}, bf16[2,2,96,256]{3,2,1,0:T(8,128)(2,1)S(1)}, u32[]{:S(2)}, u32[]{:S(2)}) collective-permute-start(bf16[2,2,96,256]{3,2,1,0:T(8,128)(2,1)S(1)} %open.1.refs_1_.mine_ref), channel_id=1, source_target_pairs={{0,2},{1,3},{2,0},{3,1},{4,6},{5,7},{6,4},{7,5},{8,10},{9,11},{10,... | collective-permute-start | bytes 589832 | tf_op jit(solution)/shard_map/ppermute | solution.py:57
  38.3 5.4 %collective-permute-start.13 = (bf16[1,2,96,256]{3,2,1,0:T(8,128)(2,1)S(1)}, bf16[1,2,96,256]{3,2,1,0:T(8,128)(2,1)S(1)}, u32[]{:S(2)}, u32[]{:S(2)}) collective-permute-start(bf16[1,2,96,256]{3,2,1,0:T(8,128)(2,1)S(1)} %bitcast.26), channel_id=1, source_target_pairs={{0,4},{1,5},{2,6},{3,7},{4,0},{5,1},{6,2},{7,3},{8,12},{9,13},{10,... | collective-permute-start | bytes 294920 | tf_op jit(solution)/shard_map/ppermute | solution.py:57
  43.8 8.1 %collective-permute-start.14 = (bf16[3,2,96,256]{3,2,1,0:T(8,128)(2,1)S(1)}, bf16[3,2,96,256]{3,2,1,0:T(8,128)(2,1)S(1)}, u32[]{:S(2)}, u32[]{:S(2)}) collective-permute-start(bf16[3,2,96,256]{3,2,1,0:T(8,128)(2,1)S(1)} %grow.1.refs_0_.a_ref), channel_id=1, source_target_pairs={{0,4},{1,5},{2,6},{3,7},{4,0},{5,1},{6,2},{7,3},{8,12},{9,13},{10,... | collective-permute-start | bytes 884744 | tf_op jit(solution)/shard_map/ppermute | solution.py:57
  44.9 7.5 %collective-permute-start.19 = (bf16[2,2,96,256]{3,2,1,0:T(8,128)(2,1)S(1)}, bf16[2,2,96,256]{3,2,1,0:T(8,128)(2,1)S(1)}, u32[]{:S(2)}, u32[]{:S(2)}) collective-permute-start(bf16[2,2,96,256]{3,2,1,0:T(8,128)(2,1)S(1)} %stack.3.refs_1_.refs_0_), channel_id=1, source_target_pairs={{0,2},{1,3},{2,0},{3,1},{4,6},{5,7},{6,4},{7,5},{8,10},{9,11},{10,... | collective-permute-start | bytes 589832 | tf_op jit(solution)/shard_map/ppermute | solution.py:57
  46.4 7.2 %collective-permute-start.15 = (bf16[3,2,96,256]{3,2,1,0:T(8,128)(2,1)S(1)}, bf16[3,2,96,256]{3,2,1,0:T(8,128)(2,1)S(1)}, u32[]{:S(2)}, u32[]{:S(2)}) collective-permute-start(bf16[3,2,96,256]{3,2,1,0:T(8,128)(2,1)S(1)} %grow.1.refs_0_.a_ref), channel_id=1, source_target_pairs={{0,1},{1,0},{2,3},{3,2},{4,5},{5,4},{6,7},{7,6},{8,9},{9,8},{10,11... | collective-permute-start | bytes 884744 | tf_op jit(solution)/shard_map/ppermute | solution.py:57
  51.9 1.8 %collective-permute-start.16 = (bf16[3,2,96,256]{3,2,1,0:T(8,128)(2,1)S(1)}, bf16[3,2,96,256]{3,2,1,0:T(8,128)(2,1)S(1)}, u32[]{:S(2)}, u32[]{:S(2)}) collective-permute-start(bf16[3,2,96,256]{3,2,1,0:T(8,128)(2,1)S(1)} %collective-permute-done.14.refs_1_.b_ref), channel_id=1, source_target_pairs={{0,1},{1,0},{2,3},{3,2},{4,5},{5,4},{6,7},{7,6},{8,9},{9,8},{10,11... | collective-permute-start | bytes 884744 | tf_op jit(solution)/shard_map/ppermute | solution.py:57
  51.9 3.0 %collective-permute-start.18 = (bf16[2,2,96,256]{3,2,1,0:T(8,128)(2,1)S(1)}, bf16[2,2,96,256]{3,2,1,0:T(8,128)(2,1)S(1)}, u32[]{:S(2)}, u32[]{:S(2)}) collective-permute-start(bf16[2,2,96,256]{3,2,1,0:T(8,128)(2,1)S(1)} %stack.3.refs_1_.refs_0_), channel_id=1, source_target_pairs={{0,1},{1,0},{2,3},{3,2},{4,5},{5,4},{6,7},{7,6},{8,9},{9,8},{10,11... | collective-permute-start | bytes 589832 | tf_op jit(solution)/shard_map/ppermute | solution.py:57
  52.4 2.5 %collective-permute-start.20 = (bf16[2,2,96,256]{3,2,1,0:T(8,128)(2,1)S(1)}, bf16[2,2,96,256]{3,2,1,0:T(8,128)(2,1)S(1)}, u32[]{:S(2)}, u32[]{:S(2)}) collective-permute-start(bf16[2,2,96,256]{3,2,1,0:T(8,128)(2,1)S(1)} %collective-permute-done.19.refs_1_), channel_id=1, source_target_pairs={{0,1},{1,0},{2,3},{3,2},{4,5},{5,4},{6,7},{7,6},{8,9},{9,8},{10,11... | collective-permute-start | bytes 589832 | tf_op jit(solution)/shard_map/ppermute | solution.py:57
  56.5 1.8 %collective-permute-start.21 = (bf16[4,2,96,256]{3,2,1,0:T(8,128)(2,1)S(1)}, bf16[4,2,96,256]{3,2,1,0:T(8,128)(2,1)S(1)}, u32[]{:S(2)}, u32[]{:S(2)}) collective-permute-start(bf16[4,2,96,256]{3,2,1,0:T(8,128)(2,1)S(1)} %get-tuple-element.85), channel_id=1, source_target_pairs={{0,1},{1,0},{2,3},{3,2},{4,5},{5,4},{6,7},{7,6},{8,9},{9,8},{10,11... | collective-permute-start | bytes 1179656 | tf_op jit(solution)/shard_map/ppermute | solution.py:57
  57.0 2.3 %collective-permute-start.17 = (bf16[4,2,96,256]{3,2,1,0:T(8,128)(2,1)S(1)}, bf16[4,2,96,256]{3,2,1,0:T(8,128)(2,1)S(1)}, u32[]{:S(2)}, u32[]{:S(2)}) collective-permute-start(bf16[4,2,96,256]{3,2,1,0:T(8,128)(2,1)S(1)} %get-tuple-element.80), channel_id=1, source_target_pairs={{0,1},{1,0},{2,3},{3,2},{4,5},{5,4},{6,7},{7,6},{8,9},{9,8},{10,11... | collective-permute-start | bytes 1179656 | tf_op jit(solution)/shard_map/ppermute | solution.py:57
  58.4 7.2 %collective-permute-start.26 = (bf16[2,2,96,256]{3,2,1,0:T(8,128)(2,1)S(1)}, bf16[2,2,96,256]{3,2,1,0:T(8,128)(2,1)S(1)}, u32[]{:S(2)}, u32[]{:S(2)}) collective-permute-start(bf16[2,2,96,256]{3,2,1,0:T(8,128)(2,1)S(1)} %get-tuple-element.96), channel_id=1, source_target_pairs={{0,4},{1,5},{2,6},{3,7},{4,0},{5,1},{6,2},{7,3},{8,12},{9,13},{10,... | collective-permute-start | bytes 589832 | tf_op jit(solution)/shard_map/ppermute | solution.py:57
  59.3 7.1 %collective-permute-start.23 = (bf16[2,2,96,256]{3,2,1,0:T(8,128)(2,1)S(1)}, bf16[2,2,96,256]{3,2,1,0:T(8,128)(2,1)S(1)}, u32[]{:S(2)}, u32[]{:S(2)}) collective-permute-start(bf16[2,2,96,256]{3,2,1,0:T(8,128)(2,1)S(1)} %get-tuple-element.89), channel_id=1, source_target_pairs={{0,2},{1,3},{2,0},{3,1},{4,6},{5,7},{6,4},{7,5},{8,10},{9,11},{10,... | collective-permute-start | bytes 589832 | tf_op jit(solution)/shard_map/ppermute | solution.py:57
  61.0 3.1 %collective-permute-start.22 = (bf16[96,256]{1,0:T(8,128)(2,1)S(1)}, bf16[96,256]{1,0:T(8,128)(2,1)S(1)}, u32[]{:S(2)}, u32[]{:S(2)}) collective-permute-start(bf16[96,256]{1,0:T(8,128)(2,1)S(1)} %shared_hidden.1.a_ref), channel_id=1, source_target_pairs={{0,1},{1,0},{2,3},{3,2},{4,5},{5,4},{6,7},{7,6},{8,9},{9,8},{10,11... | collective-permute-start | bytes 147464 | tf_op jit(solution)/shard_map/ppermute | solution.py:57
  65.7 4.7 %collective-permute-start.27 = (bf16[1,2,96,256]{3,2,1,0:T(8,128)(2,1)S(1)}, bf16[1,2,96,256]{3,2,1,0:T(8,128)(2,1)S(1)}, u32[]{:S(2)}, u32[]{:S(2)}) collective-permute-start(bf16[1,2,96,256]{3,2,1,0:T(8,128)(2,1)S(1)} %get-tuple-element.98), channel_id=1, source_target_pairs={{0,2},{1,3},{2,0},{3,1},{4,6},{5,7},{6,4},{7,5},{8,10},{9,11},{10,... | collective-permute-start | bytes 294920 | tf_op jit(solution)/shard_map/ppermute | solution.py:57
  66.5 7.9 %collective-permute-start.24 = (bf16[1,2,96,256]{3,2,1,0:T(8,128)(2,1)S(1)}, bf16[1,2,96,256]{3,2,1,0:T(8,128)(2,1)S(1)}, u32[]{:S(2)}, u32[]{:S(2)}) collective-permute-start(bf16[1,2,96,256]{3,2,1,0:T(8,128)(2,1)S(1)} %get-tuple-element.93), channel_id=1, source_target_pairs={{0,4},{1,5},{2,6},{3,7},{4,0},{5,1},{6,2},{7,3},{8,12},{9,13},{10,... | collective-permute-start | bytes 294920 | tf_op jit(solution)/shard_map/ppermute | solution.py:57
  70.4 5.6 %collective-permute-start.28 = (bf16[96,256]{1,0:T(8,128)(2,1)S(1)}, bf16[96,256]{1,0:T(8,128)(2,1)S(1)}, u32[]{:S(2)}, u32[]{:S(2)}) collective-permute-start(bf16[96,256]{1,0:T(8,128)(2,1)S(1)} %get-tuple-element.99), channel_id=1, source_target_pairs={{0,16},{8,24},{16,0},{24,8},{1,17},{9,25},{17,1},{25,9},{2,18},{10... | collective-permute-start | bytes 147464 | tf_op jit(solution)/shard_map/ppermute | solution.py:57
  73.4 5.9 %collective-permute-start.29 = (bf16[96,256]{1,0:T(8,128)(2,1)S(1)}, bf16[96,256]{1,0:T(8,128)(2,1)S(1)}, u32[]{:S(2)}, u32[]{:S(2)}) collective-permute-start(bf16[96,256]{1,0:T(8,128)(2,1)S(1)} %get-tuple-element.100), channel_id=1, source_target_pairs={{0,24},{8,16},{16,8},{24,0},{1,25},{9,17},{17,9},{25,1},{2,26},{10... | collective-permute-start | bytes 147464 | tf_op jit(solution)/shard_map/ppermute | solution.py:57
  74.4 4.9 %collective-permute-start.25 = (bf16[96,256]{1,0:T(8,128)(2,1)S(1)}, bf16[96,256]{1,0:T(8,128)(2,1)S(1)}, u32[]{:S(2)}, u32[]{:S(2)}) collective-permute-start(bf16[96,256]{1,0:T(8,128)(2,1)S(1)} %get-tuple-element.95), channel_id=1, source_target_pairs={{0,8},{8,0},{16,24},{24,16},{1,9},{9,1},{17,25},{25,17},{2,10},{10... | collective-permute-start | bytes 147464 | tf_op jit(solution)/shard_map/ppermute | solution.py:57

commit v9 on v7

--- a/solution.py
+++ b/solution.py
@@ -356,13 +356,13 @@
     )
 
 
-def rows_kernel(pairs, *refs):
+def rows_kernel(pairs, me_ref, *refs):
     merged_ref, received = refs[0], refs[1:pairs]
-    mine_ref, gain_ref, extra_ref, _ = refs[pairs : pairs + 4]
-    resid_ref, x_ref = refs[pairs + 4 : pairs + 6]
-    messages = refs[pairs + 6 :]
+    mine_ref, gain_ref, extra_ref, w_ref, _ = refs[pairs : pairs + 5]
+    resid_ref, x_ref, keep_ref, send_ref = refs[pairs + 5 : pairs + 9]
+    messages = refs[pairs + 9 :]
     rows = mine_ref.shape[0]
-    resid = mine_ref[...].astype(F32) + merged_ref[0].astype(F32)
+    resid = mine_ref[...].astype(F32) + merged_ref[...].astype(F32)
     for ref in received:
         resid = resid + ref[...].astype(F32)
     resid_ref[...] = resid
@@ -371,21 +371,42 @@
     for z, ref in enumerate(messages):
         ref[:rows, :] = x
         ref[rows:, :] = extra_ref[z + 1]
-
-
-def make_rows(merged, received, mine, gain, extra, after):
+    chunks, _, width = keep_ref.shape
+    half = w_ref.shape[1] // 2
+    part = half // 2
+    pre = dot(x, w_ref[...]).astype(BF16)
+    odd = me_ref[0] % 2
+    for core in range(2):
+        for n in range(chunks):
+            up, at = divmod(n * width, part)
+            start = up * half + core * part + at
+            piece = pre[:, start : start + width]
+
+            @pl.when(odd == core)
+            def _():
+                keep_ref[n] = piece
+
+            @pl.when(odd != core)
+            def _():
+                send_ref[n] = piece
+
+
+def make_rows(me, merged, received, mine, gain, extra, w, after):
     rows, width = mine.shape
     message = pltpu.VMEM((rows + extra.shape[1], width), BF16)
+    shared = pltpu.VMEM((w.shape[1] // 2 // width, rows, width), BF16)
     return call(
-        functools.partial(rows_kernel, merged.shape[0]),
+        functools.partial(rows_kernel, 1 + len(received)),
         "rows",
         [
             pltpu.VMEM((rows, width), F32),
             pltpu.VMEM((rows, width), BF16),
+            shared,
+            shared,
             *([message] * (extra.shape[0] - 1)),
         ],
-        (),
-        (merged, *received, mine, gain, extra),
+        (me,),
+        (merged, *received, mine, gain, extra, w),
         after,
     )
 
@@ -630,13 +651,13 @@
     return call(last_sum_kernel, "last_sum", [pltpu.VMEM((rows, width), BF16)] * zs, (), (a, b))
 
 
-def one_sum_kernel(a_ref, b_ref, *refs):
-    refs[-1][...] = add(a_ref[...], b_ref[...])
-
-
-def one_sum(a, b, after=()):
-    [out] = call(one_sum_kernel, "one_sum", [pltpu.VMEM(a.shape, BF16)], (), (a, b), after)
-    return out
+def each_sum_kernel(a_ref, b_ref, *refs):
+    for n, ref in enumerate(refs):
+        ref[...] = add(a_ref[n], b_ref[n])
+
+
+def each_sum(a, b):
+    return call(each_sum_kernel, "each_sum", [pltpu.VMEM(a.shape[1:], BF16)] * a.shape[0], (), (a, b))
 
 
 def finish_kernel(count, *refs):
@@ -657,36 +678,6 @@
         after,
     )
     return out
-
-
-def shared_in_kernel(me_ref, x_ref, w_ref, *refs):
-    refs = refs[-2:]
-    chunks, _, width = refs[0].shape
-    half = w_ref.shape[1] // 2
-    part = half // 2
-    pre = dot(x_ref[...], w_ref[...]).astype(BF16)
-    odd = me_ref[0] % 2
-    for core in range(2):
-        for n in range(chunks):
-            up, at = divmod(n * width, part)
-            start = up * half + core * part + at
-            piece = pre[:, start : start + width]
-
-            @pl.when(odd == core)
-            def _():
-                refs[0][n] = piece
-
-            @pl.when(odd != core)
-            def _():
-                refs[1][n] = piece
-
-
-def shared_in(me, x, w, after):
-    rows, width = x.shape
-    shape = (w.shape[1] // 2 // width, rows, width)
-    return call(
-        shared_in_kernel, "shared_in", [pltpu.VMEM(shape, BF16)] * 2, (me,), (x, w), after
-    )
 
 
 def open_kernel(a_ref, b_ref, keep_ref, received_ref, *refs):
@@ -825,10 +816,12 @@
         me, gathered, gain, small, pack, w_query, w_key, w_value, w_zgate, w_out, states, steps
     )
 
-    merged = one_sum(own, exchange(sib, "head", 1))
+    merged = each_sum(own, exchange(sib, "head", 1))
     received = [exchange(merged[p], "head", 2 * p) for p in range(1, pairs)]
-    [w_in] = load((w_expert_in,), (merged,))
-    resid, x, *messages = make_rows(merged, received, mine, gain_mine, extra, (w_in,))
+    [w_in] = load((w_expert_in,), (merged[0],))
+    resid, x, shared_keep, sent, *messages = make_rows(
+        me, merged[0], received, mine, gain_mine, extra, w_shared_in, (w_in,)
+    )
 
     half = seq_count // 2
     messages = [exchange(m, "seq", z + 1) for z, m in enumerate(messages)]
@@ -836,7 +829,6 @@
     natural, reverse = list(range(pairs)), bit_reversed(pairs)
     blocks = tuple(range(seqs // PER_BLOCK))
     quarters = [blocks[len(blocks) * n // 4 : len(blocks) * (n + 1) // 4] for n in range(4)]
-    shared_keep, sent = shared_in(me, x, w_shared_in, ())
     shared_received = exchange(sent, "head", 1)
     [w_down] = load((w_expert_out,), (shared_keep,))
     if half == 2:

time: 79.6 us -> 79.6 us (level)
    pallas_call x29 -> x28, Pallas kernels: 30.8 us -> 30.8 us  [call(): pl.pallas_call(body, out_shape=tuple(out_shapes), in_specs=[SMEM_SPEC] *...]
where the time goes in v9:
time: 79.6 us; the launch traced here: 79.3 us
  Pallas kernels  30.8 us (39%)
  starting transfers between devices  26 us (33%)
  waiting for transfers between devices  21.5 us (27%)
  between operations  0.94 us (1%)
    pallas_call x28, Pallas kernels, call(): pl.pallas_call(body, out_shape=tuple(out_shapes), in_specs=[SMEM_SPEC] *...  30.8 us
    ppermute x30, starting transfers between devices, exchange(): return lax.ppermute(x, axis, [(i, i ^ bit) for i in range(size)])  26 us
    ppermute x30, waiting for transfers between devices, exchange(): return lax.ppermute(x, axis, [(i, i ^ bit) for i in range(size)])  21.5 us
  transfers between devices with their start and end apart: 30, of which 13 were waited for; matrix products, arithmetic and copies ran while one was open for 0% of the time, Pallas kernels for 28%

profile of v9, /device:TPU:0, one launch (start us, length us, event | category | flops | bytes accessed | tf_op | source)
XLA Modules:
  0.0 79.3 jit_solution(2825586610318925171)
XLA Ops:
  0.6 3.0 %collective-permute-start = (bf16[96,256]{1,0:T(8,128)(2,1)}, bf16[96,256]{1,0:T(8,128)(2,1)S(1)}, u32[]{:S(2)}, u32[]{:S(2)}) collective-permute-start(bf16[96,256]{1,0:T(8,128)(2,1)} %bitcast.24), channel_id=1, source_target_pairs={{0,2},{1,3},{2,0},{3,1},{4,6},{5,7},{6,4},{7,5},{8,10},{9,11},{10,... | collective-permute-start | bytes 147464 | tf_op jit(solution)/shard_map/ppermute | solution.py:57
  3.6 1.5 %collective-permute-start.1 = (bf16[96,256]{1,0:T(8,128)(2,1)}, bf16[96,256]{1,0:T(8,128)(2,1)S(1)}, u32[]{:S(2)}, u32[]{:S(2)}) collective-permute-start(bf16[96,256]{1,0:T(8,128)(2,1)} %bitcast.25), channel_id=1, source_target_pairs={{0,4},{1,5},{2,6},{3,7},{4,0},{5,1},{6,2},{7,3},{8,12},{9,13},{10,... | collective-permute-start | bytes 147464 | tf_op jit(solution)/shard_map/ppermute | solution.py:57
  5.2 2.6 %bring.1 = (bf16[96,256]{1,0:T(8,128)(2,1)S(1)}, bf16[2048,256]{1,0:T(8,128)(2,1)S(1)}, bf16[2048,256]{1,0:T(8,128)(2,1)S(1)}, bf16[2048,512]{1,0:T(8,128)(2,1)S...) custom-call(s32[1]{0:T(128)} %bitcast.me_ref, ...), custom_call_target="tpu_custom_call" | custom-call | tf_op jit(solution)/shard_map/bring/pallas_call | solution.py:43
  7.9 2.4 %collective-permute-done.2.refs_3_ = bf16[96,256]{1,0:T(8,128)(2,1)S(1)} collective-permute-done((bf16[96,256]{1,0:T(8,128)(2,1)}, bf16[96,256]{1,0:T(8,128)(2,1)S(1)}, u32[]{:S(2)}, u32[]{:S(2)}) %collective-permute-start.2) | collective-permute-done | bytes 49184 | tf_op jit(solution)/shard_map/ppermute | solution.py:57
  10.5 1.6 %load.3.refs_8_ = bf16[2048,512]{1,0:T(8,128)(2,1)S(1)} custom-call(bf16[2048,512]{1,0:T(8,128)(2,1)} %refs_0_.3, bf16[4,96,256]{2,1,0:T(8,128)(2,1)S(1)} %stack.2.refs_1_.refs_0_), custom_call_target="tpu_custom_call" | custom-call | tf_op jit(solution)/shard_map/load/pallas_call | solution.py:43
  12.1 7.1 %front.1 = (bf16[4,96,256]{2,1,0:T(8,128)(2,1)S(1)}, bf16[4,96,256]{2,1,0:T(8,128)(2,1)S(1)}, f32[2,96,128]{2,1,0:T(8,128)S(1)}, f32[2,3,32,256]{3,2,1,0:T(8,128)S(1)}, f32[2,32,256]{2,1,0:T(8,128)S(1)}) custom-call(s32[1]{0:T(128)} %bitcast.me_ref, bf16[4,96,256]{2,1,0:T(8,128)(2,1)S(1)} %stack.2.refs_1_.refs_0_, ...), custom_call_target="tpu_custom_call" | custom-call | tf_op jit(solution)/shard_map/front/pallas_call | solution.py:43
  19.3 0.5 collective-permute-start.4
  19.8 1.1 %collective-permute-done.4.b_ref = bf16[4,96,256]{2,1,0:T(8,128)(2,1)S(1)} collective-permute-done((bf16[4,96,256]{2,1,0:T(8,128)(2,1)S(1)}, bf16[4,96,256]{2,1,0:T(8,128)(2,1)S(1)}, u32[]{:S(2)}, u32[]{:S(2)}) %collective-permute-start.4) | collective-permute-done | bytes 196640 | tf_op jit(solution)/shard_map/ppermute | solution.py:57
  21.0 0.6 collective-permute-start.5
  21.6 0.4 collective-permute-start.6
  22.0 2.5 %collective-permute-start.7 = (bf16[96,256]{1,0:T(8,128)(2,1)S(1)}, bf16[96,256]{1,0:T(8,128)(2,1)S(1)}, u32[]{:S(2)}, u32[]{:S(2)}) collective-permute-start(bf16[96,256]{1,0:T(8,128)(2,1)S(1)} %get-tuple-element.67), channel_id=1, source_target_pairs={{0,6},{1,7},{2,4},{3,5},{4,2},{5,3},{6,0},{7,1},{8,14},{9,15},{10,... | collective-permute-start | bytes 147464 | tf_op jit(solution)/shard_map/ppermute | solution.py:57
  24.5 2.2 %load.4.refs_8_.refs_3_ = bf16[1,2048,1024]{2,1,0:T(8,128)(2,1)S(1)} custom-call(bf16[1,2048,1024]{2,1,0:T(8,128)(2,1)} %refs_0_.4, bf16[96,256]{1,0:T(8,128)(2,1)S(1)} %get-tuple-element.64.refs_1_.refs_0_), custom_call_target="tpu_custom_call" | custom-call | tf_op jit(solution)/shard_map/load/pallas_call | solution.py:43
  26.7 0.2 collective-permute-done.7.refs_3_
  27.0 0.4 rows.1
  27.5 1.7 %collective-permute-start.8 = (bf16[112,256]{1,0:T(8,128)(2,1)S(1)}, bf16[112,256]{1,0:T(8,128)(2,1)S(1)}, u32[]{:S(2)}, u32[]{:S(2)}) collective-permute-start(bf16[112,256]{1,0:T(8,128)(2,1)S(1)} %get-tuple-element.72), channel_id=1, source_target_pairs={{0,8},{8,0},{16,24},{24,16},{1,9},{9,1},{17,25},{25,17},{2,10},{10... | collective-permute-start | bytes 172040 | tf_op jit(solution)/shard_map/ppermute | solution.py:57
  29.2 2.6 %collective-permute-start.10 = (bf16[112,256]{1,0:T(8,128)(2,1)S(1)}, bf16[112,256]{1,0:T(8,128)(2,1)S(1)}, u32[]{:S(2)}, u32[]{:S(2)}) collective-permute-start(bf16[112,256]{1,0:T(8,128)(2,1)S(1)} %get-tuple-element.75), channel_id=1, source_target_pairs={{0,16},{8,24},{16,0},{24,8},{1,17},{9,25},{17,1},{25,9},{2,18},{10... | collective-permute-start | bytes 172040 | tf_op jit(solution)/shard_map/ppermute | solution.py:57
  32.0 1.6 %load.5.refs_2_.refs_6_ = bf16[1,512,2048]{2,1,0:T(8,128)(2,1)S(1)} custom-call(bf16[1,512,2048]{2,1,0:T(8,128)(2,1)} %refs_0_.5, bf16[2,96,256]{2,1,0:T(8,128)(2,1)S(1)} %get-tuple-element.73.refs_1_.keep_ref), custom_call_target="tpu_custom_call" | custom-call | tf_op jit(solution)/shard_map/load/pallas_call | solution.py:43
  33.6 2.2 %collective-permute-done.10.refs_0_.a_ref.refs_7_ = bf16[112,256]{1,0:T(8,128)(2,1)S(1)} collective-permute-done((bf16[112,256]{1,0:T(8,128)(2,1)S(1)}, bf16[112,256]{1,0:T(8,128)(2,1)S(1)}, u32[]{:S(2)}, u32[]{:S(2)}) %collective-permute-start.10) | collective-permute-done | bytes 57376 | tf_op jit(solution)/shard_map/ppermute | solution.py:57
  35.8 2.1 %collective-permute-done.11.refs_1_.b_ref.refs_8_ = bf16[112,256]{1,0:T(8,128)(2,1)S(1)} collective-permute-done((bf16[112,256]{1,0:T(8,128)(2,1)S(1)}, bf16[112,256]{1,0:T(8,128)(2,1)S(1)}, u32[]{:S(2)}, u32[]{:S(2)}) %collective-permute-start.11) | collective-permute-done | bytes 57376 | tf_op jit(solution)/shard_map/ppermute | solution.py:57
  37.9 1.6 %collective-permute-start.12 = (bf16[2,2,96,256]{3,2,1,0:T(8,128)(2,1)S(1)}, bf16[2,2,96,256]{3,2,1,0:T(8,128)(2,1)S(1)}, u32[]{:S(2)}, u32[]{:S(2)}) collective-permute-start(bf16[2,2,96,256]{3,2,1,0:T(8,128)(2,1)S(1)} %open.1.refs_0_.mine_ref), channel_id=1, source_target_pairs={{0,2},{1,3},{2,0},{3,1},{4,6},{5,7},{6,4},{7,5},{8,10},{9,11},{10,... | collective-permute-start | bytes 589832 | tf_op jit(solution)/shard_map/ppermute | solution.py:57
  39.5 1.6 %collective-permute-start.13 = (bf16[1,2,96,256]{3,2,1,0:T(8,128)(2,1)S(1)}, bf16[1,2,96,256]{3,2,1,0:T(8,128)(2,1)S(1)}, u32[]{:S(2)}, u32[]{:S(2)}) collective-permute-start(bf16[1,2,96,256]{3,2,1,0:T(8,128)(2,1)S(1)} %bitcast.20), channel_id=1, source_target_pairs={{0,4},{1,5},{2,6},{3,7},{4,0},{5,1},{6,2},{7,3},{8,12},{9,13},{10,... | collective-permute-start | bytes 294920 | tf_op jit(solution)/shard_map/ppermute | solution.py:57
  41.0 3.8 %update.3 = (f32[32,4,128,128]{3,2,1,0:T(8,128)}, f32[8,128]{1,0:T(8,128)S(1)}) custom-call(f32[2,96,128]{2,1,0:T(8,128)S(1)} %get-tuple-element.77.keys_ref, f32[2,3,32,256]{3,2,1,0:T(8,128)S(1)} %get-tuple-element.78.delta_ref, f32[2,32,256]{2,1,0:T(8,128)S(1)} %get-tuple-element.79.total_ref, f32[32,4,128,128]{3,2,1,0:T(8,128)} %states_ref.5, ...), custom_call_target="tpu_custom_call" | custom-call | tf_op jit(solution)/shard_map/update/pallas_call | solution.py:43
  44.9 0.8 %collective-permute-start.14 = (bf16[3,2,96,256]{3,2,1,0:T(8,128)(2,1)S(1)}, bf16[3,2,96,256]{3,2,1,0:T(8,128)(2,1)S(1)}, u32[]{:S(2)}, u32[]{:S(2)}) collective-permute-start(bf16[3,2,96,256]{3,2,1,0:T(8,128)(2,1)S(1)} %grow.1.refs_0_.a_ref), channel_id=1, source_target_pairs={{0,4},{1,5},{2,6},{3,7},{4,0},{5,1},{6,2},{7,3},{8,12},{9,13},{10,... | collective-permute-start | bytes 884744 | tf_op jit(solution)/shard_map/ppermute | solution.py:57
  45.8 0.9 %collective-permute-start.19 = (bf16[2,2,96,256]{3,2,1,0:T(8,128)(2,1)S(1)}, bf16[2,2,96,256]{3,2,1,0:T(8,128)(2,1)S(1)}, u32[]{:S(2)}, u32[]{:S(2)}) collective-permute-start(bf16[2,2,96,256]{3,2,1,0:T(8,128)(2,1)S(1)} %stack.3.refs_1_.refs_0_), channel_id=1, source_target_pairs={{0,2},{1,3},{2,0},{3,1},{4,6},{5,7},{6,4},{7,5},{8,10},{9,11},{10,... | collective-permute-start | bytes 589832 | tf_op jit(solution)/shard_map/ppermute | solution.py:57
  46.7 5.4 %collective-permute-done.14.refs_1_.b_ref = bf16[3,2,96,256]{3,2,1,0:T(8,128)(2,1)S(1)} collective-permute-done((bf16[3,2,96,256]{3,2,1,0:T(8,128)(2,1)S(1)}, bf16[3,2,96,256]{3,2,1,0:T(8,128)(2,1)S(1)}, u32[]{:S(2)}, u32[]{:S(2)}) %collective-permute-start.14) | collective-permute-done | bytes 294944 | tf_op jit(solution)/shard_map/ppermute | solution.py:57
  52.2 0.5 collective-permute-start.18
  52.7 0.6 expert_first.2
  53.3 0.6 expert_first.3
  53.9 1.2 %expert_rest.2 = (bf16[4,2,96,256]{3,2,1,0:T(8,128)(2,1)S(1)}, bf16[4,2,96,256]{3,2,1,0:T(8,128)(2,1)S(1)}, f32[192,1]{1,0:T(8,128)S(1)}) custom-call(s32[1]{0:T(128)} %bitcast.me_ref, bf16[3,2,96,256]{3,2,1,0:T(8,128)(2,1)S(1)} %collective-permute-done.15.refs_0_, bf16[3,2,96,256]{3,2,1,0:T(8,128)(2,1)S(1)} %collective-permute-done.16.refs_1_, ...), custom_call_target="tpu_custom_call" | custom-call | tf_op jit(solution)/shard_map/expert_rest/pallas_call | solution.py:43
  55.1 0.6 collective-permute-start.17
  55.8 1.6 %expert_rest.3 = (bf16[4,2,96,256]{3,2,1,0:T(8,128)(2,1)S(1)}, bf16[4,2,96,256]{3,2,1,0:T(8,128)(2,1)S(1)}, f32[192,1]{1,0:T(8,128)}) custom-call(s32[1]{0:T(128)} %bitcast.me_ref, bf16[2,2,96,256]{3,2,1,0:T(8,128)(2,1)S(1)} %collective-permute-done.18.refs_0_, bf16[2,2,96,256]{3,2,1,0:T(8,128)(2,1)S(1)} %collective-permute-done.20.refs_1_, ...), custom_call_target="tpu_custom_call" | custom-call | tf_op jit(solution)/shard_map/expert_rest/pallas_call | solution.py:43
  57.5 0.6 collective-permute-start.23
  58.0 1.0 %collective-permute-done.21.b_ref = bf16[4,2,96,256]{3,2,1,0:T(8,128)(2,1)S(1)} collective-permute-done((bf16[4,2,96,256]{3,2,1,0:T(8,128)(2,1)S(1)}, bf16[4,2,96,256]{3,2,1,0:T(8,128)(2,1)S(1)}, u32[]{:S(2)}, u32[]{:S(2)}) %collective-permute-start.21) | collective-permute-done | bytes 393248 | tf_op jit(solution)/shard_map/ppermute | solution.py:57
  59.2 0.6 collective-permute-start.26
  59.9 3.0 %update.4 = (f32[32,4,128,128]{3,2,1,0:T(8,128)}, f32[8,128]{1,0:T(8,128)S(1)}) custom-call(f32[2,96,128]{2,1,0:T(8,128)S(1)} %get-tuple-element.77.keys_ref, f32[2,3,32,256]{3,2,1,0:T(8,128)S(1)} %get-tuple-element.78.delta_ref, f32[2,32,256]{2,1,0:T(8,128)S(1)} %get-tuple-element.79.total_ref, ...), custom_call_target="tpu_custom_call", output_to_operand_aliasing={{0}: (4, {})} | custom-call | tf_op jit(solution)/shard_map/update/pallas_call | solution.py:43
  62.9 1.9 %collective-permute-done.23.b_ref = bf16[2,2,96,256]{3,2,1,0:T(8,128)(2,1)S(1)} collective-permute-done((bf16[2,2,96,256]{3,2,1,0:T(8,128)(2,1)S(1)}, bf16[2,2,96,256]{3,2,1,0:T(8,128)(2,1)S(1)}, u32[]{:S(2)}, u32[]{:S(2)}) %collective-permute-start.23) | collective-permute-done | bytes 196640 | tf_op jit(solution)/shard_map/ppermute | solution.py:57
  64.9 0.6 collective-permute-start.24
  65.4 0.7 collective-permute-done.26.b_ref
  66.2 0.6 collective-permute-start.27
  66.8 2.7 %collective-permute-done.24.b_ref = bf16[1,2,96,256]{3,2,1,0:T(8,128)(2,1)S(1)} collective-permute-done((bf16[1,2,96,256]{3,2,1,0:T(8,128)(2,1)S(1)}, bf16[1,2,96,256]{3,2,1,0:T(8,128)(2,1)S(1)}, u32[]{:S(2)}, u32[]{:S(2)}) %collective-permute-start.24) | collective-permute-done | bytes 98336 | tf_op jit(solution)/shard_map/ppermute | solution.py:57
  69.6 0.9 %collective-permute-start.25 = (bf16[96,256]{1,0:T(8,128)(2,1)S(1)}, bf16[96,256]{1,0:T(8,128)(2,1)S(1)}, u32[]{:S(2)}, u32[]{:S(2)}) collective-permute-start(bf16[96,256]{1,0:T(8,128)(2,1)S(1)} %get-tuple-element.101), channel_id=1, source_target_pairs={{0,8},{8,0},{16,24},{24,16},{1,9},{9,1},{17,25},{25,17},{2,10},{10... | collective-permute-start | bytes 147464 | tf_op jit(solution)/shard_map/ppermute | solution.py:57
  70.5 0.4 collective-permute-done.27.b_ref
  70.9 1.8 %collective-permute-start.28 = (bf16[96,256]{1,0:T(8,128)(2,1)S(1)}, bf16[96,256]{1,0:T(8,128)(2,1)S(1)}, u32[]{:S(2)}, u32[]{:S(2)}) collective-permute-start(bf16[96,256]{1,0:T(8,128)(2,1)S(1)} %get-tuple-element.105), channel_id=1, source_target_pairs={{0,16},{8,24},{16,0},{24,8},{1,17},{9,25},{17,1},{25,9},{2,18},{10... | collective-permute-start | bytes 147464 | tf_op jit(solution)/shard_map/ppermute | solution.py:57
  72.7 1.5 %collective-permute-start.29 = (bf16[96,256]{1,0:T(8,128)(2,1)S(1)}, bf16[96,256]{1,0:T(8,128)(2,1)S(1)}, u32[]{:S(2)}, u32[]{:S(2)}) collective-permute-start(bf16[96,256]{1,0:T(8,128)(2,1)S(1)} %get-tuple-element.106.refs_1_), channel_id=1, source_target_pairs={{0,24},{8,16},{16,8},{24,0},{1,25},{9,17},{17,9},{25,1},{2,26},{10... | collective-permute-start | bytes 147464 | tf_op jit(solution)/shard_map/ppermute | solution.py:57
  74.2 0.2 shared_out.1.refs_0_
  74.4 2.9 %update.5 = (f32[32,4,128,128]{3,2,1,0:T(8,128)}, f32[8,128]{1,0:T(8,128)S(1)}) custom-call(f32[2,96,128]{2,1,0:T(8,128)S(1)} %get-tuple-element.77.keys_ref, f32[2,3,32,256]{3,2,1,0:T(8,128)S(1)} %get-tuple-element.78.delta_ref, f32[2,32,256]{2,1,0:T(8,128)S(1)} %get-tuple-element.79.total_ref, ...), custom_call_target="tpu_custom_call", output_to_operand_aliasing={{0}: (4, {})} | custom-call | tf_op jit(solution)/shard_map/update/pallas_call | solution.py:43
  77.4 1.2 %collective-permute-done.29.refs_4_ = bf16[96,256]{1,0:T(8,128)(2,1)S(1)} collective-permute-done((bf16[96,256]{1,0:T(8,128)(2,1)S(1)}, bf16[96,256]{1,0:T(8,128)(2,1)S(1)}, u32[]{:S(2)}, u32[]{:S(2)}) %collective-permute-start.29) | collective-permute-done | bytes 49184 | tf_op jit(solution)/shard_map/ppermute | solution.py:57
  78.6 0.7 finish.1
  (46 shorter events, 1.2 us)
Async XLA Ops:
  0.6 7.2 %collective-permute-start = (bf16[96,256]{1,0:T(8,128)(2,1)}, bf16[96,256]{1,0:T(8,128)(2,1)S(1)}, u32[]{:S(2)}, u32[]{:S(2)}) collective-permute-start(bf16[96,256]{1,0:T(8,128)(2,1)} %bitcast.24), channel_id=1, source_target_pairs={{0,2},{1,3},{2,0},{3,1},{4,6},{5,7},{6,4},{7,5},{8,10},{9,11},{10,... | collective-permute-start | bytes 147464 | tf_op jit(solution)/shard_map/ppermute | solution.py:57
  3.6 4.3 %collective-permute-start.1 = (bf16[96,256]{1,0:T(8,128)(2,1)}, bf16[96,256]{1,0:T(8,128)(2,1)S(1)}, u32[]{:S(2)}, u32[]{:S(2)}) collective-permute-start(bf16[96,256]{1,0:T(8,128)(2,1)} %bitcast.25), channel_id=1, source_target_pairs={{0,4},{1,5},{2,6},{3,7},{4,0},{5,1},{6,2},{7,3},{8,12},{9,13},{10,... | collective-permute-start | bytes 147464 | tf_op jit(solution)/shard_map/ppermute | solution.py:57
  5.2 5.2 %collective-permute-start.2 = (bf16[96,256]{1,0:T(8,128)(2,1)}, bf16[96,256]{1,0:T(8,128)(2,1)S(1)}, u32[]{:S(2)}, u32[]{:S(2)}) collective-permute-start(bf16[96,256]{1,0:T(8,128)(2,1)} %bitcast.26), channel_id=1, source_target_pairs={{0,6},{1,7},{2,4},{3,5},{4,2},{5,3},{6,0},{7,1},{8,14},{9,15},{10,... | collective-permute-start | bytes 147464 | tf_op jit(solution)/shard_map/ppermute | solution.py:57
  5.2 5.3 %copy-start = (bf16[2048,4]{0,1:T(4,128)(2,1)S(1)}, bf16[2048,4]{0,1:T(4,128)(2,1)}, u32[]{:S(2)}) copy-start(bf16[2048,4]{0,1:T(4,128)(2,1)} %param.30) | copy-start | bytes 49156
  5.2 5.3 %copy-start.1 = (bf16[2048,4]{0,1:T(4,128)(2,1)S(1)}, bf16[2048,4]{0,1:T(4,128)(2,1)}, u32[]{:S(2)}) copy-start(bf16[2048,4]{0,1:T(4,128)(2,1)} %param.29) | copy-start | bytes 49156
  10.4 1.8 %collective-permute-start.3 = (bf16[4,96,256]{2,1,0:T(8,128)(2,1)S(1)}, bf16[4,96,256]{2,1,0:T(8,128)(2,1)S(1)}, u32[]{:S(2)}, u32[]{:S(2)}) collective-permute-start(bf16[4,96,256]{2,1,0:T(8,128)(2,1)S(1)} %stack.2.refs_1_.refs_0_), channel_id=1, source_target_pairs={{0,1},{1,0},{2,3},{3,2},{4,5},{5,4},{6,7},{7,6},{8,9},{9,8},{10,11... | collective-permute-start | bytes 589832 | tf_op jit(solution)/shard_map/ppermute | solution.py:57
  19.3 1.6 %collective-permute-start.4 = (bf16[4,96,256]{2,1,0:T(8,128)(2,1)S(1)}, bf16[4,96,256]{2,1,0:T(8,128)(2,1)S(1)}, u32[]{:S(2)}, u32[]{:S(2)}) collective-permute-start(bf16[4,96,256]{2,1,0:T(8,128)(2,1)S(1)} %get-tuple-element.63), channel_id=1, source_target_pairs={{0,1},{1,0},{2,3},{3,2},{4,5},{5,4},{6,7},{7,6},{8,9},{9,8},{10,11... | collective-permute-start | bytes 589832 | tf_op jit(solution)/shard_map/ppermute | solution.py:57
  21.0 5.8 %collective-permute-start.5 = (bf16[96,256]{1,0:T(8,128)(2,1)S(1)}, bf16[96,256]{1,0:T(8,128)(2,1)S(1)}, u32[]{:S(2)}, u32[]{:S(2)}) collective-permute-start(bf16[96,256]{1,0:T(8,128)(2,1)S(1)} %get-tuple-element.65), channel_id=1, source_target_pairs={{0,2},{1,3},{2,0},{3,1},{4,6},{5,7},{6,4},{7,5},{8,10},{9,11},{10,... | collective-permute-start | bytes 147464 | tf_op jit(solution)/shard_map/ppermute | solution.py:57
  21.6 5.2 %collective-permute-start.6 = (bf16[96,256]{1,0:T(8,128)(2,1)S(1)}, bf16[96,256]{1,0:T(8,128)(2,1)S(1)}, u32[]{:S(2)}, u32[]{:S(2)}) collective-permute-start(bf16[96,256]{1,0:T(8,128)(2,1)S(1)} %get-tuple-element.66), channel_id=1, source_target_pairs={{0,4},{1,5},{2,6},{3,7},{4,0},{5,1},{6,2},{7,3},{8,12},{9,13},{10,... | collective-permute-start | bytes 147464 | tf_op jit(solution)/shard_map/ppermute | solution.py:57
  22.0 5.0 %collective-permute-start.7 = (bf16[96,256]{1,0:T(8,128)(2,1)S(1)}, bf16[96,256]{1,0:T(8,128)(2,1)S(1)}, u32[]{:S(2)}, u32[]{:S(2)}) collective-permute-start(bf16[96,256]{1,0:T(8,128)(2,1)S(1)} %get-tuple-element.67), channel_id=1, source_target_pairs={{0,6},{1,7},{2,4},{3,5},{4,2},{5,3},{6,0},{7,1},{8,14},{9,15},{10,... | collective-permute-start | bytes 147464 | tf_op jit(solution)/shard_map/ppermute | solution.py:57
  27.4 10.4 %collective-permute-start.9 = (bf16[2,96,256]{2,1,0:T(8,128)(2,1)S(1)}, bf16[2,96,256]{2,1,0:T(8,128)(2,1)S(1)}, u32[]{:S(2)}, u32[]{:S(2)}) collective-permute-start(bf16[2,96,256]{2,1,0:T(8,128)(2,1)S(1)} %get-tuple-element.74), channel_id=1, source_target_pairs={{0,1},{1,0},{2,3},{3,2},{4,5},{5,4},{6,7},{7,6},{8,9},{9,8},{10,11... | collective-permute-start | bytes 294920 | tf_op jit(solution)/shard_map/ppermute | solution.py:57
  27.5 6.1 %collective-permute-start.8 = (bf16[112,256]{1,0:T(8,128)(2,1)S(1)}, bf16[112,256]{1,0:T(8,128)(2,1)S(1)}, u32[]{:S(2)}, u32[]{:S(2)}) collective-permute-start(bf16[112,256]{1,0:T(8,128)(2,1)S(1)} %get-tuple-element.72), channel_id=1, source_target_pairs={{0,8},{8,0},{16,24},{24,16},{1,9},{9,1},{17,25},{25,17},{2,10},{10... | collective-permute-start | bytes 172040 | tf_op jit(solution)/shard_map/ppermute | solution.py:57
  29.2 6.6 %collective-permute-start.10 = (bf16[112,256]{1,0:T(8,128)(2,1)S(1)}, bf16[112,256]{1,0:T(8,128)(2,1)S(1)}, u32[]{:S(2)}, u32[]{:S(2)}) collective-permute-start(bf16[112,256]{1,0:T(8,128)(2,1)S(1)} %get-tuple-element.75), channel_id=1, source_target_pairs={{0,16},{8,24},{16,0},{24,8},{1,17},{9,25},{17,1},{25,9},{2,18},{10... | collective-permute-start | bytes 172040 | tf_op jit(solution)/shard_map/ppermute | solution.py:57
  31.8 6.0 %collective-permute-start.11 = (bf16[112,256]{1,0:T(8,128)(2,1)S(1)}, bf16[112,256]{1,0:T(8,128)(2,1)S(1)}, u32[]{:S(2)}, u32[]{:S(2)}) collective-permute-start(bf16[112,256]{1,0:T(8,128)(2,1)S(1)} %get-tuple-element.76), channel_id=1, source_target_pairs={{0,24},{8,16},{16,8},{24,0},{1,25},{9,17},{17,9},{25,1},{2,26},{10... | collective-permute-start | bytes 172040 | tf_op jit(solution)/shard_map/ppermute | solution.py:57
  37.9 7.0 %collective-permute-start.12 = (bf16[2,2,96,256]{3,2,1,0:T(8,128)(2,1)S(1)}, bf16[2,2,96,256]{3,2,1,0:T(8,128)(2,1)S(1)}, u32[]{:S(2)}, u32[]{:S(2)}) collective-permute-start(bf16[2,2,96,256]{3,2,1,0:T(8,128)(2,1)S(1)} %open.1.refs_0_.mine_ref), channel_id=1, source_target_pairs={{0,2},{1,3},{2,0},{3,1},{4,6},{5,7},{6,4},{7,5},{8,10},{9,11},{10,... | collective-permute-start | bytes 589832 | tf_op jit(solution)/shard_map/ppermute | solution.py:57
  39.5 5.4 %collective-permute-start.13 = (bf16[1,2,96,256]{3,2,1,0:T(8,128)(2,1)S(1)}, bf16[1,2,96,256]{3,2,1,0:T(8,128)(2,1)S(1)}, u32[]{:S(2)}, u32[]{:S(2)}) collective-permute-start(bf16[1,2,96,256]{3,2,1,0:T(8,128)(2,1)S(1)} %bitcast.20), channel_id=1, source_target_pairs={{0,4},{1,5},{2,6},{3,7},{4,0},{5,1},{6,2},{7,3},{8,12},{9,13},{10,... | collective-permute-start | bytes 294920 | tf_op jit(solution)/shard_map/ppermute | solution.py:57
  44.9 7.2 %collective-permute-start.14 = (bf16[3,2,96,256]{3,2,1,0:T(8,128)(2,1)S(1)}, bf16[3,2,96,256]{3,2,1,0:T(8,128)(2,1)S(1)}, u32[]{:S(2)}, u32[]{:S(2)}) collective-permute-start(bf16[3,2,96,256]{3,2,1,0:T(8,128)(2,1)S(1)} %grow.1.refs_0_.a_ref), channel_id=1, source_target_pairs={{0,4},{1,5},{2,6},{3,7},{4,0},{5,1},{6,2},{7,3},{8,12},{9,13},{10,... | collective-permute-start | bytes 884744 | tf_op jit(solution)/shard_map/ppermute | solution.py:57
  45.8 6.9 %collective-permute-start.19 = (bf16[2,2,96,256]{3,2,1,0:T(8,128)(2,1)S(1)}, bf16[2,2,96,256]{3,2,1,0:T(8,128)(2,1)S(1)}, u32[]{:S(2)}, u32[]{:S(2)}) collective-permute-start(bf16[2,2,96,256]{3,2,1,0:T(8,128)(2,1)S(1)} %stack.3.refs_1_.refs_0_), channel_id=1, source_target_pairs={{0,2},{1,3},{2,0},{3,1},{4,6},{5,7},{6,4},{7,5},{8,10},{9,11},{10,... | collective-permute-start | bytes 589832 | tf_op jit(solution)/shard_map/ppermute | solution.py:57
  46.7 7.2 %collective-permute-start.15 = (bf16[3,2,96,256]{3,2,1,0:T(8,128)(2,1)S(1)}, bf16[3,2,96,256]{3,2,1,0:T(8,128)(2,1)S(1)}, u32[]{:S(2)}, u32[]{:S(2)}) collective-permute-start(bf16[3,2,96,256]{3,2,1,0:T(8,128)(2,1)S(1)} %grow.1.refs_0_.a_ref), channel_id=1, source_target_pairs={{0,1},{1,0},{2,3},{3,2},{4,5},{5,4},{6,7},{7,6},{8,9},{9,8},{10,11... | collective-permute-start | bytes 884744 | tf_op jit(solution)/shard_map/ppermute | solution.py:57
  52.2 1.8 %collective-permute-start.16 = (bf16[3,2,96,256]{3,2,1,0:T(8,128)(2,1)S(1)}, bf16[3,2,96,256]{3,2,1,0:T(8,128)(2,1)S(1)}, u32[]{:S(2)}, u32[]{:S(2)}) collective-permute-start(bf16[3,2,96,256]{3,2,1,0:T(8,128)(2,1)S(1)} %collective-permute-done.14.refs_1_.b_ref), channel_id=1, source_target_pairs={{0,1},{1,0},{2,3},{3,2},{4,5},{5,4},{6,7},{7,6},{8,9},{9,8},{10,11... | collective-permute-start | bytes 884744 | tf_op jit(solution)/shard_map/ppermute | solution.py:57
  52.2 3.6 %collective-permute-start.18 = (bf16[2,2,96,256]{3,2,1,0:T(8,128)(2,1)S(1)}, bf16[2,2,96,256]{3,2,1,0:T(8,128)(2,1)S(1)}, u32[]{:S(2)}, u32[]{:S(2)}) collective-permute-start(bf16[2,2,96,256]{3,2,1,0:T(8,128)(2,1)S(1)} %stack.3.refs_1_.refs_0_), channel_id=1, source_target_pairs={{0,1},{1,0},{2,3},{3,2},{4,5},{5,4},{6,7},{7,6},{8,9},{9,8},{10,11... | collective-permute-start | bytes 589832 | tf_op jit(solution)/shard_map/ppermute | solution.py:57
  52.7 3.1 %collective-permute-start.20 = (bf16[2,2,96,256]{3,2,1,0:T(8,128)(2,1)S(1)}, bf16[2,2,96,256]{3,2,1,0:T(8,128)(2,1)S(1)}, u32[]{:S(2)}, u32[]{:S(2)}) collective-permute-start(bf16[2,2,96,256]{3,2,1,0:T(8,128)(2,1)S(1)} %collective-permute-done.19.refs_1_), channel_id=1, source_target_pairs={{0,1},{1,0},{2,3},{3,2},{4,5},{5,4},{6,7},{7,6},{8,9},{9,8},{10,11... | collective-permute-start | bytes 589832 | tf_op jit(solution)/shard_map/ppermute | solution.py:57
  55.1 2.2 %collective-permute-start.17 = (bf16[4,2,96,256]{3,2,1,0:T(8,128)(2,1)S(1)}, bf16[4,2,96,256]{3,2,1,0:T(8,128)(2,1)S(1)}, u32[]{:S(2)}, u32[]{:S(2)}) collective-permute-start(bf16[4,2,96,256]{3,2,1,0:T(8,128)(2,1)S(1)} %get-tuple-element.86), channel_id=1, source_target_pairs={{0,1},{1,0},{2,3},{3,2},{4,5},{5,4},{6,7},{7,6},{8,9},{9,8},{10,11... | collective-permute-start | bytes 1179656 | tf_op jit(solution)/shard_map/ppermute | solution.py:57
  57.3 1.7 %collective-permute-start.21 = (bf16[4,2,96,256]{3,2,1,0:T(8,128)(2,1)S(1)}, bf16[4,2,96,256]{3,2,1,0:T(8,128)(2,1)S(1)}, u32[]{:S(2)}, u32[]{:S(2)}) collective-permute-start(bf16[4,2,96,256]{3,2,1,0:T(8,128)(2,1)S(1)} %get-tuple-element.91), channel_id=1, source_target_pairs={{0,1},{1,0},{2,3},{3,2},{4,5},{5,4},{6,7},{7,6},{8,9},{9,8},{10,11... | collective-permute-start | bytes 1179656 | tf_op jit(solution)/shard_map/ppermute | solution.py:57
  57.5 7.3 %collective-permute-start.23 = (bf16[2,2,96,256]{3,2,1,0:T(8,128)(2,1)S(1)}, bf16[2,2,96,256]{3,2,1,0:T(8,128)(2,1)S(1)}, u32[]{:S(2)}, u32[]{:S(2)}) collective-permute-start(bf16[2,2,96,256]{3,2,1,0:T(8,128)(2,1)S(1)} %get-tuple-element.95), channel_id=1, source_target_pairs={{0,2},{1,3},{2,0},{3,1},{4,6},{5,7},{6,4},{7,5},{8,10},{9,11},{10,... | collective-permute-start | bytes 589832 | tf_op jit(solution)/shard_map/ppermute | solution.py:57
  59.2 7.0 %collective-permute-start.26 = (bf16[2,2,96,256]{3,2,1,0:T(8,128)(2,1)S(1)}, bf16[2,2,96,256]{3,2,1,0:T(8,128)(2,1)S(1)}, u32[]{:S(2)}, u32[]{:S(2)}) collective-permute-start(bf16[2,2,96,256]{3,2,1,0:T(8,128)(2,1)S(1)} %get-tuple-element.102), channel_id=1, source_target_pairs={{0,4},{1,5},{2,6},{3,7},{4,0},{5,1},{6,2},{7,3},{8,12},{9,13},{10,... | collective-permute-start | bytes 589832 | tf_op jit(solution)/shard_map/ppermute | solution.py:57
  59.8 3.1 %collective-permute-start.22 = (bf16[96,256]{1,0:T(8,128)(2,1)S(1)}, bf16[96,256]{1,0:T(8,128)(2,1)S(1)}, u32[]{:S(2)}, u32[]{:S(2)}) collective-permute-start(bf16[96,256]{1,0:T(8,128)(2,1)S(1)} %shared_hidden.1.a_ref), channel_id=1, source_target_pairs={{0,1},{1,0},{2,3},{3,2},{4,5},{5,4},{6,7},{7,6},{8,9},{9,8},{10,11... | collective-permute-start | bytes 147464 | tf_op jit(solution)/shard_map/ppermute | solution.py:57
  64.9 4.7 %collective-permute-start.24 = (bf16[1,2,96,256]{3,2,1,0:T(8,128)(2,1)S(1)}, bf16[1,2,96,256]{3,2,1,0:T(8,128)(2,1)S(1)}, u32[]{:S(2)}, u32[]{:S(2)}) collective-permute-start(bf16[1,2,96,256]{3,2,1,0:T(8,128)(2,1)S(1)} %get-tuple-element.99), channel_id=1, source_target_pairs={{0,4},{1,5},{2,6},{3,7},{4,0},{5,1},{6,2},{7,3},{8,12},{9,13},{10,... | collective-permute-start | bytes 294920 | tf_op jit(solution)/shard_map/ppermute | solution.py:57
  66.2 4.7 %collective-permute-start.27 = (bf16[1,2,96,256]{3,2,1,0:T(8,128)(2,1)S(1)}, bf16[1,2,96,256]{3,2,1,0:T(8,128)(2,1)S(1)}, u32[]{:S(2)}, u32[]{:S(2)}) collective-permute-start(bf16[1,2,96,256]{3,2,1,0:T(8,128)(2,1)S(1)} %get-tuple-element.104), channel_id=1, source_target_pairs={{0,2},{1,3},{2,0},{3,1},{4,6},{5,7},{6,4},{7,5},{8,10},{9,11},{10,... | collective-permute-start | bytes 294920 | tf_op jit(solution)/shard_map/ppermute | solution.py:57
  69.6 7.8 %collective-permute-start.25 = (bf16[96,256]{1,0:T(8,128)(2,1)S(1)}, bf16[96,256]{1,0:T(8,128)(2,1)S(1)}, u32[]{:S(2)}, u32[]{:S(2)}) collective-permute-start(bf16[96,256]{1,0:T(8,128)(2,1)S(1)} %get-tuple-element.101), channel_id=1, source_target_pairs={{0,8},{8,0},{16,24},{24,16},{1,9},{9,1},{17,25},{25,17},{2,10},{10... | collective-permute-start | bytes 147464 | tf_op jit(solution)/shard_map/ppermute | solution.py:57
  70.9 6.5 %collective-permute-start.28 = (bf16[96,256]{1,0:T(8,128)(2,1)S(1)}, bf16[96,256]{1,0:T(8,128)(2,1)S(1)}, u32[]{:S(2)}, u32[]{:S(2)}) collective-permute-start(bf16[96,256]{1,0:T(8,128)(2,1)S(1)} %get-tuple-element.105), channel_id=1, source_target_pairs={{0,16},{8,24},{16,0},{24,8},{1,17},{9,25},{17,1},{25,9},{2,18},{10... | collective-permute-start | bytes 147464 | tf_op jit(solution)/shard_map/ppermute | solution.py:57
  72.7 5.9 %collective-permute-start.29 = (bf16[96,256]{1,0:T(8,128)(2,1)S(1)}, bf16[96,256]{1,0:T(8,128)(2,1)S(1)}, u32[]{:S(2)}, u32[]{:S(2)}) collective-permute-start(bf16[96,256]{1,0:T(8,128)(2,1)S(1)} %get-tuple-element.106.refs_1_), channel_id=1, source_target_pairs={{0,24},{8,16},{16,8},{24,0},{1,25},{9,17},{17,9},{25,1},{2,26},{10... | collective-permute-start | bytes 147464 | tf_op jit(solution)/shard_map/ppermute | solution.py:57

commit v10 on v9

--- a/solution.py
+++ b/solution.py
@@ -889,7 +889,7 @@
             received[side] = exchange(sent, "head", bit)
         if n == 0:
             states_out, done = update(
-                keys, deltas, totals, states, quarters[2], tuple(owns), states_out
+                keys, deltas, totals, states, quarters[2] + quarters[3], tuple(owns), states_out
             )
             hidden = shared_hidden(features, *sides[0], squares[0], tuple(owns))
             hidden_received = exchange(hidden, "head", 1)
@@ -898,9 +898,8 @@
     slabs = []
     for side in range(2):
         slabs += last_sum(owns[side], received[side])
-    states_out, done = update(keys, deltas, totals, states, quarters[3], (slabs[-1],), states_out)
     received = [exchange(slabs[z], "seq", z) for z in range(1, seq_count)]
-    result = finish(base, slabs[0], received, (done,))
+    result = finish(base, slabs[0], received, ())
     layer_out = jnp.transpose(result.reshape(steps, seqs, width), (1, 0, 2))
     return (layer_out, states_out)
 

time: 79.6 us -> 79.5 us (level)
  Pallas kernels: 30.8 us -> 28.7 us
  waiting for transfers between devices: 21.5 us -> 23.6 us
    pallas_call x28 -> x27, Pallas kernels: 30.8 us -> 28.7 us  [call(): pl.pallas_call(body, out_shape=tuple(out_shapes), in_specs=[SMEM_SPEC] *...]
    ppermute x30, waiting for transfers between devices: 21.5 us -> 23.6 us  [exchange(): return lax.ppermute(x, axis, [(i, i ^ bit) for i in range(size)])]
  transfers between devices with their start and end apart: 30 -> 30, of which waited for: 13 -> 14; matrix products, arithmetic and copies ran while one was open for 0% -> 0% of each run, Pallas kernels for 28% -> 26%
where the time goes in v10:
time: 79.5 us; the launch traced here: 79.3 us
  Pallas kernels  28.7 us (36%)
  starting transfers between devices  26 us (33%)
  waiting for transfers between devices  23.6 us (30%)
  between operations  0.93 us (1%)
    pallas_call x27, Pallas kernels, call(): pl.pallas_call(body, out_shape=tuple(out_shapes), in_specs=[SMEM_SPEC] *...  28.7 us
    ppermute x30, starting transfers between devices, exchange(): return lax.ppermute(x, axis, [(i, i ^ bit) for i in range(size)])  26 us
    ppermute x30, waiting for transfers between devices, exchange(): return lax.ppermute(x, axis, [(i, i ^ bit) for i in range(size)])  23.6 us
  transfers between devices with their start and end apart: 30, of which 14 were waited for; matrix products, arithmetic and copies ran while one was open for 0% of the time, Pallas kernels for 26%

profile of v10, /device:TPU:0, one launch (start us, length us, event | category | flops | bytes accessed | tf_op | source)
XLA Modules:
  0.0 79.3 jit_solution(6796553689211854494)
XLA Ops:
  0.6 3.0 %collective-permute-start = (bf16[96,256]{1,0:T(8,128)(2,1)}, bf16[96,256]{1,0:T(8,128)(2,1)S(1)}, u32[]{:S(2)}, u32[]{:S(2)}) collective-permute-start(bf16[96,256]{1,0:T(8,128)(2,1)} %bitcast.24), channel_id=1, source_target_pairs={{0,2},{1,3},{2,0},{3,1},{4,6},{5,7},{6,4},{7,5},{8,10},{9,11},{10,... | collective-permute-start | bytes 147464 | tf_op jit(solution)/shard_map/ppermute | solution.py:57
  3.6 1.5 %collective-permute-start.1 = (bf16[96,256]{1,0:T(8,128)(2,1)}, bf16[96,256]{1,0:T(8,128)(2,1)S(1)}, u32[]{:S(2)}, u32[]{:S(2)}) collective-permute-start(bf16[96,256]{1,0:T(8,128)(2,1)} %bitcast.25), channel_id=1, source_target_pairs={{0,4},{1,5},{2,6},{3,7},{4,0},{5,1},{6,2},{7,3},{8,12},{9,13},{10,... | collective-permute-start | bytes 147464 | tf_op jit(solution)/shard_map/ppermute | solution.py:57
  5.2 2.6 %bring.1 = (bf16[96,256]{1,0:T(8,128)(2,1)S(1)}, bf16[2048,256]{1,0:T(8,128)(2,1)S(1)}, bf16[2048,256]{1,0:T(8,128)(2,1)S(1)}, bf16[2048,512]{1,0:T(8,128)(2,1)S...) custom-call(s32[1]{0:T(128)} %bitcast.me_ref, ...), custom_call_target="tpu_custom_call" | custom-call | tf_op jit(solution)/shard_map/bring/pallas_call | solution.py:43
  7.9 2.4 %collective-permute-done.2.refs_3_ = bf16[96,256]{1,0:T(8,128)(2,1)S(1)} collective-permute-done((bf16[96,256]{1,0:T(8,128)(2,1)}, bf16[96,256]{1,0:T(8,128)(2,1)S(1)}, u32[]{:S(2)}, u32[]{:S(2)}) %collective-permute-start.2) | collective-permute-done | bytes 49184 | tf_op jit(solution)/shard_map/ppermute | solution.py:57
  10.5 1.6 %load.3.refs_8_ = bf16[2048,512]{1,0:T(8,128)(2,1)S(1)} custom-call(bf16[2048,512]{1,0:T(8,128)(2,1)} %refs_0_.3, bf16[4,96,256]{2,1,0:T(8,128)(2,1)S(1)} %stack.2.refs_1_.refs_0_), custom_call_target="tpu_custom_call" | custom-call | tf_op jit(solution)/shard_map/load/pallas_call | solution.py:43
  12.1 7.1 %front.1 = (bf16[4,96,256]{2,1,0:T(8,128)(2,1)S(1)}, bf16[4,96,256]{2,1,0:T(8,128)(2,1)S(1)}, f32[2,96,128]{2,1,0:T(8,128)S(1)}, f32[2,3,32,256]{3,2,1,0:T(8,128)S(1)}, f32[2,32,256]{2,1,0:T(8,128)S(1)}) custom-call(s32[1]{0:T(128)} %bitcast.me_ref, bf16[4,96,256]{2,1,0:T(8,128)(2,1)S(1)} %stack.2.refs_1_.refs_0_, ...), custom_call_target="tpu_custom_call" | custom-call | tf_op jit(solution)/shard_map/front/pallas_call | solution.py:43
  19.3 0.5 collective-permute-start.4
  19.8 1.1 %collective-permute-done.4.b_ref = bf16[4,96,256]{2,1,0:T(8,128)(2,1)S(1)} collective-permute-done((bf16[4,96,256]{2,1,0:T(8,128)(2,1)S(1)}, bf16[4,96,256]{2,1,0:T(8,128)(2,1)S(1)}, u32[]{:S(2)}, u32[]{:S(2)}) %collective-permute-start.4) | collective-permute-done | bytes 196640 | tf_op jit(solution)/shard_map/ppermute | solution.py:57
  20.9 0.6 collective-permute-start.5
  21.6 0.4 collective-permute-start.6
  22.0 2.5 %collective-permute-start.7 = (bf16[96,256]{1,0:T(8,128)(2,1)S(1)}, bf16[96,256]{1,0:T(8,128)(2,1)S(1)}, u32[]{:S(2)}, u32[]{:S(2)}) collective-permute-start(bf16[96,256]{1,0:T(8,128)(2,1)S(1)} %get-tuple-element.65), channel_id=1, source_target_pairs={{0,6},{1,7},{2,4},{3,5},{4,2},{5,3},{6,0},{7,1},{8,14},{9,15},{10,... | collective-permute-start | bytes 147464 | tf_op jit(solution)/shard_map/ppermute | solution.py:57
  24.5 2.2 %load.4.refs_8_.refs_3_ = bf16[1,2048,1024]{2,1,0:T(8,128)(2,1)S(1)} custom-call(bf16[1,2048,1024]{2,1,0:T(8,128)(2,1)} %refs_0_.4, bf16[96,256]{1,0:T(8,128)(2,1)S(1)} %get-tuple-element.62.refs_1_.refs_0_), custom_call_target="tpu_custom_call" | custom-call | tf_op jit(solution)/shard_map/load/pallas_call | solution.py:43
  26.7 0.2 collective-permute-done.7.refs_3_
  27.0 0.4 rows.1
  27.5 1.7 %collective-permute-start.8 = (bf16[112,256]{1,0:T(8,128)(2,1)S(1)}, bf16[112,256]{1,0:T(8,128)(2,1)S(1)}, u32[]{:S(2)}, u32[]{:S(2)}) collective-permute-start(bf16[112,256]{1,0:T(8,128)(2,1)S(1)} %get-tuple-element.70), channel_id=1, source_target_pairs={{0,8},{8,0},{16,24},{24,16},{1,9},{9,1},{17,25},{25,17},{2,10},{10... | collective-permute-start | bytes 172040 | tf_op jit(solution)/shard_map/ppermute | solution.py:57
  29.2 2.6 %collective-permute-start.10 = (bf16[112,256]{1,0:T(8,128)(2,1)S(1)}, bf16[112,256]{1,0:T(8,128)(2,1)S(1)}, u32[]{:S(2)}, u32[]{:S(2)}) collective-permute-start(bf16[112,256]{1,0:T(8,128)(2,1)S(1)} %get-tuple-element.73), channel_id=1, source_target_pairs={{0,16},{8,24},{16,0},{24,8},{1,17},{9,25},{17,1},{25,9},{2,18},{10... | collective-permute-start | bytes 172040 | tf_op jit(solution)/shard_map/ppermute | solution.py:57
  32.0 1.6 %load.5.refs_2_.refs_6_ = bf16[1,512,2048]{2,1,0:T(8,128)(2,1)S(1)} custom-call(bf16[1,512,2048]{2,1,0:T(8,128)(2,1)} %refs_0_.5, bf16[2,96,256]{2,1,0:T(8,128)(2,1)S(1)} %get-tuple-element.71.refs_1_.keep_ref), custom_call_target="tpu_custom_call" | custom-call | tf_op jit(solution)/shard_map/load/pallas_call | solution.py:43
  33.6 2.2 %collective-permute-done.10.refs_0_.a_ref.refs_7_ = bf16[112,256]{1,0:T(8,128)(2,1)S(1)} collective-permute-done((bf16[112,256]{1,0:T(8,128)(2,1)S(1)}, bf16[112,256]{1,0:T(8,128)(2,1)S(1)}, u32[]{:S(2)}, u32[]{:S(2)}) %collective-permute-start.10) | collective-permute-done | bytes 57376 | tf_op jit(solution)/shard_map/ppermute | solution.py:57
  35.8 2.0 %collective-permute-done.11.refs_1_.b_ref.refs_8_ = bf16[112,256]{1,0:T(8,128)(2,1)S(1)} collective-permute-done((bf16[112,256]{1,0:T(8,128)(2,1)S(1)}, bf16[112,256]{1,0:T(8,128)(2,1)S(1)}, u32[]{:S(2)}, u32[]{:S(2)}) %collective-permute-start.11) | collective-permute-done | bytes 57376 | tf_op jit(solution)/shard_map/ppermute | solution.py:57
  37.9 1.6 %collective-permute-start.12 = (bf16[2,2,96,256]{3,2,1,0:T(8,128)(2,1)S(1)}, bf16[2,2,96,256]{3,2,1,0:T(8,128)(2,1)S(1)}, u32[]{:S(2)}, u32[]{:S(2)}) collective-permute-start(bf16[2,2,96,256]{3,2,1,0:T(8,128)(2,1)S(1)} %open.1.refs_0_.mine_ref), channel_id=1, source_target_pairs={{0,2},{1,3},{2,0},{3,1},{4,6},{5,7},{6,4},{7,5},{8,10},{9,11},{10,... | collective-permute-start | bytes 589832 | tf_op jit(solution)/shard_map/ppermute | solution.py:57
  39.5 1.6 %collective-permute-start.13 = (bf16[1,2,96,256]{3,2,1,0:T(8,128)(2,1)S(1)}, bf16[1,2,96,256]{3,2,1,0:T(8,128)(2,1)S(1)}, u32[]{:S(2)}, u32[]{:S(2)}) collective-permute-start(bf16[1,2,96,256]{3,2,1,0:T(8,128)(2,1)S(1)} %bitcast.20), channel_id=1, source_target_pairs={{0,4},{1,5},{2,6},{3,7},{4,0},{5,1},{6,2},{7,3},{8,12},{9,13},{10,... | collective-permute-start | bytes 294920 | tf_op jit(solution)/shard_map/ppermute | solution.py:57
  41.0 3.8 %update.2 = (f32[32,4,128,128]{3,2,1,0:T(8,128)}, f32[8,128]{1,0:T(8,128)S(1)}) custom-call(f32[2,96,128]{2,1,0:T(8,128)S(1)} %get-tuple-element.75.keys_ref, f32[2,3,32,256]{3,2,1,0:T(8,128)S(1)} %get-tuple-element.76.delta_ref, f32[2,32,256]{2,1,0:T(8,128)S(1)} %get-tuple-element.77.total_ref, f32[32,4,128,128]{3,2,1,0:T(8,128)} %states_ref.3, ...), custom_call_target="tpu_custom_call" | custom-call | tf_op jit(solution)/shard_map/update/pallas_call | solution.py:43
  44.9 0.9 %collective-permute-start.14 = (bf16[3,2,96,256]{3,2,1,0:T(8,128)(2,1)S(1)}, bf16[3,2,96,256]{3,2,1,0:T(8,128)(2,1)S(1)}, u32[]{:S(2)}, u32[]{:S(2)}) collective-permute-start(bf16[3,2,96,256]{3,2,1,0:T(8,128)(2,1)S(1)} %grow.1.refs_0_.a_ref), channel_id=1, source_target_pairs={{0,4},{1,5},{2,6},{3,7},{4,0},{5,1},{6,2},{7,3},{8,12},{9,13},{10,... | collective-permute-start | bytes 884744 | tf_op jit(solution)/shard_map/ppermute | solution.py:57
  45.8 1.0 %collective-permute-start.19 = (bf16[2,2,96,256]{3,2,1,0:T(8,128)(2,1)S(1)}, bf16[2,2,96,256]{3,2,1,0:T(8,128)(2,1)S(1)}, u32[]{:S(2)}, u32[]{:S(2)}) collective-permute-start(bf16[2,2,96,256]{3,2,1,0:T(8,128)(2,1)S(1)} %stack.3.refs_1_.refs_0_), channel_id=1, source_target_pairs={{0,2},{1,3},{2,0},{3,1},{4,6},{5,7},{6,4},{7,5},{8,10},{9,11},{10,... | collective-permute-start | bytes 589832 | tf_op jit(solution)/shard_map/ppermute | solution.py:57
  46.7 5.4 %collective-permute-done.14.refs_1_.b_ref = bf16[3,2,96,256]{3,2,1,0:T(8,128)(2,1)S(1)} collective-permute-done((bf16[3,2,96,256]{3,2,1,0:T(8,128)(2,1)S(1)}, bf16[3,2,96,256]{3,2,1,0:T(8,128)(2,1)S(1)}, u32[]{:S(2)}, u32[]{:S(2)}) %collective-permute-start.14) | collective-permute-done | bytes 294944 | tf_op jit(solution)/shard_map/ppermute | solution.py:57
  52.1 0.5 collective-permute-start.18
  52.7 0.6 expert_first.2
  53.3 0.6 expert_first.3
  53.9 1.2 %expert_rest.2 = (bf16[4,2,96,256]{3,2,1,0:T(8,128)(2,1)S(1)}, bf16[4,2,96,256]{3,2,1,0:T(8,128)(2,1)S(1)}, f32[192,1]{1,0:T(8,128)S(1)}) custom-call(s32[1]{0:T(128)} %bitcast.me_ref, bf16[3,2,96,256]{3,2,1,0:T(8,128)(2,1)S(1)} %collective-permute-done.15.refs_0_, bf16[3,2,96,256]{3,2,1,0:T(8,128)(2,1)S(1)} %collective-permute-done.16.refs_1_, ...), custom_call_target="tpu_custom_call" | custom-call | tf_op jit(solution)/shard_map/expert_rest/pallas_call | solution.py:43
  55.2 0.6 collective-permute-start.17
  55.7 1.6 %expert_rest.3 = (bf16[4,2,96,256]{3,2,1,0:T(8,128)(2,1)S(1)}, bf16[4,2,96,256]{3,2,1,0:T(8,128)(2,1)S(1)}, f32[192,1]{1,0:T(8,128)}) custom-call(s32[1]{0:T(128)} %bitcast.me_ref, bf16[2,2,96,256]{3,2,1,0:T(8,128)(2,1)S(1)} %collective-permute-done.18.refs_0_, bf16[2,2,96,256]{3,2,1,0:T(8,128)(2,1)S(1)} %collective-permute-done.20.refs_1_, ...), custom_call_target="tpu_custom_call" | custom-call | tf_op jit(solution)/shard_map/expert_rest/pallas_call | solution.py:43
  57.4 0.6 collective-permute-start.23
  58.0 1.0 %collective-permute-done.21.b_ref = bf16[4,2,96,256]{3,2,1,0:T(8,128)(2,1)S(1)} collective-permute-done((bf16[4,2,96,256]{3,2,1,0:T(8,128)(2,1)S(1)}, bf16[4,2,96,256]{3,2,1,0:T(8,128)(2,1)S(1)}, u32[]{:S(2)}, u32[]{:S(2)}) %collective-permute-start.21) | collective-permute-done | bytes 393248 | tf_op jit(solution)/shard_map/ppermute | solution.py:57
  59.1 0.5 collective-permute-start.26
  59.9 3.8 %update.3 = (f32[32,4,128,128]{3,2,1,0:T(8,128)}, f32[8,128]{1,0:T(8,128)S(1)}) custom-call(f32[2,96,128]{2,1,0:T(8,128)S(1)} %get-tuple-element.75.keys_ref, f32[2,3,32,256]{3,2,1,0:T(8,128)S(1)} %get-tuple-element.76.delta_ref, f32[2,32,256]{2,1,0:T(8,128)S(1)} %get-tuple-element.77.total_ref, ...), custom_call_target="tpu_custom_call", output_to_operand_aliasing={{0}: (4, {})} | custom-call | tf_op jit(solution)/shard_map/update/pallas_call | solution.py:43
  63.7 1.1 %collective-permute-done.23.b_ref = bf16[2,2,96,256]{3,2,1,0:T(8,128)(2,1)S(1)} collective-permute-done((bf16[2,2,96,256]{3,2,1,0:T(8,128)(2,1)S(1)}, bf16[2,2,96,256]{3,2,1,0:T(8,128)(2,1)S(1)}, u32[]{:S(2)}, u32[]{:S(2)}) %collective-permute-start.23) | collective-permute-done | bytes 196640 | tf_op jit(solution)/shard_map/ppermute | solution.py:57
  64.8 0.6 collective-permute-start.24
  65.4 0.8 collective-permute-done.26.b_ref
  66.2 0.6 collective-permute-start.27
  66.8 2.7 %collective-permute-done.24.b_ref = bf16[1,2,96,256]{3,2,1,0:T(8,128)(2,1)S(1)} collective-permute-done((bf16[1,2,96,256]{3,2,1,0:T(8,128)(2,1)S(1)}, bf16[1,2,96,256]{3,2,1,0:T(8,128)(2,1)S(1)}, u32[]{:S(2)}, u32[]{:S(2)}) %collective-permute-start.24) | collective-permute-done | bytes 98336 | tf_op jit(solution)/shard_map/ppermute | solution.py:57
  69.5 1.0 %collective-permute-start.25 = (bf16[96,256]{1,0:T(8,128)(2,1)S(1)}, bf16[96,256]{1,0:T(8,128)(2,1)S(1)}, u32[]{:S(2)}, u32[]{:S(2)}) collective-permute-start(bf16[96,256]{1,0:T(8,128)(2,1)S(1)} %get-tuple-element.99), channel_id=1, source_target_pairs={{0,8},{8,0},{16,24},{24,16},{1,9},{9,1},{17,25},{25,17},{2,10},{10... | collective-permute-start | bytes 147464 | tf_op jit(solution)/shard_map/ppermute | solution.py:57
  70.5 0.3 collective-permute-done.27.b_ref
  70.9 1.9 %collective-permute-start.28 = (bf16[96,256]{1,0:T(8,128)(2,1)S(1)}, bf16[96,256]{1,0:T(8,128)(2,1)S(1)}, u32[]{:S(2)}, u32[]{:S(2)}) collective-permute-start(bf16[96,256]{1,0:T(8,128)(2,1)S(1)} %get-tuple-element.103), channel_id=1, source_target_pairs={{0,16},{8,24},{16,0},{24,8},{1,17},{9,25},{17,1},{25,9},{2,18},{10... | collective-permute-start | bytes 147464 | tf_op jit(solution)/shard_map/ppermute | solution.py:57
  72.7 1.5 %collective-permute-start.29 = (bf16[96,256]{1,0:T(8,128)(2,1)S(1)}, bf16[96,256]{1,0:T(8,128)(2,1)S(1)}, u32[]{:S(2)}, u32[]{:S(2)}) collective-permute-start(bf16[96,256]{1,0:T(8,128)(2,1)S(1)} %get-tuple-element.104), channel_id=1, source_target_pairs={{0,24},{8,16},{16,8},{24,0},{1,25},{9,17},{17,9},{25,1},{2,26},{10... | collective-permute-start | bytes 147464 | tf_op jit(solution)/shard_map/ppermute | solution.py:57
  74.2 0.2 shared_out.1.refs_0_
  74.4 2.6 %collective-permute-done.28.refs_3_ = bf16[96,256]{1,0:T(8,128)(2,1)S(1)} collective-permute-done((bf16[96,256]{1,0:T(8,128)(2,1)S(1)}, bf16[96,256]{1,0:T(8,128)(2,1)S(1)}, u32[]{:S(2)}, u32[]{:S(2)}) %collective-permute-start.28) | collective-permute-done | bytes 49184 | tf_op jit(solution)/shard_map/ppermute | solution.py:57
  77.0 1.6 %collective-permute-done.29.refs_4_ = bf16[96,256]{1,0:T(8,128)(2,1)S(1)} collective-permute-done((bf16[96,256]{1,0:T(8,128)(2,1)S(1)}, bf16[96,256]{1,0:T(8,128)(2,1)S(1)}, u32[]{:S(2)}, u32[]{:S(2)}) %collective-permute-start.29) | collective-permute-done | bytes 49184 | tf_op jit(solution)/shard_map/ppermute | solution.py:57
  78.6 0.7 finish.1
  (45 shorter events, 1.2 us)
Async XLA Ops:
  0.6 7.2 %collective-permute-start = (bf16[96,256]{1,0:T(8,128)(2,1)}, bf16[96,256]{1,0:T(8,128)(2,1)S(1)}, u32[]{:S(2)}, u32[]{:S(2)}) collective-permute-start(bf16[96,256]{1,0:T(8,128)(2,1)} %bitcast.24), channel_id=1, source_target_pairs={{0,2},{1,3},{2,0},{3,1},{4,6},{5,7},{6,4},{7,5},{8,10},{9,11},{10,... | collective-permute-start | bytes 147464 | tf_op jit(solution)/shard_map/ppermute | solution.py:57
  3.6 4.3 %collective-permute-start.1 = (bf16[96,256]{1,0:T(8,128)(2,1)}, bf16[96,256]{1,0:T(8,128)(2,1)S(1)}, u32[]{:S(2)}, u32[]{:S(2)}) collective-permute-start(bf16[96,256]{1,0:T(8,128)(2,1)} %bitcast.25), channel_id=1, source_target_pairs={{0,4},{1,5},{2,6},{3,7},{4,0},{5,1},{6,2},{7,3},{8,12},{9,13},{10,... | collective-permute-start | bytes 147464 | tf_op jit(solution)/shard_map/ppermute | solution.py:57
  5.2 5.2 %collective-permute-start.2 = (bf16[96,256]{1,0:T(8,128)(2,1)}, bf16[96,256]{1,0:T(8,128)(2,1)S(1)}, u32[]{:S(2)}, u32[]{:S(2)}) collective-permute-start(bf16[96,256]{1,0:T(8,128)(2,1)} %bitcast.26), channel_id=1, source_target_pairs={{0,6},{1,7},{2,4},{3,5},{4,2},{5,3},{6,0},{7,1},{8,14},{9,15},{10,... | collective-permute-start | bytes 147464 | tf_op jit(solution)/shard_map/ppermute | solution.py:57
  5.2 5.3 %copy-start = (bf16[2048,4]{0,1:T(4,128)(2,1)S(1)}, bf16[2048,4]{0,1:T(4,128)(2,1)}, u32[]{:S(2)}) copy-start(bf16[2048,4]{0,1:T(4,128)(2,1)} %param.30) | copy-start | bytes 49156
  5.2 5.3 %copy-start.1 = (bf16[2048,4]{0,1:T(4,128)(2,1)S(1)}, bf16[2048,4]{0,1:T(4,128)(2,1)}, u32[]{:S(2)}) copy-start(bf16[2048,4]{0,1:T(4,128)(2,1)} %param.29) | copy-start | bytes 49156
  10.4 1.8 %collective-permute-start.3 = (bf16[4,96,256]{2,1,0:T(8,128)(2,1)S(1)}, bf16[4,96,256]{2,1,0:T(8,128)(2,1)S(1)}, u32[]{:S(2)}, u32[]{:S(2)}) collective-permute-start(bf16[4,96,256]{2,1,0:T(8,128)(2,1)S(1)} %stack.2.refs_1_.refs_0_), channel_id=1, source_target_pairs={{0,1},{1,0},{2,3},{3,2},{4,5},{5,4},{6,7},{7,6},{8,9},{9,8},{10,11... | collective-permute-start | bytes 589832 | tf_op jit(solution)/shard_map/ppermute | solution.py:57
  19.3 1.6 %collective-permute-start.4 = (bf16[4,96,256]{2,1,0:T(8,128)(2,1)S(1)}, bf16[4,96,256]{2,1,0:T(8,128)(2,1)S(1)}, u32[]{:S(2)}, u32[]{:S(2)}) collective-permute-start(bf16[4,96,256]{2,1,0:T(8,128)(2,1)S(1)} %get-tuple-element.61), channel_id=1, source_target_pairs={{0,1},{1,0},{2,3},{3,2},{4,5},{5,4},{6,7},{7,6},{8,9},{9,8},{10,11... | collective-permute-start | bytes 589832 | tf_op jit(solution)/shard_map/ppermute | solution.py:57
  20.9 5.8 %collective-permute-start.5 = (bf16[96,256]{1,0:T(8,128)(2,1)S(1)}, bf16[96,256]{1,0:T(8,128)(2,1)S(1)}, u32[]{:S(2)}, u32[]{:S(2)}) collective-permute-start(bf16[96,256]{1,0:T(8,128)(2,1)S(1)} %get-tuple-element.63), channel_id=1, source_target_pairs={{0,2},{1,3},{2,0},{3,1},{4,6},{5,7},{6,4},{7,5},{8,10},{9,11},{10,... | collective-permute-start | bytes 147464 | tf_op jit(solution)/shard_map/ppermute | solution.py:57
  21.6 5.2 %collective-permute-start.6 = (bf16[96,256]{1,0:T(8,128)(2,1)S(1)}, bf16[96,256]{1,0:T(8,128)(2,1)S(1)}, u32[]{:S(2)}, u32[]{:S(2)}) collective-permute-start(bf16[96,256]{1,0:T(8,128)(2,1)S(1)} %get-tuple-element.64), channel_id=1, source_target_pairs={{0,4},{1,5},{2,6},{3,7},{4,0},{5,1},{6,2},{7,3},{8,12},{9,13},{10,... | collective-permute-start | bytes 147464 | tf_op jit(solution)/shard_map/ppermute | solution.py:57
  22.0 5.0 %collective-permute-start.7 = (bf16[96,256]{1,0:T(8,128)(2,1)S(1)}, bf16[96,256]{1,0:T(8,128)(2,1)S(1)}, u32[]{:S(2)}, u32[]{:S(2)}) collective-permute-start(bf16[96,256]{1,0:T(8,128)(2,1)S(1)} %get-tuple-element.65), channel_id=1, source_target_pairs={{0,6},{1,7},{2,4},{3,5},{4,2},{5,3},{6,0},{7,1},{8,14},{9,15},{10,... | collective-permute-start | bytes 147464 | tf_op jit(solution)/shard_map/ppermute | solution.py:57
  27.4 10.4 %collective-permute-start.9 = (bf16[2,96,256]{2,1,0:T(8,128)(2,1)S(1)}, bf16[2,96,256]{2,1,0:T(8,128)(2,1)S(1)}, u32[]{:S(2)}, u32[]{:S(2)}) collective-permute-start(bf16[2,96,256]{2,1,0:T(8,128)(2,1)S(1)} %get-tuple-element.72), channel_id=1, source_target_pairs={{0,1},{1,0},{2,3},{3,2},{4,5},{5,4},{6,7},{7,6},{8,9},{9,8},{10,11... | collective-permute-start | bytes 294920 | tf_op jit(solution)/shard_map/ppermute | solution.py:57
  27.5 6.1 %collective-permute-start.8 = (bf16[112,256]{1,0:T(8,128)(2,1)S(1)}, bf16[112,256]{1,0:T(8,128)(2,1)S(1)}, u32[]{:S(2)}, u32[]{:S(2)}) collective-permute-start(bf16[112,256]{1,0:T(8,128)(2,1)S(1)} %get-tuple-element.70), channel_id=1, source_target_pairs={{0,8},{8,0},{16,24},{24,16},{1,9},{9,1},{17,25},{25,17},{2,10},{10... | collective-permute-start | bytes 172040 | tf_op jit(solution)/shard_map/ppermute | solution.py:57
  29.2 6.6 %collective-permute-start.10 = (bf16[112,256]{1,0:T(8,128)(2,1)S(1)}, bf16[112,256]{1,0:T(8,128)(2,1)S(1)}, u32[]{:S(2)}, u32[]{:S(2)}) collective-permute-start(bf16[112,256]{1,0:T(8,128)(2,1)S(1)} %get-tuple-element.73), channel_id=1, source_target_pairs={{0,16},{8,24},{16,0},{24,8},{1,17},{9,25},{17,1},{25,9},{2,18},{10... | collective-permute-start | bytes 172040 | tf_op jit(solution)/shard_map/ppermute | solution.py:57
  31.8 6.0 %collective-permute-start.11 = (bf16[112,256]{1,0:T(8,128)(2,1)S(1)}, bf16[112,256]{1,0:T(8,128)(2,1)S(1)}, u32[]{:S(2)}, u32[]{:S(2)}) collective-permute-start(bf16[112,256]{1,0:T(8,128)(2,1)S(1)} %get-tuple-element.74), channel_id=1, source_target_pairs={{0,24},{8,16},{16,8},{24,0},{1,25},{9,17},{17,9},{25,1},{2,26},{10... | collective-permute-start | bytes 172040 | tf_op jit(solution)/shard_map/ppermute | solution.py:57
  37.9 7.0 %collective-permute-start.12 = (bf16[2,2,96,256]{3,2,1,0:T(8,128)(2,1)S(1)}, bf16[2,2,96,256]{3,2,1,0:T(8,128)(2,1)S(1)}, u32[]{:S(2)}, u32[]{:S(2)}) collective-permute-start(bf16[2,2,96,256]{3,2,1,0:T(8,128)(2,1)S(1)} %open.1.refs_0_.mine_ref), channel_id=1, source_target_pairs={{0,2},{1,3},{2,0},{3,1},{4,6},{5,7},{6,4},{7,5},{8,10},{9,11},{10,... | collective-permute-start | bytes 589832 | tf_op jit(solution)/shard_map/ppermute | solution.py:57
  39.5 5.4 %collective-permute-start.13 = (bf16[1,2,96,256]{3,2,1,0:T(8,128)(2,1)S(1)}, bf16[1,2,96,256]{3,2,1,0:T(8,128)(2,1)S(1)}, u32[]{:S(2)}, u32[]{:S(2)}) collective-permute-start(bf16[1,2,96,256]{3,2,1,0:T(8,128)(2,1)S(1)} %bitcast.20), channel_id=1, source_target_pairs={{0,4},{1,5},{2,6},{3,7},{4,0},{5,1},{6,2},{7,3},{8,12},{9,13},{10,... | collective-permute-start | bytes 294920 | tf_op jit(solution)/shard_map/ppermute | solution.py:57
  44.9 7.2 %collective-permute-start.14 = (bf16[3,2,96,256]{3,2,1,0:T(8,128)(2,1)S(1)}, bf16[3,2,96,256]{3,2,1,0:T(8,128)(2,1)S(1)}, u32[]{:S(2)}, u32[]{:S(2)}) collective-permute-start(bf16[3,2,96,256]{3,2,1,0:T(8,128)(2,1)S(1)} %grow.1.refs_0_.a_ref), channel_id=1, source_target_pairs={{0,4},{1,5},{2,6},{3,7},{4,0},{5,1},{6,2},{7,3},{8,12},{9,13},{10,... | collective-permute-start | bytes 884744 | tf_op jit(solution)/shard_map/ppermute | solution.py:57
  45.8 6.9 %collective-permute-start.19 = (bf16[2,2,96,256]{3,2,1,0:T(8,128)(2,1)S(1)}, bf16[2,2,96,256]{3,2,1,0:T(8,128)(2,1)S(1)}, u32[]{:S(2)}, u32[]{:S(2)}) collective-permute-start(bf16[2,2,96,256]{3,2,1,0:T(8,128)(2,1)S(1)} %stack.3.refs_1_.refs_0_), channel_id=1, source_target_pairs={{0,2},{1,3},{2,0},{3,1},{4,6},{5,7},{6,4},{7,5},{8,10},{9,11},{10,... | collective-permute-start | bytes 589832 | tf_op jit(solution)/shard_map/ppermute | solution.py:57
  46.7 7.2 %collective-permute-start.15 = (bf16[3,2,96,256]{3,2,1,0:T(8,128)(2,1)S(1)}, bf16[3,2,96,256]{3,2,1,0:T(8,128)(2,1)S(1)}, u32[]{:S(2)}, u32[]{:S(2)}) collective-permute-start(bf16[3,2,96,256]{3,2,1,0:T(8,128)(2,1)S(1)} %grow.1.refs_0_.a_ref), channel_id=1, source_target_pairs={{0,1},{1,0},{2,3},{3,2},{4,5},{5,4},{6,7},{7,6},{8,9},{9,8},{10,11... | collective-permute-start | bytes 884744 | tf_op jit(solution)/shard_map/ppermute | solution.py:57
  52.1 1.8 %collective-permute-start.16 = (bf16[3,2,96,256]{3,2,1,0:T(8,128)(2,1)S(1)}, bf16[3,2,96,256]{3,2,1,0:T(8,128)(2,1)S(1)}, u32[]{:S(2)}, u32[]{:S(2)}) collective-permute-start(bf16[3,2,96,256]{3,2,1,0:T(8,128)(2,1)S(1)} %collective-permute-done.14.refs_1_.b_ref), channel_id=1, source_target_pairs={{0,1},{1,0},{2,3},{3,2},{4,5},{5,4},{6,7},{7,6},{8,9},{9,8},{10,11... | collective-permute-start | bytes 884744 | tf_op jit(solution)/shard_map/ppermute | solution.py:57
  52.1 3.6 %collective-permute-start.18 = (bf16[2,2,96,256]{3,2,1,0:T(8,128)(2,1)S(1)}, bf16[2,2,96,256]{3,2,1,0:T(8,128)(2,1)S(1)}, u32[]{:S(2)}, u32[]{:S(2)}) collective-permute-start(bf16[2,2,96,256]{3,2,1,0:T(8,128)(2,1)S(1)} %stack.3.refs_1_.refs_0_), channel_id=1, source_target_pairs={{0,1},{1,0},{2,3},{3,2},{4,5},{5,4},{6,7},{7,6},{8,9},{9,8},{10,11... | collective-permute-start | bytes 589832 | tf_op jit(solution)/shard_map/ppermute | solution.py:57
  52.7 3.1 %collective-permute-start.20 = (bf16[2,2,96,256]{3,2,1,0:T(8,128)(2,1)S(1)}, bf16[2,2,96,256]{3,2,1,0:T(8,128)(2,1)S(1)}, u32[]{:S(2)}, u32[]{:S(2)}) collective-permute-start(bf16[2,2,96,256]{3,2,1,0:T(8,128)(2,1)S(1)} %collective-permute-done.19.refs_1_), channel_id=1, source_target_pairs={{0,1},{1,0},{2,3},{3,2},{4,5},{5,4},{6,7},{7,6},{8,9},{9,8},{10,11... | collective-permute-start | bytes 589832 | tf_op jit(solution)/shard_map/ppermute | solution.py:57
  55.2 2.2 %collective-permute-start.17 = (bf16[4,2,96,256]{3,2,1,0:T(8,128)(2,1)S(1)}, bf16[4,2,96,256]{3,2,1,0:T(8,128)(2,1)S(1)}, u32[]{:S(2)}, u32[]{:S(2)}) collective-permute-start(bf16[4,2,96,256]{3,2,1,0:T(8,128)(2,1)S(1)} %get-tuple-element.84), channel_id=1, source_target_pairs={{0,1},{1,0},{2,3},{3,2},{4,5},{5,4},{6,7},{7,6},{8,9},{9,8},{10,11... | collective-permute-start | bytes 1179656 | tf_op jit(solution)/shard_map/ppermute | solution.py:57
  57.3 1.7 %collective-permute-start.21 = (bf16[4,2,96,256]{3,2,1,0:T(8,128)(2,1)S(1)}, bf16[4,2,96,256]{3,2,1,0:T(8,128)(2,1)S(1)}, u32[]{:S(2)}, u32[]{:S(2)}) collective-permute-start(bf16[4,2,96,256]{3,2,1,0:T(8,128)(2,1)S(1)} %get-tuple-element.89), channel_id=1, source_target_pairs={{0,1},{1,0},{2,3},{3,2},{4,5},{5,4},{6,7},{7,6},{8,9},{9,8},{10,11... | collective-permute-start | bytes 1179656 | tf_op jit(solution)/shard_map/ppermute | solution.py:57
  57.4 7.4 %collective-permute-start.23 = (bf16[2,2,96,256]{3,2,1,0:T(8,128)(2,1)S(1)}, bf16[2,2,96,256]{3,2,1,0:T(8,128)(2,1)S(1)}, u32[]{:S(2)}, u32[]{:S(2)}) collective-permute-start(bf16[2,2,96,256]{3,2,1,0:T(8,128)(2,1)S(1)} %get-tuple-element.93), channel_id=1, source_target_pairs={{0,2},{1,3},{2,0},{3,1},{4,6},{5,7},{6,4},{7,5},{8,10},{9,11},{10,... | collective-permute-start | bytes 589832 | tf_op jit(solution)/shard_map/ppermute | solution.py:57
  59.1 7.0 %collective-permute-start.26 = (bf16[2,2,96,256]{3,2,1,0:T(8,128)(2,1)S(1)}, bf16[2,2,96,256]{3,2,1,0:T(8,128)(2,1)S(1)}, u32[]{:S(2)}, u32[]{:S(2)}) collective-permute-start(bf16[2,2,96,256]{3,2,1,0:T(8,128)(2,1)S(1)} %get-tuple-element.100), channel_id=1, source_target_pairs={{0,4},{1,5},{2,6},{3,7},{4,0},{5,1},{6,2},{7,3},{8,12},{9,13},{10,... | collective-permute-start | bytes 589832 | tf_op jit(solution)/shard_map/ppermute | solution.py:57
  59.8 3.9 %collective-permute-start.22 = (bf16[96,256]{1,0:T(8,128)(2,1)S(1)}, bf16[96,256]{1,0:T(8,128)(2,1)S(1)}, u32[]{:S(2)}, u32[]{:S(2)}) collective-permute-start(bf16[96,256]{1,0:T(8,128)(2,1)S(1)} %shared_hidden.1.a_ref), channel_id=1, source_target_pairs={{0,1},{1,0},{2,3},{3,2},{4,5},{5,4},{6,7},{7,6},{8,9},{9,8},{10,11... | collective-permute-start | bytes 147464 | tf_op jit(solution)/shard_map/ppermute | solution.py:57
  64.8 4.7 %collective-permute-start.24 = (bf16[1,2,96,256]{3,2,1,0:T(8,128)(2,1)S(1)}, bf16[1,2,96,256]{3,2,1,0:T(8,128)(2,1)S(1)}, u32[]{:S(2)}, u32[]{:S(2)}) collective-permute-start(bf16[1,2,96,256]{3,2,1,0:T(8,128)(2,1)S(1)} %get-tuple-element.97), channel_id=1, source_target_pairs={{0,4},{1,5},{2,6},{3,7},{4,0},{5,1},{6,2},{7,3},{8,12},{9,13},{10,... | collective-permute-start | bytes 294920 | tf_op jit(solution)/shard_map/ppermute | solution.py:57
  66.2 4.7 %collective-permute-start.27 = (bf16[1,2,96,256]{3,2,1,0:T(8,128)(2,1)S(1)}, bf16[1,2,96,256]{3,2,1,0:T(8,128)(2,1)S(1)}, u32[]{:S(2)}, u32[]{:S(2)}) collective-permute-start(bf16[1,2,96,256]{3,2,1,0:T(8,128)(2,1)S(1)} %get-tuple-element.102), channel_id=1, source_target_pairs={{0,2},{1,3},{2,0},{3,1},{4,6},{5,7},{6,4},{7,5},{8,10},{9,11},{10,... | collective-permute-start | bytes 294920 | tf_op jit(solution)/shard_map/ppermute | solution.py:57
  69.5 4.9 %collective-permute-start.25 = (bf16[96,256]{1,0:T(8,128)(2,1)S(1)}, bf16[96,256]{1,0:T(8,128)(2,1)S(1)}, u32[]{:S(2)}, u32[]{:S(2)}) collective-permute-start(bf16[96,256]{1,0:T(8,128)(2,1)S(1)} %get-tuple-element.99), channel_id=1, source_target_pairs={{0,8},{8,0},{16,24},{24,16},{1,9},{9,1},{17,25},{25,17},{2,10},{10... | collective-permute-start | bytes 147464 | tf_op jit(solution)/shard_map/ppermute | solution.py:57
  70.9 6.1 %collective-permute-start.28 = (bf16[96,256]{1,0:T(8,128)(2,1)S(1)}, bf16[96,256]{1,0:T(8,128)(2,1)S(1)}, u32[]{:S(2)}, u32[]{:S(2)}) collective-permute-start(bf16[96,256]{1,0:T(8,128)(2,1)S(1)} %get-tuple-element.103), channel_id=1, source_target_pairs={{0,16},{8,24},{16,0},{24,8},{1,17},{9,25},{17,1},{25,9},{2,18},{10... | collective-permute-start | bytes 147464 | tf_op jit(solution)/shard_map/ppermute | solution.py:57
  72.7 5.9 %collective-permute-start.29 = (bf16[96,256]{1,0:T(8,128)(2,1)S(1)}, bf16[96,256]{1,0:T(8,128)(2,1)S(1)}, u32[]{:S(2)}, u32[]{:S(2)}) collective-permute-start(bf16[96,256]{1,0:T(8,128)(2,1)S(1)} %get-tuple-element.104), channel_id=1, source_target_pairs={{0,24},{8,16},{16,8},{24,0},{1,25},{9,17},{17,9},{25,1},{2,26},{10... | collective-permute-start | bytes 147464 | tf_op jit(solution)/shard_map/ppermute | solution.py:57
